TPU v7x, 32 devices: a whole 2x2x4 slice. The times are simulated.
32 devices in a mesh: row: 4 (over y, core), col: 8 (over z, x).
Axes of the slice: x: 2, y: 2, z: 4, core: 2. Of those that a mesh axis runs over, the one named last changes fastest.
Arguments:
- grad: bfloat16 [8192, 4096], P('row', 'col'), may hold values from -6 to 6
- basis_left: bfloat16 [8192, 8192], P('row', 'col'), may hold values from -0.0625 to 0.0625
- basis_right: bfloat16 [4096, 4096], P('row', 'col'), may hold values from -0.09375 to 0.09375
- first_moment: float32 [8192, 4096], P('col', 'row'), may hold values from -6 to 6
- second_moment: float32 [8192, 4096], P('col', 'row'), may hold values from 0.25 to 4
Outputs:
- update: bfloat16 [8192, 4096], P('row', 'col')
- first_new: float32 [8192, 4096], P('col', 'row')
- second_new: float32 [8192, 4096], P('col', 'row')
All inputs are finite; a program needn't handle non-finite values.
Results may differ from a plain program's by a relative error of at most 0.029.
Values may be sent and summed in bfloat16 or wider, within the bound.
No kernel may reach another device: no remote copies, remote signals or barrier semaphores. Data moves between devices by JAX's collectives and lax.ppermute only.
A program may use at most 128 MiB of HBM per device.

v0:
```python
import functools

import jax
import jax.numpy as jnp
from jax import lax
from jax.experimental import pallas as pl
from jax.experimental.pallas import tpu as pltpu
from jax.sharding import PartitionSpec as P

BF16 = jnp.bfloat16
F32 = jnp.float32


def dot(a, b, contract):
    return lax.dot_general(a, b, ((contract[:1], contract[1:]), ((), ())), preferred_element_type=F32)


def tie(x, *earlier):
    return lax.optimization_barrier((x, *earlier))[0]


def moments(first, second, rot):
    first = 0.9 * first + 0.1 * rot
    second = 0.95 * second + 0.05 * rot * rot
    return first, second, (first / (jnp.sqrt(second) + 1e-08)).astype(BF16)


def moments_kernel(peer_ref, rot_ref, first_ref, second_ref, *refs):
    first_new, second_new, direction = refs[-3:]
    first_new[...], second_new[...], direction[...] = moments(
        first_ref[...], second_ref[...], rot_ref[0].astype(F32)
    )


def moments_at(peer, n_row, sub, rot, first_moment, second_moment, before):
    blocks, rows, _ = rot.shape
    block = min(rows, 512)
    packed_rot = pl.BlockSpec((1, block, sub), lambda q, i, p: (q, i, 0))
    at_peer = pl.BlockSpec((block, sub), lambda q, i, p: (i, q * n_row + p[0]))
    packed = pl.BlockSpec((block, sub), lambda q, i, p: (i, q))
    kept = [pl.BlockSpec(memory_space=pl.ANY)] * len(before)
    out = jax.ShapeDtypeStruct(first_moment.shape, F32)
    return pl.pallas_call(
        moments_kernel,
        grid_spec=pltpu.PrefetchScalarGridSpec(
            num_scalar_prefetch=1,
            grid=(blocks, rows // block),
            in_specs=[packed_rot, at_peer, at_peer] + kept,
            out_specs=[at_peer, at_peer, packed],
        ),
        out_shape=[out, out, jax.ShapeDtypeStruct((rows, blocks * sub), BF16)],
        input_output_aliases={4: 0, 5: 1} if before else {},
        cost_estimate=pl.CostEstimate(
            flops=10 * rot.size, bytes_accessed=20 * rot.size, transcendentals=2 * rot.size
        ),
    )(peer.reshape(1), rot, first_moment, second_moment, *before)


def moments_sliced(peer, n_row, sub, rot, first_moment, second_moment, before):
    first_new, second_new = before if before else (first_moment, second_moment)
    directions = []
    for q in range(rot.shape[0]):
        start = (q * n_row + peer) * sub
        first, second, direction = moments(
            lax.dynamic_slice_in_dim(first_moment, start, sub, 1),
            lax.dynamic_slice_in_dim(second_moment, start, sub, 1),
            rot[q].astype(F32),
        )
        first_new = lax.dynamic_update_slice_in_dim(first_new, first, start, 1)
        second_new = lax.dynamic_update_slice_in_dim(second_new, second, start, 1)
        directions.append(direction)
    return first_new, second_new, jnp.concatenate(directions, axis=1)


def solution(mesh):
    n_row, n_col = mesh.shape["row"], mesh.shape["col"]
    n_a = 4
    n_b = n_col // n_a
    per_row = n_col // n_row

    def b_shift(x, db):
        perm = [(a * n_b + b, a * n_b + (b + db) % n_b) for a in range(n_a) for b in range(n_b)]
        return lax.ppermute(x, "col", perm)

    def a_shift(x, by):
        perm = [(a * n_b + b, (a + by) % n_a * n_b + b) for a in range(n_a) for b in range(n_b)]
        return lax.ppermute(x, "col", perm)

    def row_xor(x, k):
        return lax.ppermute(x, "row", [(r, r ^ k) for r in range(n_row)])

    def per_device(grad, basis_left, basis_right, first_moment, second_moment):
        last = {}

        def in_turn(link, x, move, depth):
            before = last.setdefault(link, [])
            if len(before) >= depth:
                x = tie(x, before[-depth])
            before.append(move(x))
            return before[-1]

        def across_b(x, k, depth=1):
            return in_turn("b", x, lambda y: b_shift(y, k), depth)

        def across_rows(x, k, depth=1):
            return row_xor(x, k) if k == 1 else in_turn("rows", x, lambda y: row_xor(y, k), depth)

        def half_sum(theirs, mine):
            got = row_xor(theirs().astype(BF16), 1)
            mine = (mine() + got.astype(F32)).astype(BF16)
            k = 2
            while k < n_row:
                got = across_rows(mine, k)
                mine = (mine.astype(F32) + got.astype(F32)).astype(BF16)
                k *= 2
            return mine, row_xor(mine, 1)

        r = lax.axis_index("row")
        c = lax.axis_index("col")
        a, b = c // n_b, c % n_b
        core = r % 2
        width = grad.shape[1]
        half = width // 2
        sub = width // n_row
        own_i = basis_left.shape[1]
        row_n = basis_right.shape[0]

        def n_at(s, h):
            return (a - s) % n_a * width + h * half

        def halves(x):
            return x[:, :half], x[:, half:]

        grad = jnp.concatenate(
            [lax.dynamic_slice_in_dim(grad, h * half, half, 1) for h in (core, 1 - core)], axis=1
        )
        grad = lax.optimization_barrier(grad)
        below, above = a_shift(grad, 1), a_shift(grad, -1)
        grads = [grad, below, a_shift(below, 1), above]

        own_left = tie(basis_left, grad)
        lefts = [own_left] + [across_b(own_left, -k) for k in range(1, n_b)]

        right_after = tie(basis_right, grad)
        right_n = jnp.zeros((n_row * row_n, sub), BF16)
        for k in range(n_row):
            part = lax.dynamic_slice_in_dim(right_after, (r ^ k) * sub, sub, 1)
            if k:
                part = across_rows(part, k, 2)
            right_n = lax.dynamic_update_slice_in_dim(right_n, part, (r ^ k) * row_n, 0)
        by_b = right_n.reshape(n_a, n_b, width, sub)

        def rows_of(which):
            return lax.dynamic_index_in_dim(by_b, which, 1, keepdims=False).reshape(n_a * width, sub)

        got = [rows_of(b)] + [across_b(rows_of((b + k) % n_b), k) for k in range(1, n_b)]
        stacked = jnp.stack(got, 0)
        right = [lax.dynamic_index_in_dim(stacked, (b - q) % n_b, 0, keepdims=False) for q in range(n_b)]
        right = jnp.concatenate(right, axis=1)

        near, far = (0, 1, 3), 2
        turns = [(k, s) for k in range(n_b) for s in near] + [(k, far) for k in reversed(range(n_b))]
        rotated = [jnp.zeros((own_i, n_a * width), BF16) for _ in range(n_b)]
        for k, s in turns:
            if (k, s) == (1, 0):
                lefts[1:] = tie(tuple(lefts[1:]), last["rows"][-1])
                sent = tie(right, last["rows"][-1])
                below, above = a_shift(sent, 1), a_shift(sent, -1)
                rights = [right, below, a_shift(below, 1), above]
            if (k, s) == (0, 1):
                grads[s] = tie(grads[s], right_n)
            if (k, s) in ((0, 3), (n_b - 1, far)):
                grads[s] = tie(grads[s], last["rows"][-1])
            g = grads[s]
            g_mine, g_theirs = halves(g)
            mine, theirs = half_sum(
                lambda: dot(lefts[k], g_theirs, (0, 0)), lambda: dot(lefts[k], g_mine, (0, 0))
            )
            rotated[k] = lax.dynamic_update_slice_in_dim(rotated[k], mine, n_at(s, core), 1)
            rotated[k] = lax.dynamic_update_slice_in_dim(rotated[k], theirs, n_at(s, 1 - core), 1)
        left = jnp.concatenate(lefts, axis=1)

        rot_k = jnp.zeros((n_col, own_i, sub), BF16)
        right_k = jnp.zeros((n_a * width, n_col * sub), BF16)
        swapped = []
        for t in near + (far,):
            right_t = tie(rights[t], *swapped[-2:-1])
            rot = dot(rotated[0], right_t, (1, 0))
            for k in range(1, n_b):
                part = dot(rotated[k], right_t, (1, 0))
                swapped.append(across_b(part.astype(BF16), k))
                rot = rot + swapped[-1].astype(F32)
            rot = rot.astype(BF16)
            for q in range(n_b):
                block = (a - t) % n_a * n_b + q
                at = (block // per_row ^ r) * per_row + block % per_row
                columns = slice(q * sub, (q + 1) * sub)
                rot_k = lax.dynamic_update_index_in_dim(rot_k, rot[:, columns], at, 0)
                right_k = lax.dynamic_update_slice_in_dim(right_k, right_t[:, columns], at * sub, 1)

        step = moments_at if sub % 128 == 0 else moments_sliced
        rots = [rot_k[k * per_row : (k + 1) * per_row] for k in range(n_row)]
        rots[1:] = [across_rows(rots[k], k, 2) for k in range(1, n_row)]

        kept, by_rows = (), [[] for _ in range(n_b)]
        for k, rot in enumerate(rots):
            if k >= 2:
                kept = tie(tuple(kept), by_rows[1][k - 2])
            *kept, direction = step(r ^ k, n_row, sub, rot, first_moment, second_moment, tuple(kept))
            if k:
                direction = across_rows(direction, k, 2)
            by_rows[0].append(direction)
            for q in range(1, n_b):
                by_rows[q].append(across_b(direction, -q, 2))
        first_new, second_new = kept
        by_rows = [jnp.concatenate(ds, axis=1) for ds in by_rows]
        direction = jnp.concatenate(by_rows, axis=0)

        def back(s, parts):
            r_mine = lax.dynamic_slice_in_dim(right_k, n_at(s, core), half, 0)
            r_theirs = lax.dynamic_slice_in_dim(right_k, n_at(s, 1 - core), half, 0)
            u_mine = u_theirs = 0.0
            for d, l in parts:
                w_mine, w_theirs = half_sum(lambda: dot(d, r_theirs, (1, 1)), lambda: dot(d, r_mine, (1, 1)))
                u_mine = u_mine + dot(l, w_mine, (1, 0))
                u_theirs = u_theirs + dot(l, w_theirs, (1, 0))
            return u_mine, u_theirs

        def joined(u):
            return jnp.concatenate([x.astype(BF16) for x in u], axis=1)

        whole = [(direction, left)]
        passed = halves(a_shift(joined(back(2, list(zip(by_rows, lefts)))), 1))
        behind = halves(a_shift(joined(back(1, whole)), -1))
        ahead = lax.optimization_barrier(back(3, whole))
        ahead = halves(a_shift(joined([u + x.astype(F32) for u, x in zip(ahead, passed)]), 1))
        own = lax.optimization_barrier(back(0, whole))
        u_mine, u_theirs = [
            (u + x.astype(F32) + y.astype(F32)).astype(BF16) for u, x, y in zip(own, behind, ahead)
        ]
        update = jnp.where(
            core == 0,
            jnp.concatenate([u_mine, u_theirs], axis=1),
            jnp.concatenate([u_theirs, u_mine], axis=1),
        )
        return update, first_new, second_new

    in_specs = (P("row", "col"), P("row", "col"), P("row", "col"), P("col", "row"), P("col", "row"))
    out_specs = (P("row", "col"), P("col", "row"), P("col", "row"))
    return jax.shard_map(per_device, mesh=mesh, in_specs=in_specs, out_specs=out_specs, check_vma=False)
```

profile of v0, /device:TPU:0, one launch (start us, length us, event | category | flops | bytes accessed | tf_op | source)
XLA Modules:
  0.0 574.8 jit_solution(7361359875459839691)
XLA Ops:
  2.5 3.1 collective-permute-start.2
  11.8 4.3 convolution_convert_fusion.17
  18.7 5.8 %collective-permute-done.4 = bf16[1024,128]{1,0:T(8,128)(2,1)} collective-permute-done((bf16[1024,128]{1,0:T(8,128)(2,1)}, bf16[1024,128]{1,0:T(8,128)(2,1)}, u32[]{:S(2)}, u32[]{:S(2)}) %collective-permute-start.4) | collective-permute-done | bytes 262176 | tf_op jit(solution)/shard_map/ppermute | solution.py:90
  25.6 28.7 %collective-permute-done.2 = bf16[2048,512]{1,0:T(8,128)(2,1)} collective-permute-done((bf16[2048,512]{1,0:T(8,128)(2,1)S(1)}, bf16[2048,512]{1,0:T(8,128)(2,1)}, u32[]{:S(2)}, u32[]{:S(2)}) %collective-permute-start.2) | collective-permute-done | bytes 2097184 | tf_op jit(solution)/shard_map/ppermute | solution.py:87
  54.2 3.8 convolution_convert_fusion.18
  61.3 3.3 fusion.5
  64.7 9.2 %collective-permute-done.8 = bf16[1024,256]{1,0:T(8,128)(2,1)S(1)} collective-permute-done((bf16[1024,256]{1,0:T(8,128)(2,1)S(1)}, bf16[1024,256]{1,0:T(8,128)(2,1)S(1)}, u32[]{:S(2)}, u32[]{:S(2)}) %collective-permute-start.8) | collective-permute-done | bytes 524320 | tf_op jit(solution)/shard_map/ppermute | solution.py:90
  76.9 2.4 constant_dynamic-update-slice_fusion.25
  79.4 18.4 %collective-permute-done.1 = bf16[2048,512]{1,0:T(8,128)(2,1)} collective-permute-done((bf16[2048,512]{1,0:T(8,128)(2,1)S(1)}, bf16[2048,512]{1,0:T(8,128)(2,1)}, u32[]{:S(2)}, u32[]{:S(2)}) %collective-permute-start.1) | collective-permute-done | bytes 2097184 | tf_op jit(solution)/shard_map/ppermute | solution.py:87
  97.7 3.3 convolution_convert_fusion.16
  105.6 4.2 fusion.6
  113.5 10.0 %collective-permute-done.11 = bf16[1024,256]{1,0:T(8,128)(2,1)S(1)} collective-permute-done((bf16[1024,256]{1,0:T(8,128)(2,1)S(1)}, bf16[1024,256]{1,0:T(8,128)(2,1)S(1)}, u32[]{:S(2)}, u32[]{:S(2)}) %collective-permute-start.11) | collective-permute-done | bytes 524320 | tf_op jit(solution)/shard_map/ppermute | solution.py:90
  123.6 3.5 convolution_convert_fusion.13
  127.0 3.8 convolution_convert_fusion.14
  131.7 3.8 convolution_convert_fusion.15
  135.5 3.5 fusion.9
  140.6 2.6 constant_dynamic-update-slice_fusion
  145.0 5.0 fusion.8
  149.9 3.4 collective-permute-done.19
  158.1 3.8 fusion.7
  161.9 5.0 collective-permute-done.20
  168.8 36.6 %collective-permute-start.35 = (bf16[2048,256]{1,0:T(8,128)(2,1)S(1)}, bf16[2048,256]{1,0:T(8,128)(2,1)S(1)}, u32[]{:S(2)}, u32[]{:S(2)}) collective-permute-start(bf16[2048,256]{1,0:T(8,128)(2,1)S(1)} %pad_maximum_fusion.5), channel_id=1, source_target_pairs={{0,6},{1,7},{2,0},{3,1},{4,2},{5,3},{6,4},{7,5},{8,14},{9,15},{10,... | collective-permute-start | bytes 3145736 | tf_op jit(solution)/shard_map/ppermute | solution.py:87
  205.6 3.5 convolution_convert_fusion.11
  211.6 3.5 fusion.11
  217.1 12.2 %collective-permute-done.24 = bf16[1024,256]{1,0:T(8,128)(2,1)S(1)} collective-permute-done((bf16[1024,256]{1,0:T(8,128)(2,1)S(1)}, bf16[1024,256]{1,0:T(8,128)(2,1)S(1)}, u32[]{:S(2)}, u32[]{:S(2)}) %collective-permute-start.24) | collective-permute-done | bytes 524320 | tf_op jit(solution)/shard_map/ppermute | solution.py:90
  230.1 2.5 broadcast_in_dim.44
  233.5 9.1 %collective-permute-done.25 = bf16[1024,256]{1,0:T(8,128)(2,1)S(1)} collective-permute-done((bf16[1024,256]{1,0:T(8,128)(2,1)S(1)}, bf16[1024,256]{1,0:T(8,128)(2,1)S(1)}, u32[]{:S(2)}, u32[]{:S(2)}) %collective-permute-start.25) | collective-permute-done | bytes 524320 | tf_op jit(solution)/shard_map/ppermute | solution.py:90
  246.7 5.2 collective-permute-done.33
  255.1 3.5 collective-permute-done.32
  263.1 9.1 %collective-permute-done.34 = bf16[1024,256]{1,0:T(8,128)(2,1)S(1)} collective-permute-done((bf16[1024,256]{1,0:T(8,128)(2,1)S(1)}, bf16[1024,256]{1,0:T(8,128)(2,1)S(1)}, u32[]{:S(2)}, u32[]{:S(2)}) %collective-permute-start.34) | collective-permute-done | bytes 524320 | tf_op jit(solution)/shard_map/ppermute | solution.py:83
  275.0 6.2 %collective-permute-done.37 = bf16[2048,256]{1,0:T(8,128)(2,1)S(1)} collective-permute-done((bf16[2048,256]{1,0:T(8,128)(2,1)S(1)}, bf16[2048,256]{1,0:T(8,128)(2,1)S(1)}, u32[]{:S(2)}, u32[]{:S(2)}) %collective-permute-start.37) | collective-permute-done | bytes 1048608 | tf_op jit(solution)/shard_map/ppermute | solution.py:87
  282.4 2.4 collective-permute-done.36
  287.6 8.9 %collective-permute-done.38 = bf16[1024,256]{1,0:T(8,128)(2,1)S(1)} collective-permute-done((bf16[1024,256]{1,0:T(8,128)(2,1)S(1)}, bf16[1024,256]{1,0:T(8,128)(2,1)S(1)}, u32[]{:S(2)}, u32[]{:S(2)}) %collective-permute-start.38) | collective-permute-done | bytes 524320 | tf_op jit(solution)/shard_map/ppermute | solution.py:83
  300.8 4.1 shard_map.76
  305.7 4.1 shard_map.77
  316.0 11.2 %collective-permute-done.42 = bf16[1024,256]{1,0:T(8,128)(2,1)S(1)} collective-permute-done((bf16[1024,256]{1,0:T(8,128)(2,1)}, bf16[1024,256]{1,0:T(8,128)(2,1)S(1)}, u32[]{:S(2)}, u32[]{:S(2)}) %collective-permute-start.42) | collective-permute-done | bytes 524320 | tf_op jit(solution)/shard_map/ppermute | solution.py:83
  328.9 4.0 shard_map.78
  334.8 2.5 collective-permute-done.45
  338.0 4.3 shard_map.79
  343.3 5.5 collective-permute-done.43
  352.5 5.4 collective-permute-done.46
  362.2 10.4 %collective-permute-done.48 = bf16[1024,256]{1,0:T(8,128)(2,1)S(1)} collective-permute-done((bf16[1024,256]{1,0:T(8,128)(2,1)S(1)}, bf16[1024,256]{1,0:T(8,128)(2,1)S(1)}, u32[]{:S(2)}, u32[]{:S(2)}) %collective-permute-start.48) | collective-permute-done | bytes 524320 | tf_op jit(solution)/shard_map/ppermute | solution.py:83
  380.1 2.3 convolution_convert_fusion.1
  384.7 6.1 %collective-permute-done.54 = bf16[1024,256]{1,0:T(8,128)(2,1)S(1)} collective-permute-done((bf16[1024,256]{1,0:T(8,128)(2,1)S(1)}, bf16[1024,256]{1,0:T(8,128)(2,1)S(1)}, u32[]{:S(2)}, u32[]{:S(2)}) %collective-permute-start.54) | collective-permute-done | bytes 524320 | tf_op jit(solution)/shard_map/ppermute | solution.py:90
  391.8 2.3 convolution_convert_fusion.2
  394.9 9.4 %collective-permute-done.55 = bf16[1024,256]{1,0:T(8,128)(2,1)S(1)} collective-permute-done((bf16[1024,256]{1,0:T(8,128)(2,1)S(1)}, bf16[1024,256]{1,0:T(8,128)(2,1)S(1)}, u32[]{:S(2)}, u32[]{:S(2)}) %collective-permute-start.55) | collective-permute-done | bytes 524320 | tf_op jit(solution)/shard_map/ppermute | solution.py:90
  404.5 2.3 fusion.2
  406.8 3.6 fusion.74
  412.7 2.6 fusion.1
  415.3 2.3 fusion
  417.7 3.6 fusion.75
  423.9 12.2 %collective-permute-done.56 = bf16[2048,256]{1,0:T(8,128)(2,1)S(1)} collective-permute-done((bf16[2048,256]{1,0:T(8,128)(2,1)S(1)}, bf16[2048,256]{1,0:T(8,128)(2,1)S(1)}, u32[]{:S(2)}, u32[]{:S(2)}) %collective-permute-start.56) | collective-permute-done | bytes 1048608 | tf_op jit(solution)/shard_map/ppermute | solution.py:90
  437.3 2.3 convolution_convert_fusion.4
  439.7 21.1 %collective-permute-done.57 = bf16[2048,256]{1,0:T(8,128)(2,1)S(1)} collective-permute-done((bf16[2048,256]{1,0:T(8,128)(2,1)S(1)}, bf16[2048,256]{1,0:T(8,128)(2,1)S(1)}, u32[]{:S(2)}, u32[]{:S(2)}) %collective-permute-start.57) | collective-permute-done | bytes 1048608 | tf_op jit(solution)/shard_map/ppermute | solution.py:90
  462.1 2.3 convolution_convert_fusion.3
  466.0 11.5 %collective-permute-start.61 = (bf16[2048,512]{1,0:T(8,128)(2,1)}, bf16[2048,512]{1,0:T(8,128)(2,1)S(1)}, u32[]{:S(2)}, u32[]{:S(2)}) collective-permute-start(bf16[2048,512]{1,0:T(8,128)(2,1)} %pad_maximum_fusion.2), channel_id=1, source_target_pairs={{0,6},{1,7},{2,0},{3,1},{4,2},{5,3},{6,4},{7,5},{8,14},{9,15},{10,... | collective-permute-start | bytes 6291464 | tf_op jit(solution)/shard_map/ppermute | solution.py:87
  477.6 2.3 fusion.72
  479.9 2.4 fusion.73
  484.3 2.5 collective-permute-done.58
  487.1 5.9 %fusion.70 = f32[2048,256]{1,0:T(8,128)S(1)} fusion(bf16[2048,2048]{1,0:T(8,128)(2,1)} %copy-done.6, bf16[2048,256]{1,0:T(8,128)(2,1)S(1)} %add_convert_fusion.6), kind=kOutput, calls=%fused_computation.187 | convolution fusion | flops 2147483648 | bytes 11534336 | tf_op jit(solution)/shard_map/dot_general | solution.py:15
  493.0 6.1 %fusion.71 = f32[2048,256]{1,0:T(8,128)S(1)} fusion(bf16[2048,2048]{1,0:T(8,128)(2,1)} %copy-done.6, bf16[2048,256]{1,0:T(8,128)(2,1)} %collective-permute-done.59), kind=kOutput, calls=%fused_computation.188 | convolution fusion | flops 2147483648 | bytes 11534336 | tf_op jit(solution)/shard_map/dot_general | solution.py:15
  499.1 26.2 %collective-permute-done.61 = bf16[2048,512]{1,0:T(8,128)(2,1)S(1)} collective-permute-done((bf16[2048,512]{1,0:T(8,128)(2,1)}, bf16[2048,512]{1,0:T(8,128)(2,1)S(1)}, u32[]{:S(2)}, u32[]{:S(2)}) %collective-permute-start.61) | collective-permute-done | bytes 2097184 | tf_op jit(solution)/shard_map/ppermute | solution.py:87
  525.3 44.8 %collective-permute-done.66 = bf16[2048,512]{1,0:T(8,128)(2,1)} collective-permute-done((bf16[2048,512]{1,0:T(8,128)(2,1)}, bf16[2048,512]{1,0:T(8,128)(2,1)}, u32[]{:S(2)}, u32[]{:S(2)}) %collective-permute-start.66) | collective-permute-done | bytes 2097184 | tf_op jit(solution)/shard_map/ppermute | solution.py:87
  570.1 2.4 add_convert_fusion.1
  (221 shorter events, 111.1 us)
Async XLA Ops:
  2.5 51.7 %collective-permute-start.2 = (bf16[2048,512]{1,0:T(8,128)(2,1)S(1)}, bf16[2048,512]{1,0:T(8,128)(2,1)}, u32[]{:S(2)}, u32[]{:S(2)}) collective-permute-start(bf16[2048,512]{1,0:T(8,128)(2,1)S(1)} %pad_maximum_fusion.1), channel_id=1, source_target_pairs={{0,2},{1,3},{2,4},{3,5},{4,6},{5,7},{6,0},{7,1},{8,10},{9,11},{10,... | collective-permute-start | bytes 6291464 | tf_op jit(solution)/shard_map/ppermute | solution.py:87
  5.6 92.1 %collective-permute-start.1 = (bf16[2048,512]{1,0:T(8,128)(2,1)S(1)}, bf16[2048,512]{1,0:T(8,128)(2,1)}, u32[]{:S(2)}, u32[]{:S(2)}) collective-permute-start(bf16[2048,512]{1,0:T(8,128)(2,1)S(1)} %pad_maximum_fusion.1), channel_id=1, source_target_pairs={{0,6},{1,7},{2,0},{3,1},{4,2},{5,3},{6,4},{7,5},{8,14},{9,15},{10,... | collective-permute-start | bytes 6291464 | tf_op jit(solution)/shard_map/ppermute | solution.py:87
  9.9 15.5 %collective-permute-start.5 = (bf16[1024,128]{1,0:T(8,128)(2,1)}, bf16[1024,128]{1,0:T(8,128)(2,1)S(1)}, u32[]{:S(2)}, u32[]{:S(2)}) collective-permute-start(bf16[1024,128]{1,0:T(8,128)(2,1)} %get-tuple-element.143), channel_id=1, source_target_pairs={{0,24},{8,16},{16,8},{24,0},{1,25},{9,17},{17,9},{25,1},{2,26},{10... | collective-permute-start | bytes 786440 | tf_op jit(solution)/shard_map/ppermute | solution.py:90
  10.6 13.9 %collective-permute-start.4 = (bf16[1024,128]{1,0:T(8,128)(2,1)}, bf16[1024,128]{1,0:T(8,128)(2,1)}, u32[]{:S(2)}, u32[]{:S(2)}) collective-permute-start(bf16[1024,128]{1,0:T(8,128)(2,1)} %get-tuple-element.144), channel_id=1, source_target_pairs={{0,16},{8,24},{16,0},{24,8},{1,17},{9,25},{17,1},{25,9},{2,18},{10... | collective-permute-start | bytes 786440 | tf_op jit(solution)/shard_map/ppermute | solution.py:90
  16.1 107.5 %collective-permute-start = (bf16[2048,1024]{1,0:T(8,128)(2,1)}, bf16[2048,1024]{1,0:T(8,128)(2,1)}, u32[]{:S(2)}, u32[]{:S(2)}) collective-permute-start(bf16[2048,1024]{1,0:T(8,128)(2,1)} %param.6), channel_id=1, source_target_pairs={{0,1},{1,0},{2,3},{3,2},{4,5},{5,4},{6,7},{7,6},{8,9},{9,8},{10,11... | collective-permute-start | bytes 12582920 | tf_op jit(solution)/shard_map/ppermute | solution.py:83
  24.5 33.6 %collective-permute-start.7 = (bf16[1024,256]{1,0:T(8,128)(2,1)}, bf16[1024,256]{1,0:T(8,128)(2,1)S(1)}, u32[]{:S(2)}, u32[]{:S(2)}) collective-permute-start(bf16[1024,256]{1,0:T(8,128)(2,1)} %convolution_convert_fusion.17), channel_id=1, source_target_pairs={{0,8},{8,0},{16,24},{24,16},{1,9},{9,1},{17,25},{25,17},{2,10},{10... | collective-permute-start | bytes 1572872 | tf_op jit(solution)/shard_map/ppermute | solution.py:90
  59.5 14.4 %collective-permute-start.8 = (bf16[1024,256]{1,0:T(8,128)(2,1)S(1)}, bf16[1024,256]{1,0:T(8,128)(2,1)S(1)}, u32[]{:S(2)}, u32[]{:S(2)}) collective-permute-start(bf16[1024,256]{1,0:T(8,128)(2,1)S(1)} %add_convert_fusion.17), channel_id=1, source_target_pairs={{0,16},{8,24},{16,0},{24,8},{1,17},{9,25},{17,1},{25,9},{2,18},{10... | collective-permute-start | bytes 1572872 | tf_op jit(solution)/shard_map/ppermute | solution.py:90
  74.7 23.1 %collective-permute-start.9 = (bf16[1024,256]{1,0:T(8,128)(2,1)}, bf16[1024,256]{1,0:T(8,128)(2,1)}, u32[]{:S(2)}, u32[]{:S(2)}) collective-permute-start(bf16[1024,256]{1,0:T(8,128)(2,1)} %fusion.5), channel_id=1, source_target_pairs={{0,16},{8,24},{16,0},{24,8},{1,17},{9,25},{17,1},{25,9},{2,18},{10... | collective-permute-start | bytes 1572872 | tf_op jit(solution)/shard_map/ppermute | solution.py:90
  79.4 21.7 %collective-permute-start.12 = (bf16[1024,256]{1,0:T(8,128)(2,1)}, bf16[1024,256]{1,0:T(8,128)(2,1)}, u32[]{:S(2)}, u32[]{:S(2)}) collective-permute-start(bf16[1024,256]{1,0:T(8,128)(2,1)} %get-tuple-element.120), channel_id=1, source_target_pairs={{0,8},{8,0},{16,24},{24,16},{1,9},{9,1},{17,25},{25,17},{2,10},{10... | collective-permute-start | bytes 1572872 | tf_op jit(solution)/shard_map/ppermute | solution.py:90
  101.1 4.5 collective-permute-start.10
  105.1 8.4 %collective-permute-start.13 = (bf16[1024,256]{1,0:T(8,128)(2,1)S(1)}, bf16[1024,256]{1,0:T(8,128)(2,1)S(1)}, u32[]{:S(2)}, u32[]{:S(2)}) collective-permute-start(bf16[1024,256]{1,0:T(8,128)(2,1)S(1)} %get-tuple-element.118), channel_id=1, source_target_pairs={{0,8},{8,0},{16,24},{24,16},{1,9},{9,1},{17,25},{25,17},{2,10},{10... | collective-permute-start | bytes 1572872 | tf_op jit(solution)/shard_map/ppermute | solution.py:90
  109.7 13.8 %collective-permute-start.11 = (bf16[1024,256]{1,0:T(8,128)(2,1)S(1)}, bf16[1024,256]{1,0:T(8,128)(2,1)S(1)}, u32[]{:S(2)}, u32[]{:S(2)}) collective-permute-start(bf16[1024,256]{1,0:T(8,128)(2,1)S(1)} %fusion.6), channel_id=1, source_target_pairs={{0,16},{8,24},{16,0},{24,8},{1,17},{9,25},{17,1},{25,9},{2,18},{10... | collective-permute-start | bytes 1572872 | tf_op jit(solution)/shard_map/ppermute | solution.py:90
  112.1 93.4 %collective-permute-start.15 = (bf16[2048,512]{1,0:T(8,128)(2,1)}, bf16[2048,512]{1,0:T(8,128)(2,1)S(1)}, u32[]{:S(2)}, u32[]{:S(2)}) collective-permute-start(bf16[2048,512]{1,0:T(8,128)(2,1)} %collective-permute-done.2), channel_id=1, source_target_pairs={{0,2},{1,3},{2,4},{3,5},{4,6},{5,7},{6,0},{7,1},{8,10},{9,11},{10,... | collective-permute-start | bytes 6291464 | tf_op jit(solution)/shard_map/ppermute | solution.py:87
  130.8 4.7 collective-permute-start.18
  131.1 102.3 %collective-permute-start.14 = (bf16[1024,256]{1,0:T(8,128)(2,1)S(1)}, bf16[1024,256]{1,0:T(8,128)(2,1)S(1)}, u32[]{:S(2)}, u32[]{:S(2)}) collective-permute-start(bf16[1024,256]{1,0:T(8,128)(2,1)S(1)} %get-tuple-element.116), channel_id=1, source_target_pairs={{0,8},{8,0},{16,24},{24,16},{1,9},{9,1},{17,25},{25,17},{2,10},{10... | collective-permute-start | bytes 1572872 | tf_op jit(solution)/shard_map/ppermute | solution.py:90
  131.6 11.8 %collective-permute-start.17 = (bf16[1024,256]{1,0:T(8,128)(2,1)S(1)}, bf16[1024,256]{1,0:T(8,128)(2,1)S(1)}, u32[]{:S(2)}, u32[]{:S(2)}) collective-permute-start(bf16[1024,256]{1,0:T(8,128)(2,1)S(1)} %convolution_convert_fusion.14), channel_id=1, source_target_pairs={{0,8},{8,0},{16,24},{24,16},{1,9},{9,1},{17,25},{25,17},{2,10},{10... | collective-permute-start | bytes 1572872 | tf_op jit(solution)/shard_map/ppermute | solution.py:90
  139.0 14.3 %collective-permute-start.19 = (bf16[1024,256]{1,0:T(8,128)(2,1)S(1)}, bf16[1024,256]{1,0:T(8,128)(2,1)S(1)}, u32[]{:S(2)}, u32[]{:S(2)}) collective-permute-start(bf16[1024,256]{1,0:T(8,128)(2,1)S(1)} %fusion.9), channel_id=1, source_target_pairs={{0,16},{8,24},{16,0},{24,8},{1,17},{9,25},{17,1},{25,9},{2,18},{10... | collective-permute-start | bytes 1572872 | tf_op jit(solution)/shard_map/ppermute | solution.py:90
  143.3 14.8 %collective-permute-start.16 = (bf16[1024,256]{1,0:T(8,128)(2,1)S(1)}, bf16[1024,256]{1,0:T(8,128)(2,1)S(1)}, u32[]{:S(2)}, u32[]{:S(2)}) collective-permute-start(bf16[1024,256]{1,0:T(8,128)(2,1)S(1)} %convolution_convert_fusion.15), channel_id=1, source_target_pairs={{0,8},{8,0},{16,24},{24,16},{1,9},{9,1},{17,25},{25,17},{2,10},{10... | collective-permute-start | bytes 1572872 | tf_op jit(solution)/shard_map/ppermute | solution.py:90
  143.5 14.2 %collective-permute-start.27 = (bf16[2048,128]{1,0:T(8,128)(2,1)S(1)}, bf16[2048,128]{1,0:T(8,128)(2,1)S(1)}, u32[]{:S(2)}, u32[]{:S(2)}) collective-permute-start(bf16[2048,128]{1,0:T(8,128)(2,1)S(1)} %bitcast.104), channel_id=1, source_target_pairs={{0,1},{1,0},{2,3},{3,2},{4,5},{5,4},{6,7},{7,6},{8,9},{9,8},{10,11... | collective-permute-start | bytes 1572872 | tf_op jit(solution)/shard_map/ppermute | solution.py:83
  153.4 13.5 %collective-permute-start.20 = (bf16[1024,256]{1,0:T(8,128)(2,1)S(1)}, bf16[1024,256]{1,0:T(8,128)(2,1)S(1)}, u32[]{:S(2)}, u32[]{:S(2)}) collective-permute-start(bf16[1024,256]{1,0:T(8,128)(2,1)S(1)} %fusion.8), channel_id=1, source_target_pairs={{0,16},{8,24},{16,0},{24,8},{1,17},{9,25},{17,1},{25,9},{2,18},{10... | collective-permute-start | bytes 1572872 | tf_op jit(solution)/shard_map/ppermute | solution.py:90
  157.7 10.7 %collective-permute-start.28 = (bf16[1024,256]{1,0:T(8,128)(2,1)S(1)}, bf16[1024,256]{1,0:T(8,128)(2,1)S(1)}, u32[]{:S(2)}, u32[]{:S(2)}) collective-permute-start(bf16[1024,256]{1,0:T(8,128)(2,1)S(1)} %get-tuple-element.128), channel_id=1, source_target_pairs={{0,8},{8,0},{16,24},{24,16},{1,9},{9,1},{17,25},{25,17},{2,10},{10... | collective-permute-start | bytes 1572872 | tf_op jit(solution)/shard_map/ppermute | solution.py:90
  166.8 38.8 %collective-permute-start.21 = (bf16[1024,256]{1,0:T(8,128)(2,1)S(1)}, bf16[1024,256]{1,0:T(8,128)(2,1)S(1)}, u32[]{:S(2)}, u32[]{:S(2)}) collective-permute-start(bf16[1024,256]{1,0:T(8,128)(2,1)S(1)} %fusion.7), channel_id=1, source_target_pairs={{0,16},{8,24},{16,0},{24,8},{1,17},{9,25},{17,1},{25,9},{2,18},{10... | collective-permute-start | bytes 1572872 | tf_op jit(solution)/shard_map/ppermute | solution.py:90
  168.6 40.8 %collective-permute-start.29 = (bf16[1024,256]{1,0:T(8,128)(2,1)S(1)}, bf16[1024,256]{1,0:T(8,128)(2,1)S(1)}, u32[]{:S(2)}, u32[]{:S(2)}) collective-permute-start(bf16[1024,256]{1,0:T(8,128)(2,1)S(1)} %get-tuple-element.126), channel_id=1, source_target_pairs={{0,8},{8,0},{16,24},{24,16},{1,9},{9,1},{17,25},{25,17},{2,10},{10... | collective-permute-start | bytes 1572872 | tf_op jit(solution)/shard_map/ppermute | solution.py:90
  168.8 86.3 %collective-permute-start.35 = (bf16[2048,256]{1,0:T(8,128)(2,1)S(1)}, bf16[2048,256]{1,0:T(8,128)(2,1)S(1)}, u32[]{:S(2)}, u32[]{:S(2)}) collective-permute-start(bf16[2048,256]{1,0:T(8,128)(2,1)S(1)} %pad_maximum_fusion.5), channel_id=1, source_target_pairs={{0,6},{1,7},{2,0},{3,1},{4,2},{5,3},{6,4},{7,5},{8,14},{9,15},{10,... | collective-permute-start | bytes 3145736 | tf_op jit(solution)/shard_map/ppermute | solution.py:87
  205.4 46.5 %collective-permute-start.33 = (bf16[2048,256]{1,0:T(8,128)(2,1)S(1)}, bf16[2048,256]{1,0:T(8,128)(2,1)S(1)}, u32[]{:S(2)}, u32[]{:S(2)}) collective-permute-start(bf16[2048,256]{1,0:T(8,128)(2,1)S(1)} %pad_maximum_fusion.5), channel_id=1, source_target_pairs={{0,2},{1,3},{2,4},{3,5},{4,6},{5,7},{6,0},{7,1},{8,10},{9,11},{10,... | collective-permute-start | bytes 3145736 | tf_op jit(solution)/shard_map/ppermute | solution.py:87
  209.7 5.5 collective-permute-start.30
  211.3 4.4 collective-permute-start.22
  215.1 14.2 %collective-permute-start.24 = (bf16[1024,256]{1,0:T(8,128)(2,1)S(1)}, bf16[1024,256]{1,0:T(8,128)(2,1)S(1)}, u32[]{:S(2)}, u32[]{:S(2)}) collective-permute-start(bf16[1024,256]{1,0:T(8,128)(2,1)S(1)} %fusion.11), channel_id=1, source_target_pairs={{0,16},{8,24},{16,0},{24,8},{1,17},{9,25},{17,1},{25,9},{2,18},{10... | collective-permute-start | bytes 1572872 | tf_op jit(solution)/shard_map/ppermute | solution.py:90
  229.3 13.3 %collective-permute-start.25 = (bf16[1024,256]{1,0:T(8,128)(2,1)S(1)}, bf16[1024,256]{1,0:T(8,128)(2,1)S(1)}, u32[]{:S(2)}, u32[]{:S(2)}) collective-permute-start(bf16[1024,256]{1,0:T(8,128)(2,1)S(1)} %fusion.10), channel_id=1, source_target_pairs={{0,16},{8,24},{16,0},{24,8},{1,17},{9,25},{17,1},{25,9},{2,18},{10... | collective-permute-start | bytes 1572872 | tf_op jit(solution)/shard_map/ppermute | solution.py:90
  230.0 12.9 %collective-permute-start.31 = (bf16[1024,256]{1,0:T(8,128)(2,1)S(1)}, bf16[1024,256]{1,0:T(8,128)(2,1)S(1)}, u32[]{:S(2)}, u32[]{:S(2)}) collective-permute-start(bf16[1024,256]{1,0:T(8,128)(2,1)S(1)} %get-tuple-element.122), channel_id=1, source_target_pairs={{0,8},{8,0},{16,24},{24,16},{1,9},{9,1},{17,25},{25,17},{2,10},{10... | collective-permute-start | bytes 1572872 | tf_op jit(solution)/shard_map/ppermute | solution.py:90
  242.8 17.3 %collective-permute-start.26 = (bf16[1024,256]{1,0:T(8,128)(2,1)S(1)}, bf16[1024,256]{1,0:T(8,128)(2,1)S(1)}, u32[]{:S(2)}, u32[]{:S(2)}) collective-permute-start(bf16[1024,256]{1,0:T(8,128)(2,1)S(1)} %get-tuple-element.114), channel_id=1, source_target_pairs={{0,8},{8,0},{16,24},{24,16},{1,9},{9,1},{17,25},{25,17},{2,10},{10... | collective-permute-start | bytes 1572872 | tf_op jit(solution)/shard_map/ppermute | solution.py:90
  244.2 14.4 %collective-permute-start.32 = (bf16[1024,256]{1,0:T(8,128)(2,1)S(1)}, bf16[1024,256]{1,0:T(8,128)(2,1)S(1)}, u32[]{:S(2)}, u32[]{:S(2)}) collective-permute-start(bf16[1024,256]{1,0:T(8,128)(2,1)S(1)} %convolution_convert_fusion.10), channel_id=1, source_target_pairs={{0,1},{1,0},{2,3},{3,2},{4,5},{5,4},{6,7},{7,6},{8,9},{9,8},{10,11... | collective-permute-start | bytes 1572872 | tf_op jit(solution)/shard_map/ppermute | solution.py:83
  251.9 29.3 %collective-permute-start.37 = (bf16[2048,256]{1,0:T(8,128)(2,1)S(1)}, bf16[2048,256]{1,0:T(8,128)(2,1)S(1)}, u32[]{:S(2)}, u32[]{:S(2)}) collective-permute-start(bf16[2048,256]{1,0:T(8,128)(2,1)S(1)} %collective-permute-done.33), channel_id=1, source_target_pairs={{0,2},{1,3},{2,4},{3,5},{4,6},{5,7},{6,0},{7,1},{8,10},{9,11},{10,... | collective-permute-start | bytes 3145736 | tf_op jit(solution)/shard_map/ppermute | solution.py:87
  258.6 13.5 %collective-permute-start.34 = (bf16[1024,256]{1,0:T(8,128)(2,1)S(1)}, bf16[1024,256]{1,0:T(8,128)(2,1)S(1)}, u32[]{:S(2)}, u32[]{:S(2)}) collective-permute-start(bf16[1024,256]{1,0:T(8,128)(2,1)S(1)} %convolution_convert_fusion.9), channel_id=1, source_target_pairs={{0,1},{1,0},{2,3},{3,2},{4,5},{5,4},{6,7},{7,6},{8,9},{9,8},{10,11... | collective-permute-start | bytes 1572872 | tf_op jit(solution)/shard_map/ppermute | solution.py:83
  272.1 12.6 %collective-permute-start.36 = (bf16[1024,256]{1,0:T(8,128)(2,1)S(1)}, bf16[1024,256]{1,0:T(8,128)(2,1)S(1)}, u32[]{:S(2)}, u32[]{:S(2)}) collective-permute-start(bf16[1024,256]{1,0:T(8,128)(2,1)S(1)} %convolution_convert_fusion.8), channel_id=1, source_target_pairs={{0,1},{1,0},{2,3},{3,2},{4,5},{5,4},{6,7},{7,6},{8,9},{9,8},{10,11... | collective-permute-start | bytes 1572872 | tf_op jit(solution)/shard_map/ppermute | solution.py:83
  284.8 11.7 %collective-permute-start.38 = (bf16[1024,256]{1,0:T(8,128)(2,1)S(1)}, bf16[1024,256]{1,0:T(8,128)(2,1)S(1)}, u32[]{:S(2)}, u32[]{:S(2)}) collective-permute-start(bf16[1024,256]{1,0:T(8,128)(2,1)S(1)} %convolution_convert_fusion.7), channel_id=1, source_target_pairs={{0,1},{1,0},{2,3},{3,2},{4,5},{5,4},{6,7},{7,6},{8,9},{9,8},{10,11... | collective-permute-start | bytes 1572872 | tf_op jit(solution)/shard_map/ppermute | solution.py:83
  299.1 5.8 %collective-permute-start.39 = (bf16[2,1024,128]{2,1,0:T(8,128)(2,1)S(1)}, bf16[2,1024,128]{2,1,0:T(8,128)(2,1)S(1)}, u32[]{:S(2)}, u32[]{:S(2)}) collective-permute-start(bf16[2,1024,128]{2,1,0:T(8,128)(2,1)S(1)} %get-tuple-element.135), channel_id=1, source_target_pairs={{0,8},{8,0},{16,24},{24,16},{1,9},{9,1},{17,25},{25,17},{2,10},{10... | collective-permute-start | bytes 1572872 | tf_op jit(solution)/shard_map/ppermute | solution.py:90
  309.8 4.8 collective-permute-start.40
  311.2 16.1 %collective-permute-start.41 = (bf16[2,1024,128]{2,1,0:T(8,128)(2,1)}, bf16[2,1024,128]{2,1,0:T(8,128)(2,1)S(1)}, u32[]{:S(2)}, u32[]{:S(2)}) collective-permute-start(bf16[2,1024,128]{2,1,0:T(8,128)(2,1)} %get-tuple-element.84), channel_id=1, source_target_pairs={{0,16},{8,24},{16,0},{24,8},{1,17},{9,25},{17,1},{25,9},{2,18},{10... | collective-permute-start | bytes 1572872 | tf_op jit(solution)/shard_map/ppermute | solution.py:90
  312.2 15.0 %collective-permute-start.42 = (bf16[1024,256]{1,0:T(8,128)(2,1)}, bf16[1024,256]{1,0:T(8,128)(2,1)S(1)}, u32[]{:S(2)}, u32[]{:S(2)}) collective-permute-start(bf16[1024,256]{1,0:T(8,128)(2,1)} %get-tuple-element.87), channel_id=1, source_target_pairs={{0,1},{1,0},{2,3},{3,2},{4,5},{5,4},{6,7},{7,6},{8,9},{9,8},{10,11... | collective-permute-start | bytes 1572872 | tf_op jit(solution)/shard_map/ppermute | solution.py:83
  314.1 23.2 %collective-permute-start.44 = (bf16[2,1024,128]{2,1,0:T(8,128)(2,1)}, bf16[2,1024,128]{2,1,0:T(8,128)(2,1)S(1)}, u32[]{:S(2)}, u32[]{:S(2)}) collective-permute-start(bf16[2,1024,128]{2,1,0:T(8,128)(2,1)} %get-tuple-element.92), channel_id=1, source_target_pairs={{0,24},{8,16},{16,8},{24,0},{1,25},{9,17},{17,9},{25,1},{2,26},{10... | collective-permute-start | bytes 1572872 | tf_op jit(solution)/shard_map/ppermute | solution.py:90
  314.6 22.6 %collective-permute-start.45 = (bf16[1024,256]{1,0:T(8,128)(2,1)}, bf16[1024,256]{1,0:T(8,128)(2,1)S(1)}, u32[]{:S(2)}, u32[]{:S(2)}) collective-permute-start(bf16[1024,256]{1,0:T(8,128)(2,1)} %collective-permute-done.40), channel_id=1, source_target_pairs={{0,1},{1,0},{2,3},{3,2},{4,5},{5,4},{6,7},{7,6},{8,9},{9,8},{10,11... | collective-permute-start | bytes 1572872 | tf_op jit(solution)/shard_map/ppermute | solution.py:83
  332.9 15.8 %collective-permute-start.43 = (bf16[1024,256]{1,0:T(8,128)(2,1)}, bf16[1024,256]{1,0:T(8,128)(2,1)}, u32[]{:S(2)}, u32[]{:S(2)}) collective-permute-start(bf16[1024,256]{1,0:T(8,128)(2,1)} %get-tuple-element.91), channel_id=1, source_target_pairs={{0,16},{8,24},{16,0},{24,8},{1,17},{9,25},{17,1},{25,9},{2,18},{10... | collective-permute-start | bytes 1572872 | tf_op jit(solution)/shard_map/ppermute | solution.py:90
  342.3 15.6 %collective-permute-start.46 = (bf16[1024,256]{1,0:T(8,128)(2,1)}, bf16[1024,256]{1,0:T(8,128)(2,1)S(1)}, u32[]{:S(2)}, u32[]{:S(2)}) collective-permute-start(bf16[1024,256]{1,0:T(8,128)(2,1)} %get-tuple-element.99), channel_id=1, source_target_pairs={{0,24},{8,16},{16,8},{24,0},{1,25},{9,17},{17,9},{25,1},{2,26},{10... | collective-permute-start | bytes 1572872 | tf_op jit(solution)/shard_map/ppermute | solution.py:90
  348.8 13.4 %collective-permute-start.47 = (bf16[1024,256]{1,0:T(8,128)(2,1)}, bf16[1024,256]{1,0:T(8,128)(2,1)S(1)}, u32[]{:S(2)}, u32[]{:S(2)}) collective-permute-start(bf16[1024,256]{1,0:T(8,128)(2,1)} %collective-permute-done.43), channel_id=1, source_target_pairs={{0,1},{1,0},{2,3},{3,2},{4,5},{5,4},{6,7},{7,6},{8,9},{9,8},{10,11... | collective-permute-start | bytes 1572872 | tf_op jit(solution)/shard_map/ppermute | solution.py:83
  357.9 14.7 %collective-permute-start.48 = (bf16[1024,256]{1,0:T(8,128)(2,1)S(1)}, bf16[1024,256]{1,0:T(8,128)(2,1)S(1)}, u32[]{:S(2)}, u32[]{:S(2)}) collective-permute-start(bf16[1024,256]{1,0:T(8,128)(2,1)S(1)} %collective-permute-done.46), channel_id=1, source_target_pairs={{0,1},{1,0},{2,3},{3,2},{4,5},{5,4},{6,7},{7,6},{8,9},{9,8},{10,11... | collective-permute-start | bytes 1572872 | tf_op jit(solution)/shard_map/ppermute | solution.py:83
  361.3 13.4 %collective-permute-start.53 = (bf16[1024,256]{1,0:T(8,128)(2,1)S(1)}, bf16[1024,256]{1,0:T(8,128)(2,1)S(1)}, u32[]{:S(2)}, u32[]{:S(2)}) collective-permute-start(bf16[1024,256]{1,0:T(8,128)(2,1)S(1)} %convolution_convert_fusion.5), channel_id=1, source_target_pairs={{0,8},{8,0},{16,24},{24,16},{1,9},{9,1},{17,25},{25,17},{2,10},{10... | collective-permute-start | bytes 1572872 | tf_op jit(solution)/shard_map/ppermute | solution.py:90
  374.5 8.4 %collective-permute-start.52 = (bf16[1024,256]{1,0:T(8,128)(2,1)S(1)}, bf16[1024,256]{1,0:T(8,128)(2,1)S(1)}, u32[]{:S(2)}, u32[]{:S(2)}) collective-permute-start(bf16[1024,256]{1,0:T(8,128)(2,1)S(1)} %convolution_convert_fusion.6), channel_id=1, source_target_pairs={{0,8},{8,0},{16,24},{24,16},{1,9},{9,1},{17,25},{25,17},{2,10},{10... | collective-permute-start | bytes 1572872 | tf_op jit(solution)/shard_map/ppermute | solution.py:90
  376.5 14.3 %collective-permute-start.54 = (bf16[1024,256]{1,0:T(8,128)(2,1)S(1)}, bf16[1024,256]{1,0:T(8,128)(2,1)S(1)}, u32[]{:S(2)}, u32[]{:S(2)}) collective-permute-start(bf16[1024,256]{1,0:T(8,128)(2,1)S(1)} %fusion.17), channel_id=1, source_target_pairs={{0,16},{8,24},{16,0},{24,8},{1,17},{9,25},{17,1},{25,9},{2,18},{10... | collective-permute-start | bytes 1572872 | tf_op jit(solution)/shard_map/ppermute | solution.py:90
  379.9 24.6 %collective-permute-start.51 = (bf16[2048,256]{1,0:T(8,128)(2,1)S(1)}, bf16[2048,256]{1,0:T(8,128)(2,1)S(1)}, u32[]{:S(2)}, u32[]{:S(2)}) collective-permute-start(bf16[2048,256]{1,0:T(8,128)(2,1)S(1)} %convolution_convert_fusion), channel_id=1, source_target_pairs={{0,8},{8,0},{16,24},{24,16},{1,9},{9,1},{17,25},{25,17},{2,10},{10... | collective-permute-start | bytes 3145736 | tf_op jit(solution)/shard_map/ppermute | solution.py:90
  382.4 30.3 %collective-permute-start.50 = (bf16[2048,256]{1,0:T(8,128)(2,1)S(1)}, bf16[2048,256]{1,0:T(8,128)(2,1)S(1)}, u32[]{:S(2)}, u32[]{:S(2)}) collective-permute-start(bf16[2048,256]{1,0:T(8,128)(2,1)S(1)} %convolution_convert_fusion.1), channel_id=1, source_target_pairs={{0,8},{8,0},{16,24},{24,16},{1,9},{9,1},{17,25},{25,17},{2,10},{10... | collective-permute-start | bytes 3145736 | tf_op jit(solution)/shard_map/ppermute | solution.py:90
  390.8 13.5 %collective-permute-start.55 = (bf16[1024,256]{1,0:T(8,128)(2,1)S(1)}, bf16[1024,256]{1,0:T(8,128)(2,1)S(1)}, u32[]{:S(2)}, u32[]{:S(2)}) collective-permute-start(bf16[1024,256]{1,0:T(8,128)(2,1)S(1)} %fusion.16), channel_id=1, source_target_pairs={{0,16},{8,24},{16,0},{24,8},{1,17},{9,25},{17,1},{25,9},{2,18},{10... | collective-permute-start | bytes 1572872 | tf_op jit(solution)/shard_map/ppermute | solution.py:90
  394.1 21.2 %collective-permute-start.49 = (bf16[2048,256]{1,0:T(8,128)(2,1)S(1)}, bf16[2048,256]{1,0:T(8,128)(2,1)S(1)}, u32[]{:S(2)}, u32[]{:S(2)}) collective-permute-start(bf16[2048,256]{1,0:T(8,128)(2,1)S(1)} %convolution_convert_fusion.2), channel_id=1, source_target_pairs={{0,8},{8,0},{16,24},{24,16},{1,9},{9,1},{17,25},{25,17},{2,10},{10... | collective-permute-start | bytes 3145736 | tf_op jit(solution)/shard_map/ppermute | solution.py:90
  394.3 26.9 %collective-permute-start.63 = (bf16[1024,256]{1,0:T(8,128)(2,1)S(1)}, bf16[1024,256]{1,0:T(8,128)(2,1)S(1)}, u32[]{:S(2)}, u32[]{:S(2)}) collective-permute-start(bf16[1024,256]{1,0:T(8,128)(2,1)S(1)} %add_convert_fusion.8), channel_id=1, source_target_pairs={{0,8},{8,0},{16,24},{24,16},{1,9},{9,1},{17,25},{25,17},{2,10},{10... | collective-permute-start | bytes 1572872 | tf_op jit(solution)/shard_map/ppermute | solution.py:90
  404.4 13.2 %collective-permute-start.64 = (bf16[1024,256]{1,0:T(8,128)(2,1)S(1)}, bf16[1024,256]{1,0:T(8,128)(2,1)S(1)}, u32[]{:S(2)}, u32[]{:S(2)}) collective-permute-start(bf16[1024,256]{1,0:T(8,128)(2,1)S(1)} %add_convert_fusion.7), channel_id=1, source_target_pairs={{0,8},{8,0},{16,24},{24,16},{1,9},{9,1},{17,25},{25,17},{2,10},{10... | collective-permute-start | bytes 1572872 | tf_op jit(solution)/shard_map/ppermute | solution.py:90
  410.4 25.6 %collective-permute-start.56 = (bf16[2048,256]{1,0:T(8,128)(2,1)S(1)}, bf16[2048,256]{1,0:T(8,128)(2,1)S(1)}, u32[]{:S(2)}, u32[]{:S(2)}) collective-permute-start(bf16[2048,256]{1,0:T(8,128)(2,1)S(1)} %fusion.2), channel_id=1, source_target_pairs={{0,16},{8,24},{16,0},{24,8},{1,17},{9,25},{17,1},{25,9},{2,18},{10... | collective-permute-start | bytes 3145736 | tf_op jit(solution)/shard_map/ppermute | solution.py:90
  422.7 59.6 %collective-permute-start.65 = (bf16[2048,512]{1,0:T(8,128)(2,1)S(1)}, bf16[2048,512]{1,0:T(8,128)(2,1)S(1)}, u32[]{:S(2)}, u32[]{:S(2)}) collective-permute-start(bf16[2048,512]{1,0:T(8,128)(2,1)S(1)} %pad_maximum_fusion.3), channel_id=1, source_target_pairs={{0,2},{1,3},{2,4},{3,5},{4,6},{5,7},{6,0},{7,1},{8,10},{9,11},{10,... | collective-permute-start | bytes 6291464 | tf_op jit(solution)/shard_map/ppermute | solution.py:87
  436.1 24.8 %collective-permute-start.57 = (bf16[2048,256]{1,0:T(8,128)(2,1)S(1)}, bf16[2048,256]{1,0:T(8,128)(2,1)S(1)}, u32[]{:S(2)}, u32[]{:S(2)}) collective-permute-start(bf16[2048,256]{1,0:T(8,128)(2,1)S(1)} %fusion.1), channel_id=1, source_target_pairs={{0,16},{8,24},{16,0},{24,8},{1,17},{9,25},{17,1},{25,9},{2,18},{10... | collective-permute-start | bytes 3145736 | tf_op jit(solution)/shard_map/ppermute | solution.py:90
  437.2 24.9 %collective-permute-start.60 = (bf16[2048,256]{1,0:T(8,128)(2,1)S(1)}, bf16[2048,256]{1,0:T(8,128)(2,1)S(1)}, u32[]{:S(2)}, u32[]{:S(2)}) collective-permute-start(bf16[2048,256]{1,0:T(8,128)(2,1)S(1)} %add_convert_fusion.5), channel_id=1, source_target_pairs={{0,8},{8,0},{16,24},{24,16},{1,9},{9,1},{17,25},{25,17},{2,10},{10... | collective-permute-start | bytes 3145736 | tf_op jit(solution)/shard_map/ppermute | solution.py:90
  461.1 18.8 %collective-permute-start.62 = (bf16[2048,256]{1,0:T(8,128)(2,1)S(1)}, bf16[2048,256]{1,0:T(8,128)(2,1)S(1)}, u32[]{:S(2)}, u32[]{:S(2)}) collective-permute-start(bf16[2048,256]{1,0:T(8,128)(2,1)S(1)} %add_convert_fusion.4), channel_id=1, source_target_pairs={{0,8},{8,0},{16,24},{24,16},{1,9},{9,1},{17,25},{25,17},{2,10},{10... | collective-permute-start | bytes 3145736 | tf_op jit(solution)/shard_map/ppermute | solution.py:90
  461.2 25.6 %collective-permute-start.58 = (bf16[2048,256]{1,0:T(8,128)(2,1)S(1)}, bf16[2048,256]{1,0:T(8,128)(2,1)S(1)}, u32[]{:S(2)}, u32[]{:S(2)}) collective-permute-start(bf16[2048,256]{1,0:T(8,128)(2,1)S(1)} %fusion), channel_id=1, source_target_pairs={{0,16},{8,24},{16,0},{24,8},{1,17},{9,25},{17,1},{25,9},{2,18},{10... | collective-permute-start | bytes 3145736 | tf_op jit(solution)/shard_map/ppermute | solution.py:90
  466.0 59.3 %collective-permute-start.61 = (bf16[2048,512]{1,0:T(8,128)(2,1)}, bf16[2048,512]{1,0:T(8,128)(2,1)S(1)}, u32[]{:S(2)}, u32[]{:S(2)}) collective-permute-start(bf16[2048,512]{1,0:T(8,128)(2,1)} %pad_maximum_fusion.2), channel_id=1, source_target_pairs={{0,6},{1,7},{2,0},{3,1},{4,2},{5,3},{6,4},{7,5},{8,14},{9,15},{10,... | collective-permute-start | bytes 6291464 | tf_op jit(solution)/shard_map/ppermute | solution.py:87
  484.3 85.9 %collective-permute-start.66 = (bf16[2048,512]{1,0:T(8,128)(2,1)}, bf16[2048,512]{1,0:T(8,128)(2,1)}, u32[]{:S(2)}, u32[]{:S(2)}) collective-permute-start(bf16[2048,512]{1,0:T(8,128)(2,1)} %pad_maximum_fusion.4), channel_id=1, source_target_pairs={{0,2},{1,3},{2,4},{3,5},{4,6},{5,7},{6,0},{7,1},{8,10},{9,11},{10,... | collective-permute-start | bytes 6291464 | tf_op jit(solution)/shard_map/ppermute | solution.py:87
  487.0 6.0 %collective-permute-start.59 = (bf16[2048,256]{1,0:T(8,128)(2,1)S(1)}, bf16[2048,256]{1,0:T(8,128)(2,1)}, u32[]{:S(2)}, u32[]{:S(2)}) collective-permute-start(bf16[2048,256]{1,0:T(8,128)(2,1)S(1)} %add_convert_fusion.6), channel_id=1, source_target_pairs={{0,8},{8,0},{16,24},{24,16},{1,9},{9,1},{17,25},{25,17},{2,10},{10... | collective-permute-start | bytes 3145736 | tf_op jit(solution)/shard_map/ppermute | solution.py:90
  (20 other events, 161.9 us)
where the time goes:
time: 584 us; the launch traced here: 575 us
  waiting for transfers between devices  296 us (51%)
  matrix products  116 us (20%)
  starting transfers between devices  98.4 us (17%)
  local copies, waits for them, and re-layouts  30.5 us (5%)
  Pallas kernels  16.5 us (3%)
  other arithmetic  15.2 us (3%)
    ppermute x9, waiting for transfers between devices, a_shift(): return lax.ppermute(x, 'col', perm)  129 us
    ppermute x48, waiting for transfers between devices, row_xor(): return lax.ppermute(x, 'row', [(r, r ^ k) for r in range(n_row)])  117 us
    dot_general x44, matrix products, dot(): lax.dot_general(a, b, ((contract[:1], contract[1:]), ((), ())), preferred...  116 us
    ppermute x9, starting transfers between devices, a_shift(): return lax.ppermute(x, 'col', perm)  58 us
    ppermute x10, waiting for transfers between devices, b_shift(): return lax.ppermute(x, 'col', perm)  49.9 us
    ppermute x48, starting transfers between devices, row_xor(): return lax.ppermute(x, 'row', [(r, r ^ k) for r in range(n_row)])  26.8 us
    pallas_call x4, Pallas kernels, moments_at(): pl.pallas_call(moments_kernel, grid_spec=pltpu.PrefetchScalarGridSpec(num...  16.5 us
    ppermute x10, starting transfers between devices, b_shift(): return lax.ppermute(x, 'col', perm)  13.6 us
  transfers between devices with their start and end apart: 67, of which 28 were waited for; matrix products, arithmetic and copies ran while one was open for 26% of the time, Pallas kernels for 2%

commit v1 on v0

--- a/solution.py
+++ b/solution.py
@@ -28,14 +28,14 @@
 def moments_kernel(peer_ref, rot_ref, first_ref, second_ref, *refs):
     first_new, second_new, direction = refs[-3:]
     first_new[...], second_new[...], direction[...] = moments(
-        first_ref[...], second_ref[...], rot_ref[0].astype(F32)
+        first_ref[...], second_ref[...], rot_ref[0].astype(F32).T
     )
 
 
 def moments_at(peer, n_row, sub, rot, first_moment, second_moment, before):
-    blocks, rows, _ = rot.shape
+    blocks, _, rows = rot.shape
     block = min(rows, 512)
-    packed_rot = pl.BlockSpec((1, block, sub), lambda q, i, p: (q, i, 0))
+    packed_rot = pl.BlockSpec((1, sub, block), lambda q, i, p: (q, 0, i))
     at_peer = pl.BlockSpec((block, sub), lambda q, i, p: (i, q * n_row + p[0]))
     packed = pl.BlockSpec((block, sub), lambda q, i, p: (i, q))
     kept = [pl.BlockSpec(memory_space=pl.ANY)] * len(before)
@@ -64,7 +64,7 @@
         first, second, direction = moments(
             lax.dynamic_slice_in_dim(first_moment, start, sub, 1),
             lax.dynamic_slice_in_dim(second_moment, start, sub, 1),
-            rot[q].astype(F32),
+            rot[q].astype(F32).T,
         )
         first_new = lax.dynamic_update_slice_in_dim(first_new, first, start, 1)
         second_new = lax.dynamic_update_slice_in_dim(second_new, second, start, 1)
@@ -105,12 +105,13 @@
         def across_rows(x, k, depth=1):
             return row_xor(x, k) if k == 1 else in_turn("rows", x, lambda y: row_xor(y, k), depth)
 
-        def half_sum(theirs, mine):
+        def half_sum(theirs, mine, depth):
             got = row_xor(theirs().astype(BF16), 1)
             mine = (mine() + got.astype(F32)).astype(BF16)
+            last["half"] = mine
             k = 2
             while k < n_row:
-                got = across_rows(mine, k)
+                got = across_rows(mine, k, depth)
                 mine = (mine.astype(F32) + got.astype(F32)).astype(BF16)
                 k *= 2
             return mine, row_xor(mine, 1)
@@ -132,7 +133,7 @@
             return x[:, :half], x[:, half:]
 
         grad = jnp.concatenate(
-            [lax.dynamic_slice_in_dim(grad, h * half, half, 1) for h in (core, 1 - core)], axis=1
+            [lax.dynamic_slice_in_dim(grad, h * half, half, 1).T for h in (core, 1 - core)], axis=0
         )
         grad = lax.optimization_barrier(grad)
         below, above = a_shift(grad, 1), a_shift(grad, -1)
@@ -142,61 +143,61 @@
         lefts = [own_left] + [across_b(own_left, -k) for k in range(1, n_b)]
 
         right_after = tie(basis_right, grad)
-        right_n = jnp.zeros((n_row * row_n, sub), BF16)
+        right_n = jnp.zeros((sub, n_row * row_n), BF16)
         for k in range(n_row):
-            part = lax.dynamic_slice_in_dim(right_after, (r ^ k) * sub, sub, 1)
+            part = lax.dynamic_slice_in_dim(right_after, (r ^ k) * sub, sub, 1).T
             if k:
                 part = across_rows(part, k, 2)
-            right_n = lax.dynamic_update_slice_in_dim(right_n, part, (r ^ k) * row_n, 0)
-        by_b = right_n.reshape(n_a, n_b, width, sub)
+            right_n = lax.dynamic_update_slice_in_dim(right_n, part, (r ^ k) * row_n, 1)
+        by_b = right_n.reshape(sub, n_a, n_b, width)
 
         def rows_of(which):
-            return lax.dynamic_index_in_dim(by_b, which, 1, keepdims=False).reshape(n_a * width, sub)
+            return lax.dynamic_index_in_dim(by_b, which, 2, keepdims=False).reshape(sub, n_a * width)
 
         got = [rows_of(b)] + [across_b(rows_of((b + k) % n_b), k) for k in range(1, n_b)]
         stacked = jnp.stack(got, 0)
         right = [lax.dynamic_index_in_dim(stacked, (b - q) % n_b, 0, keepdims=False) for q in range(n_b)]
-        right = jnp.concatenate(right, axis=1)
-
-        near, far = (0, 1, 3), 2
-        turns = [(k, s) for k in range(n_b) for s in near] + [(k, far) for k in reversed(range(n_b))]
-        rotated = [jnp.zeros((own_i, n_a * width), BF16) for _ in range(n_b)]
+        right = jnp.concatenate(right, axis=0)
+
+        near, far, last_b = (0, 1, 3), 2, n_b - 1
+        turns = [(0, 0)] + [(k, s) for k in range(1, n_b) for s in near] + [(0, 1)]
+        turns += [(k, far) for k in range(1, n_b)] + [(0, 3), (0, far)]
+        rotated = [jnp.zeros((n_a * width, own_i), BF16) for _ in range(n_b)]
         for k, s in turns:
             if (k, s) == (1, 0):
-                lefts[1:] = tie(tuple(lefts[1:]), last["rows"][-1])
+                grads[1], grads[3], *lefts[1:] = tie((grads[1], grads[3], *lefts[1:]), right_n)
+            if (k, s) == (1, 1):
                 sent = tie(right, last["rows"][-1])
                 below, above = a_shift(sent, 1), a_shift(sent, -1)
                 rights = [right, below, a_shift(below, 1), above]
-            if (k, s) == (0, 1):
-                grads[s] = tie(grads[s], right_n)
-            if (k, s) in ((0, 3), (n_b - 1, far)):
-                grads[s] = tie(grads[s], last["rows"][-1])
+            if (k, s) == (1, far):
+                grads[far] = tie(grads[far], last["rows"][-2])
             g = grads[s]
-            g_mine, g_theirs = halves(g)
+            g_mine, g_theirs = g[:half], g[half:]
             mine, theirs = half_sum(
-                lambda: dot(lefts[k], g_theirs, (0, 0)), lambda: dot(lefts[k], g_mine, (0, 0))
+                lambda: dot(g_theirs, lefts[k], (1, 0)), lambda: dot(g_mine, lefts[k], (1, 0)), 1
             )
-            rotated[k] = lax.dynamic_update_slice_in_dim(rotated[k], mine, n_at(s, core), 1)
-            rotated[k] = lax.dynamic_update_slice_in_dim(rotated[k], theirs, n_at(s, 1 - core), 1)
+            rotated[k] = lax.dynamic_update_slice_in_dim(rotated[k], mine, n_at(s, core), 0)
+            rotated[k] = lax.dynamic_update_slice_in_dim(rotated[k], theirs, n_at(s, 1 - core), 0)
         left = jnp.concatenate(lefts, axis=1)
 
-        rot_k = jnp.zeros((n_col, own_i, sub), BF16)
-        right_k = jnp.zeros((n_a * width, n_col * sub), BF16)
+        rot_k = jnp.zeros((n_col, sub, own_i), BF16)
+        right_k = jnp.zeros((n_col * sub, n_a * width), BF16)
         swapped = []
         for t in near + (far,):
             right_t = tie(rights[t], *swapped[-2:-1])
-            rot = dot(rotated[0], right_t, (1, 0))
+            rot = dot(right_t, rotated[0], (1, 0))
             for k in range(1, n_b):
-                part = dot(rotated[k], right_t, (1, 0))
+                part = dot(right_t, rotated[k], (1, 0))
                 swapped.append(across_b(part.astype(BF16), k))
                 rot = rot + swapped[-1].astype(F32)
             rot = rot.astype(BF16)
             for q in range(n_b):
                 block = (a - t) % n_a * n_b + q
                 at = (block // per_row ^ r) * per_row + block % per_row
-                columns = slice(q * sub, (q + 1) * sub)
-                rot_k = lax.dynamic_update_index_in_dim(rot_k, rot[:, columns], at, 0)
-                right_k = lax.dynamic_update_slice_in_dim(right_k, right_t[:, columns], at * sub, 1)
+                rows = slice(q * sub, (q + 1) * sub)
+                rot_k = lax.dynamic_update_index_in_dim(rot_k, rot[rows], at, 0)
+                right_k = lax.dynamic_update_slice_in_dim(right_k, right_t[rows], at * sub, 0)
 
         step = moments_at if sub % 128 == 0 else moments_sliced
         rots = [rot_k[k * per_row : (k + 1) * per_row] for k in range(n_row)]
@@ -204,8 +205,8 @@
 
         kept, by_rows = (), [[] for _ in range(n_b)]
         for k, rot in enumerate(rots):
-            if k >= 2:
-                kept = tie(tuple(kept), by_rows[1][k - 2])
+            if k == n_row - 1:
+                kept = tie(tuple(kept), by_rows[1][0])
             *kept, direction = step(r ^ k, n_row, sub, rot, first_moment, second_moment, tuple(kept))
             if k:
                 direction = across_rows(direction, k, 2)
@@ -217,11 +218,15 @@
         direction = jnp.concatenate(by_rows, axis=0)
 
         def back(s, parts):
-            r_mine = lax.dynamic_slice_in_dim(right_k, n_at(s, core), half, 0)
-            r_theirs = lax.dynamic_slice_in_dim(right_k, n_at(s, 1 - core), half, 0)
+            r_mine = lax.dynamic_slice_in_dim(right_k, n_at(s, core), half, 1)
+            r_theirs = lax.dynamic_slice_in_dim(right_k, n_at(s, 1 - core), half, 1)
             u_mine = u_theirs = 0.0
-            for d, l in parts:
-                w_mine, w_theirs = half_sum(lambda: dot(d, r_theirs, (1, 1)), lambda: dot(d, r_mine, (1, 1)))
+            for i, (d, l) in enumerate(parts):
+                if i:
+                    d = tie(d, last["half"])
+                w_mine, w_theirs = half_sum(
+                    lambda: dot(d, r_theirs, (1, 0)), lambda: dot(d, r_mine, (1, 0)), 1
+                )
                 u_mine = u_mine + dot(l, w_mine, (1, 0))
                 u_theirs = u_theirs + dot(l, w_theirs, (1, 0))
             return u_mine, u_theirs

time: 584 us -> 580 us (level)
  starting transfers between devices: 98.4 us -> 46.7 us
  waiting for transfers between devices: 296 us -> 337 us
  matrix products: 116 us -> 126 us
    ppermute x9, starting transfers between devices: 58 us -> 14.2 us  [a_shift(): return lax.ppermute(x, 'col', perm)]
    ppermute x9, waiting for transfers between devices: 129 us -> 153 us  [a_shift(): return lax.ppermute(x, 'col', perm)]
    ppermute x48, waiting for transfers between devices: 117 us -> 133 us  [row_xor(): return lax.ppermute(x, 'row', [(r, r ^ k) for r in range(n_row)])]
    dot_general x44, matrix products: 116 us -> 126 us  [dot(): lax.dot_general(a, b, ((contract[:1], contract[1:]), ((), ())), preferred...]
    dynamic_update_slice x27 -> x28, local copies, waits for them, and re-layouts: 11.7 us -> 12.2 us  [the longest x8 4.55 us: per_device(): lax.dynamic_update_slice_in_dim(rotated[k], theirs, n_at(s, 1 - core), 0)]
  transfers between devices with their start and end apart: 67 -> 67, of which waited for: 28 -> 28; matrix products, arithmetic and copies ran while one was open for 26% -> 27% of each run, Pallas kernels for 2% -> 3%
where the time goes in v1:
time: 580 us; the launch traced here: 574 us
  waiting for transfers between devices  337 us (58%)
  matrix products  126 us (22%)
  starting transfers between devices  46.7 us (8%)
  local copies, waits for them, and re-layouts  29.3 us (5%)
  Pallas kernels  17.5 us (3%)
  other arithmetic  14.8 us (3%)
    ppermute x9, waiting for transfers between devices, a_shift(): return lax.ppermute(x, 'col', perm)  153 us
    ppermute x48, waiting for transfers between devices, row_xor(): return lax.ppermute(x, 'row', [(r, r ^ k) for r in range(n_row)])  133 us
    dot_general x44, matrix products, dot(): lax.dot_general(a, b, ((contract[:1], contract[1:]), ((), ())), preferred...  126 us
    ppermute x10, waiting for transfers between devices, b_shift(): return lax.ppermute(x, 'col', perm)  50.7 us
    ppermute x48, starting transfers between devices, row_xor(): return lax.ppermute(x, 'row', [(r, r ^ k) for r in range(n_row)])  23.4 us
    pallas_call x4, Pallas kernels, moments_at(): pl.pallas_call(moments_kernel, grid_spec=pltpu.PrefetchScalarGridSpec(num...  17.5 us
    ppermute x9, starting transfers between devices, a_shift(): return lax.ppermute(x, 'col', perm)  14.2 us
  transfers between devices with their start and end apart: 67, of which 28 were waited for; matrix products, arithmetic and copies ran while one was open for 27% of the time, Pallas kernels for 3%

profile of v1, /device:TPU:0, one launch (start us, length us, event | category | flops | bytes accessed | tf_op | source)
XLA Modules:
  0.0 574.4 jit_solution(16641181459507159392)
XLA Ops:
  2.5 3.0 collective-permute-start.2
  5.5 4.3 convolution_convert_fusion.18
  9.8 3.6 collective-permute-start.1
  15.6 3.6 add_convert_fusion.17
  19.2 3.4 collective-permute-done.5
  24.7 12.7 %collective-permute-done.8 = bf16[256,1024]{1,0:T(8,128)(2,1)S(1)} collective-permute-done((bf16[256,1024]{1,0:T(8,128)(2,1)S(1)}, bf16[256,1024]{1,0:T(8,128)(2,1)S(1)}, u32[]{:S(2)}, u32[]{:S(2)}) %collective-permute-start.8) | collective-permute-done | bytes 524320 | tf_op jit(solution)/shard_map/ppermute | solution.py:90
  37.4 2.5 broadcast.29.clone.1
  48.6 56.3 %collective-permute-done = bf16[512,2048]{0,1:T(8,128)(2,1)} collective-permute-done((bf16[512,2048]{0,1:T(8,128)(2,1)S(1)}, bf16[512,2048]{0,1:T(8,128)(2,1)}, u32[]{:S(2)}, u32[]{:S(2)}) %collective-permute-start) | collective-permute-done | bytes 2097184 | tf_op jit(solution)/shard_map/ppermute | solution.py:87
  106.8 3.8 convolution_convert_fusion.13
  110.6 3.8 convolution_convert_fusion.16
  114.4 3.5 convolution_convert_fusion.14
  118.4 3.8 convolution_convert_fusion.15
  122.9 3.8 convolution_convert_fusion.17
  126.7 4.5 collective-permute-done.6
  133.2 3.5 fusion.8
  138.2 3.8 fusion.6
  142.1 3.8 fusion.7
  145.9 4.7 collective-permute-done.14
  152.9 3.8 fusion.9
  156.7 6.8 %collective-permute-done.15 = bf16[256,1024]{1,0:T(8,128)(2,1)S(1)} collective-permute-done((bf16[256,1024]{1,0:T(8,128)(2,1)S(1)}, bf16[256,1024]{1,0:T(8,128)(2,1)S(1)}, u32[]{:S(2)}, u32[]{:S(2)}) %collective-permute-start.15) | collective-permute-done | bytes 524320 | tf_op jit(solution)/shard_map/ppermute | solution.py:90
  165.1 3.8 fusion.5
  172.0 3.6 collective-permute-done.16
  175.6 3.5 convolution_convert_fusion.12
  179.2 3.5 convolution_convert_fusion.11
  185.0 29.9 %collective-permute-done.33 = bf16[256,2048]{0,1:T(8,128)(2,1)S(1)} collective-permute-done((bf16[256,2048]{0,1:T(8,128)(2,1)S(1)}, bf16[256,2048]{0,1:T(8,128)(2,1)S(1)}, u32[]{:S(2)}, u32[]{:S(2)}) %collective-permute-start.33) | collective-permute-done | bytes 1048608 | tf_op jit(solution)/shard_map/ppermute | solution.py:87
  215.1 3.5 fusion.10
  222.2 10.8 %collective-permute-done.22 = bf16[256,1024]{1,0:T(8,128)(2,1)S(1)} collective-permute-done((bf16[256,1024]{1,0:T(8,128)(2,1)S(1)}, bf16[256,1024]{1,0:T(8,128)(2,1)S(1)}, u32[]{:S(2)}, u32[]{:S(2)}) %collective-permute-start.22) | collective-permute-done | bytes 524320 | tf_op jit(solution)/shard_map/ppermute | solution.py:90
  233.8 3.5 fusion.11
  238.1 8.4 %collective-permute-done.23 = bf16[256,1024]{1,0:T(8,128)(2,1)S(1)} collective-permute-done((bf16[256,1024]{1,0:T(8,128)(2,1)S(1)}, bf16[256,1024]{1,0:T(8,128)(2,1)S(1)}, u32[]{:S(2)}, u32[]{:S(2)}) %collective-permute-start.23) | collective-permute-done | bytes 524320 | tf_op jit(solution)/shard_map/ppermute | solution.py:90
  252.1 7.1 %collective-permute-done.26 = bf16[256,1024]{1,0:T(8,128)(2,1)S(1)} collective-permute-done((bf16[256,1024]{1,0:T(8,128)(2,1)S(1)}, bf16[256,1024]{1,0:T(8,128)(2,1)S(1)}, u32[]{:S(2)}, u32[]{:S(2)}) %collective-permute-start.26) | collective-permute-done | bytes 524320 | tf_op jit(solution)/shard_map/ppermute | solution.py:90
  260.2 3.5 collective-permute-done.32
  265.7 11.5 %collective-permute-done.34 = bf16[256,1024]{1,0:T(8,128)(2,1)S(1)} collective-permute-done((bf16[256,1024]{1,0:T(8,128)(2,1)S(1)}, bf16[256,1024]{1,0:T(8,128)(2,1)S(1)}, u32[]{:S(2)}, u32[]{:S(2)}) %collective-permute-start.34) | collective-permute-done | bytes 524320 | tf_op jit(solution)/shard_map/ppermute | solution.py:83
  278.6 3.5 fusion.12
  282.5 3.5 fusion.13
  287.3 2.7 collective-permute-done.36
  290.5 3.5 fusion.14
  294.0 7.7 %collective-permute-done.38 = bf16[256,1024]{1,0:T(8,128)(2,1)S(1)} collective-permute-done((bf16[256,1024]{1,0:T(8,128)(2,1)S(1)}, bf16[256,1024]{1,0:T(8,128)(2,1)S(1)}, u32[]{:S(2)}, u32[]{:S(2)}) %collective-permute-start.38) | collective-permute-done | bytes 524320 | tf_op jit(solution)/shard_map/ppermute | solution.py:83
  301.7 3.5 fusion.15
  308.7 4.3 shard_map.76
  315.3 4.3 shard_map.77
  322.5 4.3 shard_map.78
  328.8 4.5 shard_map.79
  337.3 21.9 %collective-permute-done.42 = bf16[1024,256]{1,0:T(8,128)(2,1)S(1)} collective-permute-done((bf16[1024,256]{1,0:T(8,128)(2,1)}, bf16[1024,256]{1,0:T(8,128)(2,1)S(1)}, u32[]{:S(2)}, u32[]{:S(2)}) %collective-permute-start.42) | collective-permute-done | bytes 524320 | tf_op jit(solution)/shard_map/ppermute | solution.py:90
  361.2 2.6 constant_dynamic-update-slice_fusion.1
  363.9 2.8 constant_dynamic-update-slice_fusion
  371.9 9.6 %collective-permute-done.47 = bf16[1024,256]{1,0:T(8,128)(2,1)S(1)} collective-permute-done((bf16[1024,256]{1,0:T(8,128)(2,1)S(1)}, bf16[1024,256]{1,0:T(8,128)(2,1)S(1)}, u32[]{:S(2)}, u32[]{:S(2)}) %collective-permute-start.47) | collective-permute-done | bytes 524320 | tf_op jit(solution)/shard_map/ppermute | solution.py:83
  381.5 10.8 %collective-permute-done.48 = bf16[1024,256]{1,0:T(8,128)(2,1)S(1)} collective-permute-done((bf16[1024,256]{1,0:T(8,128)(2,1)S(1)}, bf16[1024,256]{1,0:T(8,128)(2,1)S(1)}, u32[]{:S(2)}, u32[]{:S(2)}) %collective-permute-start.48) | collective-permute-done | bytes 524320 | tf_op jit(solution)/shard_map/ppermute | solution.py:83
  400.1 10.4 %collective-permute-done.55 = bf16[1024,256]{1,0:T(8,128)(2,1)S(1)} collective-permute-done((bf16[1024,256]{1,0:T(8,128)(2,1)S(1)}, bf16[1024,256]{1,0:T(8,128)(2,1)S(1)}, u32[]{:S(2)}, u32[]{:S(2)}) %collective-permute-start.55) | collective-permute-done | bytes 524320 | tf_op jit(solution)/shard_map/ppermute | solution.py:90
  412.1 3.5 fusion.74
  416.3 3.8 fusion.3
  422.8 3.5 fusion.75
  426.4 3.5 fusion.4
  431.9 9.3 %collective-permute-done.56 = bf16[2048,256]{1,0:T(8,128)(2,1)S(1)} collective-permute-done((bf16[2048,256]{1,0:T(8,128)(2,1)S(1)}, bf16[2048,256]{1,0:T(8,128)(2,1)S(1)}, u32[]{:S(2)}, u32[]{:S(2)}) %collective-permute-start.56) | collective-permute-done | bytes 1048608 | tf_op jit(solution)/shard_map/ppermute | solution.py:90
  442.2 2.5 convolution_convert_fusion.4
  444.7 21.3 %collective-permute-done.57 = bf16[2048,256]{1,0:T(8,128)(2,1)S(1)} collective-permute-done((bf16[2048,256]{1,0:T(8,128)(2,1)S(1)}, bf16[2048,256]{1,0:T(8,128)(2,1)S(1)}, u32[]{:S(2)}, u32[]{:S(2)}) %collective-permute-start.57) | collective-permute-done | bytes 1048608 | tf_op jit(solution)/shard_map/ppermute | solution.py:90
  467.0 2.4 convolution_convert_fusion.3
  471.1 2.5 collective-permute-start.61
  473.5 2.4 fusion.72
  476.0 2.4 fusion.73
  482.3 9.6 %collective-permute-done.58 = bf16[2048,256]{1,0:T(8,128)(2,1)S(1)} collective-permute-done((bf16[2048,256]{1,0:T(8,128)(2,1)S(1)}, bf16[2048,256]{1,0:T(8,128)(2,1)S(1)}, u32[]{:S(2)}, u32[]{:S(2)}) %collective-permute-start.58) | collective-permute-done | bytes 1048608 | tf_op jit(solution)/shard_map/ppermute | solution.py:90
  492.3 5.9 %fusion.70 = f32[2048,256]{1,0:T(8,128)S(1)} fusion(bf16[2048,2048]{1,0:T(8,128)(2,1)} %copy-done.2, bf16[2048,256]{1,0:T(8,128)(2,1)S(1)} %add_convert_fusion.6), kind=kOutput, calls=%fused_computation.187 | convolution fusion | flops 2147483648 | bytes 11534336 | tf_op jit(solution)/shard_map/dot_general | solution.py:15
  498.2 6.2 %fusion.71 = f32[2048,256]{1,0:T(8,128)S(1)} fusion(bf16[2048,2048]{1,0:T(8,128)(2,1)} %copy-done.2, bf16[2048,256]{1,0:T(8,128)(2,1)} %collective-permute-done.59), kind=kOutput, calls=%fused_computation.188 | convolution fusion | flops 2147483648 | bytes 11534336 | tf_op jit(solution)/shard_map/dot_general | solution.py:15
  504.3 20.9 %collective-permute-done.61 = bf16[2048,512]{1,0:T(8,128)(2,1)S(1)} collective-permute-done((bf16[2048,512]{1,0:T(8,128)(2,1)}, bf16[2048,512]{1,0:T(8,128)(2,1)S(1)}, u32[]{:S(2)}, u32[]{:S(2)}) %collective-permute-start.61) | collective-permute-done | bytes 2097184 | tf_op jit(solution)/shard_map/ppermute | solution.py:87
  525.2 44.4 %collective-permute-done.66 = bf16[2048,512]{1,0:T(8,128)(2,1)} collective-permute-done((bf16[2048,512]{1,0:T(8,128)(2,1)}, bf16[2048,512]{1,0:T(8,128)(2,1)}, u32[]{:S(2)}, u32[]{:S(2)}) %collective-permute-start.66) | collective-permute-done | bytes 2097184 | tf_op jit(solution)/shard_map/ppermute | solution.py:87
  (203 shorter events, 96.2 us)
Async XLA Ops:
  2.5 104.2 %collective-permute-start.2 = (bf16[2048,1024]{1,0:T(8,128)(2,1)}, bf16[2048,1024]{1,0:T(8,128)(2,1)}, u32[]{:S(2)}, u32[]{:S(2)}) collective-permute-start(bf16[2048,1024]{1,0:T(8,128)(2,1)} %param.6), channel_id=1, source_target_pairs={{0,1},{1,0},{2,3},{3,2},{4,5},{5,4},{6,7},{7,6},{8,9},{9,8},{10,11... | collective-permute-start | bytes 12582920 | tf_op jit(solution)/shard_map/ppermute | solution.py:83
  9.8 5.8 %collective-permute-start.7 = (bf16[256,1024]{1,0:T(8,128)(2,1)}, bf16[256,1024]{1,0:T(8,128)(2,1)}, u32[]{:S(2)}, u32[]{:S(2)}) collective-permute-start(bf16[256,1024]{1,0:T(8,128)(2,1)} %convolution_convert_fusion.18), channel_id=1, source_target_pairs={{0,8},{8,0},{16,24},{24,16},{1,9},{9,1},{17,25},{25,17},{2,10},{10... | collective-permute-start | bytes 1572872 | tf_op jit(solution)/shard_map/ppermute | solution.py:90
  9.8 96.9 %collective-permute-start.1 = (bf16[512,2048]{0,1:T(8,128)(2,1)S(1)}, bf16[512,2048]{0,1:T(8,128)(2,1)}, u32[]{:S(2)}, u32[]{:S(2)}) collective-permute-start(bf16[512,2048]{0,1:T(8,128)(2,1)S(1)} %pad_maximum_fusion.1), channel_id=1, source_target_pairs={{0,6},{1,7},{2,0},{3,1},{4,2},{5,3},{6,4},{7,5},{8,14},{9,15},{10,... | collective-permute-start | bytes 6291464 | tf_op jit(solution)/shard_map/ppermute | solution.py:87
  13.4 91.5 %collective-permute-start = (bf16[512,2048]{0,1:T(8,128)(2,1)S(1)}, bf16[512,2048]{0,1:T(8,128)(2,1)}, u32[]{:S(2)}, u32[]{:S(2)}) collective-permute-start(bf16[512,2048]{0,1:T(8,128)(2,1)S(1)} %pad_maximum_fusion.1), channel_id=1, source_target_pairs={{0,2},{1,3},{2,4},{3,5},{4,6},{5,7},{6,0},{7,1},{8,10},{9,11},{10,... | collective-permute-start | bytes 6291464 | tf_op jit(solution)/shard_map/ppermute | solution.py:87
  14.3 8.4 %collective-permute-start.5 = (bf16[128,1024]{0,1:T(8,128)(2,1)S(1)}, bf16[128,1024]{0,1:T(8,128)(2,1)}, u32[]{:S(2)}, u32[]{:S(2)}) collective-permute-start(bf16[128,1024]{0,1:T(8,128)(2,1)S(1)} %get-tuple-element.141), channel_id=1, source_target_pairs={{0,24},{8,16},{16,8},{24,0},{1,25},{9,17},{17,9},{25,1},{2,26},{10... | collective-permute-start | bytes 786440 | tf_op jit(solution)/shard_map/ppermute | solution.py:90
  22.7 14.7 %collective-permute-start.8 = (bf16[256,1024]{1,0:T(8,128)(2,1)S(1)}, bf16[256,1024]{1,0:T(8,128)(2,1)S(1)}, u32[]{:S(2)}, u32[]{:S(2)}) collective-permute-start(bf16[256,1024]{1,0:T(8,128)(2,1)S(1)} %add_convert_fusion.17), channel_id=1, source_target_pairs={{0,16},{8,24},{16,0},{24,8},{1,17},{9,25},{17,1},{25,9},{2,18},{10... | collective-permute-start | bytes 1572872 | tf_op jit(solution)/shard_map/ppermute | solution.py:90
  24.2 20.5 %collective-permute-start.4 = (bf16[128,1024]{0,1:T(8,128)(2,1)S(1)}, bf16[128,1024]{0,1:T(8,128)(2,1)}, u32[]{:S(2)}, u32[]{:S(2)}) collective-permute-start(bf16[128,1024]{0,1:T(8,128)(2,1)S(1)} %get-tuple-element.142), channel_id=1, source_target_pairs={{0,16},{8,24},{16,0},{24,8},{1,17},{9,25},{17,1},{25,9},{2,18},{10... | collective-permute-start | bytes 786440 | tf_op jit(solution)/shard_map/ppermute | solution.py:90
  41.2 5.6 collective-permute-start.9
  104.9 67.0 %collective-permute-start.20 = (bf16[512,2048]{0,1:T(8,128)(2,1)}, bf16[512,2048]{0,1:T(8,128)(2,1)S(1)}, u32[]{:S(2)}, u32[]{:S(2)}) collective-permute-start(bf16[512,2048]{0,1:T(8,128)(2,1)} %collective-permute-done), channel_id=1, source_target_pairs={{0,2},{1,3},{2,4},{3,5},{4,6},{5,7},{6,0},{7,1},{8,10},{9,11},{10,... | collective-permute-start | bytes 6291464 | tf_op jit(solution)/shard_map/ppermute | solution.py:87
  117.8 13.4 %collective-permute-start.6 = (bf16[128,2048]{0,1:T(8,128)(2,1)S(1)}, bf16[128,2048]{0,1:T(8,128)(2,1)S(1)}, u32[]{:S(2)}, u32[]{:S(2)}) collective-permute-start(bf16[128,2048]{0,1:T(8,128)(2,1)S(1)} %bitcast.114), channel_id=1, source_target_pairs={{0,1},{1,0},{2,3},{3,2},{4,5},{5,4},{6,7},{7,6},{8,9},{9,8},{10,11... | collective-permute-start | bytes 1572872 | tf_op jit(solution)/shard_map/ppermute | solution.py:83
  122.2 10.4 %collective-permute-start.13 = (bf16[256,1024]{1,0:T(8,128)(2,1)S(1)}, bf16[256,1024]{1,0:T(8,128)(2,1)S(1)}, u32[]{:S(2)}, u32[]{:S(2)}) collective-permute-start(bf16[256,1024]{1,0:T(8,128)(2,1)S(1)} %convolution_convert_fusion.14), channel_id=1, source_target_pairs={{0,8},{8,0},{16,24},{24,16},{1,9},{9,1},{17,25},{25,17},{2,10},{10... | collective-permute-start | bytes 1572872 | tf_op jit(solution)/shard_map/ppermute | solution.py:90
  122.3 14.3 %collective-permute-start.11 = (bf16[256,1024]{1,0:T(8,128)(2,1)S(1)}, bf16[256,1024]{1,0:T(8,128)(2,1)S(1)}, u32[]{:S(2)}, u32[]{:S(2)}) collective-permute-start(bf16[256,1024]{1,0:T(8,128)(2,1)S(1)} %convolution_convert_fusion.16), channel_id=1, source_target_pairs={{0,8},{8,0},{16,24},{24,16},{1,9},{9,1},{17,25},{25,17},{2,10},{10... | collective-permute-start | bytes 1572872 | tf_op jit(solution)/shard_map/ppermute | solution.py:90
  122.8 30.1 %collective-permute-start.19 = (bf16[256,1024]{1,0:T(8,128)(2,1)S(1)}, bf16[256,1024]{1,0:T(8,128)(2,1)S(1)}, u32[]{:S(2)}, u32[]{:S(2)}) collective-permute-start(bf16[256,1024]{1,0:T(8,128)(2,1)S(1)} %convolution_convert_fusion.13), channel_id=1, source_target_pairs={{0,8},{8,0},{16,24},{24,16},{1,9},{9,1},{17,25},{25,17},{2,10},{10... | collective-permute-start | bytes 1572872 | tf_op jit(solution)/shard_map/ppermute | solution.py:90
  131.2 33.9 %collective-permute-start.10 = (bf16[256,1024]{1,0:T(8,128)(2,1)S(1)}, bf16[256,1024]{1,0:T(8,128)(2,1)S(1)}, u32[]{:S(2)}, u32[]{:S(2)}) collective-permute-start(bf16[256,1024]{1,0:T(8,128)(2,1)S(1)} %convolution_convert_fusion.17), channel_id=1, source_target_pairs={{0,8},{8,0},{16,24},{24,16},{1,9},{9,1},{17,25},{25,17},{2,10},{10... | collective-permute-start | bytes 1572872 | tf_op jit(solution)/shard_map/ppermute | solution.py:90
  132.6 9.4 %collective-permute-start.12 = (bf16[256,1024]{1,0:T(8,128)(2,1)S(1)}, bf16[256,1024]{1,0:T(8,128)(2,1)S(1)}, u32[]{:S(2)}, u32[]{:S(2)}) collective-permute-start(bf16[256,1024]{1,0:T(8,128)(2,1)S(1)} %convolution_convert_fusion.15), channel_id=1, source_target_pairs={{0,8},{8,0},{16,24},{24,16},{1,9},{9,1},{17,25},{25,17},{2,10},{10... | collective-permute-start | bytes 1572872 | tf_op jit(solution)/shard_map/ppermute | solution.py:90
  136.7 13.9 %collective-permute-start.14 = (bf16[256,1024]{1,0:T(8,128)(2,1)S(1)}, bf16[256,1024]{1,0:T(8,128)(2,1)S(1)}, u32[]{:S(2)}, u32[]{:S(2)}) collective-permute-start(bf16[256,1024]{1,0:T(8,128)(2,1)S(1)} %fusion.8), channel_id=1, source_target_pairs={{0,16},{8,24},{16,0},{24,8},{1,17},{9,25},{17,1},{25,9},{2,18},{10... | collective-permute-start | bytes 1572872 | tf_op jit(solution)/shard_map/ppermute | solution.py:90
  150.6 13.0 %collective-permute-start.15 = (bf16[256,1024]{1,0:T(8,128)(2,1)S(1)}, bf16[256,1024]{1,0:T(8,128)(2,1)S(1)}, u32[]{:S(2)}, u32[]{:S(2)}) collective-permute-start(bf16[256,1024]{1,0:T(8,128)(2,1)S(1)} %fusion.7), channel_id=1, source_target_pairs={{0,16},{8,24},{16,0},{24,8},{1,17},{9,25},{17,1},{25,9},{2,18},{10... | collective-permute-start | bytes 1572872 | tf_op jit(solution)/shard_map/ppermute | solution.py:90
  152.8 18.8 %collective-permute-start.28 = (bf16[256,1024]{1,0:T(8,128)(2,1)S(1)}, bf16[256,1024]{1,0:T(8,128)(2,1)S(1)}, u32[]{:S(2)}, u32[]{:S(2)}) collective-permute-start(bf16[256,1024]{1,0:T(8,128)(2,1)S(1)} %get-tuple-element.126), channel_id=1, source_target_pairs={{0,8},{8,0},{16,24},{24,16},{1,9},{9,1},{17,25},{25,17},{2,10},{10... | collective-permute-start | bytes 1572872 | tf_op jit(solution)/shard_map/ppermute | solution.py:90
  163.6 12.1 %collective-permute-start.16 = (bf16[256,1024]{1,0:T(8,128)(2,1)S(1)}, bf16[256,1024]{1,0:T(8,128)(2,1)S(1)}, u32[]{:S(2)}, u32[]{:S(2)}) collective-permute-start(bf16[256,1024]{1,0:T(8,128)(2,1)S(1)} %fusion.6), channel_id=1, source_target_pairs={{0,16},{8,24},{16,0},{24,8},{1,17},{9,25},{17,1},{25,9},{2,18},{10... | collective-permute-start | bytes 1572872 | tf_op jit(solution)/shard_map/ppermute | solution.py:90
  168.9 91.3 %collective-permute-start.35 = (bf16[256,2048]{0,1:T(8,128)(2,1)S(1)}, bf16[256,2048]{0,1:T(8,128)(2,1)S(1)}, u32[]{:S(2)}, u32[]{:S(2)}) collective-permute-start(bf16[256,2048]{0,1:T(8,128)(2,1)S(1)} %pad_maximum_fusion.5), channel_id=1, source_target_pairs={{0,6},{1,7},{2,0},{3,1},{4,2},{5,3},{6,4},{7,5},{8,14},{9,15},{10,... | collective-permute-start | bytes 3145736 | tf_op jit(solution)/shard_map/ppermute | solution.py:87
  171.1 43.7 %collective-permute-start.33 = (bf16[256,2048]{0,1:T(8,128)(2,1)S(1)}, bf16[256,2048]{0,1:T(8,128)(2,1)S(1)}, u32[]{:S(2)}, u32[]{:S(2)}) collective-permute-start(bf16[256,2048]{0,1:T(8,128)(2,1)S(1)} %pad_maximum_fusion.5), channel_id=1, source_target_pairs={{0,2},{1,3},{2,4},{3,5},{4,6},{5,7},{6,0},{7,1},{8,10},{9,11},{10,... | collective-permute-start | bytes 3145736 | tf_op jit(solution)/shard_map/ppermute | solution.py:87
  171.9 11.3 %collective-permute-start.29 = (bf16[256,1024]{1,0:T(8,128)(2,1)S(1)}, bf16[256,1024]{1,0:T(8,128)(2,1)S(1)}, u32[]{:S(2)}, u32[]{:S(2)}) collective-permute-start(bf16[256,1024]{1,0:T(8,128)(2,1)S(1)} %get-tuple-element.124), channel_id=1, source_target_pairs={{0,8},{8,0},{16,24},{24,16},{1,9},{9,1},{17,25},{25,17},{2,10},{10... | collective-permute-start | bytes 1572872 | tf_op jit(solution)/shard_map/ppermute | solution.py:90
  179.1 36.0 %collective-permute-start.21 = (bf16[256,1024]{1,0:T(8,128)(2,1)S(1)}, bf16[256,1024]{1,0:T(8,128)(2,1)S(1)}, u32[]{:S(2)}, u32[]{:S(2)}) collective-permute-start(bf16[256,1024]{1,0:T(8,128)(2,1)S(1)} %convolution_convert_fusion.12), channel_id=1, source_target_pairs={{0,8},{8,0},{16,24},{24,16},{1,9},{9,1},{17,25},{25,17},{2,10},{10... | collective-permute-start | bytes 1572872 | tf_op jit(solution)/shard_map/ppermute | solution.py:90
  182.6 51.1 %collective-permute-start.25 = (bf16[256,1024]{1,0:T(8,128)(2,1)S(1)}, bf16[256,1024]{1,0:T(8,128)(2,1)S(1)}, u32[]{:S(2)}, u32[]{:S(2)}) collective-permute-start(bf16[256,1024]{1,0:T(8,128)(2,1)S(1)} %convolution_convert_fusion.11), channel_id=1, source_target_pairs={{0,8},{8,0},{16,24},{24,16},{1,9},{9,1},{17,25},{25,17},{2,10},{10... | collective-permute-start | bytes 1572872 | tf_op jit(solution)/shard_map/ppermute | solution.py:90
  183.2 35.4 %collective-permute-start.17 = (bf16[256,1024]{1,0:T(8,128)(2,1)S(1)}, bf16[256,1024]{1,0:T(8,128)(2,1)S(1)}, u32[]{:S(2)}, u32[]{:S(2)}) collective-permute-start(bf16[256,1024]{1,0:T(8,128)(2,1)S(1)} %fusion.5), channel_id=1, source_target_pairs={{0,16},{8,24},{16,0},{24,8},{1,17},{9,25},{17,1},{25,9},{2,18},{10... | collective-permute-start | bytes 1572872 | tf_op jit(solution)/shard_map/ppermute | solution.py:90
  214.9 7.3 %collective-permute-start.30 = (bf16[256,1024]{1,0:T(8,128)(2,1)S(1)}, bf16[256,1024]{1,0:T(8,128)(2,1)S(1)}, u32[]{:S(2)}, u32[]{:S(2)}) collective-permute-start(bf16[256,1024]{1,0:T(8,128)(2,1)S(1)} %get-tuple-element.122), channel_id=1, source_target_pairs={{0,8},{8,0},{16,24},{24,16},{1,9},{9,1},{17,25},{25,17},{2,10},{10... | collective-permute-start | bytes 1572872 | tf_op jit(solution)/shard_map/ppermute | solution.py:90
  218.6 14.4 %collective-permute-start.22 = (bf16[256,1024]{1,0:T(8,128)(2,1)S(1)}, bf16[256,1024]{1,0:T(8,128)(2,1)S(1)}, u32[]{:S(2)}, u32[]{:S(2)}) collective-permute-start(bf16[256,1024]{1,0:T(8,128)(2,1)S(1)} %fusion.10), channel_id=1, source_target_pairs={{0,16},{8,24},{16,0},{24,8},{1,17},{9,25},{17,1},{25,9},{2,18},{10... | collective-permute-start | bytes 1572872 | tf_op jit(solution)/shard_map/ppermute | solution.py:90
  219.3 66.6 %collective-permute-start.37 = (bf16[256,2048]{0,1:T(8,128)(2,1)S(1)}, bf16[256,2048]{0,1:T(8,128)(2,1)S(1)}, u32[]{:S(2)}, u32[]{:S(2)}) collective-permute-start(bf16[256,2048]{0,1:T(8,128)(2,1)S(1)} %collective-permute-done.33), channel_id=1, source_target_pairs={{0,2},{1,3},{2,4},{3,5},{4,6},{5,7},{6,0},{7,1},{8,10},{9,11},{10,... | collective-permute-start | bytes 3145736 | tf_op jit(solution)/shard_map/ppermute | solution.py:87
  222.2 15.1 %collective-permute-start.18 = (bf16[256,1024]{1,0:T(8,128)(2,1)S(1)}, bf16[256,1024]{1,0:T(8,128)(2,1)S(1)}, u32[]{:S(2)}, u32[]{:S(2)}) collective-permute-start(bf16[256,1024]{1,0:T(8,128)(2,1)S(1)} %get-tuple-element.116), channel_id=1, source_target_pairs={{0,8},{8,0},{16,24},{24,16},{1,9},{9,1},{17,25},{25,17},{2,10},{10... | collective-permute-start | bytes 1572872 | tf_op jit(solution)/shard_map/ppermute | solution.py:90
  233.0 13.6 %collective-permute-start.23 = (bf16[256,1024]{1,0:T(8,128)(2,1)S(1)}, bf16[256,1024]{1,0:T(8,128)(2,1)S(1)}, u32[]{:S(2)}, u32[]{:S(2)}) collective-permute-start(bf16[256,1024]{1,0:T(8,128)(2,1)S(1)} %fusion.9), channel_id=1, source_target_pairs={{0,16},{8,24},{16,0},{24,8},{1,17},{9,25},{17,1},{25,9},{2,18},{10... | collective-permute-start | bytes 1572872 | tf_op jit(solution)/shard_map/ppermute | solution.py:90
  233.7 14.3 %collective-permute-start.31 = (bf16[256,1024]{1,0:T(8,128)(2,1)S(1)}, bf16[256,1024]{1,0:T(8,128)(2,1)S(1)}, u32[]{:S(2)}, u32[]{:S(2)}) collective-permute-start(bf16[256,1024]{1,0:T(8,128)(2,1)S(1)} %get-tuple-element.120), channel_id=1, source_target_pairs={{0,8},{8,0},{16,24},{24,16},{1,9},{9,1},{17,25},{25,17},{2,10},{10... | collective-permute-start | bytes 1572872 | tf_op jit(solution)/shard_map/ppermute | solution.py:90
  246.5 12.7 %collective-permute-start.26 = (bf16[256,1024]{1,0:T(8,128)(2,1)S(1)}, bf16[256,1024]{1,0:T(8,128)(2,1)S(1)}, u32[]{:S(2)}, u32[]{:S(2)}) collective-permute-start(bf16[256,1024]{1,0:T(8,128)(2,1)S(1)} %fusion.11), channel_id=1, source_target_pairs={{0,16},{8,24},{16,0},{24,8},{1,17},{9,25},{17,1},{25,9},{2,18},{10... | collective-permute-start | bytes 1572872 | tf_op jit(solution)/shard_map/ppermute | solution.py:90
  249.3 14.4 %collective-permute-start.32 = (bf16[256,1024]{1,0:T(8,128)(2,1)S(1)}, bf16[256,1024]{1,0:T(8,128)(2,1)S(1)}, u32[]{:S(2)}, u32[]{:S(2)}) collective-permute-start(bf16[256,1024]{1,0:T(8,128)(2,1)S(1)} %convolution_convert_fusion.10), channel_id=1, source_target_pairs={{0,1},{1,0},{2,3},{3,2},{4,5},{5,4},{6,7},{7,6},{8,9},{9,8},{10,11... | collective-permute-start | bytes 1572872 | tf_op jit(solution)/shard_map/ppermute | solution.py:83
  260.2 17.6 %collective-permute-start.27 = (bf16[256,1024]{1,0:T(8,128)(2,1)S(1)}, bf16[256,1024]{1,0:T(8,128)(2,1)S(1)}, u32[]{:S(2)}, u32[]{:S(2)}) collective-permute-start(bf16[256,1024]{1,0:T(8,128)(2,1)S(1)} %get-tuple-element.112), channel_id=1, source_target_pairs={{0,8},{8,0},{16,24},{24,16},{1,9},{9,1},{17,25},{25,17},{2,10},{10... | collective-permute-start | bytes 1572872 | tf_op jit(solution)/shard_map/ppermute | solution.py:90
  263.7 13.6 %collective-permute-start.34 = (bf16[256,1024]{1,0:T(8,128)(2,1)S(1)}, bf16[256,1024]{1,0:T(8,128)(2,1)S(1)}, u32[]{:S(2)}, u32[]{:S(2)}) collective-permute-start(bf16[256,1024]{1,0:T(8,128)(2,1)S(1)} %convolution_convert_fusion.9), channel_id=1, source_target_pairs={{0,1},{1,0},{2,3},{3,2},{4,5},{5,4},{6,7},{7,6},{8,9},{9,8},{10,11... | collective-permute-start | bytes 1572872 | tf_op jit(solution)/shard_map/ppermute | solution.py:83
  277.3 12.7 %collective-permute-start.36 = (bf16[256,1024]{1,0:T(8,128)(2,1)S(1)}, bf16[256,1024]{1,0:T(8,128)(2,1)S(1)}, u32[]{:S(2)}, u32[]{:S(2)}) collective-permute-start(bf16[256,1024]{1,0:T(8,128)(2,1)S(1)} %convolution_convert_fusion.8), channel_id=1, source_target_pairs={{0,1},{1,0},{2,3},{3,2},{4,5},{5,4},{6,7},{7,6},{8,9},{9,8},{10,11... | collective-permute-start | bytes 1572872 | tf_op jit(solution)/shard_map/ppermute | solution.py:83
  290.0 11.7 %collective-permute-start.38 = (bf16[256,1024]{1,0:T(8,128)(2,1)S(1)}, bf16[256,1024]{1,0:T(8,128)(2,1)S(1)}, u32[]{:S(2)}, u32[]{:S(2)}) collective-permute-start(bf16[256,1024]{1,0:T(8,128)(2,1)S(1)} %convolution_convert_fusion.7), channel_id=1, source_target_pairs={{0,1},{1,0},{2,3},{3,2},{4,5},{5,4},{6,7},{7,6},{8,9},{9,8},{10,11... | collective-permute-start | bytes 1572872 | tf_op jit(solution)/shard_map/ppermute | solution.py:83
  306.6 15.1 %collective-permute-start.41 = (bf16[2,128,1024]{2,1,0:T(8,128)(2,1)}, bf16[2,128,1024]{2,1,0:T(8,128)(2,1)S(1)}, u32[]{:S(2)}, u32[]{:S(2)}) collective-permute-start(bf16[2,128,1024]{2,1,0:T(8,128)(2,1)} %get-tuple-element.83), channel_id=1, source_target_pairs={{0,16},{8,24},{16,0},{24,8},{1,17},{9,25},{17,1},{25,9},{2,18},{10... | collective-permute-start | bytes 1572872 | tf_op jit(solution)/shard_map/ppermute | solution.py:90
  308.2 19.9 %collective-permute-start.43 = (bf16[2,128,1024]{2,1,0:T(8,128)(2,1)}, bf16[2,128,1024]{2,1,0:T(8,128)(2,1)S(1)}, u32[]{:S(2)}, u32[]{:S(2)}) collective-permute-start(bf16[2,128,1024]{2,1,0:T(8,128)(2,1)} %get-tuple-element.88), channel_id=1, source_target_pairs={{0,24},{8,16},{16,8},{24,0},{1,25},{9,17},{17,9},{25,1},{2,26},{10... | collective-permute-start | bytes 1572872 | tf_op jit(solution)/shard_map/ppermute | solution.py:90
  308.2 7.2 %collective-permute-start.39 = (bf16[2,128,1024]{2,1,0:T(8,128)(2,1)}, bf16[2,128,1024]{2,1,0:T(8,128)(2,1)}, u32[]{:S(2)}, u32[]{:S(2)}) collective-permute-start(bf16[2,128,1024]{2,1,0:T(8,128)(2,1)} %get-tuple-element.133), channel_id=1, source_target_pairs={{0,8},{8,0},{16,24},{24,16},{1,9},{9,1},{17,25},{25,17},{2,10},{10... | collective-permute-start | bytes 1572872 | tf_op jit(solution)/shard_map/ppermute | solution.py:90
  313.1 14.2 %collective-permute-start.44 = (bf16[1024,256]{1,0:T(8,128)(2,1)}, bf16[1024,256]{1,0:T(8,128)(2,1)}, u32[]{:S(2)}, u32[]{:S(2)}) collective-permute-start(bf16[1024,256]{1,0:T(8,128)(2,1)} %get-tuple-element.91), channel_id=1, source_target_pairs={{0,1},{1,0},{2,3},{3,2},{4,5},{5,4},{6,7},{7,6},{8,9},{9,8},{10,11... | collective-permute-start | bytes 1572872 | tf_op jit(solution)/shard_map/ppermute | solution.py:83
  319.7 17.0 %collective-permute-start.40 = (bf16[1024,256]{1,0:T(8,128)(2,1)}, bf16[1024,256]{1,0:T(8,128)(2,1)S(1)}, u32[]{:S(2)}, u32[]{:S(2)}) collective-permute-start(bf16[1024,256]{1,0:T(8,128)(2,1)} %get-tuple-element.82), channel_id=1, source_target_pairs={{0,8},{8,0},{16,24},{24,16},{1,9},{9,1},{17,25},{25,17},{2,10},{10... | collective-permute-start | bytes 1572872 | tf_op jit(solution)/shard_map/ppermute | solution.py:90
  333.4 25.9 %collective-permute-start.45 = (bf16[1024,256]{1,0:T(8,128)(2,1)}, bf16[1024,256]{1,0:T(8,128)(2,1)S(1)}, u32[]{:S(2)}, u32[]{:S(2)}) collective-permute-start(bf16[1024,256]{1,0:T(8,128)(2,1)} %get-tuple-element.95), channel_id=1, source_target_pairs={{0,24},{8,16},{16,8},{24,0},{1,25},{9,17},{17,9},{25,1},{2,26},{10... | collective-permute-start | bytes 1572872 | tf_op jit(solution)/shard_map/ppermute | solution.py:90
  335.3 23.9 %collective-permute-start.42 = (bf16[1024,256]{1,0:T(8,128)(2,1)}, bf16[1024,256]{1,0:T(8,128)(2,1)S(1)}, u32[]{:S(2)}, u32[]{:S(2)}) collective-permute-start(bf16[1024,256]{1,0:T(8,128)(2,1)} %get-tuple-element.87), channel_id=1, source_target_pairs={{0,16},{8,24},{16,0},{24,8},{1,17},{9,25},{17,1},{25,9},{2,18},{10... | collective-permute-start | bytes 1572872 | tf_op jit(solution)/shard_map/ppermute | solution.py:90
  336.7 32.1 %collective-permute-start.46 = (bf16[1024,256]{1,0:T(8,128)(2,1)S(1)}, bf16[1024,256]{1,0:T(8,128)(2,1)S(1)}, u32[]{:S(2)}, u32[]{:S(2)}) collective-permute-start(bf16[1024,256]{1,0:T(8,128)(2,1)S(1)} %collective-permute-done.40), channel_id=1, source_target_pairs={{0,1},{1,0},{2,3},{3,2},{4,5},{5,4},{6,7},{7,6},{8,9},{9,8},{10,11... | collective-permute-start | bytes 1572872 | tf_op jit(solution)/shard_map/ppermute | solution.py:83
  361.1 9.2 %collective-permute-start.52 = (bf16[1024,256]{1,0:T(8,128)(2,1)S(1)}, bf16[1024,256]{1,0:T(8,128)(2,1)S(1)}, u32[]{:S(2)}, u32[]{:S(2)}) collective-permute-start(bf16[1024,256]{1,0:T(8,128)(2,1)S(1)} %convolution_convert_fusion.6), channel_id=1, source_target_pairs={{0,8},{8,0},{16,24},{24,16},{1,9},{9,1},{17,25},{25,17},{2,10},{10... | collective-permute-start | bytes 1572872 | tf_op jit(solution)/shard_map/ppermute | solution.py:90
  366.7 14.8 %collective-permute-start.47 = (bf16[1024,256]{1,0:T(8,128)(2,1)S(1)}, bf16[1024,256]{1,0:T(8,128)(2,1)S(1)}, u32[]{:S(2)}, u32[]{:S(2)}) collective-permute-start(bf16[1024,256]{1,0:T(8,128)(2,1)S(1)} %collective-permute-done.42), channel_id=1, source_target_pairs={{0,1},{1,0},{2,3},{3,2},{4,5},{5,4},{6,7},{7,6},{8,9},{9,8},{10,11... | collective-permute-start | bytes 1572872 | tf_op jit(solution)/shard_map/ppermute | solution.py:83
  368.8 23.5 %collective-permute-start.48 = (bf16[1024,256]{1,0:T(8,128)(2,1)S(1)}, bf16[1024,256]{1,0:T(8,128)(2,1)S(1)}, u32[]{:S(2)}, u32[]{:S(2)}) collective-permute-start(bf16[1024,256]{1,0:T(8,128)(2,1)S(1)} %collective-permute-done.45), channel_id=1, source_target_pairs={{0,1},{1,0},{2,3},{3,2},{4,5},{5,4},{6,7},{7,6},{8,9},{9,8},{10,11... | collective-permute-start | bytes 1572872 | tf_op jit(solution)/shard_map/ppermute | solution.py:83
  371.1 22.1 %collective-permute-start.54 = (bf16[1024,256]{1,0:T(8,128)(2,1)S(1)}, bf16[1024,256]{1,0:T(8,128)(2,1)S(1)}, u32[]{:S(2)}, u32[]{:S(2)}) collective-permute-start(bf16[1024,256]{1,0:T(8,128)(2,1)S(1)} %fusion.16), channel_id=1, source_target_pairs={{0,16},{8,24},{16,0},{24,8},{1,17},{9,25},{17,1},{25,9},{2,18},{10... | collective-permute-start | bytes 1572872 | tf_op jit(solution)/shard_map/ppermute | solution.py:90
  393.4 33.0 %collective-permute-start.63 = (bf16[1024,256]{1,0:T(8,128)(2,1)S(1)}, bf16[1024,256]{1,0:T(8,128)(2,1)S(1)}, u32[]{:S(2)}, u32[]{:S(2)}) collective-permute-start(bf16[1024,256]{1,0:T(8,128)(2,1)S(1)} %add_convert_fusion.8), channel_id=1, source_target_pairs={{0,8},{8,0},{16,24},{24,16},{1,9},{9,1},{17,25},{25,17},{2,10},{10... | collective-permute-start | bytes 1572872 | tf_op jit(solution)/shard_map/ppermute | solution.py:90
  395.2 15.5 %collective-permute-start.51 = (bf16[2048,256]{1,0:T(8,128)(2,1)S(1)}, bf16[2048,256]{1,0:T(8,128)(2,1)S(1)}, u32[]{:S(2)}, u32[]{:S(2)}) collective-permute-start(bf16[2048,256]{1,0:T(8,128)(2,1)S(1)} %convolution_convert_fusion), channel_id=1, source_target_pairs={{0,8},{8,0},{16,24},{24,16},{1,9},{9,1},{17,25},{25,17},{2,10},{10... | collective-permute-start | bytes 3145736 | tf_op jit(solution)/shard_map/ppermute | solution.py:90
  396.1 14.4 %collective-permute-start.55 = (bf16[1024,256]{1,0:T(8,128)(2,1)S(1)}, bf16[1024,256]{1,0:T(8,128)(2,1)S(1)}, u32[]{:S(2)}, u32[]{:S(2)}) collective-permute-start(bf16[1024,256]{1,0:T(8,128)(2,1)S(1)} %fusion.17), channel_id=1, source_target_pairs={{0,16},{8,24},{16,0},{24,8},{1,17},{9,25},{17,1},{25,9},{2,18},{10... | collective-permute-start | bytes 1572872 | tf_op jit(solution)/shard_map/ppermute | solution.py:90
  398.1 22.0 %collective-permute-start.50 = (bf16[2048,256]{1,0:T(8,128)(2,1)S(1)}, bf16[2048,256]{1,0:T(8,128)(2,1)S(1)}, u32[]{:S(2)}, u32[]{:S(2)}) collective-permute-start(bf16[2048,256]{1,0:T(8,128)(2,1)S(1)} %convolution_convert_fusion.1), channel_id=1, source_target_pairs={{0,8},{8,0},{16,24},{24,16},{1,9},{9,1},{17,25},{25,17},{2,10},{10... | collective-permute-start | bytes 3145736 | tf_op jit(solution)/shard_map/ppermute | solution.py:90
  399.7 21.8 %collective-permute-start.49 = (bf16[2048,256]{1,0:T(8,128)(2,1)S(1)}, bf16[2048,256]{1,0:T(8,128)(2,1)S(1)}, u32[]{:S(2)}, u32[]{:S(2)}) collective-permute-start(bf16[2048,256]{1,0:T(8,128)(2,1)S(1)} %convolution_convert_fusion.2), channel_id=1, source_target_pairs={{0,8},{8,0},{16,24},{24,16},{1,9},{9,1},{17,25},{25,17},{2,10},{10... | collective-permute-start | bytes 3145736 | tf_op jit(solution)/shard_map/ppermute | solution.py:90
  410.6 12.2 %collective-permute-start.64 = (bf16[1024,256]{1,0:T(8,128)(2,1)S(1)}, bf16[1024,256]{1,0:T(8,128)(2,1)S(1)}, u32[]{:S(2)}, u32[]{:S(2)}) collective-permute-start(bf16[1024,256]{1,0:T(8,128)(2,1)S(1)} %add_convert_fusion.7), channel_id=1, source_target_pairs={{0,8},{8,0},{16,24},{24,16},{1,9},{9,1},{17,25},{25,17},{2,10},{10... | collective-permute-start | bytes 1572872 | tf_op jit(solution)/shard_map/ppermute | solution.py:90
  415.6 25.6 %collective-permute-start.56 = (bf16[2048,256]{1,0:T(8,128)(2,1)S(1)}, bf16[2048,256]{1,0:T(8,128)(2,1)S(1)}, u32[]{:S(2)}, u32[]{:S(2)}) collective-permute-start(bf16[2048,256]{1,0:T(8,128)(2,1)S(1)} %fusion.2), channel_id=1, source_target_pairs={{0,16},{8,24},{16,0},{24,8},{1,17},{9,25},{17,1},{25,9},{2,18},{10... | collective-permute-start | bytes 3145736 | tf_op jit(solution)/shard_map/ppermute | solution.py:90
  430.0 50.4 %collective-permute-start.65 = (bf16[2048,512]{1,0:T(8,128)(2,1)S(1)}, bf16[2048,512]{1,0:T(8,128)(2,1)S(1)}, u32[]{:S(2)}, u32[]{:S(2)}) collective-permute-start(bf16[2048,512]{1,0:T(8,128)(2,1)S(1)} %pad_maximum_fusion.3), channel_id=1, source_target_pairs={{0,2},{1,3},{2,4},{3,5},{4,6},{5,7},{6,0},{7,1},{8,10},{9,11},{10,... | collective-permute-start | bytes 6291464 | tf_op jit(solution)/shard_map/ppermute | solution.py:87
  441.2 24.8 %collective-permute-start.57 = (bf16[2048,256]{1,0:T(8,128)(2,1)S(1)}, bf16[2048,256]{1,0:T(8,128)(2,1)S(1)}, u32[]{:S(2)}, u32[]{:S(2)}) collective-permute-start(bf16[2048,256]{1,0:T(8,128)(2,1)S(1)} %fusion.1), channel_id=1, source_target_pairs={{0,16},{8,24},{16,0},{24,8},{1,17},{9,25},{17,1},{25,9},{2,18},{10... | collective-permute-start | bytes 3145736 | tf_op jit(solution)/shard_map/ppermute | solution.py:90
  442.2 24.9 %collective-permute-start.60 = (bf16[2048,256]{1,0:T(8,128)(2,1)S(1)}, bf16[2048,256]{1,0:T(8,128)(2,1)S(1)}, u32[]{:S(2)}, u32[]{:S(2)}) collective-permute-start(bf16[2048,256]{1,0:T(8,128)(2,1)S(1)} %add_convert_fusion.5), channel_id=1, source_target_pairs={{0,8},{8,0},{16,24},{24,16},{1,9},{9,1},{17,25},{25,17},{2,10},{10... | collective-permute-start | bytes 3145736 | tf_op jit(solution)/shard_map/ppermute | solution.py:90
  466.2 9.8 %collective-permute-start.62 = (bf16[2048,256]{1,0:T(8,128)(2,1)S(1)}, bf16[2048,256]{1,0:T(8,128)(2,1)S(1)}, u32[]{:S(2)}, u32[]{:S(2)}) collective-permute-start(bf16[2048,256]{1,0:T(8,128)(2,1)S(1)} %add_convert_fusion.4), channel_id=1, source_target_pairs={{0,8},{8,0},{16,24},{24,16},{1,9},{9,1},{17,25},{25,17},{2,10},{10... | collective-permute-start | bytes 3145736 | tf_op jit(solution)/shard_map/ppermute | solution.py:90
  466.3 25.6 %collective-permute-start.58 = (bf16[2048,256]{1,0:T(8,128)(2,1)S(1)}, bf16[2048,256]{1,0:T(8,128)(2,1)S(1)}, u32[]{:S(2)}, u32[]{:S(2)}) collective-permute-start(bf16[2048,256]{1,0:T(8,128)(2,1)S(1)} %fusion), channel_id=1, source_target_pairs={{0,16},{8,24},{16,0},{24,8},{1,17},{9,25},{17,1},{25,9},{2,18},{10... | collective-permute-start | bytes 3145736 | tf_op jit(solution)/shard_map/ppermute | solution.py:90
  471.1 54.2 %collective-permute-start.61 = (bf16[2048,512]{1,0:T(8,128)(2,1)}, bf16[2048,512]{1,0:T(8,128)(2,1)S(1)}, u32[]{:S(2)}, u32[]{:S(2)}) collective-permute-start(bf16[2048,512]{1,0:T(8,128)(2,1)} %pad_maximum_fusion.2), channel_id=1, source_target_pairs={{0,6},{1,7},{2,0},{3,1},{4,2},{5,3},{6,4},{7,5},{8,14},{9,15},{10,... | collective-permute-start | bytes 6291464 | tf_op jit(solution)/shard_map/ppermute | solution.py:87
  482.3 87.3 %collective-permute-start.66 = (bf16[2048,512]{1,0:T(8,128)(2,1)}, bf16[2048,512]{1,0:T(8,128)(2,1)}, u32[]{:S(2)}, u32[]{:S(2)}) collective-permute-start(bf16[2048,512]{1,0:T(8,128)(2,1)} %pad_maximum_fusion.4), channel_id=1, source_target_pairs={{0,2},{1,3},{2,4},{3,5},{4,6},{5,7},{6,0},{7,1},{8,10},{9,11},{10,... | collective-permute-start | bytes 6291464 | tf_op jit(solution)/shard_map/ppermute | solution.py:87
  492.2 6.0 %collective-permute-start.59 = (bf16[2048,256]{1,0:T(8,128)(2,1)S(1)}, bf16[2048,256]{1,0:T(8,128)(2,1)}, u32[]{:S(2)}, u32[]{:S(2)}) collective-permute-start(bf16[2048,256]{1,0:T(8,128)(2,1)S(1)} %add_convert_fusion.6), channel_id=1, source_target_pairs={{0,8},{8,0},{16,24},{24,16},{1,9},{9,1},{17,25},{25,17},{2,10},{10... | collective-permute-start | bytes 3145736 | tf_op jit(solution)/shard_map/ppermute | solution.py:90
  (11 other events, 162.3 us)

commit v2 on v1

--- a/solution.py
+++ b/solution.py
@@ -17,6 +17,40 @@
 
 def tie(x, *earlier):
     return lax.optimization_barrier((x, *earlier))[0]
+
+
+def product_kernel(n_pairs, *refs):
+    out = refs[-1]
+    total = None
+    for x, y in zip(refs[:n_pairs], refs[n_pairs : 2 * n_pairs]):
+        term = jnp.dot(x[...], y[...], preferred_element_type=F32)
+        total = term if total is None else total + term
+    for more in refs[2 * n_pairs : -1]:
+        total = total + more[...].astype(F32)
+    out[...] = total.astype(out.dtype)
+
+
+def product(pairs, kind, more=(), by_rows=True):
+    rows, columns = pairs[0][0].shape[0], pairs[0][1].shape[1]
+    if by_rows:
+        block = min(rows, 512)
+        grid, out = rows // block, pl.BlockSpec((block, columns), lambda i: (i, 0))
+        xs = [pl.BlockSpec((block, x.shape[1]), lambda i: (i, 0)) for x, _ in pairs]
+        ys = [pl.BlockSpec(y.shape, lambda i: (0, 0)) for _, y in pairs]
+    else:
+        block = min(columns, 256)
+        grid, out = columns // block, pl.BlockSpec((rows, block), lambda i: (0, i))
+        xs = [pl.BlockSpec(x.shape, lambda i: (0, 0)) for x, _ in pairs]
+        ys = [pl.BlockSpec((y.shape[0], block), lambda i: (0, i)) for _, y in pairs]
+    return pl.pallas_call(
+        functools.partial(product_kernel, len(pairs)),
+        grid=(grid,),
+        in_specs=xs + ys + [out] * len(more),
+        out_specs=out,
+        out_shape=jax.ShapeDtypeStruct((rows, columns), kind),
+        cost_estimate=pl.CostEstimate(flops=512 * rows * columns, bytes_accessed=0, transcendentals=0),
+        compiler_params=pltpu.CompilerParams(vmem_limit_bytes=16 * 2**20),
+    )(*[x for x, _ in pairs], *[y for _, y in pairs], *more)
 
 
 def moments(first, second, rot):
@@ -50,6 +84,7 @@
         ),
         out_shape=[out, out, jax.ShapeDtypeStruct((rows, blocks * sub), BF16)],
         input_output_aliases={4: 0, 5: 1} if before else {},
+        compiler_params=pltpu.CompilerParams(vmem_limit_bytes=16 * 2**20),
         cost_estimate=pl.CostEstimate(
             flops=10 * rot.size, bytes_accessed=20 * rot.size, transcendentals=2 * rot.size
         ),
@@ -106,8 +141,7 @@
             return row_xor(x, k) if k == 1 else in_turn("rows", x, lambda y: row_xor(y, k), depth)
 
         def half_sum(theirs, mine, depth):
-            got = row_xor(theirs().astype(BF16), 1)
-            mine = (mine() + got.astype(F32)).astype(BF16)
+            mine = mine(row_xor(theirs(), 1))
             last["half"] = mine
             k = 2
             while k < n_row:
@@ -166,21 +200,22 @@
         for k, s in turns:
             if (k, s) == (1, 0):
                 grads[1], grads[3], *lefts[1:] = tie((grads[1], grads[3], *lefts[1:]), right_n)
-            if (k, s) == (1, 1):
-                sent = tie(right, last["rows"][-1])
+                sent = tie(right, grads[1], grads[3])
                 below, above = a_shift(sent, 1), a_shift(sent, -1)
                 rights = [right, below, a_shift(below, 1), above]
+            if (k, s) == (1, 1):
+                grads[1] = tie(grads[1], right)
             if (k, s) == (1, far):
                 grads[far] = tie(grads[far], last["rows"][-2])
-            g = grads[s]
+            g = tie(grads[s], rights[1]) if (k, s) == turns[-1] else grads[s]
             g_mine, g_theirs = g[:half], g[half:]
             mine, theirs = half_sum(
-                lambda: dot(g_theirs, lefts[k], (1, 0)), lambda: dot(g_mine, lefts[k], (1, 0)), 1
+                lambda: product([(g_theirs, lefts[k])], BF16, by_rows=False),
+                lambda got: product([(g_mine, lefts[k])], BF16, (got,), by_rows=False),
+                1,
             )
             rotated[k] = lax.dynamic_update_slice_in_dim(rotated[k], mine, n_at(s, core), 0)
             rotated[k] = lax.dynamic_update_slice_in_dim(rotated[k], theirs, n_at(s, 1 - core), 0)
-        left = jnp.concatenate(lefts, axis=1)
-
         rot_k = jnp.zeros((n_col, sub, own_i), BF16)
         right_k = jnp.zeros((n_col * sub, n_a * width), BF16)
         swapped = []
@@ -209,37 +244,44 @@
                 kept = tie(tuple(kept), by_rows[1][0])
             *kept, direction = step(r ^ k, n_row, sub, rot, first_moment, second_moment, tuple(kept))
             if k:
-                direction = across_rows(direction, k, 2)
+                direction = across_rows(direction, k)
             by_rows[0].append(direction)
             for q in range(1, n_b):
-                by_rows[q].append(across_b(direction, -q, 2))
+                by_rows[q].append(across_b(direction, -q))
         first_new, second_new = kept
         by_rows = [jnp.concatenate(ds, axis=1) for ds in by_rows]
         direction = jnp.concatenate(by_rows, axis=0)
 
-        def back(s, parts):
+        def back(s, parts, kind):
             r_mine = lax.dynamic_slice_in_dim(right_k, n_at(s, core), half, 1)
             r_theirs = lax.dynamic_slice_in_dim(right_k, n_at(s, 1 - core), half, 1)
-            u_mine = u_theirs = 0.0
-            for i, (d, l) in enumerate(parts):
+            w_mine, w_theirs = [], []
+            for i, d in enumerate(parts):
+                d_mine = d
                 if i:
-                    d = tie(d, last["half"])
-                w_mine, w_theirs = half_sum(
-                    lambda: dot(d, r_theirs, (1, 0)), lambda: dot(d, r_mine, (1, 0)), 1
+                    d, d_mine = tie(d, last["half"]), tie(d, last["rows"][-1])
+                mine, theirs = half_sum(
+                    lambda: dot(d, r_theirs, (1, 0)).astype(BF16),
+                    lambda got: (dot(d_mine, r_mine, (1, 0)) + got.astype(F32)).astype(BF16),
+                    1,
                 )
-                u_mine = u_mine + dot(l, w_mine, (1, 0))
-                u_theirs = u_theirs + dot(l, w_theirs, (1, 0))
-            return u_mine, u_theirs
+                w_mine.append(mine)
+                w_theirs.append(theirs)
+            if len(parts) < n_b:
+                w_mine, w_theirs = [
+                    [w[0][k * own_i : (k + 1) * own_i] for k in range(n_b)] for w in (w_mine, w_theirs)
+                ]
+            return [product(list(zip(lefts, w)), kind) for w in (w_mine, w_theirs)]
 
         def joined(u):
-            return jnp.concatenate([x.astype(BF16) for x in u], axis=1)
-
-        whole = [(direction, left)]
-        passed = halves(a_shift(joined(back(2, list(zip(by_rows, lefts)))), 1))
-        behind = halves(a_shift(joined(back(1, whole)), -1))
-        ahead = lax.optimization_barrier(back(3, whole))
-        ahead = halves(a_shift(joined([u + x.astype(F32) for u, x in zip(ahead, passed)]), 1))
-        own = lax.optimization_barrier(back(0, whole))
+            return jnp.concatenate(u, axis=1)
+
+        whole = [direction]
+        passed = halves(a_shift(joined(back(2, by_rows, BF16)), 1))
+        behind = halves(a_shift(joined(back(1, whole, BF16)), -1))
+        ahead = [(u + x.astype(F32)).astype(BF16) for u, x in zip(back(3, whole, F32), passed)]
+        ahead = halves(a_shift(joined(ahead), 1))
+        own = back(0, whole, F32)
         u_mine, u_theirs = [
             (u + x.astype(F32) + y.astype(F32)).astype(BF16) for u, x, y in zip(own, behind, ahead)
         ]

time: 580 us -> 565 us (0.974)
  matrix products: 126 us -> 21 us
  Pallas kernels: 17.5 us -> 120 us
  waiting for transfers between devices: 337 us -> 311 us
  starting transfers between devices: 46.7 us -> 52.8 us
    pallas_call x0 -> x24, Pallas kernels: none -> 110 us  [product(): pl.pallas_call(functools.partial(product_kernel, len(pairs)), grid=(grid,...]
    dot_general x44 -> x18, matrix products: 126 us -> 21 us  [dot(): lax.dot_general(a, b, ((contract[:1], contract[1:]), ((), ())), preferred...]
    ppermute x10, waiting for transfers between devices: 50.7 us -> 114 us  [b_shift(): return lax.ppermute(x, 'col', perm)]
    ppermute x9, waiting for transfers between devices: 153 us -> 95.5 us  [a_shift(): return lax.ppermute(x, 'col', perm)]
    ppermute x48, waiting for transfers between devices: 133 us -> 101 us  [row_xor(): return lax.ppermute(x, 'row', [(r, r ^ k) for r in range(n_row)])]
    slice x0 -> x11, local copies, waits for them, and re-layouts: none -> 10 us  [the longest x5 8.39 us: per_device(): g_mine, g_theirs = (g[:half], g[half:])]
    ppermute x10, starting transfers between devices: 9.03 us -> 16.5 us  [b_shift(): return lax.ppermute(x, 'col', perm)]
    pallas_call x4, Pallas kernels: 17.5 us -> 10.7 us  [moments_at(): pl.pallas_call(moments_kernel, grid_spec=pltpu.PrefetchScalarGridSpec(num...]
  transfers between devices with their start and end apart: 67 -> 67, of which waited for: 28 -> 23; matrix products, arithmetic and copies ran while one was open for 27% -> 10% of each run, Pallas kernels for 3% -> 22%
where the time goes in v2:
time: 565 us; the launch traced here: 556 us
  waiting for transfers between devices  311 us (55%)
  Pallas kernels  120 us (21%)
  starting transfers between devices  52.8 us (9%)
  local copies, waits for them, and re-layouts  31.9 us (6%)
  matrix products  21 us (4%)
  other arithmetic  16.9 us (3%)
    ppermute x10, waiting for transfers between devices, b_shift(): return lax.ppermute(x, 'col', perm)  114 us
    pallas_call x24, Pallas kernels, product(): pl.pallas_call(functools.partial(product_kernel, len(pairs)), grid=(grid,...  110 us
    ppermute x48, waiting for transfers between devices, row_xor(): return lax.ppermute(x, 'row', [(r, r ^ k) for r in range(n_row)])  101 us
    ppermute x9, waiting for transfers between devices, a_shift(): return lax.ppermute(x, 'col', perm)  95.5 us
    ppermute x48, starting transfers between devices, row_xor(): return lax.ppermute(x, 'row', [(r, r ^ k) for r in range(n_row)])  24.9 us
    dot_general x18, matrix products, dot(): lax.dot_general(a, b, ((contract[:1], contract[1:]), ((), ())), preferred...  21 us
    ppermute x10, starting transfers between devices, b_shift(): return lax.ppermute(x, 'col', perm)  16.5 us
    ppermute x9, starting transfers between devices, a_shift(): return lax.ppermute(x, 'col', perm)  11.4 us
  transfers between devices with their start and end apart: 67, of which 23 were waited for; matrix products, arithmetic and copies ran while one was open for 10% of the time, Pallas kernels for 22%

profile of v2, /device:TPU:0, one launch (start us, length us, event | category | flops | bytes accessed | tf_op | source)
XLA Modules:
  0.0 555.7 jit_solution(2999094236371414628)
XLA Ops:
  0.7 1.7 constant_dynamic-slice_fusion.3
  5.1 2.9 collective-permute-start.2
  9.6 2.2 collective-permute-start.1
  13.7 1.7 fusion.46
  16.8 1.7 bitcast_dynamic-update-slice_fusion
  18.5 4.0 shard_map.76
  23.6 1.7 constant_dynamic-update-slice_fusion.25
  26.1 1.7 constant_dynamic-update-slice_fusion.24
  27.8 2.3 constant_dynamic-slice_fusion
  30.1 68.9 %collective-permute-done.2.refs_1_ = bf16[2048,1024]{1,0:T(8,128)(2,1)} collective-permute-done((bf16[2048,1024]{1,0:T(8,128)(2,1)}, bf16[2048,1024]{1,0:T(8,128)(2,1)}, u32[]{:S(2)}, u32[]{:S(2)}) %collective-permute-start.2) | collective-permute-done | bytes 4194336 | tf_op jit(solution)/shard_map/ppermute | solution.py:118
  98.9 1.7 collective-permute-start.6
  100.7 3.9 shard_map.77
  107.8 3.9 shard_map.84
  114.9 1.7 fusion.45
  116.6 4.4 shard_map.82
  121.1 3.9 shard_map.85
  126.6 1.7 fusion.44
  128.2 4.8 shard_map.80
  133.2 4.8 shard_map.83
  142.9 4.8 shard_map.78
  149.4 2.0 copy-done.8
  151.9 4.0 shard_map.81
  159.1 3.9 shard_map.79
  165.8 4.1 collective-permute-done.16
  170.4 1.7 fusion.43
  172.1 3.9 shard_map.88
  176.2 3.9 shard_map.86
  180.7 3.7 collective-permute-start.35
  184.8 3.9 shard_map.89
  191.1 3.9 shard_map.87
  195.6 7.6 %collective-permute-done.22 = bf16[256,1024]{1,0:T(8,128)(2,1)S(1)} collective-permute-done((bf16[256,1024]{1,0:T(8,128)(2,1)S(1)}, bf16[256,1024]{1,0:T(8,128)(2,1)S(1)}, u32[]{:S(2)}, u32[]{:S(2)}) %collective-permute-start.22) | collective-permute-done | bytes 524320 | tf_op jit(solution)/shard_map/ppermute | solution.py:125
  203.4 1.7 fusion.42
  205.1 4.0 shard_map.90
  214.1 9.5 %collective-permute-done.23 = bf16[256,1024]{1,0:T(8,128)(2,1)S(1)} collective-permute-done((bf16[256,1024]{1,0:T(8,128)(2,1)S(1)}, bf16[256,1024]{1,0:T(8,128)(2,1)S(1)}, u32[]{:S(2)}, u32[]{:S(2)}) %collective-permute-start.23) | collective-permute-done | bytes 524320 | tf_op jit(solution)/shard_map/ppermute | solution.py:125
  224.1 4.0 shard_map.91
  232.5 9.9 %collective-permute-done.27 = bf16[256,1024]{1,0:T(8,128)(2,1)S(1)} collective-permute-done((bf16[256,1024]{1,0:T(8,128)(2,1)S(1)}, bf16[256,1024]{1,0:T(8,128)(2,1)S(1)}, u32[]{:S(2)}, u32[]{:S(2)}) %collective-permute-start.27) | collective-permute-done | bytes 524320 | tf_op jit(solution)/shard_map/ppermute | solution.py:125
  249.5 21.2 %collective-permute-done.37 = bf16[256,2048]{0,1:T(8,128)(2,1)S(1)} collective-permute-done((bf16[256,2048]{0,1:T(8,128)(2,1)S(1)}, bf16[256,2048]{0,1:T(8,128)(2,1)S(1)}, u32[]{:S(2)}, u32[]{:S(2)}) %collective-permute-start.37) | collective-permute-done | bytes 1048608 | tf_op jit(solution)/shard_map/ppermute | solution.py:122
  274.9 10.7 %collective-permute-done.38 = bf16[256,1024]{1,0:T(8,128)(2,1)S(1)} collective-permute-done((bf16[256,1024]{1,0:T(8,128)(2,1)S(1)}, bf16[256,1024]{1,0:T(8,128)(2,1)S(1)}, u32[]{:S(2)}, u32[]{:S(2)}) %collective-permute-start.38) | collective-permute-done | bytes 524320 | tf_op jit(solution)/shard_map/ppermute | solution.py:118
  287.3 1.6 collective-permute-start.42
  289.8 2.6 shard_map.92
  293.9 2.6 shard_map.93
  296.6 16.3 %collective-permute-done.41.rot_ref = bf16[2,128,1024]{2,1,0:T(8,128)(2,1)S(1)} collective-permute-done((bf16[2,128,1024]{2,1,0:T(8,128)(2,1)S(1)}, bf16[2,128,1024]{2,1,0:T(8,128)(2,1)S(1)}, u32[]{:S(2)}, u32[]{:S(2)}) %collective-permute-start.41) | collective-permute-done | bytes 524320 | tf_op jit(solution)/shard_map/ppermute | solution.py:125
  312.8 2.6 shard_map.94
  317.3 2.8 shard_map.95
  320.1 8.7 %collective-permute-done.43 = bf16[1024,256]{1,0:T(8,128)(2,1)S(1)} collective-permute-done((bf16[1024,256]{1,0:T(8,128)(2,1)S(1)}, bf16[1024,256]{1,0:T(8,128)(2,1)S(1)}, u32[]{:S(2)}, u32[]{:S(2)}) %collective-permute-start.43) | collective-permute-done | bytes 524320 | tf_op jit(solution)/shard_map/ppermute | solution.py:125
  330.7 12.3 %collective-permute-done.46 = bf16[1024,256]{1,0:T(8,128)(2,1)S(1)} collective-permute-done((bf16[1024,256]{1,0:T(8,128)(2,1)S(1)}, bf16[1024,256]{1,0:T(8,128)(2,1)S(1)}, u32[]{:S(2)}, u32[]{:S(2)}) %collective-permute-start.46) | collective-permute-done | bytes 524320 | tf_op jit(solution)/shard_map/ppermute | solution.py:118
  345.6 11.7 %collective-permute-done.47 = bf16[1024,256]{1,0:T(8,128)(2,1)S(1)} collective-permute-done((bf16[1024,256]{1,0:T(8,128)(2,1)S(1)}, bf16[1024,256]{1,0:T(8,128)(2,1)S(1)}, u32[]{:S(2)}, u32[]{:S(2)}) %collective-permute-start.47) | collective-permute-done | bytes 524320 | tf_op jit(solution)/shard_map/ppermute | solution.py:118
  360.9 9.8 %collective-permute-done.48 = bf16[1024,256]{1,0:T(8,128)(2,1)S(1)} collective-permute-done((bf16[1024,256]{1,0:T(8,128)(2,1)S(1)}, bf16[1024,256]{1,0:T(8,128)(2,1)S(1)}, u32[]{:S(2)}, u32[]{:S(2)}) %collective-permute-start.48) | collective-permute-done | bytes 524320 | tf_op jit(solution)/shard_map/ppermute | solution.py:118
  377.6 10.7 %collective-permute-done.55 = bf16[1024,256]{1,0:T(8,128)(2,1)S(1)} collective-permute-done((bf16[1024,256]{1,0:T(8,128)(2,1)S(1)}, bf16[1024,256]{1,0:T(8,128)(2,1)S(1)}, u32[]{:S(2)}, u32[]{:S(2)}) %collective-permute-start.55) | collective-permute-done | bytes 524320 | tf_op jit(solution)/shard_map/ppermute | solution.py:125
  392.5 5.4 shard_map.100
  397.9 5.4 shard_map.101
  403.4 9.3 %collective-permute-done.56 = bf16[2048,256]{1,0:T(8,128)(2,1)S(1)} collective-permute-done((bf16[2048,256]{1,0:T(8,128)(2,1)S(1)}, bf16[2048,256]{1,0:T(8,128)(2,1)S(1)}, u32[]{:S(2)}, u32[]{:S(2)}) %collective-permute-start.56) | collective-permute-done | bytes 1048608 | tf_op jit(solution)/shard_map/ppermute | solution.py:125
  415.4 20.8 %collective-permute-done.57 = bf16[2048,256]{1,0:T(8,128)(2,1)S(1)} collective-permute-done((bf16[2048,256]{1,0:T(8,128)(2,1)S(1)}, bf16[2048,256]{1,0:T(8,128)(2,1)S(1)}, u32[]{:S(2)}, u32[]{:S(2)}) %collective-permute-start.57) | collective-permute-done | bytes 1048608 | tf_op jit(solution)/shard_map/ppermute | solution.py:125
  436.6 5.5 shard_map.97
  442.7 5.4 shard_map.98
  449.8 5.5 shard_map.99
  455.4 5.4 shard_map.102
  460.8 3.3 collective-permute-done.63
  468.1 5.4 shard_map.96
  474.8 5.4 shard_map.103
  480.2 28.9 %collective-permute-done.60 = bf16[2048,512]{1,0:T(8,128)(2,1)S(1)} collective-permute-done((bf16[2048,512]{1,0:T(8,128)(2,1)}, bf16[2048,512]{1,0:T(8,128)(2,1)S(1)}, u32[]{:S(2)}, u32[]{:S(2)}) %collective-permute-start.60) | collective-permute-done | bytes 2097184 | tf_op jit(solution)/shard_map/ppermute | solution.py:122
  509.1 42.1 %collective-permute-done.65 = bf16[2048,512]{1,0:T(8,128)(2,1)} collective-permute-done((bf16[2048,512]{1,0:T(8,128)(2,1)}, bf16[2048,512]{1,0:T(8,128)(2,1)}, u32[]{:S(2)}, u32[]{:S(2)}) %collective-permute-start.65) | collective-permute-done | bytes 2097184 | tf_op jit(solution)/shard_map/ppermute | solution.py:122
  551.2 2.4 add_convert_fusion.1
  553.6 1.9 maximum_select_fusion
  (234 shorter events, 91.4 us)
Async XLA Ops:
  5.1 93.8 %collective-permute-start.2 = (bf16[2048,1024]{1,0:T(8,128)(2,1)}, bf16[2048,1024]{1,0:T(8,128)(2,1)}, u32[]{:S(2)}, u32[]{:S(2)}) collective-permute-start(bf16[2048,1024]{1,0:T(8,128)(2,1)} %refs_0_.7), channel_id=1, source_target_pairs={{0,1},{1,0},{2,3},{3,2},{4,5},{5,4},{6,7},{7,6},{8,9},{9,8},{10,11... | collective-permute-start | bytes 12582920 | tf_op jit(solution)/shard_map/ppermute | solution.py:118
  8.1 98.2 %collective-permute-start = (bf16[512,2048]{1,0:T(8,128)(2,1)}, bf16[512,2048]{1,0:T(8,128)(2,1)}, u32[]{:S(2)}, u32[]{:S(2)}) collective-permute-start(bf16[512,2048]{1,0:T(8,128)(2,1)} %pad_maximum_fusion.1), channel_id=1, source_target_pairs={{0,2},{1,3},{2,4},{3,5},{4,6},{5,7},{6,0},{7,1},{8,10},{9,11},{10,... | collective-permute-start | bytes 6291464 | tf_op jit(solution)/shard_map/ppermute | solution.py:122
  9.6 98.2 %collective-permute-start.1 = (bf16[512,2048]{1,0:T(8,128)(2,1)}, bf16[512,2048]{1,0:T(8,128)(2,1)}, u32[]{:S(2)}, u32[]{:S(2)}) collective-permute-start(bf16[512,2048]{1,0:T(8,128)(2,1)} %pad_maximum_fusion.1), channel_id=1, source_target_pairs={{0,6},{1,7},{2,0},{3,1},{4,2},{5,3},{6,4},{7,5},{8,14},{9,15},{10,... | collective-permute-start | bytes 6291464 | tf_op jit(solution)/shard_map/ppermute | solution.py:122
  12.1 11.1 %collective-permute-start.4 = (bf16[128,1024]{0,1:T(8,128)(2,1)S(1)}, bf16[128,1024]{0,1:T(8,128)(2,1)}, u32[]{:S(2)}, u32[]{:S(2)}) collective-permute-start(bf16[128,1024]{0,1:T(8,128)(2,1)S(1)} %get-tuple-element.162), channel_id=1, source_target_pairs={{0,16},{8,24},{16,0},{24,8},{1,17},{9,25},{17,1},{25,9},{2,18},{10... | collective-permute-start | bytes 786440 | tf_op jit(solution)/shard_map/ppermute | solution.py:125
  15.4 10.7 %collective-permute-start.5 = (bf16[128,1024]{0,1:T(8,128)(2,1)S(1)}, bf16[128,1024]{0,1:T(8,128)(2,1)}, u32[]{:S(2)}, u32[]{:S(2)}) collective-permute-start(bf16[128,1024]{0,1:T(8,128)(2,1)S(1)} %get-tuple-element.161), channel_id=1, source_target_pairs={{0,24},{8,16},{16,8},{24,0},{1,25},{9,17},{17,9},{25,1},{2,26},{10... | collective-permute-start | bytes 786440 | tf_op jit(solution)/shard_map/ppermute | solution.py:125
  23.2 77.5 %collective-permute-start.7 = (bf16[256,1024]{1,0:T(8,128)(2,1)S(1)}, bf16[256,1024]{1,0:T(8,128)(2,1)S(1)}, u32[]{:S(2)}, u32[]{:S(2)}) collective-permute-start(bf16[256,1024]{1,0:T(8,128)(2,1)S(1)} %shard_map.76), channel_id=1, source_target_pairs={{0,8},{8,0},{16,24},{24,16},{1,9},{9,1},{17,25},{25,17},{2,10},{10... | collective-permute-start | bytes 1572872 | tf_op jit(solution)/shard_map/ppermute | solution.py:125
  98.9 13.4 %collective-permute-start.6 = (bf16[128,2048]{0,1:T(8,128)(2,1)}, bf16[128,2048]{0,1:T(8,128)(2,1)}, u32[]{:S(2)}, u32[]{:S(2)}) collective-permute-start(bf16[128,2048]{0,1:T(8,128)(2,1)} %bitcast.9), channel_id=1, source_target_pairs={{0,1},{1,0},{2,3},{3,2},{4,5},{5,4},{6,7},{7,6},{8,9},{9,8},{10,11... | collective-permute-start | bytes 1572872 | tf_op jit(solution)/shard_map/ppermute | solution.py:118
  104.6 20.4 %collective-permute-start.8 = (bf16[256,1024]{1,0:T(8,128)(2,1)S(1)}, bf16[256,1024]{1,0:T(8,128)(2,1)S(1)}, u32[]{:S(2)}, u32[]{:S(2)}) collective-permute-start(bf16[256,1024]{1,0:T(8,128)(2,1)S(1)} %shard_map.77), channel_id=1, source_target_pairs={{0,16},{8,24},{16,0},{24,8},{1,17},{9,25},{17,1},{25,9},{2,18},{10... | collective-permute-start | bytes 1572872 | tf_op jit(solution)/shard_map/ppermute | solution.py:125
  106.2 64.2 %collective-permute-start.20 = (bf16[512,2048]{1,0:T(8,128)(2,1)}, bf16[512,2048]{1,0:T(8,128)(2,1)}, u32[]{:S(2)}, u32[]{:S(2)}) collective-permute-start(bf16[512,2048]{1,0:T(8,128)(2,1)} %collective-permute-done), channel_id=1, source_target_pairs={{0,2},{1,3},{2,4},{3,5},{4,6},{5,7},{6,0},{7,1},{8,10},{9,11},{10,... | collective-permute-start | bytes 6291464 | tf_op jit(solution)/shard_map/ppermute | solution.py:122
  111.7 9.3 %collective-permute-start.13 = (bf16[256,1024]{1,0:T(8,128)(2,1)S(1)}, bf16[256,1024]{1,0:T(8,128)(2,1)S(1)}, u32[]{:S(2)}, u32[]{:S(2)}) collective-permute-start(bf16[256,1024]{1,0:T(8,128)(2,1)S(1)} %shard_map.84), channel_id=1, source_target_pairs={{0,8},{8,0},{16,24},{24,16},{1,9},{9,1},{17,25},{25,17},{2,10},{10... | collective-permute-start | bytes 1572872 | tf_op jit(solution)/shard_map/ppermute | solution.py:125
  121.0 12.3 %collective-permute-start.12 = (bf16[256,1024]{1,0:T(8,128)(2,1)S(1)}, bf16[256,1024]{1,0:T(8,128)(2,1)S(1)}, u32[]{:S(2)}, u32[]{:S(2)}) collective-permute-start(bf16[256,1024]{1,0:T(8,128)(2,1)S(1)} %shard_map.82), channel_id=1, source_target_pairs={{0,8},{8,0},{16,24},{24,16},{1,9},{9,1},{17,25},{25,17},{2,10},{10... | collective-permute-start | bytes 1572872 | tf_op jit(solution)/shard_map/ppermute | solution.py:125
  125.0 14.4 %collective-permute-start.14 = (bf16[256,1024]{1,0:T(8,128)(2,1)S(1)}, bf16[256,1024]{1,0:T(8,128)(2,1)S(1)}, u32[]{:S(2)}, u32[]{:S(2)}) collective-permute-start(bf16[256,1024]{1,0:T(8,128)(2,1)S(1)} %shard_map.85), channel_id=1, source_target_pairs={{0,16},{8,24},{16,0},{24,8},{1,17},{9,25},{17,1},{25,9},{2,18},{10... | collective-permute-start | bytes 1572872 | tf_op jit(solution)/shard_map/ppermute | solution.py:125
  133.0 18.9 %collective-permute-start.11 = (bf16[256,1024]{1,0:T(8,128)(2,1)}, bf16[256,1024]{1,0:T(8,128)(2,1)}, u32[]{:S(2)}, u32[]{:S(2)}) collective-permute-start(bf16[256,1024]{1,0:T(8,128)(2,1)} %shard_map.80), channel_id=1, source_target_pairs={{0,8},{8,0},{16,24},{24,16},{1,9},{9,1},{17,25},{25,17},{2,10},{10... | collective-permute-start | bytes 1572872 | tf_op jit(solution)/shard_map/ppermute | solution.py:125
  140.2 15.7 %collective-permute-start.15 = (bf16[256,1024]{1,0:T(8,128)(2,1)}, bf16[256,1024]{1,0:T(8,128)(2,1)}, u32[]{:S(2)}, u32[]{:S(2)}) collective-permute-start(bf16[256,1024]{1,0:T(8,128)(2,1)} %shard_map.83), channel_id=1, source_target_pairs={{0,16},{8,24},{16,0},{24,8},{1,17},{9,25},{17,1},{25,9},{2,18},{10... | collective-permute-start | bytes 1572872 | tf_op jit(solution)/shard_map/ppermute | solution.py:125
  147.7 9.7 %collective-permute-start.10 = (bf16[256,1024]{1,0:T(8,128)(2,1)}, bf16[256,1024]{1,0:T(8,128)(2,1)}, u32[]{:S(2)}, u32[]{:S(2)}) collective-permute-start(bf16[256,1024]{1,0:T(8,128)(2,1)} %shard_map.78), channel_id=1, source_target_pairs={{0,8},{8,0},{16,24},{24,16},{1,9},{9,1},{17,25},{25,17},{2,10},{10... | collective-permute-start | bytes 1572872 | tf_op jit(solution)/shard_map/ppermute | solution.py:125
  151.4 11.6 %collective-permute-start.29 = (bf16[256,1024]{1,0:T(8,128)(2,1)}, bf16[256,1024]{1,0:T(8,128)(2,1)}, u32[]{:S(2)}, u32[]{:S(2)}) collective-permute-start(bf16[256,1024]{1,0:T(8,128)(2,1)} %get-tuple-element.124), channel_id=1, source_target_pairs={{0,8},{8,0},{16,24},{24,16},{1,9},{9,1},{17,25},{25,17},{2,10},{10... | collective-permute-start | bytes 1572872 | tf_op jit(solution)/shard_map/ppermute | solution.py:125
  156.0 13.9 %collective-permute-start.16 = (bf16[256,1024]{1,0:T(8,128)(2,1)S(1)}, bf16[256,1024]{1,0:T(8,128)(2,1)S(1)}, u32[]{:S(2)}, u32[]{:S(2)}) collective-permute-start(bf16[256,1024]{1,0:T(8,128)(2,1)S(1)} %shard_map.81), channel_id=1, source_target_pairs={{0,16},{8,24},{16,0},{24,8},{1,17},{9,25},{17,1},{25,9},{2,18},{10... | collective-permute-start | bytes 1572872 | tf_op jit(solution)/shard_map/ppermute | solution.py:125
  157.4 18.7 %collective-permute-start.9 = (bf16[256,1024]{1,0:T(8,128)(2,1)S(1)}, bf16[256,1024]{1,0:T(8,128)(2,1)S(1)}, u32[]{:S(2)}, u32[]{:S(2)}) collective-permute-start(bf16[256,1024]{1,0:T(8,128)(2,1)S(1)} %get-tuple-element.116), channel_id=1, source_target_pairs={{0,8},{8,0},{16,24},{24,16},{1,9},{9,1},{17,25},{25,17},{2,10},{10... | collective-permute-start | bytes 1572872 | tf_op jit(solution)/shard_map/ppermute | solution.py:125
  157.5 37.5 %collective-permute-start.25 = (bf16[256,2048]{0,1:T(8,128)(2,1)S(1)}, bf16[256,2048]{0,1:T(8,128)(2,1)S(1)}, u32[]{:S(2)}, u32[]{:S(2)}) collective-permute-start(bf16[256,2048]{0,1:T(8,128)(2,1)S(1)} %copy-done.10), channel_id=1, source_target_pairs={{0,2},{1,3},{2,4},{3,5},{4,6},{5,7},{6,0},{7,1},{8,10},{9,11},{10,... | collective-permute-start | bytes 3145736 | tf_op jit(solution)/shard_map/ppermute | solution.py:122
  165.6 15.1 %collective-permute-start.30 = (bf16[256,1024]{1,0:T(8,128)(2,1)S(1)}, bf16[256,1024]{1,0:T(8,128)(2,1)S(1)}, u32[]{:S(2)}, u32[]{:S(2)}) collective-permute-start(bf16[256,1024]{1,0:T(8,128)(2,1)S(1)} %get-tuple-element.122), channel_id=1, source_target_pairs={{0,8},{8,0},{16,24},{24,16},{1,9},{9,1},{17,25},{25,17},{2,10},{10... | collective-permute-start | bytes 1572872 | tf_op jit(solution)/shard_map/ppermute | solution.py:125
  169.9 18.9 %collective-permute-start.17 = (bf16[256,1024]{1,0:T(8,128)(2,1)S(1)}, bf16[256,1024]{1,0:T(8,128)(2,1)S(1)}, u32[]{:S(2)}, u32[]{:S(2)}) collective-permute-start(bf16[256,1024]{1,0:T(8,128)(2,1)S(1)} %shard_map.79), channel_id=1, source_target_pairs={{0,16},{8,24},{16,0},{24,8},{1,17},{9,25},{17,1},{25,9},{2,18},{10... | collective-permute-start | bytes 1572872 | tf_op jit(solution)/shard_map/ppermute | solution.py:125
  176.1 8.7 %collective-permute-start.21 = (bf16[256,1024]{1,0:T(8,128)(2,1)S(1)}, bf16[256,1024]{1,0:T(8,128)(2,1)S(1)}, u32[]{:S(2)}, u32[]{:S(2)}) collective-permute-start(bf16[256,1024]{1,0:T(8,128)(2,1)S(1)} %shard_map.88), channel_id=1, source_target_pairs={{0,8},{8,0},{16,24},{24,16},{1,9},{9,1},{17,25},{25,17},{2,10},{10... | collective-permute-start | bytes 1572872 | tf_op jit(solution)/shard_map/ppermute | solution.py:125
  180.1 10.9 %collective-permute-start.19 = (bf16[256,1024]{1,0:T(8,128)(2,1)S(1)}, bf16[256,1024]{1,0:T(8,128)(2,1)S(1)}, u32[]{:S(2)}, u32[]{:S(2)}) collective-permute-start(bf16[256,1024]{1,0:T(8,128)(2,1)S(1)} %shard_map.86), channel_id=1, source_target_pairs={{0,8},{8,0},{16,24},{24,16},{1,9},{9,1},{17,25},{25,17},{2,10},{10... | collective-permute-start | bytes 1572872 | tf_op jit(solution)/shard_map/ppermute | solution.py:125
  180.7 62.7 %collective-permute-start.35 = (bf16[256,2048]{0,1:T(8,128)(2,1)S(1)}, bf16[256,2048]{0,1:T(8,128)(2,1)S(1)}, u32[]{:S(2)}, u32[]{:S(2)}) collective-permute-start(bf16[256,2048]{0,1:T(8,128)(2,1)S(1)} %copy-done.10), channel_id=1, source_target_pairs={{0,6},{1,7},{2,0},{3,1},{4,2},{5,3},{6,4},{7,5},{8,14},{9,15},{10,... | collective-permute-start | bytes 3145736 | tf_op jit(solution)/shard_map/ppermute | solution.py:122
  184.7 10.8 %collective-permute-start.31 = (bf16[256,1024]{1,0:T(8,128)(2,1)S(1)}, bf16[256,1024]{1,0:T(8,128)(2,1)S(1)}, u32[]{:S(2)}, u32[]{:S(2)}) collective-permute-start(bf16[256,1024]{1,0:T(8,128)(2,1)S(1)} %get-tuple-element.120), channel_id=1, source_target_pairs={{0,8},{8,0},{16,24},{24,16},{1,9},{9,1},{17,25},{25,17},{2,10},{10... | collective-permute-start | bytes 1572872 | tf_op jit(solution)/shard_map/ppermute | solution.py:125
  188.8 14.4 %collective-permute-start.22 = (bf16[256,1024]{1,0:T(8,128)(2,1)S(1)}, bf16[256,1024]{1,0:T(8,128)(2,1)S(1)}, u32[]{:S(2)}, u32[]{:S(2)}) collective-permute-start(bf16[256,1024]{1,0:T(8,128)(2,1)S(1)} %shard_map.89), channel_id=1, source_target_pairs={{0,16},{8,24},{16,0},{24,8},{1,17},{9,25},{17,1},{25,9},{2,18},{10... | collective-permute-start | bytes 1572872 | tf_op jit(solution)/shard_map/ppermute | solution.py:125
  195.3 15.9 %collective-permute-start.18 = (bf16[256,1024]{1,0:T(8,128)(2,1)S(1)}, bf16[256,1024]{1,0:T(8,128)(2,1)S(1)}, u32[]{:S(2)}, u32[]{:S(2)}) collective-permute-start(bf16[256,1024]{1,0:T(8,128)(2,1)S(1)} %get-tuple-element.114), channel_id=1, source_target_pairs={{0,8},{8,0},{16,24},{24,16},{1,9},{9,1},{17,25},{25,17},{2,10},{10... | collective-permute-start | bytes 1572872 | tf_op jit(solution)/shard_map/ppermute | solution.py:125
  203.4 7.9 %collective-permute-start.32 = (bf16[256,1024]{1,0:T(8,128)(2,1)S(1)}, bf16[256,1024]{1,0:T(8,128)(2,1)S(1)}, u32[]{:S(2)}, u32[]{:S(2)}) collective-permute-start(bf16[256,1024]{1,0:T(8,128)(2,1)S(1)} %get-tuple-element.118), channel_id=1, source_target_pairs={{0,8},{8,0},{16,24},{24,16},{1,9},{9,1},{17,25},{25,17},{2,10},{10... | collective-permute-start | bytes 1572872 | tf_op jit(solution)/shard_map/ppermute | solution.py:125
  209.1 15.0 %collective-permute-start.26 = (bf16[256,1024]{1,0:T(8,128)(2,1)S(1)}, bf16[256,1024]{1,0:T(8,128)(2,1)S(1)}, u32[]{:S(2)}, u32[]{:S(2)}) collective-permute-start(bf16[256,1024]{1,0:T(8,128)(2,1)S(1)} %shard_map.90), channel_id=1, source_target_pairs={{0,8},{8,0},{16,24},{24,16},{1,9},{9,1},{17,25},{25,17},{2,10},{10... | collective-permute-start | bytes 1572872 | tf_op jit(solution)/shard_map/ppermute | solution.py:125
  209.7 13.9 %collective-permute-start.23 = (bf16[256,1024]{1,0:T(8,128)(2,1)S(1)}, bf16[256,1024]{1,0:T(8,128)(2,1)S(1)}, u32[]{:S(2)}, u32[]{:S(2)}) collective-permute-start(bf16[256,1024]{1,0:T(8,128)(2,1)S(1)} %shard_map.87), channel_id=1, source_target_pairs={{0,16},{8,24},{16,0},{24,8},{1,17},{9,25},{17,1},{25,9},{2,18},{10... | collective-permute-start | bytes 1572872 | tf_op jit(solution)/shard_map/ppermute | solution.py:125
  212.6 18.4 %collective-permute-start.33 = (bf16[256,1024]{1,0:T(8,128)(2,1)S(1)}, bf16[256,1024]{1,0:T(8,128)(2,1)S(1)}, u32[]{:S(2)}, u32[]{:S(2)}) collective-permute-start(bf16[256,1024]{1,0:T(8,128)(2,1)S(1)} %convolution_convert_fusion.8), channel_id=1, source_target_pairs={{0,1},{1,0},{2,3},{3,2},{4,5},{5,4},{6,7},{7,6},{8,9},{9,8},{10,11... | collective-permute-start | bytes 1572872 | tf_op jit(solution)/shard_map/ppermute | solution.py:118
  223.8 8.7 %collective-permute-start.24 = (bf16[256,1024]{1,0:T(8,128)(2,1)S(1)}, bf16[256,1024]{1,0:T(8,128)(2,1)S(1)}, u32[]{:S(2)}, u32[]{:S(2)}) collective-permute-start(bf16[256,1024]{1,0:T(8,128)(2,1)S(1)} %get-tuple-element.112), channel_id=1, source_target_pairs={{0,8},{8,0},{16,24},{24,16},{1,9},{9,1},{17,25},{25,17},{2,10},{10... | collective-permute-start | bytes 1572872 | tf_op jit(solution)/shard_map/ppermute | solution.py:125
  228.1 14.4 %collective-permute-start.27 = (bf16[256,1024]{1,0:T(8,128)(2,1)S(1)}, bf16[256,1024]{1,0:T(8,128)(2,1)S(1)}, u32[]{:S(2)}, u32[]{:S(2)}) collective-permute-start(bf16[256,1024]{1,0:T(8,128)(2,1)S(1)} %shard_map.91), channel_id=1, source_target_pairs={{0,16},{8,24},{16,0},{24,8},{1,17},{9,25},{17,1},{25,9},{2,18},{10... | collective-permute-start | bytes 1572872 | tf_op jit(solution)/shard_map/ppermute | solution.py:125
  230.9 14.1 %collective-permute-start.34 = (bf16[256,1024]{1,0:T(8,128)(2,1)S(1)}, bf16[256,1024]{1,0:T(8,128)(2,1)S(1)}, u32[]{:S(2)}, u32[]{:S(2)}) collective-permute-start(bf16[256,1024]{1,0:T(8,128)(2,1)S(1)} %convolution_convert_fusion.7), channel_id=1, source_target_pairs={{0,1},{1,0},{2,3},{3,2},{4,5},{5,4},{6,7},{7,6},{8,9},{9,8},{10,11... | collective-permute-start | bytes 1572872 | tf_op jit(solution)/shard_map/ppermute | solution.py:118
  242.7 3.8 collective-permute-start.28
  243.0 27.8 %collective-permute-start.37 = (bf16[256,2048]{0,1:T(8,128)(2,1)S(1)}, bf16[256,2048]{0,1:T(8,128)(2,1)S(1)}, u32[]{:S(2)}, u32[]{:S(2)}) collective-permute-start(bf16[256,2048]{0,1:T(8,128)(2,1)S(1)} %collective-permute-done.25), channel_id=1, source_target_pairs={{0,2},{1,3},{2,4},{3,5},{4,6},{5,7},{6,0},{7,1},{8,10},{9,11},{10,... | collective-permute-start | bytes 3145736 | tf_op jit(solution)/shard_map/ppermute | solution.py:122
  245.1 27.0 %collective-permute-start.36 = (bf16[256,1024]{1,0:T(8,128)(2,1)S(1)}, bf16[256,1024]{1,0:T(8,128)(2,1)S(1)}, u32[]{:S(2)}, u32[]{:S(2)}) collective-permute-start(bf16[256,1024]{1,0:T(8,128)(2,1)S(1)} %convolution_convert_fusion.6), channel_id=1, source_target_pairs={{0,1},{1,0},{2,3},{3,2},{4,5},{5,4},{6,7},{7,6},{8,9},{9,8},{10,11... | collective-permute-start | bytes 1572872 | tf_op jit(solution)/shard_map/ppermute | solution.py:118
  272.1 13.6 %collective-permute-start.38 = (bf16[256,1024]{1,0:T(8,128)(2,1)S(1)}, bf16[256,1024]{1,0:T(8,128)(2,1)S(1)}, u32[]{:S(2)}, u32[]{:S(2)}) collective-permute-start(bf16[256,1024]{1,0:T(8,128)(2,1)S(1)} %convolution_convert_fusion.5), channel_id=1, source_target_pairs={{0,1},{1,0},{2,3},{3,2},{4,5},{5,4},{6,7},{7,6},{8,9},{9,8},{10,11... | collective-permute-start | bytes 1572872 | tf_op jit(solution)/shard_map/ppermute | solution.py:118
  287.2 6.7 %collective-permute-start.39 = (bf16[2,128,1024]{2,1,0:T(8,128)(2,1)S(1)}, bf16[2,128,1024]{2,1,0:T(8,128)(2,1)S(1)}, u32[]{:S(2)}, u32[]{:S(2)}) collective-permute-start(bf16[2,128,1024]{2,1,0:T(8,128)(2,1)S(1)} %get-tuple-element.131), channel_id=1, source_target_pairs={{0,8},{8,0},{16,24},{24,16},{1,9},{9,1},{17,25},{25,17},{2,10},{10... | collective-permute-start | bytes 1572872 | tf_op jit(solution)/shard_map/ppermute | solution.py:125
  287.3 28.1 %collective-permute-start.42 = (bf16[2,128,1024]{2,1,0:T(8,128)(2,1)S(1)}, bf16[2,128,1024]{2,1,0:T(8,128)(2,1)S(1)}, u32[]{:S(2)}, u32[]{:S(2)}) collective-permute-start(bf16[2,128,1024]{2,1,0:T(8,128)(2,1)S(1)} %get-tuple-element.88), channel_id=1, source_target_pairs={{0,24},{8,16},{16,8},{24,0},{1,25},{9,17},{17,9},{25,1},{2,26},{10... | collective-permute-start | bytes 1572872 | tf_op jit(solution)/shard_map/ppermute | solution.py:125
  288.9 23.9 %collective-permute-start.41 = (bf16[2,128,1024]{2,1,0:T(8,128)(2,1)S(1)}, bf16[2,128,1024]{2,1,0:T(8,128)(2,1)S(1)}, u32[]{:S(2)}, u32[]{:S(2)}) collective-permute-start(bf16[2,128,1024]{2,1,0:T(8,128)(2,1)S(1)} %get-tuple-element.84), channel_id=1, source_target_pairs={{0,16},{8,24},{16,0},{24,8},{1,17},{9,25},{17,1},{25,9},{2,18},{10... | collective-permute-start | bytes 1572872 | tf_op jit(solution)/shard_map/ppermute | solution.py:125
  292.5 24.8 %collective-permute-start.44 = (bf16[1024,256]{1,0:T(8,128)(2,1)S(1)}, bf16[1024,256]{1,0:T(8,128)(2,1)S(1)}, u32[]{:S(2)}, u32[]{:S(2)}) collective-permute-start(bf16[1024,256]{1,0:T(8,128)(2,1)S(1)} %get-tuple-element.92), channel_id=1, source_target_pairs={{0,1},{1,0},{2,3},{3,2},{4,5},{5,4},{6,7},{7,6},{8,9},{9,8},{10,11... | collective-permute-start | bytes 1572872 | tf_op jit(solution)/shard_map/ppermute | solution.py:118
  296.5 32.3 %collective-permute-start.40 = (bf16[1024,256]{1,0:T(8,128)(2,1)S(1)}, bf16[1024,256]{1,0:T(8,128)(2,1)S(1)}, u32[]{:S(2)}, u32[]{:S(2)}) collective-permute-start(bf16[1024,256]{1,0:T(8,128)(2,1)S(1)} %get-tuple-element.83), channel_id=1, source_target_pairs={{0,8},{8,0},{16,24},{24,16},{1,9},{9,1},{17,25},{25,17},{2,10},{10... | collective-permute-start | bytes 1572872 | tf_op jit(solution)/shard_map/ppermute | solution.py:125
  315.4 13.4 %collective-permute-start.43 = (bf16[1024,256]{1,0:T(8,128)(2,1)S(1)}, bf16[1024,256]{1,0:T(8,128)(2,1)S(1)}, u32[]{:S(2)}, u32[]{:S(2)}) collective-permute-start(bf16[1024,256]{1,0:T(8,128)(2,1)S(1)} %get-tuple-element.89), channel_id=1, source_target_pairs={{0,16},{8,24},{16,0},{24,8},{1,17},{9,25},{17,1},{25,9},{2,18},{10... | collective-permute-start | bytes 1572872 | tf_op jit(solution)/shard_map/ppermute | solution.py:125
  328.8 15.7 %collective-permute-start.45 = (bf16[1024,256]{1,0:T(8,128)(2,1)S(1)}, bf16[1024,256]{1,0:T(8,128)(2,1)S(1)}, u32[]{:S(2)}, u32[]{:S(2)}) collective-permute-start(bf16[1024,256]{1,0:T(8,128)(2,1)S(1)} %get-tuple-element.96), channel_id=1, source_target_pairs={{0,24},{8,16},{16,8},{24,0},{1,25},{9,17},{17,9},{25,1},{2,26},{10... | collective-permute-start | bytes 1572872 | tf_op jit(solution)/shard_map/ppermute | solution.py:125
  328.8 14.2 %collective-permute-start.46 = (bf16[1024,256]{1,0:T(8,128)(2,1)S(1)}, bf16[1024,256]{1,0:T(8,128)(2,1)S(1)}, u32[]{:S(2)}, u32[]{:S(2)}) collective-permute-start(bf16[1024,256]{1,0:T(8,128)(2,1)S(1)} %collective-permute-done.40), channel_id=1, source_target_pairs={{0,1},{1,0},{2,3},{3,2},{4,5},{5,4},{6,7},{7,6},{8,9},{9,8},{10,11... | collective-permute-start | bytes 1572872 | tf_op jit(solution)/shard_map/ppermute | solution.py:118
  343.0 14.3 %collective-permute-start.47 = (bf16[1024,256]{1,0:T(8,128)(2,1)S(1)}, bf16[1024,256]{1,0:T(8,128)(2,1)S(1)}, u32[]{:S(2)}, u32[]{:S(2)}) collective-permute-start(bf16[1024,256]{1,0:T(8,128)(2,1)S(1)} %collective-permute-done.43), channel_id=1, source_target_pairs={{0,1},{1,0},{2,3},{3,2},{4,5},{5,4},{6,7},{7,6},{8,9},{9,8},{10,11... | collective-permute-start | bytes 1572872 | tf_op jit(solution)/shard_map/ppermute | solution.py:118
  345.3 13.5 %collective-permute-start.52 = (bf16[1024,256]{1,0:T(8,128)(2,1)S(1)}, bf16[1024,256]{1,0:T(8,128)(2,1)S(1)}, u32[]{:S(2)}, u32[]{:S(2)}) collective-permute-start(bf16[1024,256]{1,0:T(8,128)(2,1)S(1)} %convolution_convert_fusion.4), channel_id=1, source_target_pairs={{0,8},{8,0},{16,24},{24,16},{1,9},{9,1},{17,25},{25,17},{2,10},{10... | collective-permute-start | bytes 1572872 | tf_op jit(solution)/shard_map/ppermute | solution.py:125
  357.3 13.5 %collective-permute-start.48 = (bf16[1024,256]{1,0:T(8,128)(2,1)S(1)}, bf16[1024,256]{1,0:T(8,128)(2,1)S(1)}, u32[]{:S(2)}, u32[]{:S(2)}) collective-permute-start(bf16[1024,256]{1,0:T(8,128)(2,1)S(1)} %collective-permute-done.45), channel_id=1, source_target_pairs={{0,1},{1,0},{2,3},{3,2},{4,5},{5,4},{6,7},{7,6},{8,9},{9,8},{10,11... | collective-permute-start | bytes 1572872 | tf_op jit(solution)/shard_map/ppermute | solution.py:118
  359.6 13.9 %collective-permute-start.53 = (bf16[1024,256]{1,0:T(8,128)(2,1)S(1)}, bf16[1024,256]{1,0:T(8,128)(2,1)S(1)}, u32[]{:S(2)}, u32[]{:S(2)}) collective-permute-start(bf16[1024,256]{1,0:T(8,128)(2,1)S(1)} %fusion.7), channel_id=1, source_target_pairs={{0,16},{8,24},{16,0},{24,8},{1,17},{9,25},{17,1},{25,9},{2,18},{10... | collective-permute-start | bytes 1572872 | tf_op jit(solution)/shard_map/ppermute | solution.py:125
  374.3 14.0 %collective-permute-start.55 = (bf16[1024,256]{1,0:T(8,128)(2,1)S(1)}, bf16[1024,256]{1,0:T(8,128)(2,1)S(1)}, u32[]{:S(2)}, u32[]{:S(2)}) collective-permute-start(bf16[1024,256]{1,0:T(8,128)(2,1)S(1)} %fusion.8), channel_id=1, source_target_pairs={{0,16},{8,24},{16,0},{24,8},{1,17},{9,25},{17,1},{25,9},{2,18},{10... | collective-permute-start | bytes 1572872 | tf_op jit(solution)/shard_map/ppermute | solution.py:125
  376.2 15.0 %collective-permute-start.50 = (bf16[2048,256]{1,0:T(8,128)(2,1)S(1)}, bf16[2048,256]{1,0:T(8,128)(2,1)S(1)}, u32[]{:S(2)}, u32[]{:S(2)}) collective-permute-start(bf16[2048,256]{1,0:T(8,128)(2,1)S(1)} %convolution_convert_fusion.1), channel_id=1, source_target_pairs={{0,8},{8,0},{16,24},{24,16},{1,9},{9,1},{17,25},{25,17},{2,10},{10... | collective-permute-start | bytes 3145736 | tf_op jit(solution)/shard_map/ppermute | solution.py:125
  388.3 24.4 %collective-permute-start.56 = (bf16[2048,256]{1,0:T(8,128)(2,1)S(1)}, bf16[2048,256]{1,0:T(8,128)(2,1)S(1)}, u32[]{:S(2)}, u32[]{:S(2)}) collective-permute-start(bf16[2048,256]{1,0:T(8,128)(2,1)S(1)} %fusion.2), channel_id=1, source_target_pairs={{0,16},{8,24},{16,0},{24,8},{1,17},{9,25},{17,1},{25,9},{2,18},{10... | collective-permute-start | bytes 3145736 | tf_op jit(solution)/shard_map/ppermute | solution.py:125
  389.0 8.9 %collective-permute-start.61 = (bf16[1024,256]{1,0:T(8,128)(2,1)S(1)}, bf16[1024,256]{1,0:T(8,128)(2,1)S(1)}, u32[]{:S(2)}, u32[]{:S(2)}) collective-permute-start(bf16[1024,256]{1,0:T(8,128)(2,1)S(1)} %add_convert_fusion.8.refs_2_), channel_id=1, source_target_pairs={{0,8},{8,0},{16,24},{24,16},{1,9},{9,1},{17,25},{25,17},{2,10},{10... | collective-permute-start | bytes 1572872 | tf_op jit(solution)/shard_map/ppermute | solution.py:125
  389.2 8.7 %collective-permute-start.62 = (bf16[1024,256]{1,0:T(8,128)(2,1)S(1)}, bf16[1024,256]{1,0:T(8,128)(2,1)S(1)}, u32[]{:S(2)}, u32[]{:S(2)}) collective-permute-start(bf16[1024,256]{1,0:T(8,128)(2,1)S(1)} %add_convert_fusion.7.refs_3_), channel_id=1, source_target_pairs={{0,8},{8,0},{16,24},{24,16},{1,9},{9,1},{17,25},{25,17},{2,10},{10... | collective-permute-start | bytes 1572872 | tf_op jit(solution)/shard_map/ppermute | solution.py:125
  391.1 23.0 %collective-permute-start.49 = (bf16[2048,256]{1,0:T(8,128)(2,1)S(1)}, bf16[2048,256]{1,0:T(8,128)(2,1)S(1)}, u32[]{:S(2)}, u32[]{:S(2)}) collective-permute-start(bf16[2048,256]{1,0:T(8,128)(2,1)S(1)} %convolution_convert_fusion.2), channel_id=1, source_target_pairs={{0,8},{8,0},{16,24},{24,16},{1,9},{9,1},{17,25},{25,17},{2,10},{10... | collective-permute-start | bytes 3145736 | tf_op jit(solution)/shard_map/ppermute | solution.py:125
  412.7 23.5 %collective-permute-start.57 = (bf16[2048,256]{1,0:T(8,128)(2,1)S(1)}, bf16[2048,256]{1,0:T(8,128)(2,1)S(1)}, u32[]{:S(2)}, u32[]{:S(2)}) collective-permute-start(bf16[2048,256]{1,0:T(8,128)(2,1)S(1)} %fusion.1), channel_id=1, source_target_pairs={{0,16},{8,24},{16,0},{24,8},{1,17},{9,25},{17,1},{25,9},{2,18},{10... | collective-permute-start | bytes 3145736 | tf_op jit(solution)/shard_map/ppermute | solution.py:125
  413.4 50.7 %collective-permute-start.63 = (bf16[2048,512]{1,0:T(8,128)(2,1)S(1)}, bf16[2048,512]{1,0:T(8,128)(2,1)S(1)}, u32[]{:S(2)}, u32[]{:S(2)}) collective-permute-start(bf16[2048,512]{1,0:T(8,128)(2,1)S(1)} %pad_maximum_fusion.3), channel_id=1, source_target_pairs={{0,2},{1,3},{2,4},{3,5},{4,6},{5,7},{6,0},{7,1},{8,10},{9,11},{10,... | collective-permute-start | bytes 6291464 | tf_op jit(solution)/shard_map/ppermute | solution.py:122
  414.0 28.7 %collective-permute-start.59 = (bf16[2048,256]{1,0:T(8,128)(2,1)S(1)}, bf16[2048,256]{1,0:T(8,128)(2,1)S(1)}, u32[]{:S(2)}, u32[]{:S(2)}) collective-permute-start(bf16[2048,256]{1,0:T(8,128)(2,1)S(1)} %add_convert_fusion.5), channel_id=1, source_target_pairs={{0,8},{8,0},{16,24},{24,16},{1,9},{9,1},{17,25},{25,17},{2,10},{10... | collective-permute-start | bytes 3145736 | tf_op jit(solution)/shard_map/ppermute | solution.py:125
  436.4 18.9 %collective-permute-start.64 = (bf16[2048,256]{1,0:T(8,128)(2,1)S(1)}, bf16[2048,256]{1,0:T(8,128)(2,1)S(1)}, u32[]{:S(2)}, u32[]{:S(2)}) collective-permute-start(bf16[2048,256]{1,0:T(8,128)(2,1)S(1)} %add_convert_fusion.4), channel_id=1, source_target_pairs={{0,8},{8,0},{16,24},{24,16},{1,9},{9,1},{17,25},{25,17},{2,10},{10... | collective-permute-start | bytes 3145736 | tf_op jit(solution)/shard_map/ppermute | solution.py:125
  442.0 25.6 %collective-permute-start.58 = (bf16[2048,256]{1,0:T(8,128)(2,1)S(1)}, bf16[2048,256]{1,0:T(8,128)(2,1)S(1)}, u32[]{:S(2)}, u32[]{:S(2)}) collective-permute-start(bf16[2048,256]{1,0:T(8,128)(2,1)S(1)} %fusion), channel_id=1, source_target_pairs={{0,16},{8,24},{16,0},{24,8},{1,17},{9,25},{17,1},{25,9},{2,18},{10... | collective-permute-start | bytes 3145736 | tf_op jit(solution)/shard_map/ppermute | solution.py:125
  449.7 59.4 %collective-permute-start.60 = (bf16[2048,512]{1,0:T(8,128)(2,1)}, bf16[2048,512]{1,0:T(8,128)(2,1)S(1)}, u32[]{:S(2)}, u32[]{:S(2)}) collective-permute-start(bf16[2048,512]{1,0:T(8,128)(2,1)} %pad_maximum_fusion.2), channel_id=1, source_target_pairs={{0,6},{1,7},{2,0},{3,1},{4,2},{5,3},{6,4},{7,5},{8,14},{9,15},{10,... | collective-permute-start | bytes 6291464 | tf_op jit(solution)/shard_map/ppermute | solution.py:122
  466.1 85.1 %collective-permute-start.65 = (bf16[2048,512]{1,0:T(8,128)(2,1)}, bf16[2048,512]{1,0:T(8,128)(2,1)}, u32[]{:S(2)}, u32[]{:S(2)}) collective-permute-start(bf16[2048,512]{1,0:T(8,128)(2,1)} %pad_maximum_fusion.4), channel_id=1, source_target_pairs={{0,2},{1,3},{2,4},{3,5},{4,6},{5,7},{6,0},{7,1},{8,10},{9,11},{10,... | collective-permute-start | bytes 6291464 | tf_op jit(solution)/shard_map/ppermute | solution.py:122
  467.9 5.6 %collective-permute-start.66 = (bf16[2048,256]{1,0:T(8,128)(2,1)S(1)}, bf16[2048,256]{1,0:T(8,128)(2,1)}, u32[]{:S(2)}, u32[]{:S(2)}) collective-permute-start(bf16[2048,256]{1,0:T(8,128)(2,1)S(1)} %add_convert_fusion.6), channel_id=1, source_target_pairs={{0,8},{8,0},{16,24},{24,16},{1,9},{9,1},{17,25},{25,17},{2,10},{10... | collective-permute-start | bytes 3145736 | tf_op jit(solution)/shard_map/ppermute | solution.py:125
  (22 other events, 106.2 us)

commit v3 on v2

--- a/solution.py
+++ b/solution.py
@@ -141,7 +141,7 @@
             return row_xor(x, k) if k == 1 else in_turn("rows", x, lambda y: row_xor(y, k), depth)
 
         def half_sum(theirs, mine, depth):
-            mine = mine(row_xor(theirs(), 1))
+            mine = (mine.astype(F32) + row_xor(theirs.astype(BF16), 1).astype(F32)).astype(BF16)
             last["half"] = mine
             k = 2
             while k < n_row:
@@ -163,9 +163,6 @@
         def n_at(s, h):
             return (a - s) % n_a * width + h * half
 
-        def halves(x):
-            return x[:, :half], x[:, half:]
-
         grad = jnp.concatenate(
             [lax.dynamic_slice_in_dim(grad, h * half, half, 1).T for h in (core, 1 - core)], axis=0
         )
@@ -188,7 +185,7 @@
         def rows_of(which):
             return lax.dynamic_index_in_dim(by_b, which, 2, keepdims=False).reshape(sub, n_a * width)
 
-        got = [rows_of(b)] + [across_b(rows_of((b + k) % n_b), k) for k in range(1, n_b)]
+        got = [rows_of(b)] + [across_b(rows_of((b + k) % n_b), k, 2) for k in range(1, n_b)]
         stacked = jnp.stack(got, 0)
         right = [lax.dynamic_index_in_dim(stacked, (b - q) % n_b, 0, keepdims=False) for q in range(n_b)]
         right = jnp.concatenate(right, axis=0)
@@ -207,13 +204,9 @@
                 grads[1] = tie(grads[1], right)
             if (k, s) == (1, far):
                 grads[far] = tie(grads[far], last["rows"][-2])
-            g = tie(grads[s], rights[1]) if (k, s) == turns[-1] else grads[s]
-            g_mine, g_theirs = g[:half], g[half:]
-            mine, theirs = half_sum(
-                lambda: product([(g_theirs, lefts[k])], BF16, by_rows=False),
-                lambda got: product([(g_mine, lefts[k])], BF16, (got,), by_rows=False),
-                1,
-            )
+            g = tie(grads[s], rights[1], rights[3]) if (k, s) == turns[-1] else grads[s]
+            term = product([(g, lefts[k])], BF16, by_rows=False)
+            mine, theirs = half_sum(term[half:], term[:half], 1)
             rotated[k] = lax.dynamic_update_slice_in_dim(rotated[k], mine, n_at(s, core), 0)
             rotated[k] = lax.dynamic_update_slice_in_dim(rotated[k], theirs, n_at(s, 1 - core), 0)
         rot_k = jnp.zeros((n_col, sub, own_i), BF16)
@@ -238,53 +231,41 @@
         rots = [rot_k[k * per_row : (k + 1) * per_row] for k in range(n_row)]
         rots[1:] = [across_rows(rots[k], k, 2) for k in range(1, n_row)]
 
-        kept, by_rows = (), [[] for _ in range(n_b)]
+        kept, by_rows, held = (), [[] for _ in range(n_b)], []
         for k, rot in enumerate(rots):
-            if k == n_row - 1:
-                kept = tie(tuple(kept), by_rows[1][0])
             *kept, direction = step(r ^ k, n_row, sub, rot, first_moment, second_moment, tuple(kept))
             if k:
                 direction = across_rows(direction, k)
-            by_rows[0].append(direction)
-            for q in range(1, n_b):
-                by_rows[q].append(across_b(direction, -q))
+            held.append(direction)
+            if k:
+                direction = jnp.concatenate(held, axis=1)
+                held = []
+                by_rows[0].append(direction)
+                for q in range(1, n_b):
+                    by_rows[q].append(across_b(direction, -q))
         first_new, second_new = kept
         by_rows = [jnp.concatenate(ds, axis=1) for ds in by_rows]
         direction = jnp.concatenate(by_rows, axis=0)
 
-        def back(s, parts, kind):
+        def back(s, parts, kind, more=()):
             r_mine = lax.dynamic_slice_in_dim(right_k, n_at(s, core), half, 1)
             r_theirs = lax.dynamic_slice_in_dim(right_k, n_at(s, 1 - core), half, 1)
-            w_mine, w_theirs = [], []
+            ws = []
             for i, d in enumerate(parts):
                 d_mine = d
                 if i:
                     d, d_mine = tie(d, last["half"]), tie(d, last["rows"][-1])
-                mine, theirs = half_sum(
-                    lambda: dot(d, r_theirs, (1, 0)).astype(BF16),
-                    lambda got: (dot(d_mine, r_mine, (1, 0)) + got.astype(F32)).astype(BF16),
-                    1,
-                )
-                w_mine.append(mine)
-                w_theirs.append(theirs)
+                ws.append(jnp.concatenate(half_sum(dot(d, r_theirs, (1, 0)), dot(d_mine, r_mine, (1, 0)), 1), axis=1))
             if len(parts) < n_b:
-                w_mine, w_theirs = [
-                    [w[0][k * own_i : (k + 1) * own_i] for k in range(n_b)] for w in (w_mine, w_theirs)
-                ]
-            return [product(list(zip(lefts, w)), kind) for w in (w_mine, w_theirs)]
-
-        def joined(u):
-            return jnp.concatenate(u, axis=1)
+                ws = [ws[0][k * own_i : (k + 1) * own_i] for k in range(n_b)]
+            return product(list(zip(lefts, ws)), kind, more)
 
         whole = [direction]
-        passed = halves(a_shift(joined(back(2, by_rows, BF16)), 1))
-        behind = halves(a_shift(joined(back(1, whole, BF16)), -1))
-        ahead = [(u + x.astype(F32)).astype(BF16) for u, x in zip(back(3, whole, F32), passed)]
-        ahead = halves(a_shift(joined(ahead), 1))
-        own = back(0, whole, F32)
-        u_mine, u_theirs = [
-            (u + x.astype(F32) + y.astype(F32)).astype(BF16) for u, x, y in zip(own, behind, ahead)
-        ]
+        passed = a_shift(back(2, by_rows, BF16), 1)
+        behind = a_shift(back(1, whole, BF16), -1)
+        ahead = a_shift((back(3, whole, F32) + passed.astype(F32)).astype(BF16), 1)
+        update = back(0, whole, F32) + behind.astype(F32) + ahead.astype(F32)
+        u_mine, u_theirs = update[:, :half].astype(BF16), update[:, half:].astype(BF16)
         update = jnp.where(
             core == 0,
             jnp.concatenate([u_mine, u_theirs], axis=1),

time: 565 us -> 606 us (1.073)
  waiting for transfers between devices: 311 us -> 365 us
  Pallas kernels: 120 us -> 87.1 us
  other arithmetic: 16.9 us -> 27.8 us
  matrix products: 21 us -> 30.1 us
    ppermute x9, waiting for transfers between devices: 95.5 us -> 216 us  [a_shift(): return lax.ppermute(x, 'col', perm)]
    ppermute x10 -> x9, waiting for transfers between devices: 114 us -> 36.2 us  [b_shift(): return lax.ppermute(x, 'col', perm)]
    pallas_call x24 -> x12, Pallas kernels: 110 us -> 68.6 us  [product(): pl.pallas_call(functools.partial(product_kernel, len(pairs)), grid=(grid,...]
    ppermute x48, waiting for transfers between devices: 101 us -> 113 us  [row_xor(): return lax.ppermute(x, 'row', [(r, r ^ k) for r in range(n_row)])]
    dot_general x18, matrix products: 21 us -> 30.1 us  [dot(): lax.dot_general(a, b, ((contract[:1], contract[1:]), ((), ())), preferred...]
    pallas_call x4, Pallas kernels: 10.7 us -> 18.5 us  [moments_at(): pl.pallas_call(moments_kernel, grid_spec=pltpu.PrefetchScalarGridSpec(num...]
    slice x11 -> x9, local copies, waits for them, and re-layouts: 10 us -> 2.8 us  [the longest x8 2.66 us: per_device(): mine, theirs = half_sum(term[half:], term[:half], 1)]
    ppermute x10 -> x9, starting transfers between devices: 16.5 us -> 14.2 us  [b_shift(): return lax.ppermute(x, 'col', perm)]
  transfers between devices with their start and end apart: 67 -> 66, of which waited for: 23 -> 26; matrix products, arithmetic and copies ran while one was open for 10% -> 13% of each run, Pallas kernels for 22% -> 15%
where the time goes in v3:
time: 606 us; the launch traced here: 597 us
  waiting for transfers between devices  365 us (60%)
  Pallas kernels  87.1 us (14%)
  starting transfers between devices  52.7 us (9%)
  local copies, waits for them, and re-layouts  31.6 us (5%)
  matrix products  30.1 us (5%)
  other arithmetic  27.8 us (5%)
    ppermute x9, waiting for transfers between devices, a_shift(): return lax.ppermute(x, 'col', perm)  216 us
    ppermute x48, waiting for transfers between devices, row_xor(): return lax.ppermute(x, 'row', [(r, r ^ k) for r in range(n_row)])  113 us
    pallas_call x12, Pallas kernels, product(): pl.pallas_call(functools.partial(product_kernel, len(pairs)), grid=(grid,...  68.6 us
    ppermute x9, waiting for transfers between devices, b_shift(): return lax.ppermute(x, 'col', perm)  36.2 us
    dot_general x18, matrix products, dot(): lax.dot_general(a, b, ((contract[:1], contract[1:]), ((), ())), preferred...  30.1 us
    ppermute x48, starting transfers between devices, row_xor(): return lax.ppermute(x, 'row', [(r, r ^ k) for r in range(n_row)])  27.3 us
    pallas_call x4, Pallas kernels, moments_at(): pl.pallas_call(moments_kernel, grid_spec=pltpu.PrefetchScalarGridSpec(num...  18.5 us
    ppermute x9, starting transfers between devices, b_shift(): return lax.ppermute(x, 'col', perm)  14.2 us
  transfers between devices with their start and end apart: 66, of which 26 were waited for; matrix products, arithmetic and copies ran while one was open for 13% of the time, Pallas kernels for 15%

profile of v3, /device:TPU:0, one launch (start us, length us, event | category | flops | bytes accessed | tf_op | source)
XLA Modules:
  0.0 596.5 jit_solution(17670853631359709801)
XLA Ops:
  0.7 1.7 constant_dynamic-slice_fusion.3
  5.8 3.0 collective-permute-start.2
  10.4 2.2 collective-permute-start.1
  12.7 1.9 dynamic-slice_bitcast_fusion
  17.2 1.7 bitcast_dynamic-update-slice_fusion
  19.9 4.7 shard_map.76
  29.1 1.7 constant_dynamic-update-slice_fusion.23
  30.7 2.2 constant_dynamic-slice_fusion
  34.6 1.8 collective-permute-start.8
  36.4 23.0 %collective-permute-done.refs_0_ = bf16[512,2048]{1,0:T(8,128)(2,1)} collective-permute-done((bf16[512,2048]{1,0:T(8,128)(2,1)S(1)}, bf16[512,2048]{1,0:T(8,128)(2,1)}, u32[]{:S(2)}, u32[]{:S(2)}) %collective-permute-start) | collective-permute-done | bytes 2097184 | tf_op jit(solution)/shard_map/ppermute | solution.py:122
  59.3 42.9 %collective-permute-done.1.refs_0_ = bf16[512,2048]{1,0:T(8,128)(2,1)} collective-permute-done((bf16[512,2048]{1,0:T(8,128)(2,1)S(1)}, bf16[512,2048]{1,0:T(8,128)(2,1)}, u32[]{:S(2)}, u32[]{:S(2)}) %collective-permute-start.1) | collective-permute-done | bytes 2097184 | tf_op jit(solution)/shard_map/ppermute | solution.py:122
  102.3 4.7 shard_map.80
  107.1 3.8 collective-permute-done.6
  113.5 1.8 collective-permute-start.20
  115.3 5.5 shard_map.79
  125.9 5.5 shard_map.78
  132.5 2.1 add_convert_fusion.18
  134.6 4.5 collective-permute-done.14
  140.6 2.5 broadcast.29.clone
  143.1 2.4 constant_dynamic-update-slice_fusion.14
  145.5 5.5 shard_map.77
  154.5 1.9 constant_dynamic-update-slice_fusion.13
  156.3 2.2 constant_dynamic-update-slice_fusion.12
  159.9 2.4 collective-permute-done.20.refs_0_
  162.3 4.6 collective-permute-done.16
  166.9 4.7 shard_map.82
  174.8 11.5 %collective-permute-done.17 = bf16[256,1024]{1,0:T(8,128)(2,1)S(1)} collective-permute-done((bf16[256,1024]{1,0:T(8,128)(2,1)S(1)}, bf16[256,1024]{1,0:T(8,128)(2,1)S(1)}, u32[]{:S(2)}, u32[]{:S(2)}) %collective-permute-start.17) | collective-permute-done | bytes 524320 | tf_op jit(solution)/shard_map/ppermute | solution.py:125
  188.6 2.5 collective-permute-start.26
  191.1 5.5 shard_map.81
  201.9 13.1 %collective-permute-done.25 = bf16[256,2048]{0,1:T(8,128)(2,1)S(1)} collective-permute-done((bf16[256,2048]{0,1:T(8,128)(2,1)S(1)}, bf16[256,2048]{0,1:T(8,128)(2,1)S(1)}, u32[]{:S(2)}, u32[]{:S(2)}) %collective-permute-start.25) | collective-permute-done | bytes 1048608 | tf_op jit(solution)/shard_map/ppermute | solution.py:122
  214.9 20.6 %collective-permute-done.26 = bf16[256,2048]{0,1:T(8,128)(2,1)S(1)} collective-permute-done((bf16[256,2048]{0,1:T(8,128)(2,1)S(1)}, bf16[256,2048]{0,1:T(8,128)(2,1)S(1)}, u32[]{:S(2)}, u32[]{:S(2)}) %collective-permute-start.26) | collective-permute-done | bytes 1048608 | tf_op jit(solution)/shard_map/ppermute | solution.py:122
  235.5 4.7 shard_map.83
  242.8 3.5 convolution_convert_fusion.8
  247.9 6.8 %collective-permute-done.23 = bf16[256,1024]{1,0:T(8,128)(2,1)S(1)} collective-permute-done((bf16[256,1024]{1,0:T(8,128)(2,1)S(1)}, bf16[256,1024]{1,0:T(8,128)(2,1)S(1)}, u32[]{:S(2)}, u32[]{:S(2)}) %collective-permute-start.23) | collective-permute-done | bytes 524320 | tf_op jit(solution)/shard_map/ppermute | solution.py:125
  256.8 3.5 convolution_convert_fusion.7
  261.9 7.7 %collective-permute-done.28 = bf16[256,1024]{1,0:T(8,128)(2,1)S(1)} collective-permute-done((bf16[256,1024]{1,0:T(8,128)(2,1)S(1)}, bf16[256,1024]{1,0:T(8,128)(2,1)S(1)}, u32[]{:S(2)}, u32[]{:S(2)}) %collective-permute-start.28) | collective-permute-done | bytes 524320 | tf_op jit(solution)/shard_map/ppermute | solution.py:125
  271.0 3.5 convolution_convert_fusion.6
  279.0 18.5 %collective-permute-done.37 = bf16[256,2048]{0,1:T(8,128)(2,1)S(1)} collective-permute-done((bf16[256,2048]{0,1:T(8,128)(2,1)S(1)}, bf16[256,2048]{0,1:T(8,128)(2,1)S(1)}, u32[]{:S(2)}, u32[]{:S(2)}) %collective-permute-start.37) | collective-permute-done | bytes 1048608 | tf_op jit(solution)/shard_map/ppermute | solution.py:122
  297.5 3.5 convolution_convert_fusion.5
  303.9 10.7 %collective-permute-done.38 = bf16[256,1024]{1,0:T(8,128)(2,1)S(1)} collective-permute-done((bf16[256,1024]{1,0:T(8,128)(2,1)S(1)}, bf16[256,1024]{1,0:T(8,128)(2,1)S(1)}, u32[]{:S(2)}, u32[]{:S(2)}) %collective-permute-start.38) | collective-permute-done | bytes 524320 | tf_op jit(solution)/shard_map/ppermute | solution.py:118
  316.6 1.7 collective-permute-start.42
  318.8 2.6 shard_map.84
  321.4 2.6 shard_map.85
  324.4 17.7 %collective-permute-done.41.rot_ref = bf16[2,128,1024]{2,1,0:T(8,128)(2,1)S(1)} collective-permute-done((bf16[2,128,1024]{2,1,0:T(8,128)(2,1)S(1)}, bf16[2,128,1024]{2,1,0:T(8,128)(2,1)S(1)}, u32[]{:S(2)}, u32[]{:S(2)}) %collective-permute-start.41) | collective-permute-done | bytes 524320 | tf_op jit(solution)/shard_map/ppermute | solution.py:125
  342.1 2.6 shard_map.86
  348.1 10.7 %shard_map.87 = (f32[1024,1024]{1,0:T(8,128)}, f32[1024,1024]{1,0:T(8,128)}, bf16[1024,256]{1,0:T(8,128)(2,1)S(1)}) custom-call(s32[1]{0:T(128)} %bitcast.23.peer_ref, bf16[2,128,1024]{2,1,0:T(8,128)(2,1)S(1)} %collective-permute-done.42.rot_ref, f32[1024,1024]{1,0:T(8,128)S(1)} %copy-done, ...), custom_call_target="tpu_custom_call", output_to_operand_aliasing={{0}: (4, {}), {1}: (5, {})} | custom-call | flops 2621440 | bytes 5242880 | tf_op jit(solution)/shard_map/pallas_call | solution.py:77
  359.3 13.1 %collective-permute-done.44 = bf16[1024,256]{1,0:T(8,128)(2,1)S(1)} collective-permute-done((bf16[1024,256]{1,0:T(8,128)(2,1)S(1)}, bf16[1024,256]{1,0:T(8,128)(2,1)S(1)}, u32[]{:S(2)}, u32[]{:S(2)}) %collective-permute-start.44) | collective-permute-done | bytes 524320 | tf_op jit(solution)/shard_map/ppermute | solution.py:125
  374.7 11.4 %collective-permute-done.46 = bf16[1024,256]{1,0:T(8,128)(2,1)S(1)} collective-permute-done((bf16[1024,256]{1,0:T(8,128)(2,1)S(1)}, bf16[1024,256]{1,0:T(8,128)(2,1)S(1)}, u32[]{:S(2)}, u32[]{:S(2)}) %collective-permute-start.46) | collective-permute-done | bytes 524320 | tf_op jit(solution)/shard_map/ppermute | solution.py:118
  386.0 1.7 collective-permute-start.47
  388.9 10.2 %collective-permute-done.47 = bf16[1024,256]{1,0:T(8,128)(2,1)S(1)} collective-permute-done((bf16[1024,256]{1,0:T(8,128)(2,1)S(1)}, bf16[1024,256]{1,0:T(8,128)(2,1)S(1)}, u32[]{:S(2)}, u32[]{:S(2)}) %collective-permute-start.47) | collective-permute-done | bytes 524320 | tf_op jit(solution)/shard_map/ppermute | solution.py:118
  407.0 9.7 %collective-permute-done.54 = bf16[1024,256]{1,0:T(8,128)(2,1)S(1)} collective-permute-done((bf16[1024,256]{1,0:T(8,128)(2,1)S(1)}, bf16[1024,256]{1,0:T(8,128)(2,1)S(1)}, u32[]{:S(2)}, u32[]{:S(2)}) %collective-permute-start.54) | collective-permute-done | bytes 524320 | tf_op jit(solution)/shard_map/ppermute | solution.py:125
  420.4 20.6 %collective-permute-done.55 = bf16[2048,256]{1,0:T(8,128)(2,1)S(1)} collective-permute-done((bf16[2048,256]{1,0:T(8,128)(2,1)S(1)}, bf16[2048,256]{1,0:T(8,128)(2,1)S(1)}, u32[]{:S(2)}, u32[]{:S(2)}) %collective-permute-start.55) | collective-permute-done | bytes 1048608 | tf_op jit(solution)/shard_map/ppermute | solution.py:125
  444.1 6.9 %shard_map.91 = bf16[2048,512]{1,0:T(8,128)(2,1)S(1)} custom-call(bf16[2048,1024]{1,0:T(8,128)(2,1)} %refs_0_.3, bf16[2048,1024]{1,0:T(8,128)(2,1)} %collective-permute-done.2.refs_1_, bf16[1024,512]{1,0:T(8,128)(2,1)S(1)} %pad_maximum_fusion.7.refs_2_, bf16[1024,512]{1,0:T(8,128)(2,1)S(1)} %pad_maximum_fusion.8.refs_3_), custom_call_target="tpu_custom_call" | custom-call | flops 536870912 | tf_op jit(solution)/shard_map/pallas_call | solution.py:45
  452.2 12.3 %collective-permute-done.56 = bf16[2048,256]{1,0:T(8,128)(2,1)S(1)} collective-permute-done((bf16[2048,256]{1,0:T(8,128)(2,1)S(1)}, bf16[2048,256]{1,0:T(8,128)(2,1)S(1)}, u32[]{:S(2)}, u32[]{:S(2)}) %collective-permute-start.56) | collective-permute-done | bytes 1048608 | tf_op jit(solution)/shard_map/ppermute | solution.py:125
  466.4 6.9 %shard_map.89 = bf16[2048,512]{1,0:T(8,128)(2,1)S(1)} custom-call(bf16[2048,1024]{1,0:T(8,128)(2,1)} %refs_0_.3, bf16[2048,1024]{1,0:T(8,128)(2,1)} %collective-permute-done.2.refs_1_, bf16[1024,512]{1,0:T(8,128)(2,1)S(1)} %get-tuple-element.120.refs_2_, bf16[1024,512]{1,0:T(8,128)(2,1)S(1)} %get-tuple-element.119.refs_3_), custom_call_target="tpu_custom_call" | custom-call | flops 536870912 | tf_op jit(solution)/shard_map/pallas_call | solution.py:45
  475.1 6.9 %shard_map.90 = f32[2048,512]{1,0:T(8,128)S(1)} custom-call(bf16[2048,1024]{1,0:T(8,128)(2,1)} %refs_0_.3, bf16[2048,1024]{1,0:T(8,128)(2,1)} %collective-permute-done.2.refs_1_, bf16[1024,512]{1,0:T(8,128)(2,1)S(1)} %get-tuple-element.124.refs_2_, bf16[1024,512]{1,0:T(8,128)(2,1)S(1)} %get-tuple-element.123.refs_3_), custom_call_target="tpu_custom_call" | custom-call | flops 536870912 | tf_op jit(solution)/shard_map/pallas_call | solution.py:45
  482.1 19.6 %collective-permute-done.64 = bf16[2048,512]{1,0:T(8,128)(2,1)S(1)} collective-permute-done((bf16[2048,512]{1,0:T(8,128)(2,1)S(1)}, bf16[2048,512]{1,0:T(8,128)(2,1)S(1)}, u32[]{:S(2)}, u32[]{:S(2)}) %collective-permute-start.64) | collective-permute-done | bytes 2097184 | tf_op jit(solution)/shard_map/ppermute | solution.py:122
  501.6 2.1 add_convert_fusion.1
  504.1 2.8 collective-permute-done.58
  508.3 6.9 %shard_map.88 = f32[2048,512]{1,0:T(8,128)S(1)} custom-call(bf16[2048,1024]{1,0:T(8,128)(2,1)} %refs_0_.3, bf16[2048,1024]{1,0:T(8,128)(2,1)} %collective-permute-done.2.refs_1_, bf16[1024,512]{1,0:T(8,128)(2,1)S(1)} %get-tuple-element.122.refs_2_, bf16[1024,512]{1,0:T(8,128)(2,1)S(1)} %get-tuple-element.121.refs_3_), custom_call_target="tpu_custom_call" | custom-call | flops 536870912 | tf_op jit(solution)/shard_map/pallas_call | solution.py:45
  515.2 31.5 %collective-permute-done.60 = bf16[2048,512]{1,0:T(8,128)(2,1)} collective-permute-done((bf16[2048,512]{1,0:T(8,128)(2,1)S(1)}, bf16[2048,512]{1,0:T(8,128)(2,1)}, u32[]{:S(2)}, u32[]{:S(2)}) %collective-permute-start.60) | collective-permute-done | bytes 2097184 | tf_op jit(solution)/shard_map/ppermute | solution.py:122
  546.7 44.5 %collective-permute-done.65 = bf16[2048,512]{1,0:T(8,128)(2,1)} collective-permute-done((bf16[2048,512]{1,0:T(8,128)(2,1)}, bf16[2048,512]{1,0:T(8,128)(2,1)}, u32[]{:S(2)}, u32[]{:S(2)}) %collective-permute-start.65) | collective-permute-done | bytes 2097184 | tf_op jit(solution)/shard_map/ppermute | solution.py:122
  591.2 3.1 add_convert_fusion
  594.5 1.8 maximum_select_fusion
  (212 shorter events, 88.2 us)
Async XLA Ops:
  5.8 96.4 %collective-permute-start.2 = (bf16[2048,1024]{1,0:T(8,128)(2,1)}, bf16[2048,1024]{1,0:T(8,128)(2,1)}, u32[]{:S(2)}, u32[]{:S(2)}) collective-permute-start(bf16[2048,1024]{1,0:T(8,128)(2,1)} %refs_0_.3), channel_id=1, source_target_pairs={{0,1},{1,0},{2,3},{3,2},{4,5},{5,4},{6,7},{7,6},{8,9},{9,8},{10,11... | collective-permute-start | bytes 12582920 | tf_op jit(solution)/shard_map/ppermute | solution.py:118
  8.8 50.5 %collective-permute-start = (bf16[512,2048]{1,0:T(8,128)(2,1)S(1)}, bf16[512,2048]{1,0:T(8,128)(2,1)}, u32[]{:S(2)}, u32[]{:S(2)}) collective-permute-start(bf16[512,2048]{1,0:T(8,128)(2,1)S(1)} %pad_maximum_fusion.1.refs_0_), channel_id=1, source_target_pairs={{0,2},{1,3},{2,4},{3,5},{4,6},{5,7},{6,0},{7,1},{8,10},{9,11},{10,... | collective-permute-start | bytes 6291464 | tf_op jit(solution)/shard_map/ppermute | solution.py:122
  10.4 91.9 %collective-permute-start.1 = (bf16[512,2048]{1,0:T(8,128)(2,1)S(1)}, bf16[512,2048]{1,0:T(8,128)(2,1)}, u32[]{:S(2)}, u32[]{:S(2)}) collective-permute-start(bf16[512,2048]{1,0:T(8,128)(2,1)S(1)} %pad_maximum_fusion.1.refs_0_), channel_id=1, source_target_pairs={{0,6},{1,7},{2,0},{3,1},{4,2},{5,3},{6,4},{7,5},{8,14},{9,15},{10,... | collective-permute-start | bytes 6291464 | tf_op jit(solution)/shard_map/ppermute | solution.py:122
  14.5 4.3 collective-permute-start.3
  14.5 12.6 %collective-permute-start.4 = (bf16[128,1024]{0,1:T(8,128)(2,1)}, bf16[128,1024]{0,1:T(8,128)(2,1)}, u32[]{:S(2)}, u32[]{:S(2)}) collective-permute-start(bf16[128,1024]{0,1:T(8,128)(2,1)} %get-tuple-element.136), channel_id=1, source_target_pairs={{0,16},{8,24},{16,0},{24,8},{1,17},{9,25},{17,1},{25,9},{2,18},{10... | collective-permute-start | bytes 786440 | tf_op jit(solution)/shard_map/ppermute | solution.py:125
  19.5 9.5 %collective-permute-start.5 = (bf16[128,1024]{0,1:T(8,128)(2,1)S(1)}, bf16[128,1024]{0,1:T(8,128)(2,1)}, u32[]{:S(2)}, u32[]{:S(2)}) collective-permute-start(bf16[128,1024]{0,1:T(8,128)(2,1)S(1)} %get-tuple-element.135), channel_id=1, source_target_pairs={{0,24},{8,16},{16,8},{24,0},{1,25},{9,17},{17,9},{25,1},{2,26},{10... | collective-permute-start | bytes 786440 | tf_op jit(solution)/shard_map/ppermute | solution.py:125
  27.1 6.2 %collective-permute-start.7 = (bf16[256,1024]{1,0:T(8,128)(2,1)}, bf16[256,1024]{1,0:T(8,128)(2,1)}, u32[]{:S(2)}, u32[]{:S(2)}) collective-permute-start(bf16[256,1024]{1,0:T(8,128)(2,1)} %slice.180), channel_id=1, source_target_pairs={{0,8},{8,0},{16,24},{24,16},{1,9},{9,1},{17,25},{25,17},{2,10},{10... | collective-permute-start | bytes 1572872 | tf_op jit(solution)/shard_map/ppermute | solution.py:125
  33.0 78.0 %collective-permute-start.6 = (bf16[128,2048]{0,1:T(8,128)(2,1)}, bf16[128,2048]{0,1:T(8,128)(2,1)}, u32[]{:S(2)}, u32[]{:S(2)}) collective-permute-start(bf16[128,2048]{0,1:T(8,128)(2,1)} %bitcast.9), channel_id=1, source_target_pairs={{0,1},{1,0},{2,3},{3,2},{4,5},{5,4},{6,7},{7,6},{8,9},{9,8},{10,11... | collective-permute-start | bytes 1572872 | tf_op jit(solution)/shard_map/ppermute | solution.py:118
  34.6 89.1 %collective-permute-start.8 = (bf16[256,1024]{1,0:T(8,128)(2,1)S(1)}, bf16[256,1024]{1,0:T(8,128)(2,1)S(1)}, u32[]{:S(2)}, u32[]{:S(2)}) collective-permute-start(bf16[256,1024]{1,0:T(8,128)(2,1)S(1)} %add_convert_fusion.22), channel_id=1, source_target_pairs={{0,16},{8,24},{16,0},{24,8},{1,17},{9,25},{17,1},{25,9},{2,18},{10... | collective-permute-start | bytes 1572872 | tf_op jit(solution)/shard_map/ppermute | solution.py:125
  107.1 15.5 %collective-permute-start.13 = (bf16[256,1024]{1,0:T(8,128)(2,1)S(1)}, bf16[256,1024]{1,0:T(8,128)(2,1)S(1)}, u32[]{:S(2)}, u32[]{:S(2)}) collective-permute-start(bf16[256,1024]{1,0:T(8,128)(2,1)S(1)} %slice.188), channel_id=1, source_target_pairs={{0,8},{8,0},{16,24},{24,16},{1,9},{9,1},{17,25},{25,17},{2,10},{10... | collective-permute-start | bytes 1572872 | tf_op jit(solution)/shard_map/ppermute | solution.py:125
  113.5 48.8 %collective-permute-start.20 = (bf16[512,2048]{1,0:T(8,128)(2,1)}, bf16[512,2048]{1,0:T(8,128)(2,1)S(1)}, u32[]{:S(2)}, u32[]{:S(2)}) collective-permute-start(bf16[512,2048]{1,0:T(8,128)(2,1)} %collective-permute-done.refs_0_), channel_id=1, source_target_pairs={{0,2},{1,3},{2,4},{3,5},{4,6},{5,7},{6,0},{7,1},{8,10},{9,11},{10,... | collective-permute-start | bytes 6291464 | tf_op jit(solution)/shard_map/ppermute | solution.py:122
  122.6 9.9 %collective-permute-start.12 = (bf16[256,1024]{1,0:T(8,128)(2,1)}, bf16[256,1024]{1,0:T(8,128)(2,1)}, u32[]{:S(2)}, u32[]{:S(2)}) collective-permute-start(bf16[256,1024]{1,0:T(8,128)(2,1)} %slice.186), channel_id=1, source_target_pairs={{0,8},{8,0},{16,24},{24,16},{1,9},{9,1},{17,25},{25,17},{2,10},{10... | collective-permute-start | bytes 1572872 | tf_op jit(solution)/shard_map/ppermute | solution.py:125
  124.4 14.7 %collective-permute-start.14 = (bf16[256,1024]{1,0:T(8,128)(2,1)}, bf16[256,1024]{1,0:T(8,128)(2,1)}, u32[]{:S(2)}, u32[]{:S(2)}) collective-permute-start(bf16[256,1024]{1,0:T(8,128)(2,1)} %add_convert_fusion.17), channel_id=1, source_target_pairs={{0,16},{8,24},{16,0},{24,8},{1,17},{9,25},{17,1},{25,9},{2,18},{10... | collective-permute-start | bytes 1572872 | tf_op jit(solution)/shard_map/ppermute | solution.py:125
  132.3 19.4 %collective-permute-start.11 = (bf16[256,1024]{1,0:T(8,128)(2,1)}, bf16[256,1024]{1,0:T(8,128)(2,1)}, u32[]{:S(2)}, u32[]{:S(2)}) collective-permute-start(bf16[256,1024]{1,0:T(8,128)(2,1)} %slice.184), channel_id=1, source_target_pairs={{0,8},{8,0},{16,24},{24,16},{1,9},{9,1},{17,25},{25,17},{2,10},{10... | collective-permute-start | bytes 1572872 | tf_op jit(solution)/shard_map/ppermute | solution.py:125
  139.1 13.9 %collective-permute-start.15 = (bf16[256,1024]{1,0:T(8,128)(2,1)}, bf16[256,1024]{1,0:T(8,128)(2,1)}, u32[]{:S(2)}, u32[]{:S(2)}) collective-permute-start(bf16[256,1024]{1,0:T(8,128)(2,1)} %add_convert_fusion.18), channel_id=1, source_target_pairs={{0,16},{8,24},{16,0},{24,8},{1,17},{9,25},{17,1},{25,9},{2,18},{10... | collective-permute-start | bytes 1572872 | tf_op jit(solution)/shard_map/ppermute | solution.py:125
  145.5 8.9 %collective-permute-start.30 = (bf16[256,1024]{1,0:T(8,128)(2,1)}, bf16[256,1024]{1,0:T(8,128)(2,1)}, u32[]{:S(2)}, u32[]{:S(2)}) collective-permute-start(bf16[256,1024]{1,0:T(8,128)(2,1)} %get-tuple-element.116), channel_id=1, source_target_pairs={{0,8},{8,0},{16,24},{24,16},{1,9},{9,1},{17,25},{25,17},{2,10},{10... | collective-permute-start | bytes 1572872 | tf_op jit(solution)/shard_map/ppermute | solution.py:125
  151.1 20.7 %collective-permute-start.10 = (bf16[256,1024]{1,0:T(8,128)(2,1)S(1)}, bf16[256,1024]{1,0:T(8,128)(2,1)S(1)}, u32[]{:S(2)}, u32[]{:S(2)}) collective-permute-start(bf16[256,1024]{1,0:T(8,128)(2,1)S(1)} %slice.182), channel_id=1, source_target_pairs={{0,8},{8,0},{16,24},{24,16},{1,9},{9,1},{17,25},{25,17},{2,10},{10... | collective-permute-start | bytes 1572872 | tf_op jit(solution)/shard_map/ppermute | solution.py:125
  152.9 14.0 %collective-permute-start.16 = (bf16[256,1024]{1,0:T(8,128)(2,1)S(1)}, bf16[256,1024]{1,0:T(8,128)(2,1)S(1)}, u32[]{:S(2)}, u32[]{:S(2)}) collective-permute-start(bf16[256,1024]{1,0:T(8,128)(2,1)S(1)} %add_convert_fusion.19), channel_id=1, source_target_pairs={{0,16},{8,24},{16,0},{24,8},{1,17},{9,25},{17,1},{25,9},{2,18},{10... | collective-permute-start | bytes 1572872 | tf_op jit(solution)/shard_map/ppermute | solution.py:125
  158.6 14.0 %collective-permute-start.31 = (bf16[256,1024]{1,0:T(8,128)(2,1)S(1)}, bf16[256,1024]{1,0:T(8,128)(2,1)S(1)}, u32[]{:S(2)}, u32[]{:S(2)}) collective-permute-start(bf16[256,1024]{1,0:T(8,128)(2,1)S(1)} %get-tuple-element.114), channel_id=1, source_target_pairs={{0,8},{8,0},{16,24},{24,16},{1,9},{9,1},{17,25},{25,17},{2,10},{10... | collective-permute-start | bytes 1572872 | tf_op jit(solution)/shard_map/ppermute | solution.py:125
  159.3 27.5 %collective-permute-start.9 = (bf16[256,1024]{1,0:T(8,128)(2,1)S(1)}, bf16[256,1024]{1,0:T(8,128)(2,1)S(1)}, u32[]{:S(2)}, u32[]{:S(2)}) collective-permute-start(bf16[256,1024]{1,0:T(8,128)(2,1)S(1)} %get-tuple-element.108), channel_id=1, source_target_pairs={{0,8},{8,0},{16,24},{24,16},{1,9},{9,1},{17,25},{25,17},{2,10},{10... | collective-permute-start | bytes 1572872 | tf_op jit(solution)/shard_map/ppermute | solution.py:125
  171.7 2.9 collective-permute-start.21
  172.0 14.4 %collective-permute-start.17 = (bf16[256,1024]{1,0:T(8,128)(2,1)S(1)}, bf16[256,1024]{1,0:T(8,128)(2,1)S(1)}, u32[]{:S(2)}, u32[]{:S(2)}) collective-permute-start(bf16[256,1024]{1,0:T(8,128)(2,1)S(1)} %add_convert_fusion.20), channel_id=1, source_target_pairs={{0,16},{8,24},{16,0},{24,8},{1,17},{9,25},{17,1},{25,9},{2,18},{10... | collective-permute-start | bytes 1572872 | tf_op jit(solution)/shard_map/ppermute | solution.py:125
  174.4 22.4 %collective-permute-start.32 = (bf16[256,1024]{1,0:T(8,128)(2,1)S(1)}, bf16[256,1024]{1,0:T(8,128)(2,1)S(1)}, u32[]{:S(2)}, u32[]{:S(2)}) collective-permute-start(bf16[256,1024]{1,0:T(8,128)(2,1)S(1)} %get-tuple-element.112), channel_id=1, source_target_pairs={{0,8},{8,0},{16,24},{24,16},{1,9},{9,1},{17,25},{25,17},{2,10},{10... | collective-permute-start | bytes 1572872 | tf_op jit(solution)/shard_map/ppermute | solution.py:125
  186.4 13.5 %collective-permute-start.22 = (bf16[256,1024]{1,0:T(8,128)(2,1)S(1)}, bf16[256,1024]{1,0:T(8,128)(2,1)S(1)}, u32[]{:S(2)}, u32[]{:S(2)}) collective-permute-start(bf16[256,1024]{1,0:T(8,128)(2,1)S(1)} %add_convert_fusion.14), channel_id=1, source_target_pairs={{0,16},{8,24},{16,0},{24,8},{1,17},{9,25},{17,1},{25,9},{2,18},{10... | collective-permute-start | bytes 1572872 | tf_op jit(solution)/shard_map/ppermute | solution.py:125
  186.9 28.0 %collective-permute-start.25 = (bf16[256,2048]{0,1:T(8,128)(2,1)S(1)}, bf16[256,2048]{0,1:T(8,128)(2,1)S(1)}, u32[]{:S(2)}, u32[]{:S(2)}) collective-permute-start(bf16[256,2048]{0,1:T(8,128)(2,1)S(1)} %copy-done.4), channel_id=1, source_target_pairs={{0,2},{1,3},{2,4},{3,5},{4,6},{5,7},{6,0},{7,1},{8,10},{9,11},{10,... | collective-permute-start | bytes 3145736 | tf_op jit(solution)/shard_map/ppermute | solution.py:122
  188.6 46.9 %collective-permute-start.26 = (bf16[256,2048]{0,1:T(8,128)(2,1)S(1)}, bf16[256,2048]{0,1:T(8,128)(2,1)S(1)}, u32[]{:S(2)}, u32[]{:S(2)}) collective-permute-start(bf16[256,2048]{0,1:T(8,128)(2,1)S(1)} %copy-done.4), channel_id=1, source_target_pairs={{0,6},{1,7},{2,0},{3,1},{4,2},{5,3},{6,4},{7,5},{8,14},{9,15},{10,... | collective-permute-start | bytes 3145736 | tf_op jit(solution)/shard_map/ppermute | solution.py:122
  196.6 5.1 collective-permute-start.19
  196.9 45.1 %collective-permute-start.18 = (bf16[256,1024]{1,0:T(8,128)(2,1)S(1)}, bf16[256,1024]{1,0:T(8,128)(2,1)S(1)}, u32[]{:S(2)}, u32[]{:S(2)}) collective-permute-start(bf16[256,1024]{1,0:T(8,128)(2,1)S(1)} %get-tuple-element.106), channel_id=1, source_target_pairs={{0,8},{8,0},{16,24},{24,16},{1,9},{9,1},{17,25},{25,17},{2,10},{10... | collective-permute-start | bytes 1572872 | tf_op jit(solution)/shard_map/ppermute | solution.py:125
  200.9 41.1 %collective-permute-start.33 = (bf16[256,1024]{1,0:T(8,128)(2,1)S(1)}, bf16[256,1024]{1,0:T(8,128)(2,1)S(1)}, u32[]{:S(2)}, u32[]{:S(2)}) collective-permute-start(bf16[256,1024]{1,0:T(8,128)(2,1)S(1)} %get-tuple-element.110), channel_id=1, source_target_pairs={{0,8},{8,0},{16,24},{24,16},{1,9},{9,1},{17,25},{25,17},{2,10},{10... | collective-permute-start | bytes 1572872 | tf_op jit(solution)/shard_map/ppermute | solution.py:125
  240.3 14.7 %collective-permute-start.27 = (bf16[256,1024]{1,0:T(8,128)(2,1)S(1)}, bf16[256,1024]{1,0:T(8,128)(2,1)S(1)}, u32[]{:S(2)}, u32[]{:S(2)}) collective-permute-start(bf16[256,1024]{1,0:T(8,128)(2,1)S(1)} %slice.194), channel_id=1, source_target_pairs={{0,8},{8,0},{16,24},{24,16},{1,9},{9,1},{17,25},{25,17},{2,10},{10... | collective-permute-start | bytes 1572872 | tf_op jit(solution)/shard_map/ppermute | solution.py:125
  240.4 14.3 %collective-permute-start.23 = (bf16[256,1024]{1,0:T(8,128)(2,1)S(1)}, bf16[256,1024]{1,0:T(8,128)(2,1)S(1)}, u32[]{:S(2)}, u32[]{:S(2)}) collective-permute-start(bf16[256,1024]{1,0:T(8,128)(2,1)S(1)} %add_convert_fusion.15), channel_id=1, source_target_pairs={{0,16},{8,24},{16,0},{24,8},{1,17},{9,25},{17,1},{25,9},{2,18},{10... | collective-permute-start | bytes 1572872 | tf_op jit(solution)/shard_map/ppermute | solution.py:125
  246.3 14.1 %collective-permute-start.34 = (bf16[256,1024]{1,0:T(8,128)(2,1)S(1)}, bf16[256,1024]{1,0:T(8,128)(2,1)S(1)}, u32[]{:S(2)}, u32[]{:S(2)}) collective-permute-start(bf16[256,1024]{1,0:T(8,128)(2,1)S(1)} %convolution_convert_fusion.8), channel_id=1, source_target_pairs={{0,1},{1,0},{2,3},{3,2},{4,5},{5,4},{6,7},{7,6},{8,9},{9,8},{10,11... | collective-permute-start | bytes 1572872 | tf_op jit(solution)/shard_map/ppermute | solution.py:118
  254.9 6.9 %collective-permute-start.24 = (bf16[256,1024]{1,0:T(8,128)(2,1)S(1)}, bf16[256,1024]{1,0:T(8,128)(2,1)S(1)}, u32[]{:S(2)}, u32[]{:S(2)}) collective-permute-start(bf16[256,1024]{1,0:T(8,128)(2,1)S(1)} %get-tuple-element.104), channel_id=1, source_target_pairs={{0,8},{8,0},{16,24},{24,16},{1,9},{9,1},{17,25},{25,17},{2,10},{10... | collective-permute-start | bytes 1572872 | tf_op jit(solution)/shard_map/ppermute | solution.py:125
  255.2 14.4 %collective-permute-start.28 = (bf16[256,1024]{1,0:T(8,128)(2,1)S(1)}, bf16[256,1024]{1,0:T(8,128)(2,1)S(1)}, u32[]{:S(2)}, u32[]{:S(2)}) collective-permute-start(bf16[256,1024]{1,0:T(8,128)(2,1)S(1)} %add_convert_fusion.12), channel_id=1, source_target_pairs={{0,16},{8,24},{16,0},{24,8},{1,17},{9,25},{17,1},{25,9},{2,18},{10... | collective-permute-start | bytes 1572872 | tf_op jit(solution)/shard_map/ppermute | solution.py:125
  260.4 14.1 %collective-permute-start.35 = (bf16[256,1024]{1,0:T(8,128)(2,1)S(1)}, bf16[256,1024]{1,0:T(8,128)(2,1)S(1)}, u32[]{:S(2)}, u32[]{:S(2)}) collective-permute-start(bf16[256,1024]{1,0:T(8,128)(2,1)S(1)} %convolution_convert_fusion.7), channel_id=1, source_target_pairs={{0,1},{1,0},{2,3},{3,2},{4,5},{5,4},{6,7},{7,6},{8,9},{9,8},{10,11... | collective-permute-start | bytes 1572872 | tf_op jit(solution)/shard_map/ppermute | solution.py:118
  269.8 6.2 %collective-permute-start.29 = (bf16[256,1024]{1,0:T(8,128)(2,1)S(1)}, bf16[256,1024]{1,0:T(8,128)(2,1)S(1)}, u32[]{:S(2)}, u32[]{:S(2)}) collective-permute-start(bf16[256,1024]{1,0:T(8,128)(2,1)S(1)} %get-tuple-element.102), channel_id=1, source_target_pairs={{0,8},{8,0},{16,24},{24,16},{1,9},{9,1},{17,25},{25,17},{2,10},{10... | collective-permute-start | bytes 1572872 | tf_op jit(solution)/shard_map/ppermute | solution.py:125
  270.1 27.4 %collective-permute-start.37 = (bf16[256,2048]{0,1:T(8,128)(2,1)S(1)}, bf16[256,2048]{0,1:T(8,128)(2,1)S(1)}, u32[]{:S(2)}, u32[]{:S(2)}) collective-permute-start(bf16[256,2048]{0,1:T(8,128)(2,1)S(1)} %collective-permute-done.25), channel_id=1, source_target_pairs={{0,2},{1,3},{2,4},{3,5},{4,6},{5,7},{6,0},{7,1},{8,10},{9,11},{10,... | collective-permute-start | bytes 3145736 | tf_op jit(solution)/shard_map/ppermute | solution.py:122
  274.4 26.5 %collective-permute-start.36 = (bf16[256,1024]{1,0:T(8,128)(2,1)S(1)}, bf16[256,1024]{1,0:T(8,128)(2,1)S(1)}, u32[]{:S(2)}, u32[]{:S(2)}) collective-permute-start(bf16[256,1024]{1,0:T(8,128)(2,1)S(1)} %convolution_convert_fusion.6), channel_id=1, source_target_pairs={{0,1},{1,0},{2,3},{3,2},{4,5},{5,4},{6,7},{7,6},{8,9},{9,8},{10,11... | collective-permute-start | bytes 1572872 | tf_op jit(solution)/shard_map/ppermute | solution.py:118
  301.0 13.6 %collective-permute-start.38 = (bf16[256,1024]{1,0:T(8,128)(2,1)S(1)}, bf16[256,1024]{1,0:T(8,128)(2,1)S(1)}, u32[]{:S(2)}, u32[]{:S(2)}) collective-permute-start(bf16[256,1024]{1,0:T(8,128)(2,1)S(1)} %convolution_convert_fusion.5), channel_id=1, source_target_pairs={{0,1},{1,0},{2,3},{3,2},{4,5},{5,4},{6,7},{7,6},{8,9},{9,8},{10,11... | collective-permute-start | bytes 1572872 | tf_op jit(solution)/shard_map/ppermute | solution.py:118
  316.1 5.3 collective-permute-start.39
  316.6 28.1 %collective-permute-start.42 = (bf16[2,128,1024]{2,1,0:T(8,128)(2,1)S(1)}, bf16[2,128,1024]{2,1,0:T(8,128)(2,1)S(1)}, u32[]{:S(2)}, u32[]{:S(2)}) collective-permute-start(bf16[2,128,1024]{2,1,0:T(8,128)(2,1)S(1)} %get-tuple-element.83), channel_id=1, source_target_pairs={{0,24},{8,16},{16,8},{24,0},{1,25},{9,17},{17,9},{25,1},{2,26},{10... | collective-permute-start | bytes 1572872 | tf_op jit(solution)/shard_map/ppermute | solution.py:125
  318.2 23.8 %collective-permute-start.41 = (bf16[2,128,1024]{2,1,0:T(8,128)(2,1)S(1)}, bf16[2,128,1024]{2,1,0:T(8,128)(2,1)S(1)}, u32[]{:S(2)}, u32[]{:S(2)}) collective-permute-start(bf16[2,128,1024]{2,1,0:T(8,128)(2,1)S(1)} %get-tuple-element.79), channel_id=1, source_target_pairs={{0,16},{8,24},{16,0},{24,8},{1,17},{9,25},{17,1},{25,9},{2,18},{10... | collective-permute-start | bytes 1572872 | tf_op jit(solution)/shard_map/ppermute | solution.py:125
  324.0 22.2 %collective-permute-start.40 = (bf16[1024,256]{1,0:T(8,128)(2,1)S(1)}, bf16[1024,256]{1,0:T(8,128)(2,1)S(1)}, u32[]{:S(2)}, u32[]{:S(2)}) collective-permute-start(bf16[1024,256]{1,0:T(8,128)(2,1)S(1)} %get-tuple-element.78), channel_id=1, source_target_pairs={{0,8},{8,0},{16,24},{24,16},{1,9},{9,1},{17,25},{25,17},{2,10},{10... | collective-permute-start | bytes 1572872 | tf_op jit(solution)/shard_map/ppermute | solution.py:125
  344.7 14.1 %collective-permute-start.43 = (bf16[1024,256]{1,0:T(8,128)(2,1)S(1)}, bf16[1024,256]{1,0:T(8,128)(2,1)S(1)}, u32[]{:S(2)}, u32[]{:S(2)}) collective-permute-start(bf16[1024,256]{1,0:T(8,128)(2,1)S(1)} %get-tuple-element.84), channel_id=1, source_target_pairs={{0,16},{8,24},{16,0},{24,8},{1,17},{9,25},{17,1},{25,9},{2,18},{10... | collective-permute-start | bytes 1572872 | tf_op jit(solution)/shard_map/ppermute | solution.py:125
  346.3 26.1 %collective-permute-start.45 = (bf16[1024,512]{1,0:T(8,128)(2,1)S(1)}, bf16[1024,512]{1,0:T(8,128)(2,1)S(1)}, u32[]{:S(2)}, u32[]{:S(2)}) collective-permute-start(bf16[1024,512]{1,0:T(8,128)(2,1)S(1)} %pad_maximum_fusion.6), channel_id=1, source_target_pairs={{0,1},{1,0},{2,3},{3,2},{4,5},{5,4},{6,7},{7,6},{8,9},{9,8},{10,11... | collective-permute-start | bytes 3145736 | tf_op jit(solution)/shard_map/ppermute | solution.py:118
  358.8 13.6 %collective-permute-start.44 = (bf16[1024,256]{1,0:T(8,128)(2,1)S(1)}, bf16[1024,256]{1,0:T(8,128)(2,1)S(1)}, u32[]{:S(2)}, u32[]{:S(2)}) collective-permute-start(bf16[1024,256]{1,0:T(8,128)(2,1)S(1)} %get-tuple-element.88), channel_id=1, source_target_pairs={{0,24},{8,16},{16,8},{24,0},{1,25},{9,17},{17,9},{25,1},{2,26},{10... | collective-permute-start | bytes 1572872 | tf_op jit(solution)/shard_map/ppermute | solution.py:125
  372.4 13.6 %collective-permute-start.46 = (bf16[1024,256]{1,0:T(8,128)(2,1)S(1)}, bf16[1024,256]{1,0:T(8,128)(2,1)S(1)}, u32[]{:S(2)}, u32[]{:S(2)}) collective-permute-start(bf16[1024,256]{1,0:T(8,128)(2,1)S(1)} %collective-permute-done.43), channel_id=1, source_target_pairs={{0,1},{1,0},{2,3},{3,2},{4,5},{5,4},{6,7},{7,6},{8,9},{9,8},{10,11... | collective-permute-start | bytes 1572872 | tf_op jit(solution)/shard_map/ppermute | solution.py:118
  374.6 13.3 %collective-permute-start.51 = (bf16[1024,256]{1,0:T(8,128)(2,1)S(1)}, bf16[1024,256]{1,0:T(8,128)(2,1)S(1)}, u32[]{:S(2)}, u32[]{:S(2)}) collective-permute-start(bf16[1024,256]{1,0:T(8,128)(2,1)S(1)} %convolution_convert_fusion.4), channel_id=1, source_target_pairs={{0,8},{8,0},{16,24},{24,16},{1,9},{9,1},{17,25},{25,17},{2,10},{10... | collective-permute-start | bytes 1572872 | tf_op jit(solution)/shard_map/ppermute | solution.py:125
  386.0 13.1 %collective-permute-start.47 = (bf16[1024,256]{1,0:T(8,128)(2,1)S(1)}, bf16[1024,256]{1,0:T(8,128)(2,1)S(1)}, u32[]{:S(2)}, u32[]{:S(2)}) collective-permute-start(bf16[1024,256]{1,0:T(8,128)(2,1)S(1)} %collective-permute-done.44), channel_id=1, source_target_pairs={{0,1},{1,0},{2,3},{3,2},{4,5},{5,4},{6,7},{7,6},{8,9},{9,8},{10,11... | collective-permute-start | bytes 1572872 | tf_op jit(solution)/shard_map/ppermute | solution.py:118
  388.7 13.3 %collective-permute-start.52 = (bf16[1024,256]{1,0:T(8,128)(2,1)S(1)}, bf16[1024,256]{1,0:T(8,128)(2,1)S(1)}, u32[]{:S(2)}, u32[]{:S(2)}) collective-permute-start(bf16[1024,256]{1,0:T(8,128)(2,1)S(1)} %fusion.7), channel_id=1, source_target_pairs={{0,16},{8,24},{16,0},{24,8},{1,17},{9,25},{17,1},{25,9},{2,18},{10... | collective-permute-start | bytes 1572872 | tf_op jit(solution)/shard_map/ppermute | solution.py:125
  401.4 4.3 collective-permute-start.50
  402.7 14.0 %collective-permute-start.54 = (bf16[1024,256]{1,0:T(8,128)(2,1)S(1)}, bf16[1024,256]{1,0:T(8,128)(2,1)S(1)}, u32[]{:S(2)}, u32[]{:S(2)}) collective-permute-start(bf16[1024,256]{1,0:T(8,128)(2,1)S(1)} %fusion.8), channel_id=1, source_target_pairs={{0,16},{8,24},{16,0},{24,8},{1,17},{9,25},{17,1},{25,9},{2,18},{10... | collective-permute-start | bytes 1572872 | tf_op jit(solution)/shard_map/ppermute | solution.py:125
  405.6 13.5 %collective-permute-start.49 = (bf16[2048,256]{1,0:T(8,128)(2,1)S(1)}, bf16[2048,256]{1,0:T(8,128)(2,1)S(1)}, u32[]{:S(2)}, u32[]{:S(2)}) collective-permute-start(bf16[2048,256]{1,0:T(8,128)(2,1)S(1)} %convolution_convert_fusion.1), channel_id=1, source_target_pairs={{0,8},{8,0},{16,24},{24,16},{1,9},{9,1},{17,25},{25,17},{2,10},{10... | collective-permute-start | bytes 3145736 | tf_op jit(solution)/shard_map/ppermute | solution.py:125
  416.7 24.3 %collective-permute-start.55 = (bf16[2048,256]{1,0:T(8,128)(2,1)S(1)}, bf16[2048,256]{1,0:T(8,128)(2,1)S(1)}, u32[]{:S(2)}, u32[]{:S(2)}) collective-permute-start(bf16[2048,256]{1,0:T(8,128)(2,1)S(1)} %fusion.2), channel_id=1, source_target_pairs={{0,16},{8,24},{16,0},{24,8},{1,17},{9,25},{17,1},{25,9},{2,18},{10... | collective-permute-start | bytes 3145736 | tf_op jit(solution)/shard_map/ppermute | solution.py:125
  418.3 25.7 %collective-permute-start.62 = (bf16[1024,256]{1,0:T(8,128)(2,1)S(1)}, bf16[1024,256]{1,0:T(8,128)(2,1)S(1)}, u32[]{:S(2)}, u32[]{:S(2)}) collective-permute-start(bf16[1024,256]{1,0:T(8,128)(2,1)S(1)} %add_convert_fusion.6), channel_id=1, source_target_pairs={{0,8},{8,0},{16,24},{24,16},{1,9},{9,1},{17,25},{25,17},{2,10},{10... | collective-permute-start | bytes 1572872 | tf_op jit(solution)/shard_map/ppermute | solution.py:125
  418.5 25.5 %collective-permute-start.63 = (bf16[1024,256]{1,0:T(8,128)(2,1)S(1)}, bf16[1024,256]{1,0:T(8,128)(2,1)S(1)}, u32[]{:S(2)}, u32[]{:S(2)}) collective-permute-start(bf16[1024,256]{1,0:T(8,128)(2,1)S(1)} %add_convert_fusion.5), channel_id=1, source_target_pairs={{0,8},{8,0},{16,24},{24,16},{1,9},{9,1},{17,25},{25,17},{2,10},{10... | collective-permute-start | bytes 1572872 | tf_op jit(solution)/shard_map/ppermute | solution.py:125
  441.0 23.4 %collective-permute-start.56 = (bf16[2048,256]{1,0:T(8,128)(2,1)S(1)}, bf16[2048,256]{1,0:T(8,128)(2,1)S(1)}, u32[]{:S(2)}, u32[]{:S(2)}) collective-permute-start(bf16[2048,256]{1,0:T(8,128)(2,1)S(1)} %fusion.1), channel_id=1, source_target_pairs={{0,16},{8,24},{16,0},{24,8},{1,17},{9,25},{17,1},{25,9},{2,18},{10... | collective-permute-start | bytes 3145736 | tf_op jit(solution)/shard_map/ppermute | solution.py:125
  443.9 20.9 %collective-permute-start.48 = (bf16[2048,256]{1,0:T(8,128)(2,1)S(1)}, bf16[2048,256]{1,0:T(8,128)(2,1)S(1)}, u32[]{:S(2)}, u32[]{:S(2)}) collective-permute-start(bf16[2048,256]{1,0:T(8,128)(2,1)S(1)} %convolution_convert_fusion.2), channel_id=1, source_target_pairs={{0,8},{8,0},{16,24},{24,16},{1,9},{9,1},{17,25},{25,17},{2,10},{10... | collective-permute-start | bytes 3145736 | tf_op jit(solution)/shard_map/ppermute | solution.py:125
  451.1 50.6 %collective-permute-start.64 = (bf16[2048,512]{1,0:T(8,128)(2,1)S(1)}, bf16[2048,512]{1,0:T(8,128)(2,1)S(1)}, u32[]{:S(2)}, u32[]{:S(2)}) collective-permute-start(bf16[2048,512]{1,0:T(8,128)(2,1)S(1)} %shard_map.91), channel_id=1, source_target_pairs={{0,2},{1,3},{2,4},{3,5},{4,6},{5,7},{6,0},{7,1},{8,10},{9,11},{10,... | collective-permute-start | bytes 6291464 | tf_op jit(solution)/shard_map/ppermute | solution.py:122
  451.6 14.6 %collective-permute-start.59 = (bf16[2048,256]{1,0:T(8,128)(2,1)S(1)}, bf16[2048,256]{1,0:T(8,128)(2,1)S(1)}, u32[]{:S(2)}, u32[]{:S(2)}) collective-permute-start(bf16[2048,256]{1,0:T(8,128)(2,1)S(1)} %add_convert_fusion.3), channel_id=1, source_target_pairs={{0,8},{8,0},{16,24},{24,16},{1,9},{9,1},{17,25},{25,17},{2,10},{10... | collective-permute-start | bytes 3145736 | tf_op jit(solution)/shard_map/ppermute | solution.py:125
  464.7 10.2 %collective-permute-start.61 = (bf16[2048,256]{1,0:T(8,128)(2,1)S(1)}, bf16[2048,256]{1,0:T(8,128)(2,1)S(1)}, u32[]{:S(2)}, u32[]{:S(2)}) collective-permute-start(bf16[2048,256]{1,0:T(8,128)(2,1)S(1)} %add_convert_fusion.2), channel_id=1, source_target_pairs={{0,8},{8,0},{16,24},{24,16},{1,9},{9,1},{17,25},{25,17},{2,10},{10... | collective-permute-start | bytes 3145736 | tf_op jit(solution)/shard_map/ppermute | solution.py:125
  473.3 73.4 %collective-permute-start.60 = (bf16[2048,512]{1,0:T(8,128)(2,1)S(1)}, bf16[2048,512]{1,0:T(8,128)(2,1)}, u32[]{:S(2)}, u32[]{:S(2)}) collective-permute-start(bf16[2048,512]{1,0:T(8,128)(2,1)S(1)} %shard_map.89), channel_id=1, source_target_pairs={{0,6},{1,7},{2,0},{3,1},{4,2},{5,3},{6,4},{7,5},{8,14},{9,15},{10,... | collective-permute-start | bytes 6291464 | tf_op jit(solution)/shard_map/ppermute | solution.py:122
  473.5 30.2 %collective-permute-start.57 = (bf16[2048,256]{1,0:T(8,128)(2,1)S(1)}, bf16[2048,256]{1,0:T(8,128)(2,1)S(1)}, u32[]{:S(2)}, u32[]{:S(2)}) collective-permute-start(bf16[2048,256]{1,0:T(8,128)(2,1)S(1)} %fusion), channel_id=1, source_target_pairs={{0,16},{8,24},{16,0},{24,8},{1,17},{9,25},{17,1},{25,9},{2,18},{10... | collective-permute-start | bytes 3145736 | tf_op jit(solution)/shard_map/ppermute | solution.py:125
  503.8 87.5 %collective-permute-start.65 = (bf16[2048,512]{1,0:T(8,128)(2,1)}, bf16[2048,512]{1,0:T(8,128)(2,1)}, u32[]{:S(2)}, u32[]{:S(2)}) collective-permute-start(bf16[2048,512]{1,0:T(8,128)(2,1)} %add_convert_fusion.1), channel_id=1, source_target_pairs={{0,2},{1,3},{2,4},{3,5},{4,6},{5,7},{6,0},{7,1},{8,10},{9,11},{10,... | collective-permute-start | bytes 6291464 | tf_op jit(solution)/shard_map/ppermute | solution.py:122
  (13 other events, 205.2 us)

commit v4 on v3

--- a/solution.py
+++ b/solution.py
@@ -204,7 +204,7 @@
                 grads[1] = tie(grads[1], right)
             if (k, s) == (1, far):
                 grads[far] = tie(grads[far], last["rows"][-2])
-            g = tie(grads[s], rights[1], rights[3]) if (k, s) == turns[-1] else grads[s]
+            g = tie(grads[s], rights[1], rights[3]) if (k, s) == (0, 3) else grads[s]
             term = product([(g, lefts[k])], BF16, by_rows=False)
             mine, theirs = half_sum(term[half:], term[:half], 1)
             rotated[k] = lax.dynamic_update_slice_in_dim(rotated[k], mine, n_at(s, core), 0)
@@ -229,7 +229,7 @@
 
         step = moments_at if sub % 128 == 0 else moments_sliced
         rots = [rot_k[k * per_row : (k + 1) * per_row] for k in range(n_row)]
-        rots[1:] = [across_rows(rots[k], k, 2) for k in range(1, n_row)]
+        rots[1:] = [across_rows(rots[k], k) for k in range(1, n_row)]
 
         kept, by_rows, held = (), [[] for _ in range(n_b)], []
         for k, rot in enumerate(rots):
@@ -247,25 +247,40 @@
         by_rows = [jnp.concatenate(ds, axis=1) for ds in by_rows]
         direction = jnp.concatenate(by_rows, axis=0)
 
-        def back(s, parts, kind, more=()):
+        def back(s, parts, kind):
             r_mine = lax.dynamic_slice_in_dim(right_k, n_at(s, core), half, 1)
             r_theirs = lax.dynamic_slice_in_dim(right_k, n_at(s, 1 - core), half, 1)
-            ws = []
+            w_mine, w_theirs = [], []
             for i, d in enumerate(parts):
                 d_mine = d
                 if i:
                     d, d_mine = tie(d, last["half"]), tie(d, last["rows"][-1])
-                ws.append(jnp.concatenate(half_sum(dot(d, r_theirs, (1, 0)), dot(d_mine, r_mine, (1, 0)), 1), axis=1))
+                mine, theirs = half_sum(
+                    dot(d, r_theirs, (1, 0)), dot(d_mine, r_mine, (1, 0)), 1
+                )
+                w_mine.append(mine)
+                w_theirs.append(theirs)
             if len(parts) < n_b:
-                ws = [ws[0][k * own_i : (k + 1) * own_i] for k in range(n_b)]
-            return product(list(zip(lefts, ws)), kind, more)
+                w_mine, w_theirs = [
+                    [w[0][k * own_i : (k + 1) * own_i] for k in range(n_b)] for w in (w_mine, w_theirs)
+                ]
+            return [product(list(zip(lefts, w)), kind) for w in (w_mine, w_theirs)]
+
+        def joined(u):
+            return jnp.concatenate(u, axis=1)
+
+        def halves(x):
+            return x[:, :half], x[:, half:]
 
         whole = [direction]
-        passed = a_shift(back(2, by_rows, BF16), 1)
-        behind = a_shift(back(1, whole, BF16), -1)
-        ahead = a_shift((back(3, whole, F32) + passed.astype(F32)).astype(BF16), 1)
-        update = back(0, whole, F32) + behind.astype(F32) + ahead.astype(F32)
-        u_mine, u_theirs = update[:, :half].astype(BF16), update[:, half:].astype(BF16)
+        passed = halves(a_shift(joined(back(2, by_rows, BF16)), 1))
+        behind = halves(a_shift(joined(back(1, whole, BF16)), -1))
+        ahead = [(u + x.astype(F32)).astype(BF16) for u, x in zip(back(3, whole, F32), passed)]
+        ahead = halves(a_shift(joined(ahead), 1))
+        own = back(0, whole, F32)
+        u_mine, u_theirs = [
+            (u + x.astype(F32) + y.astype(F32)).astype(BF16) for u, x, y in zip(own, behind, ahead)
+        ]
         update = jnp.where(
             core == 0,
             jnp.concatenate([u_mine, u_theirs], axis=1),

time: 606 us -> 574 us (0.947)
  waiting for transfers between devices: 365 us -> 331 us
  Pallas kernels: 87.1 us -> 95 us
    ppermute x9, waiting for transfers between devices: 216 us -> 183 us  [a_shift(): return lax.ppermute(x, 'col', perm)]
    pallas_call x12 -> x16, Pallas kernels: 68.6 us -> 84.4 us  [product(): pl.pallas_call(functools.partial(product_kernel, len(pairs)), grid=(grid,...]
    ppermute x48, waiting for transfers between devices: 113 us -> 103 us  [row_xor(): return lax.ppermute(x, 'row', [(r, r ^ k) for r in range(n_row)])]
    ppermute x9, waiting for transfers between devices: 36.2 us -> 45.1 us  [b_shift(): return lax.ppermute(x, 'col', perm)]
    pallas_call x4, Pallas kernels: 18.5 us -> 10.7 us  [moments_at(): pl.pallas_call(moments_kernel, grid_spec=pltpu.PrefetchScalarGridSpec(num...]
  transfers between devices with their start and end apart: 66 -> 66, of which waited for: 26 -> 29; matrix products, arithmetic and copies ran while one was open for 13% -> 13% of each run, Pallas kernels for 15% -> 17%
where the time goes in v4:
time: 574 us; the launch traced here: 565 us
  waiting for transfers between devices  331 us (58%)
  Pallas kernels  95 us (17%)
  starting transfers between devices  47.3 us (8%)
  local copies, waits for them, and re-layouts  32.1 us (6%)
  matrix products  29.7 us (5%)
  other arithmetic  27.8 us (5%)
    ppermute x9, waiting for transfers between devices, a_shift(): return lax.ppermute(x, 'col', perm)  183 us
    ppermute x48, waiting for transfers between devices, row_xor(): return lax.ppermute(x, 'row', [(r, r ^ k) for r in range(n_row)])  103 us
    pallas_call x16, Pallas kernels, product(): pl.pallas_call(functools.partial(product_kernel, len(pairs)), grid=(grid,...  84.4 us
    ppermute x9, waiting for transfers between devices, b_shift(): return lax.ppermute(x, 'col', perm)  45.1 us
    dot_general x18, matrix products, dot(): lax.dot_general(a, b, ((contract[:1], contract[1:]), ((), ())), preferred...  29.7 us
    ppermute x48, starting transfers between devices, row_xor(): return lax.ppermute(x, 'row', [(r, r ^ k) for r in range(n_row)])  24.4 us
    ppermute x9, starting transfers between devices, b_shift(): return lax.ppermute(x, 'col', perm)  13.3 us
  transfers between devices with their start and end apart: 66, of which 29 were waited for; matrix products, arithmetic and copies ran while one was open for 13% of the time, Pallas kernels for 17%

profile of v4, /device:TPU:0, one launch (start us, length us, event | category | flops | bytes accessed | tf_op | source)
XLA Modules:
  0.0 565.4 jit_solution(13052074843301684589)
XLA Ops:
  0.7 1.7 constant_dynamic-slice_fusion.3
  5.8 3.0 collective-permute-start.2
  10.4 2.2 collective-permute-start.1
  12.7 1.9 dynamic-slice_bitcast_fusion
  18.6 4.7 shard_map.76
  28.8 1.7 constant_dynamic-update-slice_fusion.23
  30.5 2.2 constant_dynamic-slice_fusion
  34.3 1.8 collective-permute-start.8
  36.1 23.2 %collective-permute-done.refs_0_ = bf16[512,2048]{1,0:T(8,128)(2,1)} collective-permute-done((bf16[512,2048]{1,0:T(8,128)(2,1)S(1)}, bf16[512,2048]{1,0:T(8,128)(2,1)}, u32[]{:S(2)}, u32[]{:S(2)}) %collective-permute-start) | collective-permute-done | bytes 2097184 | tf_op jit(solution)/shard_map/ppermute | solution.py:122
  59.3 42.9 %collective-permute-done.1.refs_0_ = bf16[512,2048]{1,0:T(8,128)(2,1)} collective-permute-done((bf16[512,2048]{1,0:T(8,128)(2,1)S(1)}, bf16[512,2048]{1,0:T(8,128)(2,1)}, u32[]{:S(2)}, u32[]{:S(2)}) %collective-permute-start.1) | collective-permute-done | bytes 2097184 | tf_op jit(solution)/shard_map/ppermute | solution.py:122
  102.3 4.7 shard_map.80
  107.2 3.8 collective-permute-done.6
  113.5 1.8 collective-permute-start.22
  115.3 5.5 shard_map.79
  126.0 5.5 shard_map.78
  132.6 2.1 add_convert_fusion.20
  134.6 4.5 collective-permute-done.14
  140.6 2.5 broadcast.29.clone
  143.2 2.4 constant_dynamic-update-slice_fusion.14
  145.6 5.5 shard_map.77
  154.5 1.9 constant_dynamic-update-slice_fusion.13
  156.4 2.3 constant_dynamic-update-slice_fusion.12
  160.1 2.3 collective-permute-done.22.refs_0_
  162.3 4.6 collective-permute-done.16
  166.9 2.5 collective-permute-start.20
  169.5 4.7 shard_map.82
  177.2 11.7 %collective-permute-done.17 = bf16[256,1024]{1,0:T(8,128)(2,1)S(1)} collective-permute-done((bf16[256,1024]{1,0:T(8,128)(2,1)S(1)}, bf16[256,1024]{1,0:T(8,128)(2,1)S(1)}, u32[]{:S(2)}, u32[]{:S(2)}) %collective-permute-start.17) | collective-permute-done | bytes 524320 | tf_op jit(solution)/shard_map/ppermute | solution.py:125
  190.3 19.7 %collective-permute-done.20 = bf16[256,2048]{0,1:T(8,128)(2,1)S(1)} collective-permute-done((bf16[256,2048]{0,1:T(8,128)(2,1)S(1)}, bf16[256,2048]{0,1:T(8,128)(2,1)S(1)}, u32[]{:S(2)}, u32[]{:S(2)}) %collective-permute-start.20) | collective-permute-done | bytes 1048608 | tf_op jit(solution)/shard_map/ppermute | solution.py:122
  210.0 5.5 shard_map.81
  219.2 4.8 shard_map.83
  226.8 3.5 convolution_convert_fusion.8
  231.8 6.7 %collective-permute-done.25 = bf16[256,1024]{1,0:T(8,128)(2,1)S(1)} collective-permute-done((bf16[256,1024]{1,0:T(8,128)(2,1)S(1)}, bf16[256,1024]{1,0:T(8,128)(2,1)S(1)}, u32[]{:S(2)}, u32[]{:S(2)}) %collective-permute-start.25) | collective-permute-done | bytes 524320 | tf_op jit(solution)/shard_map/ppermute | solution.py:125
  240.4 3.5 convolution_convert_fusion.7
  245.4 8.0 %collective-permute-done.28 = bf16[256,1024]{1,0:T(8,128)(2,1)S(1)} collective-permute-done((bf16[256,1024]{1,0:T(8,128)(2,1)S(1)}, bf16[256,1024]{1,0:T(8,128)(2,1)S(1)}, u32[]{:S(2)}, u32[]{:S(2)}) %collective-permute-start.28) | collective-permute-done | bytes 524320 | tf_op jit(solution)/shard_map/ppermute | solution.py:125
  255.1 3.5 convolution_convert_fusion.6
  262.8 19.0 %collective-permute-done.37 = bf16[256,2048]{0,1:T(8,128)(2,1)S(1)} collective-permute-done((bf16[256,2048]{0,1:T(8,128)(2,1)S(1)}, bf16[256,2048]{0,1:T(8,128)(2,1)S(1)}, u32[]{:S(2)}, u32[]{:S(2)}) %collective-permute-start.37) | collective-permute-done | bytes 1048608 | tf_op jit(solution)/shard_map/ppermute | solution.py:122
  281.8 3.5 convolution_convert_fusion.5
  287.9 11.0 %collective-permute-done.38 = bf16[256,1024]{1,0:T(8,128)(2,1)S(1)} collective-permute-done((bf16[256,1024]{1,0:T(8,128)(2,1)S(1)}, bf16[256,1024]{1,0:T(8,128)(2,1)S(1)}, u32[]{:S(2)}, u32[]{:S(2)}) %collective-permute-start.38) | collective-permute-done | bytes 524320 | tf_op jit(solution)/shard_map/ppermute | solution.py:118
  302.6 2.6 shard_map.84
  305.2 2.6 shard_map.85
  307.8 7.1 %collective-permute-done.41.rot_ref = bf16[2,128,1024]{2,1,0:T(8,128)(2,1)S(1)} collective-permute-done((bf16[2,128,1024]{2,1,0:T(8,128)(2,1)S(1)}, bf16[2,128,1024]{2,1,0:T(8,128)(2,1)S(1)}, u32[]{:S(2)}, u32[]{:S(2)}) %collective-permute-start.41) | collective-permute-done | bytes 524320 | tf_op jit(solution)/shard_map/ppermute | solution.py:125
  315.8 2.7 shard_map.86
  318.5 10.5 %collective-permute-done.42.rot_ref = bf16[2,128,1024]{2,1,0:T(8,128)(2,1)S(1)} collective-permute-done((bf16[2,128,1024]{2,1,0:T(8,128)(2,1)S(1)}, bf16[2,128,1024]{2,1,0:T(8,128)(2,1)S(1)}, u32[]{:S(2)}, u32[]{:S(2)}) %collective-permute-start.42) | collective-permute-done | bytes 524320 | tf_op jit(solution)/shard_map/ppermute | solution.py:125
  332.1 2.8 shard_map.87
  334.9 7.9 %collective-permute-done.43 = bf16[1024,256]{1,0:T(8,128)(2,1)S(1)} collective-permute-done((bf16[1024,256]{1,0:T(8,128)(2,1)S(1)}, bf16[1024,256]{1,0:T(8,128)(2,1)S(1)}, u32[]{:S(2)}, u32[]{:S(2)}) %collective-permute-start.43) | collective-permute-done | bytes 524320 | tf_op jit(solution)/shard_map/ppermute | solution.py:125
  343.2 12.0 %collective-permute-done.45 = bf16[1024,512]{1,0:T(8,128)(2,1)S(1)} collective-permute-done((bf16[1024,512]{1,0:T(8,128)(2,1)S(1)}, bf16[1024,512]{1,0:T(8,128)(2,1)S(1)}, u32[]{:S(2)}, u32[]{:S(2)}) %collective-permute-start.45) | collective-permute-done | bytes 1048608 | tf_op jit(solution)/shard_map/ppermute | solution.py:118
  357.7 10.0 %collective-permute-done.46 = bf16[1024,256]{1,0:T(8,128)(2,1)S(1)} collective-permute-done((bf16[1024,256]{1,0:T(8,128)(2,1)S(1)}, bf16[1024,256]{1,0:T(8,128)(2,1)S(1)}, u32[]{:S(2)}, u32[]{:S(2)}) %collective-permute-start.46) | collective-permute-done | bytes 524320 | tf_op jit(solution)/shard_map/ppermute | solution.py:118
  371.2 8.2 %collective-permute-done.47 = bf16[1024,256]{1,0:T(8,128)(2,1)S(1)} collective-permute-done((bf16[1024,256]{1,0:T(8,128)(2,1)S(1)}, bf16[1024,256]{1,0:T(8,128)(2,1)S(1)}, u32[]{:S(2)}, u32[]{:S(2)}) %collective-permute-start.47) | collective-permute-done | bytes 524320 | tf_op jit(solution)/shard_map/ppermute | solution.py:118
  386.6 10.4 %collective-permute-done.54 = bf16[1024,256]{1,0:T(8,128)(2,1)S(1)} collective-permute-done((bf16[1024,256]{1,0:T(8,128)(2,1)S(1)}, bf16[1024,256]{1,0:T(8,128)(2,1)S(1)}, u32[]{:S(2)}, u32[]{:S(2)}) %collective-permute-start.54) | collective-permute-done | bytes 524320 | tf_op jit(solution)/shard_map/ppermute | solution.py:125
  401.5 5.4 shard_map.92
  407.0 5.4 shard_map.93
  412.4 9.0 %collective-permute-done.55 = bf16[2048,256]{1,0:T(8,128)(2,1)S(1)} collective-permute-done((bf16[2048,256]{1,0:T(8,128)(2,1)S(1)}, bf16[2048,256]{1,0:T(8,128)(2,1)S(1)}, u32[]{:S(2)}, u32[]{:S(2)}) %collective-permute-start.55) | collective-permute-done | bytes 1048608 | tf_op jit(solution)/shard_map/ppermute | solution.py:125
  424.4 20.4 %collective-permute-done.56 = bf16[2048,256]{1,0:T(8,128)(2,1)S(1)} collective-permute-done((bf16[2048,256]{1,0:T(8,128)(2,1)S(1)}, bf16[2048,256]{1,0:T(8,128)(2,1)S(1)}, u32[]{:S(2)}, u32[]{:S(2)}) %collective-permute-start.56) | collective-permute-done | bytes 1048608 | tf_op jit(solution)/shard_map/ppermute | solution.py:125
  445.2 5.4 shard_map.89
  451.7 5.5 shard_map.90
  458.8 5.5 shard_map.91
  464.4 5.4 shard_map.94
  469.8 3.3 collective-permute-done.62
  476.7 5.4 shard_map.88
  483.4 5.4 shard_map.95
  488.9 29.4 %collective-permute-done.59 = bf16[2048,512]{1,0:T(8,128)(2,1)} collective-permute-done((bf16[2048,512]{1,0:T(8,128)(2,1)}, bf16[2048,512]{1,0:T(8,128)(2,1)}, u32[]{:S(2)}, u32[]{:S(2)}) %collective-permute-start.59) | collective-permute-done | bytes 2097184 | tf_op jit(solution)/shard_map/ppermute | solution.py:122
  518.2 42.0 %collective-permute-done.64 = bf16[2048,512]{1,0:T(8,128)(2,1)} collective-permute-done((bf16[2048,512]{1,0:T(8,128)(2,1)}, bf16[2048,512]{1,0:T(8,128)(2,1)}, u32[]{:S(2)}, u32[]{:S(2)}) %collective-permute-start.64) | collective-permute-done | bytes 2097184 | tf_op jit(solution)/shard_map/ppermute | solution.py:122
  560.2 3.0 add_convert_fusion.1
  563.3 1.9 maximum_select_fusion
  (221 shorter events, 91.8 us)
Async XLA Ops:
  5.8 96.4 %collective-permute-start.2 = (bf16[2048,1024]{1,0:T(8,128)(2,1)}, bf16[2048,1024]{1,0:T(8,128)(2,1)}, u32[]{:S(2)}, u32[]{:S(2)}) collective-permute-start(bf16[2048,1024]{1,0:T(8,128)(2,1)} %refs_0_.7), channel_id=1, source_target_pairs={{0,1},{1,0},{2,3},{3,2},{4,5},{5,4},{6,7},{7,6},{8,9},{9,8},{10,11... | collective-permute-start | bytes 12582920 | tf_op jit(solution)/shard_map/ppermute | solution.py:118
  8.8 50.5 %collective-permute-start = (bf16[512,2048]{1,0:T(8,128)(2,1)S(1)}, bf16[512,2048]{1,0:T(8,128)(2,1)}, u32[]{:S(2)}, u32[]{:S(2)}) collective-permute-start(bf16[512,2048]{1,0:T(8,128)(2,1)S(1)} %pad_maximum_fusion.1.refs_0_), channel_id=1, source_target_pairs={{0,2},{1,3},{2,4},{3,5},{4,6},{5,7},{6,0},{7,1},{8,10},{9,11},{10,... | collective-permute-start | bytes 6291464 | tf_op jit(solution)/shard_map/ppermute | solution.py:122
  10.4 91.9 %collective-permute-start.1 = (bf16[512,2048]{1,0:T(8,128)(2,1)S(1)}, bf16[512,2048]{1,0:T(8,128)(2,1)}, u32[]{:S(2)}, u32[]{:S(2)}) collective-permute-start(bf16[512,2048]{1,0:T(8,128)(2,1)S(1)} %pad_maximum_fusion.1.refs_0_), channel_id=1, source_target_pairs={{0,6},{1,7},{2,0},{3,1},{4,2},{5,3},{6,4},{7,5},{8,14},{9,15},{10,... | collective-permute-start | bytes 6291464 | tf_op jit(solution)/shard_map/ppermute | solution.py:122
  14.5 2.7 collective-permute-start.3
  14.5 11.3 %collective-permute-start.4 = (bf16[128,1024]{0,1:T(8,128)(2,1)}, bf16[128,1024]{0,1:T(8,128)(2,1)}, u32[]{:S(2)}, u32[]{:S(2)}) collective-permute-start(bf16[128,1024]{0,1:T(8,128)(2,1)} %get-tuple-element.144), channel_id=1, source_target_pairs={{0,16},{8,24},{16,0},{24,8},{1,17},{9,25},{17,1},{25,9},{2,18},{10... | collective-permute-start | bytes 786440 | tf_op jit(solution)/shard_map/ppermute | solution.py:125
  18.3 10.6 %collective-permute-start.5 = (bf16[128,1024]{0,1:T(8,128)(2,1)S(1)}, bf16[128,1024]{0,1:T(8,128)(2,1)}, u32[]{:S(2)}, u32[]{:S(2)}) collective-permute-start(bf16[128,1024]{0,1:T(8,128)(2,1)S(1)} %get-tuple-element.143), channel_id=1, source_target_pairs={{0,24},{8,16},{16,8},{24,0},{1,25},{9,17},{17,9},{25,1},{2,26},{10... | collective-permute-start | bytes 786440 | tf_op jit(solution)/shard_map/ppermute | solution.py:125
  25.8 7.2 %collective-permute-start.7 = (bf16[256,1024]{1,0:T(8,128)(2,1)}, bf16[256,1024]{1,0:T(8,128)(2,1)}, u32[]{:S(2)}, u32[]{:S(2)}) collective-permute-start(bf16[256,1024]{1,0:T(8,128)(2,1)} %slice.217), channel_id=1, source_target_pairs={{0,8},{8,0},{16,24},{24,16},{1,9},{9,1},{17,25},{25,17},{2,10},{10... | collective-permute-start | bytes 1572872 | tf_op jit(solution)/shard_map/ppermute | solution.py:125
  32.7 78.2 %collective-permute-start.6 = (bf16[128,2048]{0,1:T(8,128)(2,1)}, bf16[128,2048]{0,1:T(8,128)(2,1)}, u32[]{:S(2)}, u32[]{:S(2)}) collective-permute-start(bf16[128,2048]{0,1:T(8,128)(2,1)} %bitcast.9), channel_id=1, source_target_pairs={{0,1},{1,0},{2,3},{3,2},{4,5},{5,4},{6,7},{7,6},{8,9},{9,8},{10,11... | collective-permute-start | bytes 1572872 | tf_op jit(solution)/shard_map/ppermute | solution.py:118
  34.3 89.4 %collective-permute-start.8 = (bf16[256,1024]{1,0:T(8,128)(2,1)S(1)}, bf16[256,1024]{1,0:T(8,128)(2,1)S(1)}, u32[]{:S(2)}, u32[]{:S(2)}) collective-permute-start(bf16[256,1024]{1,0:T(8,128)(2,1)S(1)} %add_convert_fusion.24), channel_id=1, source_target_pairs={{0,16},{8,24},{16,0},{24,8},{1,17},{9,25},{17,1},{25,9},{2,18},{10... | collective-permute-start | bytes 1572872 | tf_op jit(solution)/shard_map/ppermute | solution.py:125
  107.1 15.6 %collective-permute-start.13 = (bf16[256,1024]{1,0:T(8,128)(2,1)S(1)}, bf16[256,1024]{1,0:T(8,128)(2,1)S(1)}, u32[]{:S(2)}, u32[]{:S(2)}) collective-permute-start(bf16[256,1024]{1,0:T(8,128)(2,1)S(1)} %slice.225), channel_id=1, source_target_pairs={{0,8},{8,0},{16,24},{24,16},{1,9},{9,1},{17,25},{25,17},{2,10},{10... | collective-permute-start | bytes 1572872 | tf_op jit(solution)/shard_map/ppermute | solution.py:125
  113.5 48.8 %collective-permute-start.22 = (bf16[512,2048]{1,0:T(8,128)(2,1)}, bf16[512,2048]{1,0:T(8,128)(2,1)S(1)}, u32[]{:S(2)}, u32[]{:S(2)}) collective-permute-start(bf16[512,2048]{1,0:T(8,128)(2,1)} %collective-permute-done.refs_0_), channel_id=1, source_target_pairs={{0,2},{1,3},{2,4},{3,5},{4,6},{5,7},{6,0},{7,1},{8,10},{9,11},{10,... | collective-permute-start | bytes 6291464 | tf_op jit(solution)/shard_map/ppermute | solution.py:122
  122.6 9.9 %collective-permute-start.12 = (bf16[256,1024]{1,0:T(8,128)(2,1)}, bf16[256,1024]{1,0:T(8,128)(2,1)}, u32[]{:S(2)}, u32[]{:S(2)}) collective-permute-start(bf16[256,1024]{1,0:T(8,128)(2,1)} %slice.223), channel_id=1, source_target_pairs={{0,8},{8,0},{16,24},{24,16},{1,9},{9,1},{17,25},{25,17},{2,10},{10... | collective-permute-start | bytes 1572872 | tf_op jit(solution)/shard_map/ppermute | solution.py:125
  124.5 14.7 %collective-permute-start.14 = (bf16[256,1024]{1,0:T(8,128)(2,1)}, bf16[256,1024]{1,0:T(8,128)(2,1)}, u32[]{:S(2)}, u32[]{:S(2)}) collective-permute-start(bf16[256,1024]{1,0:T(8,128)(2,1)} %add_convert_fusion.19), channel_id=1, source_target_pairs={{0,16},{8,24},{16,0},{24,8},{1,17},{9,25},{17,1},{25,9},{2,18},{10... | collective-permute-start | bytes 1572872 | tf_op jit(solution)/shard_map/ppermute | solution.py:125
  132.3 19.4 %collective-permute-start.11 = (bf16[256,1024]{1,0:T(8,128)(2,1)}, bf16[256,1024]{1,0:T(8,128)(2,1)}, u32[]{:S(2)}, u32[]{:S(2)}) collective-permute-start(bf16[256,1024]{1,0:T(8,128)(2,1)} %slice.221), channel_id=1, source_target_pairs={{0,8},{8,0},{16,24},{24,16},{1,9},{9,1},{17,25},{25,17},{2,10},{10... | collective-permute-start | bytes 1572872 | tf_op jit(solution)/shard_map/ppermute | solution.py:125
  139.1 13.9 %collective-permute-start.15 = (bf16[256,1024]{1,0:T(8,128)(2,1)}, bf16[256,1024]{1,0:T(8,128)(2,1)}, u32[]{:S(2)}, u32[]{:S(2)}) collective-permute-start(bf16[256,1024]{1,0:T(8,128)(2,1)} %add_convert_fusion.20), channel_id=1, source_target_pairs={{0,16},{8,24},{16,0},{24,8},{1,17},{9,25},{17,1},{25,9},{2,18},{10... | collective-permute-start | bytes 1572872 | tf_op jit(solution)/shard_map/ppermute | solution.py:125
  145.6 8.9 %collective-permute-start.30 = (bf16[256,1024]{1,0:T(8,128)(2,1)}, bf16[256,1024]{1,0:T(8,128)(2,1)}, u32[]{:S(2)}, u32[]{:S(2)}) collective-permute-start(bf16[256,1024]{1,0:T(8,128)(2,1)} %get-tuple-element.116), channel_id=1, source_target_pairs={{0,8},{8,0},{16,24},{24,16},{1,9},{9,1},{17,25},{25,17},{2,10},{10... | collective-permute-start | bytes 1572872 | tf_op jit(solution)/shard_map/ppermute | solution.py:125
  151.1 23.1 %collective-permute-start.10 = (bf16[256,1024]{1,0:T(8,128)(2,1)S(1)}, bf16[256,1024]{1,0:T(8,128)(2,1)S(1)}, u32[]{:S(2)}, u32[]{:S(2)}) collective-permute-start(bf16[256,1024]{1,0:T(8,128)(2,1)S(1)} %slice.219), channel_id=1, source_target_pairs={{0,8},{8,0},{16,24},{24,16},{1,9},{9,1},{17,25},{25,17},{2,10},{10... | collective-permute-start | bytes 1572872 | tf_op jit(solution)/shard_map/ppermute | solution.py:125
  153.0 14.0 %collective-permute-start.16 = (bf16[256,1024]{1,0:T(8,128)(2,1)S(1)}, bf16[256,1024]{1,0:T(8,128)(2,1)S(1)}, u32[]{:S(2)}, u32[]{:S(2)}) collective-permute-start(bf16[256,1024]{1,0:T(8,128)(2,1)S(1)} %add_convert_fusion.21), channel_id=1, source_target_pairs={{0,16},{8,24},{16,0},{24,8},{1,17},{9,25},{17,1},{25,9},{2,18},{10... | collective-permute-start | bytes 1572872 | tf_op jit(solution)/shard_map/ppermute | solution.py:125
  158.7 15.8 %collective-permute-start.31 = (bf16[256,1024]{1,0:T(8,128)(2,1)S(1)}, bf16[256,1024]{1,0:T(8,128)(2,1)S(1)}, u32[]{:S(2)}, u32[]{:S(2)}) collective-permute-start(bf16[256,1024]{1,0:T(8,128)(2,1)S(1)} %get-tuple-element.114), channel_id=1, source_target_pairs={{0,8},{8,0},{16,24},{24,16},{1,9},{9,1},{17,25},{25,17},{2,10},{10... | collective-permute-start | bytes 1572872 | tf_op jit(solution)/shard_map/ppermute | solution.py:125
  159.5 29.7 %collective-permute-start.9 = (bf16[256,1024]{1,0:T(8,128)(2,1)S(1)}, bf16[256,1024]{1,0:T(8,128)(2,1)S(1)}, u32[]{:S(2)}, u32[]{:S(2)}) collective-permute-start(bf16[256,1024]{1,0:T(8,128)(2,1)S(1)} %get-tuple-element.108), channel_id=1, source_target_pairs={{0,8},{8,0},{16,24},{24,16},{1,9},{9,1},{17,25},{25,17},{2,10},{10... | collective-permute-start | bytes 1572872 | tf_op jit(solution)/shard_map/ppermute | solution.py:125
  162.3 27.9 %collective-permute-start.19 = (bf16[256,2048]{0,1:T(8,128)(2,1)S(1)}, bf16[256,2048]{0,1:T(8,128)(2,1)S(1)}, u32[]{:S(2)}, u32[]{:S(2)}) collective-permute-start(bf16[256,2048]{0,1:T(8,128)(2,1)S(1)} %copy-done.5), channel_id=1, source_target_pairs={{0,2},{1,3},{2,4},{3,5},{4,6},{5,7},{6,0},{7,1},{8,10},{9,11},{10,... | collective-permute-start | bytes 3145736 | tf_op jit(solution)/shard_map/ppermute | solution.py:122
  166.9 43.1 %collective-permute-start.20 = (bf16[256,2048]{0,1:T(8,128)(2,1)S(1)}, bf16[256,2048]{0,1:T(8,128)(2,1)S(1)}, u32[]{:S(2)}, u32[]{:S(2)}) collective-permute-start(bf16[256,2048]{0,1:T(8,128)(2,1)S(1)} %copy-done.5), channel_id=1, source_target_pairs={{0,6},{1,7},{2,0},{3,1},{4,2},{5,3},{6,4},{7,5},{8,14},{9,15},{10,... | collective-permute-start | bytes 3145736 | tf_op jit(solution)/shard_map/ppermute | solution.py:122
  174.6 14.4 %collective-permute-start.17 = (bf16[256,1024]{1,0:T(8,128)(2,1)S(1)}, bf16[256,1024]{1,0:T(8,128)(2,1)S(1)}, u32[]{:S(2)}, u32[]{:S(2)}) collective-permute-start(bf16[256,1024]{1,0:T(8,128)(2,1)S(1)} %add_convert_fusion.22), channel_id=1, source_target_pairs={{0,16},{8,24},{16,0},{24,8},{1,17},{9,25},{17,1},{25,9},{2,18},{10... | collective-permute-start | bytes 1572872 | tf_op jit(solution)/shard_map/ppermute | solution.py:125
  176.8 39.6 %collective-permute-start.32 = (bf16[256,1024]{1,0:T(8,128)(2,1)S(1)}, bf16[256,1024]{1,0:T(8,128)(2,1)S(1)}, u32[]{:S(2)}, u32[]{:S(2)}) collective-permute-start(bf16[256,1024]{1,0:T(8,128)(2,1)S(1)} %get-tuple-element.112), channel_id=1, source_target_pairs={{0,8},{8,0},{16,24},{24,16},{1,9},{9,1},{17,25},{25,17},{2,10},{10... | collective-permute-start | bytes 1572872 | tf_op jit(solution)/shard_map/ppermute | solution.py:125
  188.9 28.3 %collective-permute-start.24 = (bf16[256,1024]{1,0:T(8,128)(2,1)S(1)}, bf16[256,1024]{1,0:T(8,128)(2,1)S(1)}, u32[]{:S(2)}, u32[]{:S(2)}) collective-permute-start(bf16[256,1024]{1,0:T(8,128)(2,1)S(1)} %add_convert_fusion.16), channel_id=1, source_target_pairs={{0,16},{8,24},{16,0},{24,8},{1,17},{9,25},{17,1},{25,9},{2,18},{10... | collective-permute-start | bytes 1572872 | tf_op jit(solution)/shard_map/ppermute | solution.py:125
  215.5 3.5 collective-permute-start.21
  215.8 10.0 %collective-permute-start.18 = (bf16[256,1024]{1,0:T(8,128)(2,1)S(1)}, bf16[256,1024]{1,0:T(8,128)(2,1)S(1)}, u32[]{:S(2)}, u32[]{:S(2)}) collective-permute-start(bf16[256,1024]{1,0:T(8,128)(2,1)S(1)} %get-tuple-element.106), channel_id=1, source_target_pairs={{0,8},{8,0},{16,24},{24,16},{1,9},{9,1},{17,25},{25,17},{2,10},{10... | collective-permute-start | bytes 1572872 | tf_op jit(solution)/shard_map/ppermute | solution.py:125
  218.3 7.6 %collective-permute-start.33 = (bf16[256,1024]{1,0:T(8,128)(2,1)S(1)}, bf16[256,1024]{1,0:T(8,128)(2,1)S(1)}, u32[]{:S(2)}, u32[]{:S(2)}) collective-permute-start(bf16[256,1024]{1,0:T(8,128)(2,1)S(1)} %get-tuple-element.110), channel_id=1, source_target_pairs={{0,8},{8,0},{16,24},{24,16},{1,9},{9,1},{17,25},{25,17},{2,10},{10... | collective-permute-start | bytes 1572872 | tf_op jit(solution)/shard_map/ppermute | solution.py:125
  224.0 14.8 %collective-permute-start.27 = (bf16[256,1024]{1,0:T(8,128)(2,1)S(1)}, bf16[256,1024]{1,0:T(8,128)(2,1)S(1)}, u32[]{:S(2)}, u32[]{:S(2)}) collective-permute-start(bf16[256,1024]{1,0:T(8,128)(2,1)S(1)} %slice.231), channel_id=1, source_target_pairs={{0,8},{8,0},{16,24},{24,16},{1,9},{9,1},{17,25},{25,17},{2,10},{10... | collective-permute-start | bytes 1572872 | tf_op jit(solution)/shard_map/ppermute | solution.py:125
  224.6 13.9 %collective-permute-start.25 = (bf16[256,1024]{1,0:T(8,128)(2,1)S(1)}, bf16[256,1024]{1,0:T(8,128)(2,1)S(1)}, u32[]{:S(2)}, u32[]{:S(2)}) collective-permute-start(bf16[256,1024]{1,0:T(8,128)(2,1)S(1)} %add_convert_fusion.17), channel_id=1, source_target_pairs={{0,16},{8,24},{16,0},{24,8},{1,17},{9,25},{17,1},{25,9},{2,18},{10... | collective-permute-start | bytes 1572872 | tf_op jit(solution)/shard_map/ppermute | solution.py:125
  230.2 13.7 %collective-permute-start.34 = (bf16[256,1024]{1,0:T(8,128)(2,1)S(1)}, bf16[256,1024]{1,0:T(8,128)(2,1)S(1)}, u32[]{:S(2)}, u32[]{:S(2)}) collective-permute-start(bf16[256,1024]{1,0:T(8,128)(2,1)S(1)} %convolution_convert_fusion.8), channel_id=1, source_target_pairs={{0,1},{1,0},{2,3},{3,2},{4,5},{5,4},{6,7},{7,6},{8,9},{9,8},{10,11... | collective-permute-start | bytes 1572872 | tf_op jit(solution)/shard_map/ppermute | solution.py:118
  238.7 6.7 %collective-permute-start.26 = (bf16[256,1024]{1,0:T(8,128)(2,1)S(1)}, bf16[256,1024]{1,0:T(8,128)(2,1)S(1)}, u32[]{:S(2)}, u32[]{:S(2)}) collective-permute-start(bf16[256,1024]{1,0:T(8,128)(2,1)S(1)} %get-tuple-element.104), channel_id=1, source_target_pairs={{0,8},{8,0},{16,24},{24,16},{1,9},{9,1},{17,25},{25,17},{2,10},{10... | collective-permute-start | bytes 1572872 | tf_op jit(solution)/shard_map/ppermute | solution.py:125
  239.0 14.4 %collective-permute-start.28 = (bf16[256,1024]{1,0:T(8,128)(2,1)S(1)}, bf16[256,1024]{1,0:T(8,128)(2,1)S(1)}, u32[]{:S(2)}, u32[]{:S(2)}) collective-permute-start(bf16[256,1024]{1,0:T(8,128)(2,1)S(1)} %add_convert_fusion.14), channel_id=1, source_target_pairs={{0,16},{8,24},{16,0},{24,8},{1,17},{9,25},{17,1},{25,9},{2,18},{10... | collective-permute-start | bytes 1572872 | tf_op jit(solution)/shard_map/ppermute | solution.py:125
  243.9 14.6 %collective-permute-start.35 = (bf16[256,1024]{1,0:T(8,128)(2,1)S(1)}, bf16[256,1024]{1,0:T(8,128)(2,1)S(1)}, u32[]{:S(2)}, u32[]{:S(2)}) collective-permute-start(bf16[256,1024]{1,0:T(8,128)(2,1)S(1)} %convolution_convert_fusion.7), channel_id=1, source_target_pairs={{0,1},{1,0},{2,3},{3,2},{4,5},{5,4},{6,7},{7,6},{8,9},{9,8},{10,11... | collective-permute-start | bytes 1572872 | tf_op jit(solution)/shard_map/ppermute | solution.py:118
  253.6 6.2 %collective-permute-start.29 = (bf16[256,1024]{1,0:T(8,128)(2,1)S(1)}, bf16[256,1024]{1,0:T(8,128)(2,1)S(1)}, u32[]{:S(2)}, u32[]{:S(2)}) collective-permute-start(bf16[256,1024]{1,0:T(8,128)(2,1)S(1)} %get-tuple-element.102), channel_id=1, source_target_pairs={{0,8},{8,0},{16,24},{24,16},{1,9},{9,1},{17,25},{25,17},{2,10},{10... | collective-permute-start | bytes 1572872 | tf_op jit(solution)/shard_map/ppermute | solution.py:125
  253.9 27.9 %collective-permute-start.37 = (bf16[256,2048]{0,1:T(8,128)(2,1)S(1)}, bf16[256,2048]{0,1:T(8,128)(2,1)S(1)}, u32[]{:S(2)}, u32[]{:S(2)}) collective-permute-start(bf16[256,2048]{0,1:T(8,128)(2,1)S(1)} %collective-permute-done.19), channel_id=1, source_target_pairs={{0,2},{1,3},{2,4},{3,5},{4,6},{5,7},{6,0},{7,1},{8,10},{9,11},{10,... | collective-permute-start | bytes 3145736 | tf_op jit(solution)/shard_map/ppermute | solution.py:122
  258.5 26.8 %collective-permute-start.36 = (bf16[256,1024]{1,0:T(8,128)(2,1)S(1)}, bf16[256,1024]{1,0:T(8,128)(2,1)S(1)}, u32[]{:S(2)}, u32[]{:S(2)}) collective-permute-start(bf16[256,1024]{1,0:T(8,128)(2,1)S(1)} %convolution_convert_fusion.6), channel_id=1, source_target_pairs={{0,1},{1,0},{2,3},{3,2},{4,5},{5,4},{6,7},{7,6},{8,9},{9,8},{10,11... | collective-permute-start | bytes 1572872 | tf_op jit(solution)/shard_map/ppermute | solution.py:118
  285.3 13.6 %collective-permute-start.38 = (bf16[256,1024]{1,0:T(8,128)(2,1)S(1)}, bf16[256,1024]{1,0:T(8,128)(2,1)S(1)}, u32[]{:S(2)}, u32[]{:S(2)}) collective-permute-start(bf16[256,1024]{1,0:T(8,128)(2,1)S(1)} %convolution_convert_fusion.5), channel_id=1, source_target_pairs={{0,1},{1,0},{2,3},{3,2},{4,5},{5,4},{6,7},{7,6},{8,9},{9,8},{10,11... | collective-permute-start | bytes 1572872 | tf_op jit(solution)/shard_map/ppermute | solution.py:118
  300.5 4.7 collective-permute-start.39
  300.6 14.3 %collective-permute-start.41 = (bf16[2,128,1024]{2,1,0:T(8,128)(2,1)S(1)}, bf16[2,128,1024]{2,1,0:T(8,128)(2,1)S(1)}, u32[]{:S(2)}, u32[]{:S(2)}) collective-permute-start(bf16[2,128,1024]{2,1,0:T(8,128)(2,1)S(1)} %get-tuple-element.79), channel_id=1, source_target_pairs={{0,16},{8,24},{16,0},{24,8},{1,17},{9,25},{17,1},{25,9},{2,18},{10... | collective-permute-start | bytes 1572872 | tf_op jit(solution)/shard_map/ppermute | solution.py:125
  307.8 22.4 %collective-permute-start.40 = (bf16[1024,256]{1,0:T(8,128)(2,1)S(1)}, bf16[1024,256]{1,0:T(8,128)(2,1)S(1)}, u32[]{:S(2)}, u32[]{:S(2)}) collective-permute-start(bf16[1024,256]{1,0:T(8,128)(2,1)S(1)} %get-tuple-element.78), channel_id=1, source_target_pairs={{0,8},{8,0},{16,24},{24,16},{1,9},{9,1},{17,25},{25,17},{2,10},{10... | collective-permute-start | bytes 1572872 | tf_op jit(solution)/shard_map/ppermute | solution.py:125
  314.9 14.1 %collective-permute-start.42 = (bf16[2,128,1024]{2,1,0:T(8,128)(2,1)S(1)}, bf16[2,128,1024]{2,1,0:T(8,128)(2,1)S(1)}, u32[]{:S(2)}, u32[]{:S(2)}) collective-permute-start(bf16[2,128,1024]{2,1,0:T(8,128)(2,1)S(1)} %get-tuple-element.83), channel_id=1, source_target_pairs={{0,24},{8,16},{16,8},{24,0},{1,25},{9,17},{17,9},{25,1},{2,26},{10... | collective-permute-start | bytes 1572872 | tf_op jit(solution)/shard_map/ppermute | solution.py:125
  329.0 13.8 %collective-permute-start.43 = (bf16[1024,256]{1,0:T(8,128)(2,1)S(1)}, bf16[1024,256]{1,0:T(8,128)(2,1)S(1)}, u32[]{:S(2)}, u32[]{:S(2)}) collective-permute-start(bf16[1024,256]{1,0:T(8,128)(2,1)S(1)} %get-tuple-element.84), channel_id=1, source_target_pairs={{0,16},{8,24},{16,0},{24,8},{1,17},{9,25},{17,1},{25,9},{2,18},{10... | collective-permute-start | bytes 1572872 | tf_op jit(solution)/shard_map/ppermute | solution.py:125
  330.4 24.8 %collective-permute-start.45 = (bf16[1024,512]{1,0:T(8,128)(2,1)S(1)}, bf16[1024,512]{1,0:T(8,128)(2,1)S(1)}, u32[]{:S(2)}, u32[]{:S(2)}) collective-permute-start(bf16[1024,512]{1,0:T(8,128)(2,1)S(1)} %pad_maximum_fusion.6), channel_id=1, source_target_pairs={{0,1},{1,0},{2,3},{3,2},{4,5},{5,4},{6,7},{7,6},{8,9},{9,8},{10,11... | collective-permute-start | bytes 3145736 | tf_op jit(solution)/shard_map/ppermute | solution.py:118
  342.8 14.1 %collective-permute-start.44 = (bf16[1024,256]{1,0:T(8,128)(2,1)S(1)}, bf16[1024,256]{1,0:T(8,128)(2,1)S(1)}, u32[]{:S(2)}, u32[]{:S(2)}) collective-permute-start(bf16[1024,256]{1,0:T(8,128)(2,1)S(1)} %get-tuple-element.88), channel_id=1, source_target_pairs={{0,24},{8,16},{16,8},{24,0},{1,25},{9,17},{17,9},{25,1},{2,26},{10... | collective-permute-start | bytes 1572872 | tf_op jit(solution)/shard_map/ppermute | solution.py:125
  355.2 12.6 %collective-permute-start.46 = (bf16[1024,256]{1,0:T(8,128)(2,1)S(1)}, bf16[1024,256]{1,0:T(8,128)(2,1)S(1)}, u32[]{:S(2)}, u32[]{:S(2)}) collective-permute-start(bf16[1024,256]{1,0:T(8,128)(2,1)S(1)} %collective-permute-done.43), channel_id=1, source_target_pairs={{0,1},{1,0},{2,3},{3,2},{4,5},{5,4},{6,7},{7,6},{8,9},{9,8},{10,11... | collective-permute-start | bytes 1572872 | tf_op jit(solution)/shard_map/ppermute | solution.py:118
  357.7 11.8 %collective-permute-start.51 = (bf16[1024,256]{1,0:T(8,128)(2,1)S(1)}, bf16[1024,256]{1,0:T(8,128)(2,1)S(1)}, u32[]{:S(2)}, u32[]{:S(2)}) collective-permute-start(bf16[1024,256]{1,0:T(8,128)(2,1)S(1)} %convolution_convert_fusion.4), channel_id=1, source_target_pairs={{0,8},{8,0},{16,24},{24,16},{1,9},{9,1},{17,25},{25,17},{2,10},{10... | collective-permute-start | bytes 1572872 | tf_op jit(solution)/shard_map/ppermute | solution.py:125
  367.8 11.7 %collective-permute-start.47 = (bf16[1024,256]{1,0:T(8,128)(2,1)S(1)}, bf16[1024,256]{1,0:T(8,128)(2,1)S(1)}, u32[]{:S(2)}, u32[]{:S(2)}) collective-permute-start(bf16[1024,256]{1,0:T(8,128)(2,1)S(1)} %collective-permute-done.44), channel_id=1, source_target_pairs={{0,1},{1,0},{2,3},{3,2},{4,5},{5,4},{6,7},{7,6},{8,9},{9,8},{10,11... | collective-permute-start | bytes 1572872 | tf_op jit(solution)/shard_map/ppermute | solution.py:118
  370.2 12.0 %collective-permute-start.52 = (bf16[1024,256]{1,0:T(8,128)(2,1)S(1)}, bf16[1024,256]{1,0:T(8,128)(2,1)S(1)}, u32[]{:S(2)}, u32[]{:S(2)}) collective-permute-start(bf16[1024,256]{1,0:T(8,128)(2,1)S(1)} %fusion.7), channel_id=1, source_target_pairs={{0,16},{8,24},{16,0},{24,8},{1,17},{9,25},{17,1},{25,9},{2,18},{10... | collective-permute-start | bytes 1572872 | tf_op jit(solution)/shard_map/ppermute | solution.py:125
  381.7 3.6 collective-permute-start.50
  383.0 14.0 %collective-permute-start.54 = (bf16[1024,256]{1,0:T(8,128)(2,1)S(1)}, bf16[1024,256]{1,0:T(8,128)(2,1)S(1)}, u32[]{:S(2)}, u32[]{:S(2)}) collective-permute-start(bf16[1024,256]{1,0:T(8,128)(2,1)S(1)} %fusion.8), channel_id=1, source_target_pairs={{0,16},{8,24},{16,0},{24,8},{1,17},{9,25},{17,1},{25,9},{2,18},{10... | collective-permute-start | bytes 1572872 | tf_op jit(solution)/shard_map/ppermute | solution.py:125
  385.2 15.0 %collective-permute-start.49 = (bf16[2048,256]{1,0:T(8,128)(2,1)S(1)}, bf16[2048,256]{1,0:T(8,128)(2,1)S(1)}, u32[]{:S(2)}, u32[]{:S(2)}) collective-permute-start(bf16[2048,256]{1,0:T(8,128)(2,1)S(1)} %convolution_convert_fusion.1), channel_id=1, source_target_pairs={{0,8},{8,0},{16,24},{24,16},{1,9},{9,1},{17,25},{25,17},{2,10},{10... | collective-permute-start | bytes 3145736 | tf_op jit(solution)/shard_map/ppermute | solution.py:125
  397.0 24.4 %collective-permute-start.55 = (bf16[2048,256]{1,0:T(8,128)(2,1)S(1)}, bf16[2048,256]{1,0:T(8,128)(2,1)S(1)}, u32[]{:S(2)}, u32[]{:S(2)}) collective-permute-start(bf16[2048,256]{1,0:T(8,128)(2,1)S(1)} %fusion.2), channel_id=1, source_target_pairs={{0,16},{8,24},{16,0},{24,8},{1,17},{9,25},{17,1},{25,9},{2,18},{10... | collective-permute-start | bytes 3145736 | tf_op jit(solution)/shard_map/ppermute | solution.py:125
  398.0 8.9 %collective-permute-start.60 = (bf16[1024,256]{1,0:T(8,128)(2,1)S(1)}, bf16[1024,256]{1,0:T(8,128)(2,1)S(1)}, u32[]{:S(2)}, u32[]{:S(2)}) collective-permute-start(bf16[1024,256]{1,0:T(8,128)(2,1)S(1)} %add_convert_fusion.8.refs_2_), channel_id=1, source_target_pairs={{0,8},{8,0},{16,24},{24,16},{1,9},{9,1},{17,25},{25,17},{2,10},{10... | collective-permute-start | bytes 1572872 | tf_op jit(solution)/shard_map/ppermute | solution.py:125
  398.3 8.7 %collective-permute-start.61 = (bf16[1024,256]{1,0:T(8,128)(2,1)S(1)}, bf16[1024,256]{1,0:T(8,128)(2,1)S(1)}, u32[]{:S(2)}, u32[]{:S(2)}) collective-permute-start(bf16[1024,256]{1,0:T(8,128)(2,1)S(1)} %add_convert_fusion.7.refs_3_), channel_id=1, source_target_pairs={{0,8},{8,0},{16,24},{24,16},{1,9},{9,1},{17,25},{25,17},{2,10},{10... | collective-permute-start | bytes 1572872 | tf_op jit(solution)/shard_map/ppermute | solution.py:125
  400.1 23.0 %collective-permute-start.48 = (bf16[2048,256]{1,0:T(8,128)(2,1)S(1)}, bf16[2048,256]{1,0:T(8,128)(2,1)S(1)}, u32[]{:S(2)}, u32[]{:S(2)}) collective-permute-start(bf16[2048,256]{1,0:T(8,128)(2,1)S(1)} %convolution_convert_fusion.2), channel_id=1, source_target_pairs={{0,8},{8,0},{16,24},{24,16},{1,9},{9,1},{17,25},{25,17},{2,10},{10... | collective-permute-start | bytes 3145736 | tf_op jit(solution)/shard_map/ppermute | solution.py:125
  421.4 23.4 %collective-permute-start.56 = (bf16[2048,256]{1,0:T(8,128)(2,1)S(1)}, bf16[2048,256]{1,0:T(8,128)(2,1)S(1)}, u32[]{:S(2)}, u32[]{:S(2)}) collective-permute-start(bf16[2048,256]{1,0:T(8,128)(2,1)S(1)} %fusion.1), channel_id=1, source_target_pairs={{0,16},{8,24},{16,0},{24,8},{1,17},{9,25},{17,1},{25,9},{2,18},{10... | collective-permute-start | bytes 3145736 | tf_op jit(solution)/shard_map/ppermute | solution.py:125
  422.4 50.7 %collective-permute-start.62 = (bf16[2048,512]{1,0:T(8,128)(2,1)S(1)}, bf16[2048,512]{1,0:T(8,128)(2,1)S(1)}, u32[]{:S(2)}, u32[]{:S(2)}) collective-permute-start(bf16[2048,512]{1,0:T(8,128)(2,1)S(1)} %pad_maximum_fusion.3), channel_id=1, source_target_pairs={{0,2},{1,3},{2,4},{3,5},{4,6},{5,7},{6,0},{7,1},{8,10},{9,11},{10,... | collective-permute-start | bytes 6291464 | tf_op jit(solution)/shard_map/ppermute | solution.py:122
  423.0 28.7 %collective-permute-start.58 = (bf16[2048,256]{1,0:T(8,128)(2,1)S(1)}, bf16[2048,256]{1,0:T(8,128)(2,1)S(1)}, u32[]{:S(2)}, u32[]{:S(2)}) collective-permute-start(bf16[2048,256]{1,0:T(8,128)(2,1)S(1)} %add_convert_fusion.5), channel_id=1, source_target_pairs={{0,8},{8,0},{16,24},{24,16},{1,9},{9,1},{17,25},{25,17},{2,10},{10... | collective-permute-start | bytes 3145736 | tf_op jit(solution)/shard_map/ppermute | solution.py:125
  445.1 19.2 %collective-permute-start.63 = (bf16[2048,256]{1,0:T(8,128)(2,1)S(1)}, bf16[2048,256]{1,0:T(8,128)(2,1)S(1)}, u32[]{:S(2)}, u32[]{:S(2)}) collective-permute-start(bf16[2048,256]{1,0:T(8,128)(2,1)S(1)} %add_convert_fusion.4), channel_id=1, source_target_pairs={{0,8},{8,0},{16,24},{24,16},{1,9},{9,1},{17,25},{25,17},{2,10},{10... | collective-permute-start | bytes 3145736 | tf_op jit(solution)/shard_map/ppermute | solution.py:125
  450.7 25.6 %collective-permute-start.57 = (bf16[2048,256]{1,0:T(8,128)(2,1)S(1)}, bf16[2048,256]{1,0:T(8,128)(2,1)S(1)}, u32[]{:S(2)}, u32[]{:S(2)}) collective-permute-start(bf16[2048,256]{1,0:T(8,128)(2,1)S(1)} %fusion), channel_id=1, source_target_pairs={{0,16},{8,24},{16,0},{24,8},{1,17},{9,25},{17,1},{25,9},{2,18},{10... | collective-permute-start | bytes 3145736 | tf_op jit(solution)/shard_map/ppermute | solution.py:125
  458.8 59.5 %collective-permute-start.59 = (bf16[2048,512]{1,0:T(8,128)(2,1)}, bf16[2048,512]{1,0:T(8,128)(2,1)}, u32[]{:S(2)}, u32[]{:S(2)}) collective-permute-start(bf16[2048,512]{1,0:T(8,128)(2,1)} %pad_maximum_fusion.2), channel_id=1, source_target_pairs={{0,6},{1,7},{2,0},{3,1},{4,2},{5,3},{6,4},{7,5},{8,14},{9,15},{10,... | collective-permute-start | bytes 6291464 | tf_op jit(solution)/shard_map/ppermute | solution.py:122
  475.1 85.1 %collective-permute-start.64 = (bf16[2048,512]{1,0:T(8,128)(2,1)}, bf16[2048,512]{1,0:T(8,128)(2,1)}, u32[]{:S(2)}, u32[]{:S(2)}) collective-permute-start(bf16[2048,512]{1,0:T(8,128)(2,1)} %pad_maximum_fusion.4), channel_id=1, source_target_pairs={{0,2},{1,3},{2,4},{3,5},{4,6},{5,7},{6,0},{7,1},{8,10},{9,11},{10,... | collective-permute-start | bytes 6291464 | tf_op jit(solution)/shard_map/ppermute | solution.py:122
  476.6 5.6 collective-permute-start.65
  (14 other events, 196.2 us)

commit v5 on v2

--- a/solution.py
+++ b/solution.py
@@ -207,7 +207,7 @@
                 grads[1] = tie(grads[1], right)
             if (k, s) == (1, far):
                 grads[far] = tie(grads[far], last["rows"][-2])
-            g = tie(grads[s], rights[1]) if (k, s) == turns[-1] else grads[s]
+            g = tie(grads[s], rights[2]) if (k, s) == turns[-1] else grads[s]
             g_mine, g_theirs = g[:half], g[half:]
             mine, theirs = half_sum(
                 lambda: product([(g_theirs, lefts[k])], BF16, by_rows=False),
@@ -241,7 +241,7 @@
         kept, by_rows = (), [[] for _ in range(n_b)]
         for k, rot in enumerate(rots):
             if k == n_row - 1:
-                kept = tie(tuple(kept), by_rows[1][0])
+                kept = tie(tuple(kept), by_rows[1][1])
             *kept, direction = step(r ^ k, n_row, sub, rot, first_moment, second_moment, tuple(kept))
             if k:
                 direction = across_rows(direction, k)

time: 565 us -> 577 us (1.021)
  waiting for transfers between devices: 311 us -> 291 us
  Pallas kernels: 120 us -> 131 us
  local copies, waits for them, and re-layouts: 31.9 us -> 41.2 us
  matrix products: 21 us -> 27.9 us
    ppermute x9, waiting for transfers between devices: 95.5 us -> 82 us  [a_shift(): return lax.ppermute(x, 'col', perm)]
    pallas_call x4, Pallas kernels: 10.7 us -> 18.8 us  [moments_at(): pl.pallas_call(moments_kernel, grid_spec=pltpu.PrefetchScalarGridSpec(num...]
    ppermute x10, waiting for transfers between devices: 114 us -> 107 us  [b_shift(): return lax.ppermute(x, 'col', perm)]
    dot_general x18, matrix products: 21 us -> 27.9 us  [dot(): lax.dot_general(a, b, ((contract[:1], contract[1:]), ((), ())), preferred...]
    dynamic_update_slice x8, local copies, waits for them, and re-layouts: 1.38 us -> 7.63 us  [per_device(): lax.dynamic_update_slice_in_dim(rotated[k], theirs, n_at(s, 1 - core), 0)]
  transfers between devices with their start and end apart: 67 -> 67, of which waited for: 23 -> 24; matrix products, arithmetic and copies ran while one was open for 10% -> 13% of each run, Pallas kernels for 22% -> 23%
where the time goes in v5:
time: 577 us; the launch traced here: 571 us
  waiting for transfers between devices  291 us (50%)
  Pallas kernels  131 us (23%)
  starting transfers between devices  55 us (10%)
  local copies, waits for them, and re-layouts  41.2 us (7%)
  matrix products  27.9 us (5%)
  other arithmetic  22.5 us (4%)
    pallas_call x24, Pallas kernels, product(): pl.pallas_call(functools.partial(product_kernel, len(pairs)), grid=(grid,...  112 us
    ppermute x10, waiting for transfers between devices, b_shift(): return lax.ppermute(x, 'col', perm)  107 us
    ppermute x48, waiting for transfers between devices, row_xor(): return lax.ppermute(x, 'row', [(r, r ^ k) for r in range(n_row)])  102 us
    ppermute x9, waiting for transfers between devices, a_shift(): return lax.ppermute(x, 'col', perm)  82 us
    dot_general x18, matrix products, dot(): lax.dot_general(a, b, ((contract[:1], contract[1:]), ((), ())), preferred...  27.9 us
    ppermute x48, starting transfers between devices, row_xor(): return lax.ppermute(x, 'row', [(r, r ^ k) for r in range(n_row)])  24.1 us
    pallas_call x4, Pallas kernels, moments_at(): pl.pallas_call(moments_kernel, grid_spec=pltpu.PrefetchScalarGridSpec(num...  18.8 us
    ppermute x10, starting transfers between devices, b_shift(): return lax.ppermute(x, 'col', perm)  16.6 us
  transfers between devices with their start and end apart: 67, of which 24 were waited for; matrix products, arithmetic and copies ran while one was open for 13% of the time, Pallas kernels for 23%

profile of v5, /device:TPU:0, one launch (start us, length us, event | category | flops | bytes accessed | tf_op | source)
XLA Modules:
  0.0 571.0 jit_solution(16123939330162224304)
XLA Ops:
  5.1 2.9 collective-permute-start.2
  9.6 2.2 collective-permute-start.1
  18.5 4.0 shard_map.76
  27.8 2.3 constant_dynamic-slice_fusion
  30.1 68.9 %collective-permute-done.2.refs_1_ = bf16[2048,1024]{1,0:T(8,128)(2,1)} collective-permute-done((bf16[2048,1024]{1,0:T(8,128)(2,1)}, bf16[2048,1024]{1,0:T(8,128)(2,1)}, u32[]{:S(2)}, u32[]{:S(2)}) %collective-permute-start.2) | collective-permute-done | bytes 4194336 | tf_op jit(solution)/shard_map/ppermute | solution.py:118
  100.7 3.9 shard_map.77
  107.8 3.9 shard_map.84
  116.6 4.0 shard_map.82
  120.7 3.9 shard_map.85
  127.8 3.9 shard_map.80
  132.0 4.8 shard_map.78
  137.1 3.9 shard_map.83
  143.3 6.0 %shard_map.81 = bf16[256,1024]{1,0:T(8,128)(2,1)} custom-call(bf16[256,2048]{1,0:T(8,128)(2,1)S(1)} %get-tuple-element.138.refs_0_, bf16[2048,1024]{1,0:T(8,128)(2,1)} %collective-permute-done.2.refs_1_, bf16[256,1024]{1,0:T(8,128)(2,1)S(1)} %collective-permute-done.11.refs_2_), custom_call_target="tpu_custom_call" | custom-call | flops 134217728 | tf_op jit(solution)/shard_map/pallas_call | solution.py:45
  149.3 5.9 %collective-permute-done.15 = bf16[256,1024]{1,0:T(8,128)(2,1)S(1)} collective-permute-done((bf16[256,1024]{1,0:T(8,128)(2,1)S(1)}, bf16[256,1024]{1,0:T(8,128)(2,1)S(1)}, u32[]{:S(2)}, u32[]{:S(2)}) %collective-permute-start.15) | collective-permute-done | bytes 524320 | tf_op jit(solution)/shard_map/ppermute | solution.py:125
  158.1 4.8 shard_map.79
  162.9 1.9 constant_dynamic-update-slice_fusion.14
  165.8 3.7 collective-permute-done.16
  171.8 4.0 shard_map.88
  178.0 5.6 shard_map.86
  184.0 1.8 collective-permute-start.26
  186.6 2.4 constant_dynamic-update-slice_fusion.11
  190.9 3.9 shard_map.89
  196.4 1.9 constant_dynamic-update-slice_fusion.22
  198.3 4.1 shard_map.87
  202.4 2.2 constant_dynamic-update-slice_fusion.21
  205.9 5.7 collective-permute-done.26
  213.6 4.1 shard_map.90
  220.7 2.2 convolution_convert_fusion.8
  224.3 7.8 %collective-permute-done.23 = bf16[256,1024]{1,0:T(8,128)(2,1)S(1)} collective-permute-done((bf16[256,1024]{1,0:T(8,128)(2,1)S(1)}, bf16[256,1024]{1,0:T(8,128)(2,1)S(1)}, u32[]{:S(2)}, u32[]{:S(2)}) %collective-permute-start.23) | collective-permute-done | bytes 524320 | tf_op jit(solution)/shard_map/ppermute | solution.py:125
  235.2 3.9 shard_map.91
  240.7 2.5 convolution_convert_fusion.7
  245.8 7.4 %collective-permute-done.28 = bf16[256,1024]{1,0:T(8,128)(2,1)S(1)} collective-permute-done((bf16[256,1024]{1,0:T(8,128)(2,1)S(1)}, bf16[256,1024]{1,0:T(8,128)(2,1)S(1)}, u32[]{:S(2)}, u32[]{:S(2)}) %collective-permute-start.28) | collective-permute-done | bytes 524320 | tf_op jit(solution)/shard_map/ppermute | solution.py:125
  254.2 4.7 collective-permute-done.36
  261.8 2.3 fusion.3
  264.5 2.5 fusion.4
  267.0 2.5 convolution_convert_fusion.5
  269.5 4.3 collective-permute-done.37
  276.6 9.8 %collective-permute-done.38 = bf16[256,1024]{1,0:T(8,128)(2,1)S(1)} collective-permute-done((bf16[256,1024]{1,0:T(8,128)(2,1)S(1)}, bf16[256,1024]{1,0:T(8,128)(2,1)S(1)}, u32[]{:S(2)}, u32[]{:S(2)}) %collective-permute-start.38) | collective-permute-done | bytes 524320 | tf_op jit(solution)/shard_map/ppermute | solution.py:118
  286.4 2.6 fusion.6
  293.0 2.6 shard_map.92
  297.1 2.6 shard_map.93
  301.1 15.5 %collective-permute-done.41.rot_ref = bf16[2,128,1024]{2,1,0:T(8,128)(2,1)S(1)} collective-permute-done((bf16[2,128,1024]{2,1,0:T(8,128)(2,1)S(1)}, bf16[2,128,1024]{2,1,0:T(8,128)(2,1)S(1)}, u32[]{:S(2)}, u32[]{:S(2)}) %collective-permute-start.41) | collective-permute-done | bytes 524320 | tf_op jit(solution)/shard_map/ppermute | solution.py:125
  316.6 2.6 shard_map.94
  323.6 10.5 %collective-permute-done.45 = bf16[1024,256]{1,0:T(8,128)(2,1)S(1)} collective-permute-done((bf16[1024,256]{1,0:T(8,128)(2,1)S(1)}, bf16[1024,256]{1,0:T(8,128)(2,1)S(1)}, u32[]{:S(2)}, u32[]{:S(2)}) %collective-permute-start.45) | collective-permute-done | bytes 524320 | tf_op jit(solution)/shard_map/ppermute | solution.py:118
  334.1 11.0 %shard_map.95 = (f32[1024,1024]{1,0:T(8,128)}, f32[1024,1024]{1,0:T(8,128)}, bf16[1024,256]{1,0:T(8,128)(2,1)S(1)}) custom-call(s32[1]{0:T(128)} %bitcast.23.peer_ref, bf16[2,128,1024]{2,1,0:T(8,128)(2,1)S(1)} %collective-permute-done.42.rot_ref, f32[1024,1024]{1,0:T(8,128)S(1)} %copy-done, ...), custom_call_target="tpu_custom_call", output_to_operand_aliasing={{0}: (4, {}), {1}: (5, {})} | custom-call | flops 2621440 | bytes 5242880 | tf_op jit(solution)/shard_map/pallas_call | solution.py:77
  348.1 10.3 %collective-permute-done.46 = bf16[1024,256]{1,0:T(8,128)(2,1)S(1)} collective-permute-done((bf16[1024,256]{1,0:T(8,128)(2,1)S(1)}, bf16[1024,256]{1,0:T(8,128)(2,1)S(1)}, u32[]{:S(2)}, u32[]{:S(2)}) %collective-permute-start.46) | collective-permute-done | bytes 524320 | tf_op jit(solution)/shard_map/ppermute | solution.py:125
  363.5 11.3 %collective-permute-done.48 = bf16[1024,256]{1,0:T(8,128)(2,1)S(1)} collective-permute-done((bf16[1024,256]{1,0:T(8,128)(2,1)S(1)}, bf16[1024,256]{1,0:T(8,128)(2,1)S(1)}, u32[]{:S(2)}, u32[]{:S(2)}) %collective-permute-start.48) | collective-permute-done | bytes 524320 | tf_op jit(solution)/shard_map/ppermute | solution.py:118
  378.1 11.9 %collective-permute-done.53 = bf16[1024,256]{1,0:T(8,128)(2,1)S(1)} collective-permute-done((bf16[1024,256]{1,0:T(8,128)(2,1)S(1)}, bf16[1024,256]{1,0:T(8,128)(2,1)S(1)}, u32[]{:S(2)}, u32[]{:S(2)}) %collective-permute-start.53) | collective-permute-done | bytes 524320 | tf_op jit(solution)/shard_map/ppermute | solution.py:125
  394.4 9.9 %collective-permute-done.55 = bf16[1024,256]{1,0:T(8,128)(2,1)S(1)} collective-permute-done((bf16[1024,256]{1,0:T(8,128)(2,1)S(1)}, bf16[1024,256]{1,0:T(8,128)(2,1)S(1)}, u32[]{:S(2)}, u32[]{:S(2)}) %collective-permute-start.55) | collective-permute-done | bytes 524320 | tf_op jit(solution)/shard_map/ppermute | solution.py:125
  408.8 5.4 shard_map.100
  414.2 5.4 shard_map.101
  419.7 8.5 %collective-permute-done.56 = bf16[2048,256]{1,0:T(8,128)(2,1)S(1)} collective-permute-done((bf16[2048,256]{1,0:T(8,128)(2,1)S(1)}, bf16[2048,256]{1,0:T(8,128)(2,1)S(1)}, u32[]{:S(2)}, u32[]{:S(2)}) %collective-permute-start.56) | collective-permute-done | bytes 1048608 | tf_op jit(solution)/shard_map/ppermute | solution.py:125
  431.1 19.9 %collective-permute-done.57 = bf16[2048,256]{1,0:T(8,128)(2,1)S(1)} collective-permute-done((bf16[2048,256]{1,0:T(8,128)(2,1)S(1)}, bf16[2048,256]{1,0:T(8,128)(2,1)S(1)}, u32[]{:S(2)}, u32[]{:S(2)}) %collective-permute-start.57) | collective-permute-done | bytes 1048608 | tf_op jit(solution)/shard_map/ppermute | solution.py:125
  451.5 5.5 shard_map.97
  458.0 5.4 shard_map.98
  464.9 3.5 collective-permute-start.60
  468.6 5.5 shard_map.99
  474.1 5.4 shard_map.102
  483.0 5.4 shard_map.96
  489.7 5.4 shard_map.103
  495.1 29.7 %collective-permute-done.60 = bf16[2048,512]{1,0:T(8,128)(2,1)S(1)} collective-permute-done((bf16[2048,512]{1,0:T(8,128)(2,1)}, bf16[2048,512]{1,0:T(8,128)(2,1)S(1)}, u32[]{:S(2)}, u32[]{:S(2)}) %collective-permute-start.60) | collective-permute-done | bytes 2097184 | tf_op jit(solution)/shard_map/ppermute | solution.py:122
  524.8 41.6 %collective-permute-done.65 = bf16[2048,512]{1,0:T(8,128)(2,1)} collective-permute-done((bf16[2048,512]{1,0:T(8,128)(2,1)}, bf16[2048,512]{1,0:T(8,128)(2,1)}, u32[]{:S(2)}, u32[]{:S(2)}) %collective-permute-start.65) | collective-permute-done | bytes 2097184 | tf_op jit(solution)/shard_map/ppermute | solution.py:122
  566.4 2.4 add_convert_fusion.1
  568.8 1.9 maximum_select_fusion
  (242 shorter events, 110.8 us)
Async XLA Ops:
  5.1 93.8 %collective-permute-start.2 = (bf16[2048,1024]{1,0:T(8,128)(2,1)}, bf16[2048,1024]{1,0:T(8,128)(2,1)}, u32[]{:S(2)}, u32[]{:S(2)}) collective-permute-start(bf16[2048,1024]{1,0:T(8,128)(2,1)} %refs_0_.7), channel_id=1, source_target_pairs={{0,1},{1,0},{2,3},{3,2},{4,5},{5,4},{6,7},{7,6},{8,9},{9,8},{10,11... | collective-permute-start | bytes 12582920 | tf_op jit(solution)/shard_map/ppermute | solution.py:118
  8.1 98.2 %collective-permute-start = (bf16[512,2048]{1,0:T(8,128)(2,1)}, bf16[512,2048]{1,0:T(8,128)(2,1)}, u32[]{:S(2)}, u32[]{:S(2)}) collective-permute-start(bf16[512,2048]{1,0:T(8,128)(2,1)} %pad_maximum_fusion.1), channel_id=1, source_target_pairs={{0,2},{1,3},{2,4},{3,5},{4,6},{5,7},{6,0},{7,1},{8,10},{9,11},{10,... | collective-permute-start | bytes 6291464 | tf_op jit(solution)/shard_map/ppermute | solution.py:122
  9.6 98.2 %collective-permute-start.1 = (bf16[512,2048]{1,0:T(8,128)(2,1)}, bf16[512,2048]{1,0:T(8,128)(2,1)}, u32[]{:S(2)}, u32[]{:S(2)}) collective-permute-start(bf16[512,2048]{1,0:T(8,128)(2,1)} %pad_maximum_fusion.1), channel_id=1, source_target_pairs={{0,6},{1,7},{2,0},{3,1},{4,2},{5,3},{6,4},{7,5},{8,14},{9,15},{10,... | collective-permute-start | bytes 6291464 | tf_op jit(solution)/shard_map/ppermute | solution.py:122
  12.1 11.1 %collective-permute-start.4 = (bf16[128,1024]{0,1:T(8,128)(2,1)S(1)}, bf16[128,1024]{0,1:T(8,128)(2,1)}, u32[]{:S(2)}, u32[]{:S(2)}) collective-permute-start(bf16[128,1024]{0,1:T(8,128)(2,1)S(1)} %get-tuple-element.162), channel_id=1, source_target_pairs={{0,16},{8,24},{16,0},{24,8},{1,17},{9,25},{17,1},{25,9},{2,18},{10... | collective-permute-start | bytes 786440 | tf_op jit(solution)/shard_map/ppermute | solution.py:125
  15.4 10.7 %collective-permute-start.5 = (bf16[128,1024]{0,1:T(8,128)(2,1)S(1)}, bf16[128,1024]{0,1:T(8,128)(2,1)}, u32[]{:S(2)}, u32[]{:S(2)}) collective-permute-start(bf16[128,1024]{0,1:T(8,128)(2,1)S(1)} %get-tuple-element.161), channel_id=1, source_target_pairs={{0,24},{8,16},{16,8},{24,0},{1,25},{9,17},{17,9},{25,1},{2,26},{10... | collective-permute-start | bytes 786440 | tf_op jit(solution)/shard_map/ppermute | solution.py:125
  23.2 77.5 %collective-permute-start.7 = (bf16[256,1024]{1,0:T(8,128)(2,1)S(1)}, bf16[256,1024]{1,0:T(8,128)(2,1)S(1)}, u32[]{:S(2)}, u32[]{:S(2)}) collective-permute-start(bf16[256,1024]{1,0:T(8,128)(2,1)S(1)} %shard_map.76), channel_id=1, source_target_pairs={{0,8},{8,0},{16,24},{24,16},{1,9},{9,1},{17,25},{25,17},{2,10},{10... | collective-permute-start | bytes 1572872 | tf_op jit(solution)/shard_map/ppermute | solution.py:125
  98.9 13.4 %collective-permute-start.6 = (bf16[128,2048]{0,1:T(8,128)(2,1)}, bf16[128,2048]{0,1:T(8,128)(2,1)}, u32[]{:S(2)}, u32[]{:S(2)}) collective-permute-start(bf16[128,2048]{0,1:T(8,128)(2,1)} %bitcast.9), channel_id=1, source_target_pairs={{0,1},{1,0},{2,3},{3,2},{4,5},{5,4},{6,7},{7,6},{8,9},{9,8},{10,11... | collective-permute-start | bytes 1572872 | tf_op jit(solution)/shard_map/ppermute | solution.py:118
  104.6 20.0 %collective-permute-start.8 = (bf16[256,1024]{1,0:T(8,128)(2,1)S(1)}, bf16[256,1024]{1,0:T(8,128)(2,1)S(1)}, u32[]{:S(2)}, u32[]{:S(2)}) collective-permute-start(bf16[256,1024]{1,0:T(8,128)(2,1)S(1)} %shard_map.77), channel_id=1, source_target_pairs={{0,16},{8,24},{16,0},{24,8},{1,17},{9,25},{17,1},{25,9},{2,18},{10... | collective-permute-start | bytes 1572872 | tf_op jit(solution)/shard_map/ppermute | solution.py:125
  106.2 63.9 %collective-permute-start.20 = (bf16[512,2048]{1,0:T(8,128)(2,1)}, bf16[512,2048]{1,0:T(8,128)(2,1)}, u32[]{:S(2)}, u32[]{:S(2)}) collective-permute-start(bf16[512,2048]{1,0:T(8,128)(2,1)} %collective-permute-done), channel_id=1, source_target_pairs={{0,2},{1,3},{2,4},{3,5},{4,6},{5,7},{6,0},{7,1},{8,10},{9,11},{10,... | collective-permute-start | bytes 6291464 | tf_op jit(solution)/shard_map/ppermute | solution.py:122
  111.7 8.9 %collective-permute-start.13 = (bf16[256,1024]{1,0:T(8,128)(2,1)S(1)}, bf16[256,1024]{1,0:T(8,128)(2,1)S(1)}, u32[]{:S(2)}, u32[]{:S(2)}) collective-permute-start(bf16[256,1024]{1,0:T(8,128)(2,1)S(1)} %shard_map.84), channel_id=1, source_target_pairs={{0,8},{8,0},{16,24},{24,16},{1,9},{9,1},{17,25},{25,17},{2,10},{10... | collective-permute-start | bytes 1572872 | tf_op jit(solution)/shard_map/ppermute | solution.py:125
  120.6 16.6 %collective-permute-start.12 = (bf16[256,1024]{1,0:T(8,128)(2,1)S(1)}, bf16[256,1024]{1,0:T(8,128)(2,1)S(1)}, u32[]{:S(2)}, u32[]{:S(2)}) collective-permute-start(bf16[256,1024]{1,0:T(8,128)(2,1)S(1)} %shard_map.82), channel_id=1, source_target_pairs={{0,8},{8,0},{16,24},{24,16},{1,9},{9,1},{17,25},{25,17},{2,10},{10... | collective-permute-start | bytes 1572872 | tf_op jit(solution)/shard_map/ppermute | solution.py:125
  124.6 16.4 %collective-permute-start.14 = (bf16[256,1024]{1,0:T(8,128)(2,1)S(1)}, bf16[256,1024]{1,0:T(8,128)(2,1)S(1)}, u32[]{:S(2)}, u32[]{:S(2)}) collective-permute-start(bf16[256,1024]{1,0:T(8,128)(2,1)S(1)} %shard_map.85), channel_id=1, source_target_pairs={{0,16},{8,24},{16,0},{24,8},{1,17},{9,25},{17,1},{25,9},{2,18},{10... | collective-permute-start | bytes 1572872 | tf_op jit(solution)/shard_map/ppermute | solution.py:125
  131.8 11.6 %collective-permute-start.11 = (bf16[256,1024]{1,0:T(8,128)(2,1)S(1)}, bf16[256,1024]{1,0:T(8,128)(2,1)S(1)}, u32[]{:S(2)}, u32[]{:S(2)}) collective-permute-start(bf16[256,1024]{1,0:T(8,128)(2,1)S(1)} %shard_map.80), channel_id=1, source_target_pairs={{0,8},{8,0},{16,24},{24,16},{1,9},{9,1},{17,25},{25,17},{2,10},{10... | collective-permute-start | bytes 1572872 | tf_op jit(solution)/shard_map/ppermute | solution.py:125
  136.8 21.3 %collective-permute-start.10 = (bf16[256,1024]{1,0:T(8,128)(2,1)}, bf16[256,1024]{1,0:T(8,128)(2,1)}, u32[]{:S(2)}, u32[]{:S(2)}) collective-permute-start(bf16[256,1024]{1,0:T(8,128)(2,1)} %shard_map.78), channel_id=1, source_target_pairs={{0,8},{8,0},{16,24},{24,16},{1,9},{9,1},{17,25},{25,17},{2,10},{10... | collective-permute-start | bytes 1572872 | tf_op jit(solution)/shard_map/ppermute | solution.py:125
  141.1 14.1 %collective-permute-start.15 = (bf16[256,1024]{1,0:T(8,128)(2,1)S(1)}, bf16[256,1024]{1,0:T(8,128)(2,1)S(1)}, u32[]{:S(2)}, u32[]{:S(2)}) collective-permute-start(bf16[256,1024]{1,0:T(8,128)(2,1)S(1)} %shard_map.83), channel_id=1, source_target_pairs={{0,16},{8,24},{16,0},{24,8},{1,17},{9,25},{17,1},{25,9},{2,18},{10... | collective-permute-start | bytes 1572872 | tf_op jit(solution)/shard_map/ppermute | solution.py:125
  143.3 19.5 %collective-permute-start.30 = (bf16[256,1024]{1,0:T(8,128)(2,1)}, bf16[256,1024]{1,0:T(8,128)(2,1)}, u32[]{:S(2)}, u32[]{:S(2)}) collective-permute-start(bf16[256,1024]{1,0:T(8,128)(2,1)} %get-tuple-element.124), channel_id=1, source_target_pairs={{0,8},{8,0},{16,24},{24,16},{1,9},{9,1},{17,25},{25,17},{2,10},{10... | collective-permute-start | bytes 1572872 | tf_op jit(solution)/shard_map/ppermute | solution.py:125
  156.0 13.5 %collective-permute-start.16 = (bf16[256,1024]{1,0:T(8,128)(2,1)}, bf16[256,1024]{1,0:T(8,128)(2,1)}, u32[]{:S(2)}, u32[]{:S(2)}) collective-permute-start(bf16[256,1024]{1,0:T(8,128)(2,1)} %shard_map.81), channel_id=1, source_target_pairs={{0,16},{8,24},{16,0},{24,8},{1,17},{9,25},{17,1},{25,9},{2,18},{10... | collective-permute-start | bytes 1572872 | tf_op jit(solution)/shard_map/ppermute | solution.py:125
  156.6 27.0 %collective-permute-start.25 = (bf16[256,2048]{0,1:T(8,128)(2,1)}, bf16[256,2048]{0,1:T(8,128)(2,1)}, u32[]{:S(2)}, u32[]{:S(2)}) collective-permute-start(bf16[256,2048]{0,1:T(8,128)(2,1)} %pad_maximum_fusion.5), channel_id=1, source_target_pairs={{0,2},{1,3},{2,4},{3,5},{4,6},{5,7},{6,0},{7,1},{8,10},{9,11},{10,... | collective-permute-start | bytes 3145736 | tf_op jit(solution)/shard_map/ppermute | solution.py:122
  165.8 18.2 %collective-permute-start.31 = (bf16[256,1024]{1,0:T(8,128)(2,1)S(1)}, bf16[256,1024]{1,0:T(8,128)(2,1)S(1)}, u32[]{:S(2)}, u32[]{:S(2)}) collective-permute-start(bf16[256,1024]{1,0:T(8,128)(2,1)S(1)} %get-tuple-element.122), channel_id=1, source_target_pairs={{0,8},{8,0},{16,24},{24,16},{1,9},{9,1},{17,25},{25,17},{2,10},{10... | collective-permute-start | bytes 1572872 | tf_op jit(solution)/shard_map/ppermute | solution.py:125
  169.5 25.3 %collective-permute-start.17 = (bf16[256,1024]{1,0:T(8,128)(2,1)}, bf16[256,1024]{1,0:T(8,128)(2,1)}, u32[]{:S(2)}, u32[]{:S(2)}) collective-permute-start(bf16[256,1024]{1,0:T(8,128)(2,1)} %shard_map.79), channel_id=1, source_target_pairs={{0,16},{8,24},{16,0},{24,8},{1,17},{9,25},{17,1},{25,9},{2,18},{10... | collective-permute-start | bytes 1572872 | tf_op jit(solution)/shard_map/ppermute | solution.py:125
  175.8 13.2 %collective-permute-start.21 = (bf16[256,1024]{1,0:T(8,128)(2,1)S(1)}, bf16[256,1024]{1,0:T(8,128)(2,1)S(1)}, u32[]{:S(2)}, u32[]{:S(2)}) collective-permute-start(bf16[256,1024]{1,0:T(8,128)(2,1)S(1)} %shard_map.88), channel_id=1, source_target_pairs={{0,8},{8,0},{16,24},{24,16},{1,9},{9,1},{17,25},{25,17},{2,10},{10... | collective-permute-start | bytes 1572872 | tf_op jit(solution)/shard_map/ppermute | solution.py:125
  177.5 18.9 %collective-permute-start.9 = (bf16[256,1024]{1,0:T(8,128)(2,1)}, bf16[256,1024]{1,0:T(8,128)(2,1)}, u32[]{:S(2)}, u32[]{:S(2)}) collective-permute-start(bf16[256,1024]{1,0:T(8,128)(2,1)} %get-tuple-element.116), channel_id=1, source_target_pairs={{0,8},{8,0},{16,24},{24,16},{1,9},{9,1},{17,25},{25,17},{2,10},{10... | collective-permute-start | bytes 1572872 | tf_op jit(solution)/shard_map/ppermute | solution.py:125
  183.6 14.7 %collective-permute-start.19 = (bf16[256,1024]{1,0:T(8,128)(2,1)}, bf16[256,1024]{1,0:T(8,128)(2,1)S(1)}, u32[]{:S(2)}, u32[]{:S(2)}) collective-permute-start(bf16[256,1024]{1,0:T(8,128)(2,1)} %shard_map.86), channel_id=1, source_target_pairs={{0,8},{8,0},{16,24},{24,16},{1,9},{9,1},{17,25},{25,17},{2,10},{10... | collective-permute-start | bytes 1572872 | tf_op jit(solution)/shard_map/ppermute | solution.py:125
  184.0 27.6 %collective-permute-start.26 = (bf16[256,2048]{0,1:T(8,128)(2,1)}, bf16[256,2048]{0,1:T(8,128)(2,1)}, u32[]{:S(2)}, u32[]{:S(2)}) collective-permute-start(bf16[256,2048]{0,1:T(8,128)(2,1)} %collective-permute-done.25), channel_id=1, source_target_pairs={{0,2},{1,3},{2,4},{3,5},{4,6},{5,7},{6,0},{7,1},{8,10},{9,11},{10,... | collective-permute-start | bytes 3145736 | tf_op jit(solution)/shard_map/ppermute | solution.py:122
  189.9 15.0 %collective-permute-start.32 = (bf16[256,1024]{1,0:T(8,128)(2,1)}, bf16[256,1024]{1,0:T(8,128)(2,1)}, u32[]{:S(2)}, u32[]{:S(2)}) collective-permute-start(bf16[256,1024]{1,0:T(8,128)(2,1)} %get-tuple-element.120), channel_id=1, source_target_pairs={{0,8},{8,0},{16,24},{24,16},{1,9},{9,1},{17,25},{25,17},{2,10},{10... | collective-permute-start | bytes 1572872 | tf_op jit(solution)/shard_map/ppermute | solution.py:125
  194.9 16.7 %collective-permute-start.22 = (bf16[256,1024]{1,0:T(8,128)(2,1)S(1)}, bf16[256,1024]{1,0:T(8,128)(2,1)S(1)}, u32[]{:S(2)}, u32[]{:S(2)}) collective-permute-start(bf16[256,1024]{1,0:T(8,128)(2,1)S(1)} %shard_map.89), channel_id=1, source_target_pairs={{0,16},{8,24},{16,0},{24,8},{1,17},{9,25},{17,1},{25,9},{2,18},{10... | collective-permute-start | bytes 1572872 | tf_op jit(solution)/shard_map/ppermute | solution.py:125
  204.6 15.2 %collective-permute-start.18 = (bf16[256,1024]{1,0:T(8,128)(2,1)S(1)}, bf16[256,1024]{1,0:T(8,128)(2,1)S(1)}, u32[]{:S(2)}, u32[]{:S(2)}) collective-permute-start(bf16[256,1024]{1,0:T(8,128)(2,1)S(1)} %get-tuple-element.114), channel_id=1, source_target_pairs={{0,8},{8,0},{16,24},{24,16},{1,9},{9,1},{17,25},{25,17},{2,10},{10... | collective-permute-start | bytes 1572872 | tf_op jit(solution)/shard_map/ppermute | solution.py:125
  211.8 8.8 %collective-permute-start.33 = (bf16[256,1024]{1,0:T(8,128)(2,1)S(1)}, bf16[256,1024]{1,0:T(8,128)(2,1)S(1)}, u32[]{:S(2)}, u32[]{:S(2)}) collective-permute-start(bf16[256,1024]{1,0:T(8,128)(2,1)S(1)} %get-tuple-element.118), channel_id=1, source_target_pairs={{0,8},{8,0},{16,24},{24,16},{1,9},{9,1},{17,25},{25,17},{2,10},{10... | collective-permute-start | bytes 1572872 | tf_op jit(solution)/shard_map/ppermute | solution.py:125
  217.7 17.5 %collective-permute-start.27 = (bf16[256,1024]{1,0:T(8,128)(2,1)S(1)}, bf16[256,1024]{1,0:T(8,128)(2,1)S(1)}, u32[]{:S(2)}, u32[]{:S(2)}) collective-permute-start(bf16[256,1024]{1,0:T(8,128)(2,1)S(1)} %shard_map.90), channel_id=1, source_target_pairs={{0,8},{8,0},{16,24},{24,16},{1,9},{9,1},{17,25},{25,17},{2,10},{10... | collective-permute-start | bytes 1572872 | tf_op jit(solution)/shard_map/ppermute | solution.py:125
  218.2 13.9 %collective-permute-start.23 = (bf16[256,1024]{1,0:T(8,128)(2,1)S(1)}, bf16[256,1024]{1,0:T(8,128)(2,1)S(1)}, u32[]{:S(2)}, u32[]{:S(2)}) collective-permute-start(bf16[256,1024]{1,0:T(8,128)(2,1)S(1)} %shard_map.87), channel_id=1, source_target_pairs={{0,16},{8,24},{16,0},{24,8},{1,17},{9,25},{17,1},{25,9},{2,18},{10... | collective-permute-start | bytes 1572872 | tf_op jit(solution)/shard_map/ppermute | solution.py:125
  222.8 20.4 %collective-permute-start.34 = (bf16[256,1024]{1,0:T(8,128)(2,1)}, bf16[256,1024]{1,0:T(8,128)(2,1)}, u32[]{:S(2)}, u32[]{:S(2)}) collective-permute-start(bf16[256,1024]{1,0:T(8,128)(2,1)} %convolution_convert_fusion.8), channel_id=1, source_target_pairs={{0,1},{1,0},{2,3},{3,2},{4,5},{5,4},{6,7},{7,6},{8,9},{9,8},{10,11... | collective-permute-start | bytes 1572872 | tf_op jit(solution)/shard_map/ppermute | solution.py:118
  233.4 11.4 %collective-permute-start.24 = (bf16[256,1024]{1,0:T(8,128)(2,1)}, bf16[256,1024]{1,0:T(8,128)(2,1)}, u32[]{:S(2)}, u32[]{:S(2)}) collective-permute-start(bf16[256,1024]{1,0:T(8,128)(2,1)} %get-tuple-element.112), channel_id=1, source_target_pairs={{0,8},{8,0},{16,24},{24,16},{1,9},{9,1},{17,25},{25,17},{2,10},{10... | collective-permute-start | bytes 1572872 | tf_op jit(solution)/shard_map/ppermute | solution.py:125
  233.4 25.6 %collective-permute-start.36 = (bf16[256,2048]{0,1:T(8,128)(2,1)S(1)}, bf16[256,2048]{0,1:T(8,128)(2,1)S(1)}, u32[]{:S(2)}, u32[]{:S(2)}) collective-permute-start(bf16[256,2048]{0,1:T(8,128)(2,1)S(1)} %copy-done.14), channel_id=1, source_target_pairs={{0,6},{1,7},{2,0},{3,1},{4,2},{5,3},{6,4},{7,5},{8,14},{9,15},{10,... | collective-permute-start | bytes 3145736 | tf_op jit(solution)/shard_map/ppermute | solution.py:122
  239.1 14.1 %collective-permute-start.28 = (bf16[256,1024]{1,0:T(8,128)(2,1)S(1)}, bf16[256,1024]{1,0:T(8,128)(2,1)S(1)}, u32[]{:S(2)}, u32[]{:S(2)}) collective-permute-start(bf16[256,1024]{1,0:T(8,128)(2,1)S(1)} %shard_map.91), channel_id=1, source_target_pairs={{0,16},{8,24},{16,0},{24,8},{1,17},{9,25},{17,1},{25,9},{2,18},{10... | collective-permute-start | bytes 1572872 | tf_op jit(solution)/shard_map/ppermute | solution.py:125
  243.2 17.0 %collective-permute-start.35 = (bf16[256,1024]{1,0:T(8,128)(2,1)S(1)}, bf16[256,1024]{1,0:T(8,128)(2,1)S(1)}, u32[]{:S(2)}, u32[]{:S(2)}) collective-permute-start(bf16[256,1024]{1,0:T(8,128)(2,1)S(1)} %convolution_convert_fusion.7), channel_id=1, source_target_pairs={{0,1},{1,0},{2,3},{3,2},{4,5},{5,4},{6,7},{7,6},{8,9},{9,8},{10,11... | collective-permute-start | bytes 1572872 | tf_op jit(solution)/shard_map/ppermute | solution.py:118
  253.4 8.3 %collective-permute-start.29 = (bf16[256,1024]{1,0:T(8,128)(2,1)S(1)}, bf16[256,1024]{1,0:T(8,128)(2,1)S(1)}, u32[]{:S(2)}, u32[]{:S(2)}) collective-permute-start(bf16[256,1024]{1,0:T(8,128)(2,1)S(1)} %get-tuple-element.110), channel_id=1, source_target_pairs={{0,8},{8,0},{16,24},{24,16},{1,9},{9,1},{17,25},{25,17},{2,10},{10... | collective-permute-start | bytes 1572872 | tf_op jit(solution)/shard_map/ppermute | solution.py:125
  260.2 13.6 %collective-permute-start.37 = (bf16[256,1024]{1,0:T(8,128)(2,1)S(1)}, bf16[256,1024]{1,0:T(8,128)(2,1)S(1)}, u32[]{:S(2)}, u32[]{:S(2)}) collective-permute-start(bf16[256,1024]{1,0:T(8,128)(2,1)S(1)} %convolution_convert_fusion.6), channel_id=1, source_target_pairs={{0,1},{1,0},{2,3},{3,2},{4,5},{5,4},{6,7},{7,6},{8,9},{9,8},{10,11... | collective-permute-start | bytes 1572872 | tf_op jit(solution)/shard_map/ppermute | solution.py:118
  273.8 12.6 %collective-permute-start.38 = (bf16[256,1024]{1,0:T(8,128)(2,1)S(1)}, bf16[256,1024]{1,0:T(8,128)(2,1)S(1)}, u32[]{:S(2)}, u32[]{:S(2)}) collective-permute-start(bf16[256,1024]{1,0:T(8,128)(2,1)S(1)} %convolution_convert_fusion.5), channel_id=1, source_target_pairs={{0,1},{1,0},{2,3},{3,2},{4,5},{5,4},{6,7},{7,6},{8,9},{9,8},{10,11... | collective-permute-start | bytes 1572872 | tf_op jit(solution)/shard_map/ppermute | solution.py:118
  289.3 7.8 %collective-permute-start.39 = (bf16[2,128,1024]{2,1,0:T(8,128)(2,1)S(1)}, bf16[2,128,1024]{2,1,0:T(8,128)(2,1)S(1)}, u32[]{:S(2)}, u32[]{:S(2)}) collective-permute-start(bf16[2,128,1024]{2,1,0:T(8,128)(2,1)S(1)} %get-tuple-element.131), channel_id=1, source_target_pairs={{0,8},{8,0},{16,24},{24,16},{1,9},{9,1},{17,25},{25,17},{2,10},{10... | collective-permute-start | bytes 1572872 | tf_op jit(solution)/shard_map/ppermute | solution.py:125
  291.1 28.1 %collective-permute-start.42 = (bf16[2,128,1024]{2,1,0:T(8,128)(2,1)S(1)}, bf16[2,128,1024]{2,1,0:T(8,128)(2,1)S(1)}, u32[]{:S(2)}, u32[]{:S(2)}) collective-permute-start(bf16[2,128,1024]{2,1,0:T(8,128)(2,1)S(1)} %get-tuple-element.88), channel_id=1, source_target_pairs={{0,24},{8,16},{16,8},{24,0},{1,25},{9,17},{17,9},{25,1},{2,26},{10... | collective-permute-start | bytes 1572872 | tf_op jit(solution)/shard_map/ppermute | solution.py:125
  292.5 24.1 %collective-permute-start.41 = (bf16[2,128,1024]{2,1,0:T(8,128)(2,1)S(1)}, bf16[2,128,1024]{2,1,0:T(8,128)(2,1)S(1)}, u32[]{:S(2)}, u32[]{:S(2)}) collective-permute-start(bf16[2,128,1024]{2,1,0:T(8,128)(2,1)S(1)} %get-tuple-element.84), channel_id=1, source_target_pairs={{0,16},{8,24},{16,0},{24,8},{1,17},{9,25},{17,1},{25,9},{2,18},{10... | collective-permute-start | bytes 1572872 | tf_op jit(solution)/shard_map/ppermute | solution.py:125
  295.6 25.1 %collective-permute-start.44 = (bf16[1024,256]{1,0:T(8,128)(2,1)S(1)}, bf16[1024,256]{1,0:T(8,128)(2,1)S(1)}, u32[]{:S(2)}, u32[]{:S(2)}) collective-permute-start(bf16[1024,256]{1,0:T(8,128)(2,1)S(1)} %get-tuple-element.92), channel_id=1, source_target_pairs={{0,1},{1,0},{2,3},{3,2},{4,5},{5,4},{6,7},{7,6},{8,9},{9,8},{10,11... | collective-permute-start | bytes 1572872 | tf_op jit(solution)/shard_map/ppermute | solution.py:118
  299.7 21.0 %collective-permute-start.40 = (bf16[1024,256]{1,0:T(8,128)(2,1)S(1)}, bf16[1024,256]{1,0:T(8,128)(2,1)S(1)}, u32[]{:S(2)}, u32[]{:S(2)}) collective-permute-start(bf16[1024,256]{1,0:T(8,128)(2,1)S(1)} %get-tuple-element.83), channel_id=1, source_target_pairs={{0,8},{8,0},{16,24},{24,16},{1,9},{9,1},{17,25},{25,17},{2,10},{10... | collective-permute-start | bytes 1572872 | tf_op jit(solution)/shard_map/ppermute | solution.py:125
  319.2 25.8 %collective-permute-start.43 = (bf16[1024,256]{1,0:T(8,128)(2,1)S(1)}, bf16[1024,256]{1,0:T(8,128)(2,1)S(1)}, u32[]{:S(2)}, u32[]{:S(2)}) collective-permute-start(bf16[1024,256]{1,0:T(8,128)(2,1)S(1)} %get-tuple-element.89), channel_id=1, source_target_pairs={{0,16},{8,24},{16,0},{24,8},{1,17},{9,25},{17,1},{25,9},{2,18},{10... | collective-permute-start | bytes 1572872 | tf_op jit(solution)/shard_map/ppermute | solution.py:125
  320.7 13.3 %collective-permute-start.45 = (bf16[1024,256]{1,0:T(8,128)(2,1)S(1)}, bf16[1024,256]{1,0:T(8,128)(2,1)S(1)}, u32[]{:S(2)}, u32[]{:S(2)}) collective-permute-start(bf16[1024,256]{1,0:T(8,128)(2,1)S(1)} %collective-permute-done.40), channel_id=1, source_target_pairs={{0,1},{1,0},{2,3},{3,2},{4,5},{5,4},{6,7},{7,6},{8,9},{9,8},{10,11... | collective-permute-start | bytes 1572872 | tf_op jit(solution)/shard_map/ppermute | solution.py:118
  345.1 13.4 %collective-permute-start.46 = (bf16[1024,256]{1,0:T(8,128)(2,1)S(1)}, bf16[1024,256]{1,0:T(8,128)(2,1)S(1)}, u32[]{:S(2)}, u32[]{:S(2)}) collective-permute-start(bf16[1024,256]{1,0:T(8,128)(2,1)S(1)} %get-tuple-element.97), channel_id=1, source_target_pairs={{0,24},{8,16},{16,8},{24,0},{1,25},{9,17},{17,9},{25,1},{2,26},{10... | collective-permute-start | bytes 1572872 | tf_op jit(solution)/shard_map/ppermute | solution.py:125
  346.6 14.5 %collective-permute-start.47 = (bf16[1024,256]{1,0:T(8,128)(2,1)S(1)}, bf16[1024,256]{1,0:T(8,128)(2,1)S(1)}, u32[]{:S(2)}, u32[]{:S(2)}) collective-permute-start(bf16[1024,256]{1,0:T(8,128)(2,1)S(1)} %collective-permute-done.43), channel_id=1, source_target_pairs={{0,1},{1,0},{2,3},{3,2},{4,5},{5,4},{6,7},{7,6},{8,9},{9,8},{10,11... | collective-permute-start | bytes 1572872 | tf_op jit(solution)/shard_map/ppermute | solution.py:118
  361.1 13.7 %collective-permute-start.48 = (bf16[1024,256]{1,0:T(8,128)(2,1)S(1)}, bf16[1024,256]{1,0:T(8,128)(2,1)S(1)}, u32[]{:S(2)}, u32[]{:S(2)}) collective-permute-start(bf16[1024,256]{1,0:T(8,128)(2,1)S(1)} %collective-permute-done.46), channel_id=1, source_target_pairs={{0,1},{1,0},{2,3},{3,2},{4,5},{5,4},{6,7},{7,6},{8,9},{9,8},{10,11... | collective-permute-start | bytes 1572872 | tf_op jit(solution)/shard_map/ppermute | solution.py:118
  375.6 14.4 %collective-permute-start.54 = (bf16[1024,256]{1,0:T(8,128)(2,1)S(1)}, bf16[1024,256]{1,0:T(8,128)(2,1)S(1)}, u32[]{:S(2)}, u32[]{:S(2)}) collective-permute-start(bf16[1024,256]{1,0:T(8,128)(2,1)S(1)} %convolution_convert_fusion.3), channel_id=1, source_target_pairs={{0,8},{8,0},{16,24},{24,16},{1,9},{9,1},{17,25},{25,17},{2,10},{10... | collective-permute-start | bytes 1572872 | tf_op jit(solution)/shard_map/ppermute | solution.py:125
  375.7 14.3 %collective-permute-start.53 = (bf16[1024,256]{1,0:T(8,128)(2,1)S(1)}, bf16[1024,256]{1,0:T(8,128)(2,1)S(1)}, u32[]{:S(2)}, u32[]{:S(2)}) collective-permute-start(bf16[1024,256]{1,0:T(8,128)(2,1)S(1)} %fusion.7), channel_id=1, source_target_pairs={{0,16},{8,24},{16,0},{24,8},{1,17},{9,25},{17,1},{25,9},{2,18},{10... | collective-permute-start | bytes 1572872 | tf_op jit(solution)/shard_map/ppermute | solution.py:125
  377.9 15.2 %collective-permute-start.51 = (bf16[2048,256]{1,0:T(8,128)(2,1)S(1)}, bf16[2048,256]{1,0:T(8,128)(2,1)S(1)}, u32[]{:S(2)}, u32[]{:S(2)}) collective-permute-start(bf16[2048,256]{1,0:T(8,128)(2,1)S(1)} %convolution_convert_fusion), channel_id=1, source_target_pairs={{0,8},{8,0},{16,24},{24,16},{1,9},{9,1},{17,25},{25,17},{2,10},{10... | collective-permute-start | bytes 3145736 | tf_op jit(solution)/shard_map/ppermute | solution.py:125
  390.8 13.6 %collective-permute-start.55 = (bf16[1024,256]{1,0:T(8,128)(2,1)S(1)}, bf16[1024,256]{1,0:T(8,128)(2,1)S(1)}, u32[]{:S(2)}, u32[]{:S(2)}) collective-permute-start(bf16[1024,256]{1,0:T(8,128)(2,1)S(1)} %fusion.8), channel_id=1, source_target_pairs={{0,16},{8,24},{16,0},{24,8},{1,17},{9,25},{17,1},{25,9},{2,18},{10... | collective-permute-start | bytes 1572872 | tf_op jit(solution)/shard_map/ppermute | solution.py:125
  393.0 14.5 %collective-permute-start.50 = (bf16[2048,256]{1,0:T(8,128)(2,1)S(1)}, bf16[2048,256]{1,0:T(8,128)(2,1)S(1)}, u32[]{:S(2)}, u32[]{:S(2)}) collective-permute-start(bf16[2048,256]{1,0:T(8,128)(2,1)S(1)} %convolution_convert_fusion.1), channel_id=1, source_target_pairs={{0,8},{8,0},{16,24},{24,16},{1,9},{9,1},{17,25},{25,17},{2,10},{10... | collective-permute-start | bytes 3145736 | tf_op jit(solution)/shard_map/ppermute | solution.py:125
  404.3 23.8 %collective-permute-start.56 = (bf16[2048,256]{1,0:T(8,128)(2,1)S(1)}, bf16[2048,256]{1,0:T(8,128)(2,1)S(1)}, u32[]{:S(2)}, u32[]{:S(2)}) collective-permute-start(bf16[2048,256]{1,0:T(8,128)(2,1)S(1)} %fusion.2), channel_id=1, source_target_pairs={{0,16},{8,24},{16,0},{24,8},{1,17},{9,25},{17,1},{25,9},{2,18},{10... | collective-permute-start | bytes 3145736 | tf_op jit(solution)/shard_map/ppermute | solution.py:125
  405.3 8.9 %collective-permute-start.61 = (bf16[1024,256]{1,0:T(8,128)(2,1)S(1)}, bf16[1024,256]{1,0:T(8,128)(2,1)S(1)}, u32[]{:S(2)}, u32[]{:S(2)}) collective-permute-start(bf16[1024,256]{1,0:T(8,128)(2,1)S(1)} %add_convert_fusion.8.refs_2_), channel_id=1, source_target_pairs={{0,8},{8,0},{16,24},{24,16},{1,9},{9,1},{17,25},{25,17},{2,10},{10... | collective-permute-start | bytes 1572872 | tf_op jit(solution)/shard_map/ppermute | solution.py:125
  405.5 8.7 %collective-permute-start.62 = (bf16[1024,256]{1,0:T(8,128)(2,1)S(1)}, bf16[1024,256]{1,0:T(8,128)(2,1)S(1)}, u32[]{:S(2)}, u32[]{:S(2)}) collective-permute-start(bf16[1024,256]{1,0:T(8,128)(2,1)S(1)} %add_convert_fusion.7.refs_3_), channel_id=1, source_target_pairs={{0,8},{8,0},{16,24},{24,16},{1,9},{9,1},{17,25},{25,17},{2,10},{10... | collective-permute-start | bytes 1572872 | tf_op jit(solution)/shard_map/ppermute | solution.py:125
  407.4 22.4 %collective-permute-start.49 = (bf16[2048,256]{1,0:T(8,128)(2,1)S(1)}, bf16[2048,256]{1,0:T(8,128)(2,1)S(1)}, u32[]{:S(2)}, u32[]{:S(2)}) collective-permute-start(bf16[2048,256]{1,0:T(8,128)(2,1)S(1)} %convolution_convert_fusion.2), channel_id=1, source_target_pairs={{0,8},{8,0},{16,24},{24,16},{1,9},{9,1},{17,25},{25,17},{2,10},{10... | collective-permute-start | bytes 3145736 | tf_op jit(solution)/shard_map/ppermute | solution.py:125
  428.1 22.9 %collective-permute-start.57 = (bf16[2048,256]{1,0:T(8,128)(2,1)S(1)}, bf16[2048,256]{1,0:T(8,128)(2,1)S(1)}, u32[]{:S(2)}, u32[]{:S(2)}) collective-permute-start(bf16[2048,256]{1,0:T(8,128)(2,1)S(1)} %fusion.1), channel_id=1, source_target_pairs={{0,16},{8,24},{16,0},{24,8},{1,17},{9,25},{17,1},{25,9},{2,18},{10... | collective-permute-start | bytes 3145736 | tf_op jit(solution)/shard_map/ppermute | solution.py:125
  429.2 50.7 %collective-permute-start.63 = (bf16[2048,512]{1,0:T(8,128)(2,1)S(1)}, bf16[2048,512]{1,0:T(8,128)(2,1)S(1)}, u32[]{:S(2)}, u32[]{:S(2)}) collective-permute-start(bf16[2048,512]{1,0:T(8,128)(2,1)S(1)} %pad_maximum_fusion.3), channel_id=1, source_target_pairs={{0,2},{1,3},{2,4},{3,5},{4,6},{5,7},{6,0},{7,1},{8,10},{9,11},{10,... | collective-permute-start | bytes 6291464 | tf_op jit(solution)/shard_map/ppermute | solution.py:122
  429.7 28.2 %collective-permute-start.59 = (bf16[2048,256]{1,0:T(8,128)(2,1)S(1)}, bf16[2048,256]{1,0:T(8,128)(2,1)S(1)}, u32[]{:S(2)}, u32[]{:S(2)}) collective-permute-start(bf16[2048,256]{1,0:T(8,128)(2,1)S(1)} %add_convert_fusion.5), channel_id=1, source_target_pairs={{0,8},{8,0},{16,24},{24,16},{1,9},{9,1},{17,25},{25,17},{2,10},{10... | collective-permute-start | bytes 3145736 | tf_op jit(solution)/shard_map/ppermute | solution.py:125
  451.3 22.7 %collective-permute-start.64 = (bf16[2048,256]{1,0:T(8,128)(2,1)S(1)}, bf16[2048,256]{1,0:T(8,128)(2,1)S(1)}, u32[]{:S(2)}, u32[]{:S(2)}) collective-permute-start(bf16[2048,256]{1,0:T(8,128)(2,1)S(1)} %add_convert_fusion.4), channel_id=1, source_target_pairs={{0,8},{8,0},{16,24},{24,16},{1,9},{9,1},{17,25},{25,17},{2,10},{10... | collective-permute-start | bytes 3145736 | tf_op jit(solution)/shard_map/ppermute | solution.py:125
  456.9 25.6 %collective-permute-start.58 = (bf16[2048,256]{1,0:T(8,128)(2,1)S(1)}, bf16[2048,256]{1,0:T(8,128)(2,1)S(1)}, u32[]{:S(2)}, u32[]{:S(2)}) collective-permute-start(bf16[2048,256]{1,0:T(8,128)(2,1)S(1)} %fusion), channel_id=1, source_target_pairs={{0,16},{8,24},{16,0},{24,8},{1,17},{9,25},{17,1},{25,9},{2,18},{10... | collective-permute-start | bytes 3145736 | tf_op jit(solution)/shard_map/ppermute | solution.py:125
  464.9 59.9 %collective-permute-start.60 = (bf16[2048,512]{1,0:T(8,128)(2,1)}, bf16[2048,512]{1,0:T(8,128)(2,1)S(1)}, u32[]{:S(2)}, u32[]{:S(2)}) collective-permute-start(bf16[2048,512]{1,0:T(8,128)(2,1)} %pad_maximum_fusion.2), channel_id=1, source_target_pairs={{0,6},{1,7},{2,0},{3,1},{4,2},{5,3},{6,4},{7,5},{8,14},{9,15},{10,... | collective-permute-start | bytes 6291464 | tf_op jit(solution)/shard_map/ppermute | solution.py:122
  481.8 84.6 %collective-permute-start.65 = (bf16[2048,512]{1,0:T(8,128)(2,1)}, bf16[2048,512]{1,0:T(8,128)(2,1)}, u32[]{:S(2)}, u32[]{:S(2)}) collective-permute-start(bf16[2048,512]{1,0:T(8,128)(2,1)} %pad_maximum_fusion.4), channel_id=1, source_target_pairs={{0,2},{1,3},{2,4},{3,5},{4,6},{5,7},{6,0},{7,1},{8,10},{9,11},{10,... | collective-permute-start | bytes 6291464 | tf_op jit(solution)/shard_map/ppermute | solution.py:122
  (26 other events, 162.7 us)

commit v6 on v2

--- a/solution.py
+++ b/solution.py
@@ -207,7 +207,7 @@
                 grads[1] = tie(grads[1], right)
             if (k, s) == (1, far):
                 grads[far] = tie(grads[far], last["rows"][-2])
-            g = tie(grads[s], rights[1]) if (k, s) == turns[-1] else grads[s]
+            g = tie(grads[s], rights[2], rights[3]) if (k, s) == turns[-1] else grads[s]
             g_mine, g_theirs = g[:half], g[half:]
             mine, theirs = half_sum(
                 lambda: product([(g_theirs, lefts[k])], BF16, by_rows=False),

time: 565 us -> 581 us (1.028)
  Pallas kernels: 120 us -> 129 us
    ppermute x48, waiting for transfers between devices: 101 us -> 83.1 us  [row_xor(): return lax.ppermute(x, 'row', [(r, r ^ k) for r in range(n_row)])]
    ppermute x9, waiting for transfers between devices: 95.5 us -> 111 us  [a_shift(): return lax.ppermute(x, 'col', perm)]
    pallas_call x4, Pallas kernels: 10.7 us -> 18.9 us  [moments_at(): pl.pallas_call(moments_kernel, grid_spec=pltpu.PrefetchScalarGridSpec(num...]
    ppermute x10, waiting for transfers between devices: 114 us -> 122 us  [b_shift(): return lax.ppermute(x, 'col', perm)]
  transfers between devices with their start and end apart: 67 -> 67, of which waited for: 23 -> 25; matrix products, arithmetic and copies ran while one was open for 10% -> 10% of each run, Pallas kernels for 22% -> 22%
where the time goes in v6:
time: 581 us; the launch traced here: 571 us
  waiting for transfers between devices  316 us (54%)
  Pallas kernels  129 us (22%)
  starting transfers between devices  55.6 us (10%)
  local copies, waits for them, and re-layouts  31.9 us (5%)
  matrix products  21 us (4%)
  other arithmetic  16.9 us (3%)
    ppermute x10, waiting for transfers between devices, b_shift(): return lax.ppermute(x, 'col', perm)  122 us
    ppermute x9, waiting for transfers between devices, a_shift(): return lax.ppermute(x, 'col', perm)  111 us
    pallas_call x24, Pallas kernels, product(): pl.pallas_call(functools.partial(product_kernel, len(pairs)), grid=(grid,...  110 us
    ppermute x48, waiting for transfers between devices, row_xor(): return lax.ppermute(x, 'row', [(r, r ^ k) for r in range(n_row)])  83.1 us
    ppermute x48, starting transfers between devices, row_xor(): return lax.ppermute(x, 'row', [(r, r ^ k) for r in range(n_row)])  26.1 us
    dot_general x18, matrix products, dot(): lax.dot_general(a, b, ((contract[:1], contract[1:]), ((), ())), preferred...  21 us
    pallas_call x4, Pallas kernels, moments_at(): pl.pallas_call(moments_kernel, grid_spec=pltpu.PrefetchScalarGridSpec(num...  18.9 us
    ppermute x10, starting transfers between devices, b_shift(): return lax.ppermute(x, 'col', perm)  16.5 us
  transfers between devices with their start and end apart: 67, of which 25 were waited for; matrix products, arithmetic and copies ran while one was open for 10% of the time, Pallas kernels for 22%

profile of v6, /device:TPU:0, one launch (start us, length us, event | category | flops | bytes accessed | tf_op | source)
XLA Modules:
  0.0 571.5 jit_solution(16183072279578307327)
XLA Ops:
  0.7 1.7 constant_dynamic-slice_fusion.3
  5.1 2.9 collective-permute-start.2
  9.6 2.2 collective-permute-start.1
  13.7 1.7 fusion.46
  18.5 4.0 shard_map.76
  27.8 2.3 constant_dynamic-slice_fusion
  30.1 68.9 %collective-permute-done.2.refs_1_ = bf16[2048,1024]{1,0:T(8,128)(2,1)} collective-permute-done((bf16[2048,1024]{1,0:T(8,128)(2,1)}, bf16[2048,1024]{1,0:T(8,128)(2,1)}, u32[]{:S(2)}, u32[]{:S(2)}) %collective-permute-start.2) | collective-permute-done | bytes 4194336 | tf_op jit(solution)/shard_map/ppermute | solution.py:118
  98.9 1.7 collective-permute-start.6
  100.7 3.9 shard_map.77
  107.8 3.9 shard_map.84
  114.9 1.7 fusion.45
  116.6 4.4 shard_map.82
  121.1 3.9 shard_map.85
  126.6 1.7 fusion.44
  128.2 4.8 shard_map.80
  133.2 4.8 shard_map.83
  142.9 4.8 shard_map.78
  149.4 2.0 copy-done.8
  151.9 4.0 shard_map.81
  159.1 3.9 shard_map.79
  165.8 4.1 collective-permute-done.16
  170.4 1.7 fusion.43
  172.1 3.9 shard_map.88
  176.2 3.9 shard_map.86
  180.7 4.2 collective-permute-done.25
  184.9 1.7 collective-permute-start.27
  187.5 3.9 shard_map.89
  193.8 3.9 shard_map.87
  198.3 12.5 %collective-permute-done.27 = bf16[256,2048]{0,1:T(8,128)(2,1)S(1)} collective-permute-done((bf16[256,2048]{0,1:T(8,128)(2,1)S(1)}, bf16[256,2048]{0,1:T(8,128)(2,1)S(1)}, u32[]{:S(2)}, u32[]{:S(2)}) %collective-permute-start.27) | collective-permute-done | bytes 1048608 | tf_op jit(solution)/shard_map/ppermute | solution.py:122
  210.8 21.5 %collective-permute-done.26 = bf16[256,2048]{0,1:T(8,128)(2,1)S(1)} collective-permute-done((bf16[256,2048]{0,1:T(8,128)(2,1)S(1)}, bf16[256,2048]{0,1:T(8,128)(2,1)S(1)}, u32[]{:S(2)}, u32[]{:S(2)}) %collective-permute-start.26) | collective-permute-done | bytes 1048608 | tf_op jit(solution)/shard_map/ppermute | solution.py:122
  232.5 1.7 fusion.42
  234.2 4.0 shard_map.90
  243.2 9.5 %collective-permute-done.23 = bf16[256,1024]{1,0:T(8,128)(2,1)S(1)} collective-permute-done((bf16[256,1024]{1,0:T(8,128)(2,1)S(1)}, bf16[256,1024]{1,0:T(8,128)(2,1)S(1)}, u32[]{:S(2)}, u32[]{:S(2)}) %collective-permute-start.23) | collective-permute-done | bytes 524320 | tf_op jit(solution)/shard_map/ppermute | solution.py:125
  253.2 4.0 shard_map.91
  261.6 9.9 %collective-permute-done.29 = bf16[256,1024]{1,0:T(8,128)(2,1)S(1)} collective-permute-done((bf16[256,1024]{1,0:T(8,128)(2,1)S(1)}, bf16[256,1024]{1,0:T(8,128)(2,1)S(1)}, u32[]{:S(2)}, u32[]{:S(2)}) %collective-permute-start.29) | collective-permute-done | bytes 524320 | tf_op jit(solution)/shard_map/ppermute | solution.py:125
  279.9 7.9 %collective-permute-done.37 = bf16[256,1024]{1,0:T(8,128)(2,1)S(1)} collective-permute-done((bf16[256,1024]{1,0:T(8,128)(2,1)S(1)}, bf16[256,1024]{1,0:T(8,128)(2,1)S(1)}, u32[]{:S(2)}, u32[]{:S(2)}) %collective-permute-start.37) | collective-permute-done | bytes 524320 | tf_op jit(solution)/shard_map/ppermute | solution.py:118
  290.5 9.9 %collective-permute-done.38 = bf16[256,1024]{1,0:T(8,128)(2,1)S(1)} collective-permute-done((bf16[256,1024]{1,0:T(8,128)(2,1)S(1)}, bf16[256,1024]{1,0:T(8,128)(2,1)S(1)}, u32[]{:S(2)}, u32[]{:S(2)}) %collective-permute-start.38) | collective-permute-done | bytes 524320 | tf_op jit(solution)/shard_map/ppermute | solution.py:118
  302.1 2.5 collective-permute-start.42
  305.0 2.6 shard_map.92
  309.1 2.6 shard_map.93
  311.7 16.5 %collective-permute-done.41.rot_ref = bf16[2,128,1024]{2,1,0:T(8,128)(2,1)S(1)} collective-permute-done((bf16[2,128,1024]{2,1,0:T(8,128)(2,1)S(1)}, bf16[2,128,1024]{2,1,0:T(8,128)(2,1)S(1)}, u32[]{:S(2)}, u32[]{:S(2)}) %collective-permute-start.41) | collective-permute-done | bytes 524320 | tf_op jit(solution)/shard_map/ppermute | solution.py:125
  328.3 2.6 shard_map.94
  330.9 1.7 collective-permute-start.43
  333.0 11.0 %shard_map.95 = (f32[1024,1024]{1,0:T(8,128)}, f32[1024,1024]{1,0:T(8,128)}, bf16[1024,256]{1,0:T(8,128)(2,1)S(1)}) custom-call(s32[1]{0:T(128)} %bitcast.23.peer_ref, bf16[2,128,1024]{2,1,0:T(8,128)(2,1)S(1)} %collective-permute-done.42.rot_ref, f32[1024,1024]{1,0:T(8,128)S(1)} %copy-done, ...), custom_call_target="tpu_custom_call", output_to_operand_aliasing={{0}: (4, {}), {1}: (5, {})} | custom-call | flops 2621440 | bytes 5242880 | tf_op jit(solution)/shard_map/pallas_call | solution.py:77
  346.4 12.5 %collective-permute-done.46 = bf16[1024,256]{1,0:T(8,128)(2,1)S(1)} collective-permute-done((bf16[1024,256]{1,0:T(8,128)(2,1)S(1)}, bf16[1024,256]{1,0:T(8,128)(2,1)S(1)}, u32[]{:S(2)}, u32[]{:S(2)}) %collective-permute-start.46) | collective-permute-done | bytes 524320 | tf_op jit(solution)/shard_map/ppermute | solution.py:118
  361.3 11.7 %collective-permute-done.47 = bf16[1024,256]{1,0:T(8,128)(2,1)S(1)} collective-permute-done((bf16[1024,256]{1,0:T(8,128)(2,1)S(1)}, bf16[1024,256]{1,0:T(8,128)(2,1)S(1)}, u32[]{:S(2)}, u32[]{:S(2)}) %collective-permute-start.47) | collective-permute-done | bytes 524320 | tf_op jit(solution)/shard_map/ppermute | solution.py:118
  376.7 9.7 %collective-permute-done.48 = bf16[1024,256]{1,0:T(8,128)(2,1)S(1)} collective-permute-done((bf16[1024,256]{1,0:T(8,128)(2,1)S(1)}, bf16[1024,256]{1,0:T(8,128)(2,1)S(1)}, u32[]{:S(2)}, u32[]{:S(2)}) %collective-permute-start.48) | collective-permute-done | bytes 524320 | tf_op jit(solution)/shard_map/ppermute | solution.py:118
  393.4 10.5 %collective-permute-done.55 = bf16[1024,256]{1,0:T(8,128)(2,1)S(1)} collective-permute-done((bf16[1024,256]{1,0:T(8,128)(2,1)S(1)}, bf16[1024,256]{1,0:T(8,128)(2,1)S(1)}, u32[]{:S(2)}, u32[]{:S(2)}) %collective-permute-start.55) | collective-permute-done | bytes 524320 | tf_op jit(solution)/shard_map/ppermute | solution.py:125
  408.3 5.4 shard_map.100
  413.7 5.4 shard_map.101
  419.2 9.1 %collective-permute-done.56 = bf16[2048,256]{1,0:T(8,128)(2,1)S(1)} collective-permute-done((bf16[2048,256]{1,0:T(8,128)(2,1)S(1)}, bf16[2048,256]{1,0:T(8,128)(2,1)S(1)}, u32[]{:S(2)}, u32[]{:S(2)}) %collective-permute-start.56) | collective-permute-done | bytes 1048608 | tf_op jit(solution)/shard_map/ppermute | solution.py:125
  429.2 1.8 collective-permute-start.63
  432.7 19.0 %collective-permute-done.57 = bf16[2048,256]{1,0:T(8,128)(2,1)S(1)} collective-permute-done((bf16[2048,256]{1,0:T(8,128)(2,1)S(1)}, bf16[2048,256]{1,0:T(8,128)(2,1)S(1)}, u32[]{:S(2)}, u32[]{:S(2)}) %collective-permute-start.57) | collective-permute-done | bytes 1048608 | tf_op jit(solution)/shard_map/ppermute | solution.py:125
  452.2 5.5 shard_map.97
  458.5 5.4 shard_map.98
  465.5 1.9 collective-permute-start.60
  467.5 5.5 shard_map.99
  473.1 5.4 shard_map.102
  483.7 5.4 shard_map.96
  490.4 5.4 shard_map.103
  495.9 28.9 %collective-permute-done.60 = bf16[2048,512]{1,0:T(8,128)(2,1)S(1)} collective-permute-done((bf16[2048,512]{1,0:T(8,128)(2,1)}, bf16[2048,512]{1,0:T(8,128)(2,1)S(1)}, u32[]{:S(2)}, u32[]{:S(2)}) %collective-permute-start.60) | collective-permute-done | bytes 2097184 | tf_op jit(solution)/shard_map/ppermute | solution.py:122
  524.7 42.2 %collective-permute-done.65 = bf16[2048,512]{1,0:T(8,128)(2,1)} collective-permute-done((bf16[2048,512]{1,0:T(8,128)(2,1)}, bf16[2048,512]{1,0:T(8,128)(2,1)}, u32[]{:S(2)}, u32[]{:S(2)}) %collective-permute-start.65) | collective-permute-done | bytes 2097184 | tf_op jit(solution)/shard_map/ppermute | solution.py:122
  567.0 2.4 add_convert_fusion.1
  569.4 1.9 maximum_select_fusion
  (234 shorter events, 97.1 us)
Async XLA Ops:
  5.1 93.8 %collective-permute-start.2 = (bf16[2048,1024]{1,0:T(8,128)(2,1)}, bf16[2048,1024]{1,0:T(8,128)(2,1)}, u32[]{:S(2)}, u32[]{:S(2)}) collective-permute-start(bf16[2048,1024]{1,0:T(8,128)(2,1)} %refs_0_.7), channel_id=1, source_target_pairs={{0,1},{1,0},{2,3},{3,2},{4,5},{5,4},{6,7},{7,6},{8,9},{9,8},{10,11... | collective-permute-start | bytes 12582920 | tf_op jit(solution)/shard_map/ppermute | solution.py:118
  8.1 98.2 %collective-permute-start = (bf16[512,2048]{1,0:T(8,128)(2,1)}, bf16[512,2048]{1,0:T(8,128)(2,1)}, u32[]{:S(2)}, u32[]{:S(2)}) collective-permute-start(bf16[512,2048]{1,0:T(8,128)(2,1)} %pad_maximum_fusion.1), channel_id=1, source_target_pairs={{0,2},{1,3},{2,4},{3,5},{4,6},{5,7},{6,0},{7,1},{8,10},{9,11},{10,... | collective-permute-start | bytes 6291464 | tf_op jit(solution)/shard_map/ppermute | solution.py:122
  9.6 98.2 %collective-permute-start.1 = (bf16[512,2048]{1,0:T(8,128)(2,1)}, bf16[512,2048]{1,0:T(8,128)(2,1)}, u32[]{:S(2)}, u32[]{:S(2)}) collective-permute-start(bf16[512,2048]{1,0:T(8,128)(2,1)} %pad_maximum_fusion.1), channel_id=1, source_target_pairs={{0,6},{1,7},{2,0},{3,1},{4,2},{5,3},{6,4},{7,5},{8,14},{9,15},{10,... | collective-permute-start | bytes 6291464 | tf_op jit(solution)/shard_map/ppermute | solution.py:122
  12.1 11.1 %collective-permute-start.4 = (bf16[128,1024]{0,1:T(8,128)(2,1)S(1)}, bf16[128,1024]{0,1:T(8,128)(2,1)}, u32[]{:S(2)}, u32[]{:S(2)}) collective-permute-start(bf16[128,1024]{0,1:T(8,128)(2,1)S(1)} %get-tuple-element.162), channel_id=1, source_target_pairs={{0,16},{8,24},{16,0},{24,8},{1,17},{9,25},{17,1},{25,9},{2,18},{10... | collective-permute-start | bytes 786440 | tf_op jit(solution)/shard_map/ppermute | solution.py:125
  15.4 10.7 %collective-permute-start.5 = (bf16[128,1024]{0,1:T(8,128)(2,1)S(1)}, bf16[128,1024]{0,1:T(8,128)(2,1)}, u32[]{:S(2)}, u32[]{:S(2)}) collective-permute-start(bf16[128,1024]{0,1:T(8,128)(2,1)S(1)} %get-tuple-element.161), channel_id=1, source_target_pairs={{0,24},{8,16},{16,8},{24,0},{1,25},{9,17},{17,9},{25,1},{2,26},{10... | collective-permute-start | bytes 786440 | tf_op jit(solution)/shard_map/ppermute | solution.py:125
  23.2 77.5 %collective-permute-start.7 = (bf16[256,1024]{1,0:T(8,128)(2,1)S(1)}, bf16[256,1024]{1,0:T(8,128)(2,1)S(1)}, u32[]{:S(2)}, u32[]{:S(2)}) collective-permute-start(bf16[256,1024]{1,0:T(8,128)(2,1)S(1)} %shard_map.76), channel_id=1, source_target_pairs={{0,8},{8,0},{16,24},{24,16},{1,9},{9,1},{17,25},{25,17},{2,10},{10... | collective-permute-start | bytes 1572872 | tf_op jit(solution)/shard_map/ppermute | solution.py:125
  98.9 13.4 %collective-permute-start.6 = (bf16[128,2048]{0,1:T(8,128)(2,1)}, bf16[128,2048]{0,1:T(8,128)(2,1)}, u32[]{:S(2)}, u32[]{:S(2)}) collective-permute-start(bf16[128,2048]{0,1:T(8,128)(2,1)} %bitcast.9), channel_id=1, source_target_pairs={{0,1},{1,0},{2,3},{3,2},{4,5},{5,4},{6,7},{7,6},{8,9},{9,8},{10,11... | collective-permute-start | bytes 1572872 | tf_op jit(solution)/shard_map/ppermute | solution.py:118
  104.6 20.4 %collective-permute-start.8 = (bf16[256,1024]{1,0:T(8,128)(2,1)S(1)}, bf16[256,1024]{1,0:T(8,128)(2,1)S(1)}, u32[]{:S(2)}, u32[]{:S(2)}) collective-permute-start(bf16[256,1024]{1,0:T(8,128)(2,1)S(1)} %shard_map.77), channel_id=1, source_target_pairs={{0,16},{8,24},{16,0},{24,8},{1,17},{9,25},{17,1},{25,9},{2,18},{10... | collective-permute-start | bytes 1572872 | tf_op jit(solution)/shard_map/ppermute | solution.py:125
  106.2 64.2 %collective-permute-start.20 = (bf16[512,2048]{1,0:T(8,128)(2,1)}, bf16[512,2048]{1,0:T(8,128)(2,1)}, u32[]{:S(2)}, u32[]{:S(2)}) collective-permute-start(bf16[512,2048]{1,0:T(8,128)(2,1)} %collective-permute-done), channel_id=1, source_target_pairs={{0,2},{1,3},{2,4},{3,5},{4,6},{5,7},{6,0},{7,1},{8,10},{9,11},{10,... | collective-permute-start | bytes 6291464 | tf_op jit(solution)/shard_map/ppermute | solution.py:122
  111.7 9.3 %collective-permute-start.13 = (bf16[256,1024]{1,0:T(8,128)(2,1)S(1)}, bf16[256,1024]{1,0:T(8,128)(2,1)S(1)}, u32[]{:S(2)}, u32[]{:S(2)}) collective-permute-start(bf16[256,1024]{1,0:T(8,128)(2,1)S(1)} %shard_map.84), channel_id=1, source_target_pairs={{0,8},{8,0},{16,24},{24,16},{1,9},{9,1},{17,25},{25,17},{2,10},{10... | collective-permute-start | bytes 1572872 | tf_op jit(solution)/shard_map/ppermute | solution.py:125
  121.0 12.3 %collective-permute-start.12 = (bf16[256,1024]{1,0:T(8,128)(2,1)S(1)}, bf16[256,1024]{1,0:T(8,128)(2,1)S(1)}, u32[]{:S(2)}, u32[]{:S(2)}) collective-permute-start(bf16[256,1024]{1,0:T(8,128)(2,1)S(1)} %shard_map.82), channel_id=1, source_target_pairs={{0,8},{8,0},{16,24},{24,16},{1,9},{9,1},{17,25},{25,17},{2,10},{10... | collective-permute-start | bytes 1572872 | tf_op jit(solution)/shard_map/ppermute | solution.py:125
  125.0 14.4 %collective-permute-start.14 = (bf16[256,1024]{1,0:T(8,128)(2,1)S(1)}, bf16[256,1024]{1,0:T(8,128)(2,1)S(1)}, u32[]{:S(2)}, u32[]{:S(2)}) collective-permute-start(bf16[256,1024]{1,0:T(8,128)(2,1)S(1)} %shard_map.85), channel_id=1, source_target_pairs={{0,16},{8,24},{16,0},{24,8},{1,17},{9,25},{17,1},{25,9},{2,18},{10... | collective-permute-start | bytes 1572872 | tf_op jit(solution)/shard_map/ppermute | solution.py:125
  133.0 18.9 %collective-permute-start.11 = (bf16[256,1024]{1,0:T(8,128)(2,1)}, bf16[256,1024]{1,0:T(8,128)(2,1)}, u32[]{:S(2)}, u32[]{:S(2)}) collective-permute-start(bf16[256,1024]{1,0:T(8,128)(2,1)} %shard_map.80), channel_id=1, source_target_pairs={{0,8},{8,0},{16,24},{24,16},{1,9},{9,1},{17,25},{25,17},{2,10},{10... | collective-permute-start | bytes 1572872 | tf_op jit(solution)/shard_map/ppermute | solution.py:125
  140.2 15.7 %collective-permute-start.15 = (bf16[256,1024]{1,0:T(8,128)(2,1)}, bf16[256,1024]{1,0:T(8,128)(2,1)}, u32[]{:S(2)}, u32[]{:S(2)}) collective-permute-start(bf16[256,1024]{1,0:T(8,128)(2,1)} %shard_map.83), channel_id=1, source_target_pairs={{0,16},{8,24},{16,0},{24,8},{1,17},{9,25},{17,1},{25,9},{2,18},{10... | collective-permute-start | bytes 1572872 | tf_op jit(solution)/shard_map/ppermute | solution.py:125
  147.7 9.7 %collective-permute-start.10 = (bf16[256,1024]{1,0:T(8,128)(2,1)}, bf16[256,1024]{1,0:T(8,128)(2,1)}, u32[]{:S(2)}, u32[]{:S(2)}) collective-permute-start(bf16[256,1024]{1,0:T(8,128)(2,1)} %shard_map.78), channel_id=1, source_target_pairs={{0,8},{8,0},{16,24},{24,16},{1,9},{9,1},{17,25},{25,17},{2,10},{10... | collective-permute-start | bytes 1572872 | tf_op jit(solution)/shard_map/ppermute | solution.py:125
  151.4 11.6 %collective-permute-start.31 = (bf16[256,1024]{1,0:T(8,128)(2,1)}, bf16[256,1024]{1,0:T(8,128)(2,1)}, u32[]{:S(2)}, u32[]{:S(2)}) collective-permute-start(bf16[256,1024]{1,0:T(8,128)(2,1)} %get-tuple-element.124), channel_id=1, source_target_pairs={{0,8},{8,0},{16,24},{24,16},{1,9},{9,1},{17,25},{25,17},{2,10},{10... | collective-permute-start | bytes 1572872 | tf_op jit(solution)/shard_map/ppermute | solution.py:125
  156.0 13.9 %collective-permute-start.16 = (bf16[256,1024]{1,0:T(8,128)(2,1)S(1)}, bf16[256,1024]{1,0:T(8,128)(2,1)S(1)}, u32[]{:S(2)}, u32[]{:S(2)}) collective-permute-start(bf16[256,1024]{1,0:T(8,128)(2,1)S(1)} %shard_map.81), channel_id=1, source_target_pairs={{0,16},{8,24},{16,0},{24,8},{1,17},{9,25},{17,1},{25,9},{2,18},{10... | collective-permute-start | bytes 1572872 | tf_op jit(solution)/shard_map/ppermute | solution.py:125
  157.4 18.7 %collective-permute-start.9 = (bf16[256,1024]{1,0:T(8,128)(2,1)S(1)}, bf16[256,1024]{1,0:T(8,128)(2,1)S(1)}, u32[]{:S(2)}, u32[]{:S(2)}) collective-permute-start(bf16[256,1024]{1,0:T(8,128)(2,1)S(1)} %get-tuple-element.116), channel_id=1, source_target_pairs={{0,8},{8,0},{16,24},{24,16},{1,9},{9,1},{17,25},{25,17},{2,10},{10... | collective-permute-start | bytes 1572872 | tf_op jit(solution)/shard_map/ppermute | solution.py:125
  157.5 27.4 %collective-permute-start.25 = (bf16[256,2048]{0,1:T(8,128)(2,1)S(1)}, bf16[256,2048]{0,1:T(8,128)(2,1)S(1)}, u32[]{:S(2)}, u32[]{:S(2)}) collective-permute-start(bf16[256,2048]{0,1:T(8,128)(2,1)S(1)} %copy-done.10), channel_id=1, source_target_pairs={{0,2},{1,3},{2,4},{3,5},{4,6},{5,7},{6,0},{7,1},{8,10},{9,11},{10,... | collective-permute-start | bytes 3145736 | tf_op jit(solution)/shard_map/ppermute | solution.py:122
  165.6 21.0 %collective-permute-start.32 = (bf16[256,1024]{1,0:T(8,128)(2,1)S(1)}, bf16[256,1024]{1,0:T(8,128)(2,1)S(1)}, u32[]{:S(2)}, u32[]{:S(2)}) collective-permute-start(bf16[256,1024]{1,0:T(8,128)(2,1)S(1)} %get-tuple-element.122), channel_id=1, source_target_pairs={{0,8},{8,0},{16,24},{24,16},{1,9},{9,1},{17,25},{25,17},{2,10},{10... | collective-permute-start | bytes 1572872 | tf_op jit(solution)/shard_map/ppermute | solution.py:125
  169.9 21.6 %collective-permute-start.17 = (bf16[256,1024]{1,0:T(8,128)(2,1)S(1)}, bf16[256,1024]{1,0:T(8,128)(2,1)S(1)}, u32[]{:S(2)}, u32[]{:S(2)}) collective-permute-start(bf16[256,1024]{1,0:T(8,128)(2,1)S(1)} %shard_map.79), channel_id=1, source_target_pairs={{0,16},{8,24},{16,0},{24,8},{1,17},{9,25},{17,1},{25,9},{2,18},{10... | collective-permute-start | bytes 1572872 | tf_op jit(solution)/shard_map/ppermute | solution.py:125
  176.1 11.4 %collective-permute-start.21 = (bf16[256,1024]{1,0:T(8,128)(2,1)S(1)}, bf16[256,1024]{1,0:T(8,128)(2,1)S(1)}, u32[]{:S(2)}, u32[]{:S(2)}) collective-permute-start(bf16[256,1024]{1,0:T(8,128)(2,1)S(1)} %shard_map.88), channel_id=1, source_target_pairs={{0,8},{8,0},{16,24},{24,16},{1,9},{9,1},{17,25},{25,17},{2,10},{10... | collective-permute-start | bytes 1572872 | tf_op jit(solution)/shard_map/ppermute | solution.py:125
  180.1 13.6 %collective-permute-start.19 = (bf16[256,1024]{1,0:T(8,128)(2,1)S(1)}, bf16[256,1024]{1,0:T(8,128)(2,1)S(1)}, u32[]{:S(2)}, u32[]{:S(2)}) collective-permute-start(bf16[256,1024]{1,0:T(8,128)(2,1)S(1)} %shard_map.86), channel_id=1, source_target_pairs={{0,8},{8,0},{16,24},{24,16},{1,9},{9,1},{17,25},{25,17},{2,10},{10... | collective-permute-start | bytes 1572872 | tf_op jit(solution)/shard_map/ppermute | solution.py:125
  184.9 25.9 %collective-permute-start.27 = (bf16[256,2048]{0,1:T(8,128)(2,1)S(1)}, bf16[256,2048]{0,1:T(8,128)(2,1)S(1)}, u32[]{:S(2)}, u32[]{:S(2)}) collective-permute-start(bf16[256,2048]{0,1:T(8,128)(2,1)S(1)} %copy-done.10), channel_id=1, source_target_pairs={{0,6},{1,7},{2,0},{3,1},{4,2},{5,3},{6,4},{7,5},{8,14},{9,15},{10,... | collective-permute-start | bytes 3145736 | tf_op jit(solution)/shard_map/ppermute | solution.py:122
  186.6 45.6 %collective-permute-start.26 = (bf16[256,2048]{0,1:T(8,128)(2,1)S(1)}, bf16[256,2048]{0,1:T(8,128)(2,1)S(1)}, u32[]{:S(2)}, u32[]{:S(2)}) collective-permute-start(bf16[256,2048]{0,1:T(8,128)(2,1)S(1)} %collective-permute-done.25), channel_id=1, source_target_pairs={{0,2},{1,3},{2,4},{3,5},{4,6},{5,7},{6,0},{7,1},{8,10},{9,11},{10,... | collective-permute-start | bytes 3145736 | tf_op jit(solution)/shard_map/ppermute | solution.py:122
  187.4 10.8 %collective-permute-start.33 = (bf16[256,1024]{1,0:T(8,128)(2,1)S(1)}, bf16[256,1024]{1,0:T(8,128)(2,1)S(1)}, u32[]{:S(2)}, u32[]{:S(2)}) collective-permute-start(bf16[256,1024]{1,0:T(8,128)(2,1)S(1)} %get-tuple-element.120), channel_id=1, source_target_pairs={{0,8},{8,0},{16,24},{24,16},{1,9},{9,1},{17,25},{25,17},{2,10},{10... | collective-permute-start | bytes 1572872 | tf_op jit(solution)/shard_map/ppermute | solution.py:125
  191.5 40.8 %collective-permute-start.22 = (bf16[256,1024]{1,0:T(8,128)(2,1)S(1)}, bf16[256,1024]{1,0:T(8,128)(2,1)S(1)}, u32[]{:S(2)}, u32[]{:S(2)}) collective-permute-start(bf16[256,1024]{1,0:T(8,128)(2,1)S(1)} %shard_map.89), channel_id=1, source_target_pairs={{0,16},{8,24},{16,0},{24,8},{1,17},{9,25},{17,1},{25,9},{2,18},{10... | collective-permute-start | bytes 1572872 | tf_op jit(solution)/shard_map/ppermute | solution.py:125
  197.9 42.3 %collective-permute-start.18 = (bf16[256,1024]{1,0:T(8,128)(2,1)S(1)}, bf16[256,1024]{1,0:T(8,128)(2,1)S(1)}, u32[]{:S(2)}, u32[]{:S(2)}) collective-permute-start(bf16[256,1024]{1,0:T(8,128)(2,1)S(1)} %get-tuple-element.114), channel_id=1, source_target_pairs={{0,8},{8,0},{16,24},{24,16},{1,9},{9,1},{17,25},{25,17},{2,10},{10... | collective-permute-start | bytes 1572872 | tf_op jit(solution)/shard_map/ppermute | solution.py:125
  232.4 7.9 %collective-permute-start.34 = (bf16[256,1024]{1,0:T(8,128)(2,1)S(1)}, bf16[256,1024]{1,0:T(8,128)(2,1)S(1)}, u32[]{:S(2)}, u32[]{:S(2)}) collective-permute-start(bf16[256,1024]{1,0:T(8,128)(2,1)S(1)} %get-tuple-element.118), channel_id=1, source_target_pairs={{0,8},{8,0},{16,24},{24,16},{1,9},{9,1},{17,25},{25,17},{2,10},{10... | collective-permute-start | bytes 1572872 | tf_op jit(solution)/shard_map/ppermute | solution.py:125
  238.2 15.0 %collective-permute-start.28 = (bf16[256,1024]{1,0:T(8,128)(2,1)S(1)}, bf16[256,1024]{1,0:T(8,128)(2,1)S(1)}, u32[]{:S(2)}, u32[]{:S(2)}) collective-permute-start(bf16[256,1024]{1,0:T(8,128)(2,1)S(1)} %shard_map.90), channel_id=1, source_target_pairs={{0,8},{8,0},{16,24},{24,16},{1,9},{9,1},{17,25},{25,17},{2,10},{10... | collective-permute-start | bytes 1572872 | tf_op jit(solution)/shard_map/ppermute | solution.py:125
  238.7 13.9 %collective-permute-start.23 = (bf16[256,1024]{1,0:T(8,128)(2,1)S(1)}, bf16[256,1024]{1,0:T(8,128)(2,1)S(1)}, u32[]{:S(2)}, u32[]{:S(2)}) collective-permute-start(bf16[256,1024]{1,0:T(8,128)(2,1)S(1)} %shard_map.87), channel_id=1, source_target_pairs={{0,16},{8,24},{16,0},{24,8},{1,17},{9,25},{17,1},{25,9},{2,18},{10... | collective-permute-start | bytes 1572872 | tf_op jit(solution)/shard_map/ppermute | solution.py:125
  241.7 18.4 %collective-permute-start.35 = (bf16[256,1024]{1,0:T(8,128)(2,1)S(1)}, bf16[256,1024]{1,0:T(8,128)(2,1)S(1)}, u32[]{:S(2)}, u32[]{:S(2)}) collective-permute-start(bf16[256,1024]{1,0:T(8,128)(2,1)S(1)} %convolution_convert_fusion.8), channel_id=1, source_target_pairs={{0,1},{1,0},{2,3},{3,2},{4,5},{5,4},{6,7},{7,6},{8,9},{9,8},{10,11... | collective-permute-start | bytes 1572872 | tf_op jit(solution)/shard_map/ppermute | solution.py:118
  252.9 8.7 %collective-permute-start.24 = (bf16[256,1024]{1,0:T(8,128)(2,1)S(1)}, bf16[256,1024]{1,0:T(8,128)(2,1)S(1)}, u32[]{:S(2)}, u32[]{:S(2)}) collective-permute-start(bf16[256,1024]{1,0:T(8,128)(2,1)S(1)} %get-tuple-element.112), channel_id=1, source_target_pairs={{0,8},{8,0},{16,24},{24,16},{1,9},{9,1},{17,25},{25,17},{2,10},{10... | collective-permute-start | bytes 1572872 | tf_op jit(solution)/shard_map/ppermute | solution.py:125
  257.2 14.4 %collective-permute-start.29 = (bf16[256,1024]{1,0:T(8,128)(2,1)S(1)}, bf16[256,1024]{1,0:T(8,128)(2,1)S(1)}, u32[]{:S(2)}, u32[]{:S(2)}) collective-permute-start(bf16[256,1024]{1,0:T(8,128)(2,1)S(1)} %shard_map.91), channel_id=1, source_target_pairs={{0,16},{8,24},{16,0},{24,8},{1,17},{9,25},{17,1},{25,9},{2,18},{10... | collective-permute-start | bytes 1572872 | tf_op jit(solution)/shard_map/ppermute | solution.py:125
  260.0 14.1 %collective-permute-start.36 = (bf16[256,1024]{1,0:T(8,128)(2,1)S(1)}, bf16[256,1024]{1,0:T(8,128)(2,1)S(1)}, u32[]{:S(2)}, u32[]{:S(2)}) collective-permute-start(bf16[256,1024]{1,0:T(8,128)(2,1)S(1)} %convolution_convert_fusion.7), channel_id=1, source_target_pairs={{0,1},{1,0},{2,3},{3,2},{4,5},{5,4},{6,7},{7,6},{8,9},{9,8},{10,11... | collective-permute-start | bytes 1572872 | tf_op jit(solution)/shard_map/ppermute | solution.py:118
  271.8 3.8 collective-permute-start.30
  274.1 13.6 %collective-permute-start.37 = (bf16[256,1024]{1,0:T(8,128)(2,1)S(1)}, bf16[256,1024]{1,0:T(8,128)(2,1)S(1)}, u32[]{:S(2)}, u32[]{:S(2)}) collective-permute-start(bf16[256,1024]{1,0:T(8,128)(2,1)S(1)} %convolution_convert_fusion.6), channel_id=1, source_target_pairs={{0,1},{1,0},{2,3},{3,2},{4,5},{5,4},{6,7},{7,6},{8,9},{9,8},{10,11... | collective-permute-start | bytes 1572872 | tf_op jit(solution)/shard_map/ppermute | solution.py:118
  287.7 12.7 %collective-permute-start.38 = (bf16[256,1024]{1,0:T(8,128)(2,1)S(1)}, bf16[256,1024]{1,0:T(8,128)(2,1)S(1)}, u32[]{:S(2)}, u32[]{:S(2)}) collective-permute-start(bf16[256,1024]{1,0:T(8,128)(2,1)S(1)} %convolution_convert_fusion.5), channel_id=1, source_target_pairs={{0,1},{1,0},{2,3},{3,2},{4,5},{5,4},{6,7},{7,6},{8,9},{9,8},{10,11... | collective-permute-start | bytes 1572872 | tf_op jit(solution)/shard_map/ppermute | solution.py:118
  302.0 7.1 %collective-permute-start.39 = (bf16[2,128,1024]{2,1,0:T(8,128)(2,1)S(1)}, bf16[2,128,1024]{2,1,0:T(8,128)(2,1)S(1)}, u32[]{:S(2)}, u32[]{:S(2)}) collective-permute-start(bf16[2,128,1024]{2,1,0:T(8,128)(2,1)S(1)} %get-tuple-element.131), channel_id=1, source_target_pairs={{0,8},{8,0},{16,24},{24,16},{1,9},{9,1},{17,25},{25,17},{2,10},{10... | collective-permute-start | bytes 1572872 | tf_op jit(solution)/shard_map/ppermute | solution.py:125
  302.1 28.8 %collective-permute-start.42 = (bf16[2,128,1024]{2,1,0:T(8,128)(2,1)S(1)}, bf16[2,128,1024]{2,1,0:T(8,128)(2,1)S(1)}, u32[]{:S(2)}, u32[]{:S(2)}) collective-permute-start(bf16[2,128,1024]{2,1,0:T(8,128)(2,1)S(1)} %get-tuple-element.88), channel_id=1, source_target_pairs={{0,24},{8,16},{16,8},{24,0},{1,25},{9,17},{17,9},{25,1},{2,26},{10... | collective-permute-start | bytes 1572872 | tf_op jit(solution)/shard_map/ppermute | solution.py:125
  304.6 23.7 %collective-permute-start.41 = (bf16[2,128,1024]{2,1,0:T(8,128)(2,1)S(1)}, bf16[2,128,1024]{2,1,0:T(8,128)(2,1)S(1)}, u32[]{:S(2)}, u32[]{:S(2)}) collective-permute-start(bf16[2,128,1024]{2,1,0:T(8,128)(2,1)S(1)} %get-tuple-element.84), channel_id=1, source_target_pairs={{0,16},{8,24},{16,0},{24,8},{1,17},{9,25},{17,1},{25,9},{2,18},{10... | collective-permute-start | bytes 1572872 | tf_op jit(solution)/shard_map/ppermute | solution.py:125
  307.6 25.3 %collective-permute-start.44 = (bf16[1024,256]{1,0:T(8,128)(2,1)S(1)}, bf16[1024,256]{1,0:T(8,128)(2,1)S(1)}, u32[]{:S(2)}, u32[]{:S(2)}) collective-permute-start(bf16[1024,256]{1,0:T(8,128)(2,1)S(1)} %get-tuple-element.92), channel_id=1, source_target_pairs={{0,1},{1,0},{2,3},{3,2},{4,5},{5,4},{6,7},{7,6},{8,9},{9,8},{10,11... | collective-permute-start | bytes 1572872 | tf_op jit(solution)/shard_map/ppermute | solution.py:118
  311.7 32.8 %collective-permute-start.40 = (bf16[1024,256]{1,0:T(8,128)(2,1)S(1)}, bf16[1024,256]{1,0:T(8,128)(2,1)S(1)}, u32[]{:S(2)}, u32[]{:S(2)}) collective-permute-start(bf16[1024,256]{1,0:T(8,128)(2,1)S(1)} %get-tuple-element.83), channel_id=1, source_target_pairs={{0,8},{8,0},{16,24},{24,16},{1,9},{9,1},{17,25},{25,17},{2,10},{10... | collective-permute-start | bytes 1572872 | tf_op jit(solution)/shard_map/ppermute | solution.py:125
  330.9 13.7 %collective-permute-start.43 = (bf16[1024,256]{1,0:T(8,128)(2,1)S(1)}, bf16[1024,256]{1,0:T(8,128)(2,1)S(1)}, u32[]{:S(2)}, u32[]{:S(2)}) collective-permute-start(bf16[1024,256]{1,0:T(8,128)(2,1)S(1)} %get-tuple-element.89), channel_id=1, source_target_pairs={{0,16},{8,24},{16,0},{24,8},{1,17},{9,25},{17,1},{25,9},{2,18},{10... | collective-permute-start | bytes 1572872 | tf_op jit(solution)/shard_map/ppermute | solution.py:125
  344.5 15.8 %collective-permute-start.45 = (bf16[1024,256]{1,0:T(8,128)(2,1)S(1)}, bf16[1024,256]{1,0:T(8,128)(2,1)S(1)}, u32[]{:S(2)}, u32[]{:S(2)}) collective-permute-start(bf16[1024,256]{1,0:T(8,128)(2,1)S(1)} %get-tuple-element.96), channel_id=1, source_target_pairs={{0,24},{8,16},{16,8},{24,0},{1,25},{9,17},{17,9},{25,1},{2,26},{10... | collective-permute-start | bytes 1572872 | tf_op jit(solution)/shard_map/ppermute | solution.py:125
  344.6 14.3 %collective-permute-start.46 = (bf16[1024,256]{1,0:T(8,128)(2,1)S(1)}, bf16[1024,256]{1,0:T(8,128)(2,1)S(1)}, u32[]{:S(2)}, u32[]{:S(2)}) collective-permute-start(bf16[1024,256]{1,0:T(8,128)(2,1)S(1)} %collective-permute-done.40), channel_id=1, source_target_pairs={{0,1},{1,0},{2,3},{3,2},{4,5},{5,4},{6,7},{7,6},{8,9},{9,8},{10,11... | collective-permute-start | bytes 1572872 | tf_op jit(solution)/shard_map/ppermute | solution.py:118
  358.9 14.1 %collective-permute-start.47 = (bf16[1024,256]{1,0:T(8,128)(2,1)S(1)}, bf16[1024,256]{1,0:T(8,128)(2,1)S(1)}, u32[]{:S(2)}, u32[]{:S(2)}) collective-permute-start(bf16[1024,256]{1,0:T(8,128)(2,1)S(1)} %collective-permute-done.43), channel_id=1, source_target_pairs={{0,1},{1,0},{2,3},{3,2},{4,5},{5,4},{6,7},{7,6},{8,9},{9,8},{10,11... | collective-permute-start | bytes 1572872 | tf_op jit(solution)/shard_map/ppermute | solution.py:118
  361.2 13.4 %collective-permute-start.52 = (bf16[1024,256]{1,0:T(8,128)(2,1)S(1)}, bf16[1024,256]{1,0:T(8,128)(2,1)S(1)}, u32[]{:S(2)}, u32[]{:S(2)}) collective-permute-start(bf16[1024,256]{1,0:T(8,128)(2,1)S(1)} %convolution_convert_fusion.4), channel_id=1, source_target_pairs={{0,8},{8,0},{16,24},{24,16},{1,9},{9,1},{17,25},{25,17},{2,10},{10... | collective-permute-start | bytes 1572872 | tf_op jit(solution)/shard_map/ppermute | solution.py:125
  373.0 13.3 %collective-permute-start.48 = (bf16[1024,256]{1,0:T(8,128)(2,1)S(1)}, bf16[1024,256]{1,0:T(8,128)(2,1)S(1)}, u32[]{:S(2)}, u32[]{:S(2)}) collective-permute-start(bf16[1024,256]{1,0:T(8,128)(2,1)S(1)} %collective-permute-done.45), channel_id=1, source_target_pairs={{0,1},{1,0},{2,3},{3,2},{4,5},{5,4},{6,7},{7,6},{8,9},{9,8},{10,11... | collective-permute-start | bytes 1572872 | tf_op jit(solution)/shard_map/ppermute | solution.py:118
  375.3 13.8 %collective-permute-start.53 = (bf16[1024,256]{1,0:T(8,128)(2,1)S(1)}, bf16[1024,256]{1,0:T(8,128)(2,1)S(1)}, u32[]{:S(2)}, u32[]{:S(2)}) collective-permute-start(bf16[1024,256]{1,0:T(8,128)(2,1)S(1)} %fusion.7), channel_id=1, source_target_pairs={{0,16},{8,24},{16,0},{24,8},{1,17},{9,25},{17,1},{25,9},{2,18},{10... | collective-permute-start | bytes 1572872 | tf_op jit(solution)/shard_map/ppermute | solution.py:125
  389.9 14.0 %collective-permute-start.55 = (bf16[1024,256]{1,0:T(8,128)(2,1)S(1)}, bf16[1024,256]{1,0:T(8,128)(2,1)S(1)}, u32[]{:S(2)}, u32[]{:S(2)}) collective-permute-start(bf16[1024,256]{1,0:T(8,128)(2,1)S(1)} %fusion.8), channel_id=1, source_target_pairs={{0,16},{8,24},{16,0},{24,8},{1,17},{9,25},{17,1},{25,9},{2,18},{10... | collective-permute-start | bytes 1572872 | tf_op jit(solution)/shard_map/ppermute | solution.py:125
  392.0 15.0 %collective-permute-start.50 = (bf16[2048,256]{1,0:T(8,128)(2,1)S(1)}, bf16[2048,256]{1,0:T(8,128)(2,1)S(1)}, u32[]{:S(2)}, u32[]{:S(2)}) collective-permute-start(bf16[2048,256]{1,0:T(8,128)(2,1)S(1)} %convolution_convert_fusion.1), channel_id=1, source_target_pairs={{0,8},{8,0},{16,24},{24,16},{1,9},{9,1},{17,25},{25,17},{2,10},{10... | collective-permute-start | bytes 3145736 | tf_op jit(solution)/shard_map/ppermute | solution.py:125
  403.9 24.4 %collective-permute-start.56 = (bf16[2048,256]{1,0:T(8,128)(2,1)S(1)}, bf16[2048,256]{1,0:T(8,128)(2,1)S(1)}, u32[]{:S(2)}, u32[]{:S(2)}) collective-permute-start(bf16[2048,256]{1,0:T(8,128)(2,1)S(1)} %fusion.2), channel_id=1, source_target_pairs={{0,16},{8,24},{16,0},{24,8},{1,17},{9,25},{17,1},{25,9},{2,18},{10... | collective-permute-start | bytes 3145736 | tf_op jit(solution)/shard_map/ppermute | solution.py:125
  404.8 8.9 %collective-permute-start.61 = (bf16[1024,256]{1,0:T(8,128)(2,1)S(1)}, bf16[1024,256]{1,0:T(8,128)(2,1)S(1)}, u32[]{:S(2)}, u32[]{:S(2)}) collective-permute-start(bf16[1024,256]{1,0:T(8,128)(2,1)S(1)} %add_convert_fusion.8.refs_2_), channel_id=1, source_target_pairs={{0,8},{8,0},{16,24},{24,16},{1,9},{9,1},{17,25},{25,17},{2,10},{10... | collective-permute-start | bytes 1572872 | tf_op jit(solution)/shard_map/ppermute | solution.py:125
  405.0 8.7 %collective-permute-start.62 = (bf16[1024,256]{1,0:T(8,128)(2,1)S(1)}, bf16[1024,256]{1,0:T(8,128)(2,1)S(1)}, u32[]{:S(2)}, u32[]{:S(2)}) collective-permute-start(bf16[1024,256]{1,0:T(8,128)(2,1)S(1)} %add_convert_fusion.7.refs_3_), channel_id=1, source_target_pairs={{0,8},{8,0},{16,24},{24,16},{1,9},{9,1},{17,25},{25,17},{2,10},{10... | collective-permute-start | bytes 1572872 | tf_op jit(solution)/shard_map/ppermute | solution.py:125
  406.9 24.5 %collective-permute-start.49 = (bf16[2048,256]{1,0:T(8,128)(2,1)S(1)}, bf16[2048,256]{1,0:T(8,128)(2,1)S(1)}, u32[]{:S(2)}, u32[]{:S(2)}) collective-permute-start(bf16[2048,256]{1,0:T(8,128)(2,1)S(1)} %convolution_convert_fusion.2), channel_id=1, source_target_pairs={{0,8},{8,0},{16,24},{24,16},{1,9},{9,1},{17,25},{25,17},{2,10},{10... | collective-permute-start | bytes 3145736 | tf_op jit(solution)/shard_map/ppermute | solution.py:125
  428.3 23.5 %collective-permute-start.57 = (bf16[2048,256]{1,0:T(8,128)(2,1)S(1)}, bf16[2048,256]{1,0:T(8,128)(2,1)S(1)}, u32[]{:S(2)}, u32[]{:S(2)}) collective-permute-start(bf16[2048,256]{1,0:T(8,128)(2,1)S(1)} %fusion.1), channel_id=1, source_target_pairs={{0,16},{8,24},{16,0},{24,8},{1,17},{9,25},{17,1},{25,9},{2,18},{10... | collective-permute-start | bytes 3145736 | tf_op jit(solution)/shard_map/ppermute | solution.py:125
  429.2 50.7 %collective-permute-start.63 = (bf16[2048,512]{1,0:T(8,128)(2,1)S(1)}, bf16[2048,512]{1,0:T(8,128)(2,1)S(1)}, u32[]{:S(2)}, u32[]{:S(2)}) collective-permute-start(bf16[2048,512]{1,0:T(8,128)(2,1)S(1)} %pad_maximum_fusion.3), channel_id=1, source_target_pairs={{0,2},{1,3},{2,4},{3,5},{4,6},{5,7},{6,0},{7,1},{8,10},{9,11},{10,... | collective-permute-start | bytes 6291464 | tf_op jit(solution)/shard_map/ppermute | solution.py:122
  431.3 27.1 %collective-permute-start.59 = (bf16[2048,256]{1,0:T(8,128)(2,1)S(1)}, bf16[2048,256]{1,0:T(8,128)(2,1)S(1)}, u32[]{:S(2)}, u32[]{:S(2)}) collective-permute-start(bf16[2048,256]{1,0:T(8,128)(2,1)S(1)} %add_convert_fusion.5), channel_id=1, source_target_pairs={{0,8},{8,0},{16,24},{24,16},{1,9},{9,1},{17,25},{25,17},{2,10},{10... | collective-permute-start | bytes 3145736 | tf_op jit(solution)/shard_map/ppermute | solution.py:125
  452.0 21.0 %collective-permute-start.64 = (bf16[2048,256]{1,0:T(8,128)(2,1)S(1)}, bf16[2048,256]{1,0:T(8,128)(2,1)S(1)}, u32[]{:S(2)}, u32[]{:S(2)}) collective-permute-start(bf16[2048,256]{1,0:T(8,128)(2,1)S(1)} %add_convert_fusion.4), channel_id=1, source_target_pairs={{0,8},{8,0},{16,24},{24,16},{1,9},{9,1},{17,25},{25,17},{2,10},{10... | collective-permute-start | bytes 3145736 | tf_op jit(solution)/shard_map/ppermute | solution.py:125
  457.7 25.6 %collective-permute-start.58 = (bf16[2048,256]{1,0:T(8,128)(2,1)S(1)}, bf16[2048,256]{1,0:T(8,128)(2,1)S(1)}, u32[]{:S(2)}, u32[]{:S(2)}) collective-permute-start(bf16[2048,256]{1,0:T(8,128)(2,1)S(1)} %fusion), channel_id=1, source_target_pairs={{0,16},{8,24},{16,0},{24,8},{1,17},{9,25},{17,1},{25,9},{2,18},{10... | collective-permute-start | bytes 3145736 | tf_op jit(solution)/shard_map/ppermute | solution.py:125
  465.5 59.2 %collective-permute-start.60 = (bf16[2048,512]{1,0:T(8,128)(2,1)}, bf16[2048,512]{1,0:T(8,128)(2,1)S(1)}, u32[]{:S(2)}, u32[]{:S(2)}) collective-permute-start(bf16[2048,512]{1,0:T(8,128)(2,1)} %pad_maximum_fusion.2), channel_id=1, source_target_pairs={{0,6},{1,7},{2,0},{3,1},{4,2},{5,3},{6,4},{7,5},{8,14},{9,15},{10,... | collective-permute-start | bytes 6291464 | tf_op jit(solution)/shard_map/ppermute | solution.py:122
  481.9 85.1 %collective-permute-start.65 = (bf16[2048,512]{1,0:T(8,128)(2,1)}, bf16[2048,512]{1,0:T(8,128)(2,1)}, u32[]{:S(2)}, u32[]{:S(2)}) collective-permute-start(bf16[2048,512]{1,0:T(8,128)(2,1)} %pad_maximum_fusion.4), channel_id=1, source_target_pairs={{0,2},{1,3},{2,4},{3,5},{4,6},{5,7},{6,0},{7,1},{8,10},{9,11},{10,... | collective-permute-start | bytes 6291464 | tf_op jit(solution)/shard_map/ppermute | solution.py:122
  483.5 5.6 collective-permute-start.66
  (22 other events, 107.1 us)
